TPU v7x, 32 devices: a whole 2x2x4 slice. The times are simulated.
32 devices in a mesh: lat: 16 (over z, x, core), chan: 2 (over y).
Axes of the slice: x: 2, y: 2, z: 4, core: 2. Of those that a mesh axis runs over, the one named last changes fastest.
Arguments:
- grid: bfloat16 [384, 720, 512], P('lat', None, 'chan'), may hold values from -6 to 6
- basis: float32 [384, 384, 384], P('lat'), may hold values from -16 to 16, as said below
- mix_weight: bfloat16 [2, 512, 512], P(None, None, 'chan'), may hold values from -0.1875 to 0.1875
- spectral_gain: float32 [384], replicated, may hold values from 0.5 to 4
- conv_weight: float32 [9, 512], P(None, 'chan'), may hold values from -2 to 2
- lat_offsets: int32 [9], replicated, may hold values from -1 to 1
- lon_offsets: int32 [9], replicated, may hold values from -3 to 3
- ln_gain: float32 [512], replicated, may hold values from 0.1 to 1.9
- up_weight: bfloat16 [512, 512], replicated, may hold values from -0.25 to 0.25
- down_weight: bfloat16 [512, 512], replicated, may hold values from -0.25 to 0.25
Outputs:
- result: bfloat16 [384, 720, 512], P('lat', None, 'chan')
Inputs may be any that keep to these rules, and one draw needn't show every extreme that they name: basis[m, l, t] is the orthonormal associated Legendre function of degree l and order m at cos(theta_t) times a factor between 0.8 and 1.25; it is zero for l < m.
All inputs are finite; a program needn't handle non-finite values.
Results may differ from a plain program's by a relative error of at most 0.01.
Values may be sent and summed in bfloat16 or wider, within the bound.
No kernel may reach another device: no remote copies, remote signals or barrier semaphores. Data moves between devices by JAX's collectives and lax.ppermute only.
A program may use at most 192 MiB of HBM per device.

v0:
```python
import math

import jax
import jax.numpy as jnp
from jax import lax
from jax.sharding import PartitionSpec as P

MMAX = 384
L = 384


def padded_2(value, sides, width):
    for axis, dim in sides:
        size, length = (lax.axis_size(axis), value.shape[dim])
        up = [(i, (i + 1) % size) for i in range(size - 1)]
        down = [(j, i) for i, j in up]
        last = lax.slice_in_dim(value, length - width, length, axis=dim)
        first = lax.slice_in_dim(value, 0, width, axis=dim)
        before = lax.ppermute(last, axis, up)
        after = lax.ppermute(first, axis, down)
        value = jnp.concatenate([before, value, after], axis=dim)
    return value


def cycle_angle(rows, nlat):
    return math.pi * (rows.astype(jnp.float32) + 0.5) / nlat


def complex_mix(real_in, imag_in, real_w, imag_w):
    real_out = jnp.dot(real_in, real_w, preferred_element_type=jnp.float32) - jnp.dot(
        imag_in, imag_w, preferred_element_type=jnp.float32
    )
    imag_out = jnp.dot(real_in, imag_w, preferred_element_type=jnp.float32) + jnp.dot(
        imag_in, real_w, preferred_element_type=jnp.float32
    )
    return (real_out, imag_out)


def on_device(
    grid,
    basis,
    mix_weight,
    spectral_gain,
    conv_weight,
    lat_offsets,
    lon_offsets,
    ln_gain,
    up_weight,
    down_weight,
):
    cycles, nlon, width = grid.shape
    groups = lax.axis_size("lat")
    rank = lax.axis_index("lat")
    nlat = cycles * groups
    modes = basis.shape[0]
    points = jnp.arange(nlon, dtype=jnp.int32)
    all_orders = jnp.arange(MMAX, dtype=jnp.int32)
    phase = points[:, None] * all_orders[None, :] % nlon
    angle = 2.0 * math.pi * phase.astype(jnp.float32) / nlon
    fwd_table = (
        jnp.stack([jnp.cos(angle), -jnp.sin(angle)], axis=-1)
        .reshape(nlon, 2 * MMAX)
        .astype(jnp.bfloat16)
    )
    weight_m = jnp.where(all_orders == 0, 1.0, 2.0).astype(jnp.float32)[None, :]
    inv_table = (
        jnp.stack([weight_m * jnp.cos(angle), -weight_m * jnp.sin(angle)], axis=-1)
        .reshape(nlon, 2 * MMAX)
        .T.astype(jnp.bfloat16)
    )
    spec = jnp.einsum("tpc,pk->tkc", grid, fwd_table, preferred_element_type=jnp.float32) * (
        1.0 / nlon
    )
    spec = spec.astype(jnp.bfloat16).reshape(cycles, groups, modes, 2, width)
    gathered = lax.all_to_all(spec, "lat", split_axis=1, concat_axis=0, tiled=True).reshape(
        nlat, modes, 2 * width
    )
    theta = cycle_angle(jnp.arange(nlat, dtype=jnp.int32), nlat)
    quad = math.pi / nlat * jnp.sin(theta)
    fwd_leg = (basis * quad[None, None, :]).astype(jnp.bfloat16)
    inv_leg = basis.astype(jnp.bfloat16)
    coeff = jnp.einsum(
        "jlt,tjk->jlk", fwd_leg, gathered, preferred_element_type=jnp.float32
    ).astype(jnp.bfloat16)
    coeff = coeff.reshape(modes, L, 2, width)
    piece = lax.all_gather(coeff, "chan", axis=3, tiled=True)
    count = piece.shape[3]
    real_w = mix_weight[0]
    imag_w = mix_weight[1]
    real_out, imag_out = complex_mix(
        piece[:, :, 0, :].reshape(-1, count), piece[:, :, 1, :].reshape(-1, count), real_w, imag_w
    )
    summed_modes = jnp.concatenate([real_out, imag_out], axis=1)
    mixed = (summed_modes.reshape(modes, L, 2 * width) * spectral_gain[None, :, None]).astype(
        jnp.bfloat16
    )
    back = jnp.einsum("jlt,jlk->tjk", inv_leg, mixed, preferred_element_type=jnp.float32).astype(
        jnp.bfloat16
    )
    back = lax.all_to_all(
        back.reshape(nlat, 1, modes, 2, width), "lat", split_axis=0, concat_axis=1, tiled=True
    )
    back = back.reshape(cycles, 2 * MMAX, width)
    spectral = jnp.einsum("tkc,kp->tpc", back, inv_table, preferred_element_type=jnp.float32)
    padded = padded_2(grid, (("lat", 0),), 1)
    own_cycles = rank * cycles + jnp.arange(cycles, dtype=jnp.int32)
    here = jnp.sin(cycle_angle(own_cycles, nlat))
    local = jnp.zeros((cycles, nlon, width), jnp.float32)
    for tap in range(conv_weight.shape[0]):
        shift = lat_offsets[tap]
        source = lax.dynamic_slice_in_dim(padded, 1 + shift, cycles, 0)
        source = jnp.roll(source, -lon_offsets[tap], axis=1)
        ratio = (jnp.sin(cycle_angle(own_cycles + shift, nlat)) / here)[:, None, None]
        local = local + conv_weight[tap][None, None, :] * ratio * source.astype(jnp.float32)
    summed = (spectral + local + grid.astype(jnp.float32)).astype(jnp.bfloat16)
    block = lax.all_to_all(summed, "chan", split_axis=1, concat_axis=2, tiled=True)
    count, span, channels = block.shape
    rows = block.reshape(-1, channels).astype(jnp.float32)
    center = jnp.mean(rows, axis=-1, keepdims=True)
    spread = jnp.mean((rows - center) ** 2, axis=-1, keepdims=True)
    normed = ((rows - center) / jnp.sqrt(spread + 1e-05) * ln_gain).astype(jnp.bfloat16)
    hidden = jax.nn.gelu(
        jnp.dot(normed, up_weight, preferred_element_type=jnp.float32), approximate=True
    ).astype(jnp.bfloat16)
    output = (jnp.dot(hidden, down_weight, preferred_element_type=jnp.float32) + rows).astype(
        jnp.bfloat16
    )
    return lax.all_to_all(
        output.reshape(count, span, channels), "chan", split_axis=2, concat_axis=1, tiled=True
    )


def solution(mesh):
    return jax.shard_map(
        on_device,
        mesh=mesh,
        in_specs=(
            P("lat", None, "chan"),
            P("lat", None, None),
            P(None, None, "chan"),
            P(),
            P(None, "chan"),
            P(),
            P(),
            P(),
            P(),
            P(),
        ),
        out_specs=P("lat", None, "chan"),
        check_vma=False,
    )
```

profile of v0, /device:TPU:26, one launch (start us, length us, event | category | flops | bytes accessed | tf_op | source)
XLA Modules:
  0.0 1543.9 jit_solution(14814724098846459203)
XLA Ops:
  14.3 13.0 fusion.13
  27.4 14.5 reshape.566
  58.2 203.4 %all-to-all-done = bf16[24,16,24,2,256]{4,3,2,0,1:T(2,128)(2,1)} async-done(((bf16[24,16,24,2,256]{4,3,2,0,1:T(2,128)(2,1)}), bf16[24,16,24,2,256]{4,3,2,0,1:T(2,128)(2,1)}, u32[]{:S(2)}, u32[]{:S(2)}) %all-to-all-start) | async-done | bytes 9437216 | tf_op jit(solution)/shard_map/all_to_all | solution.py:75
  261.6 15.6 %reshape.578 = bf16[384,24,512]{2,1,0:T(8,128)(2,1)} reshape(bf16[16,24,1,24,2,256]{5,4,3,1,0,2:T(2,128)(2,1)} %bitcast.4) | data formatting | bytes 18874368 | tf_op jit(solution)/shard_map/reshape | solution.py:75
  277.3 21.2 %fusion.35 = bf16[24,384,512]{2,1,0:T(8,128)(2,1)} fusion(bf16[384,24,512]{2,1,0:T(8,128)(2,1)} %reshape.578, f32[24,384,384]{2,1,0:T(8,128)} %param.13, f32[384]{0:T(512)S(1)} %sine_multiply_fusion), kind=kOutput, calls=%fused_computation.64 | convolution fusion | flops 3635675136 | bytes 33031680 | tf_op jit(solution)/shard_map/jlt,tjk->jlk/dot_general | solution.py:82
  307.1 225.4 %all-gather.2.cloned.1.call-done = bf16[24,384,2,512]{3,1,0,2:T(8,128)(2,1)} async-done(((bf16[24,384,2,256]{3,1,0,2:T(8,128)(2,1)}), bf16[24,384,2,512]{3,1,0,2:T(8,128)(2,1)}) %all-gather.2.cloned.1.call-update) | async-done | bytes 18874384 | tf_op jit(solution)/shard_map/all_gather | solution.py:86
  554.2 13.7 convolution_subtract_fusion
  568.0 14.1 convolution_add_fusion
  582.1 14.3 pad_maximum_fusion
  596.4 17.2 %fusion.38 = bf16[24,512,384]{2,1,0:T(8,128)(2,1)} fusion(f32[24,384,384]{2,1,0:T(8,128)} %param.13, f32[64,24,8,384]{3,2,1,0:T(8,128)} %bitcast.109, f32[384]{0:T(512)S(1)} %copy-done.4), kind=kOutput, calls=%fused_computation.65 | convolution fusion | flops 3641573376 | bytes 42468864 | tf_op jit(solution)/shard_map/jlt,jlk->tjk/dot_general | solution.py:97
  675.7 13.0 collective-permute-done
  698.8 53.8 %constant_dynamic-slice_fusion.8 = (bf16[24,720,256]{2,1,0:T(8,128)(2,1)}, bf16[24,720,256]{2,1,0:T(8,128)(2,1)}, bf16[24,720,256]{2,1,0:T(8,128)(2,1)}, bf16[24...) fusion(bf16[26,720,256]{2,1,0:T(8,128)(2,1)} %constant_dynamic-, ...), kind=kLoop, calls=%fused_computation.115 | loop fusion | bytes 159252512 | tf_op jit(solution)/shard_map/dynamic_slice | solution.py:111
  752.6 83.7 %all-to-all-done.1 = bf16[384,1,24,2,256]{4,2,3,1,0:T(8,128)(2,1)} async-done(((bf16[384,1,24,2,256]{4,2,3,1,0:T(8,128)(2,1)}), bf16[384,1,24,2,256]{4,2,3,1,0:T(8,128)(2,1)}, u32[]{:S(2)}, u32[]{:S(2)}) %all-to-all-start.1) | async-done | bytes 9437216 | tf_op jit(solution)/shard_map/all_to_all | solution.py:100
  836.3 14.8 copy.45
  851.0 14.5 reshape.571
  865.6 90.5 %fusion.12 = bf16[24,720,256]{2,1,0:T(8,128)(2,1)} fusion(bf16[24,720,256]{2,1,0:T(8,128)(2,1)} %param.12, s32[]{:T(128)S(6)} %select_n.125, bf16[24,720,256]{2,1,0:T(8,128)(2,1)} %get-tuple-element.9, s32[]{:T(128)S(6)} %select_n.123, bf16[24,720,256]{2,1,0:T(8,128)(2,1)} %get-tuple-element.10, s32[]{:T(128)S(6)} %select_n.121, ...), kind=kOutput, calls=%fused_computation.37 | convolution fusion | flops 7046922240 | bytes 108085280 | tf_op jit(solution)/shard_map/tkc,kp->tpc/dot_general | solution.py:104
  966.3 109.6 %all_to_all.57 = bf16[24,720,256]{2,0,1:T(8,128)(2,1)} all-to-all(bf16[24,720,256]{2,0,1:T(8,128)(2,1)} %copy.47), channel_id=1, replica_groups=mesh['lat'=16,'chan'=2] {'chan'}, dimensions={1} | all-to-all | bytes 17694720 | tf_op jit(solution)/shard_map/all_to_all | solution.py:116
  1086.9 129.2 %bitcast_reduce_fusion = f32[24,360]{1,0:T(8,128)S(1)} fusion(f32[24,2,360,256]{3,0,2,1:T(8,128)} %convert.21), kind=kLoop, calls=%fused_computation.31 | loop fusion | flops 4415040 | bytes 17729280 | tf_op jit(solution)/shard_map/reduce_sum | solution.py:119
  1216.2 127.1 %fusion.10 = f32[24,360]{1,0:T(8,128)S(1)} fusion(f32[24,360]{1,0:T(8,128)S(1)} %broadcast_multiply_fusion, f32[24,2,360,256]{3,0,2,1:T(8,128)} %convert.21), kind=kLoop, calls=%fused_computation.34 | loop fusion | flops 13262400 | bytes 17763840 | tf_op jit(solution)/shard_map/reduce_sum | solution.py:120
  1343.4 15.8 %copy.48 = f32[24,2,360,256]{3,1,2,0:T(2,128)} copy(bf16[24,2,360,256]{3,0,2,1:T(8,128)(2,1)} %bitcast.113) | data formatting | bytes 26542080 | tf_op jit(solution)/shard_map/convert_element_type | solution.py:118
  1359.4 13.3 copy.58
  1372.7 23.3 %add_convert_fusion = bf16[8640,512]{1,0:T(8,128)(2,1)} fusion(f32[8640,512]{1,0:T(8,128)} %bitcast.119, bf16[512,512]{1,0:T(8,128)(2,1)S(1)} %copy-done, bf16[512,512]{1,0:T(8,128)(2,1)S(1)} %copy-done.6, f32[512]{0:T(512)S(1)} %copy-done.7, f32[8640]{0:T(1024)S(1)} %sqrt.12, f32[8640]{0:T(1024)S(1)} %div.154), kind=kOutput, calls=%fused_computation.38 | convolution fusion | flops 9126051840 | bytes 27661824 | tf_op jit(solution)/shard_map/dot_general | solution.py:125
  1395.9 12.8 copy.49
  1408.7 115.4 %all_to_all.58 = bf16[24,360,512]{1,0,2:T(8,128)(2,1)} all-to-all(bf16[24,360,512]{1,0,2:T(8,128)(2,1)} %copy.49), channel_id=1, replica_groups=mesh['lat'=16,'chan'=2] {'chan'}, dimensions={2} | all-to-all | bytes 17694720 | tf_op jit(solution)/shard_map/all_to_all | solution.py:128
  (68 shorter events, 143.6 us)
Async XLA Ops:
  6.5 1366.1 %copy-start = (bf16[512,512]{1,0:T(8,128)(2,1)S(1)}, bf16[512,512]{1,0:T(8,128)(2,1)}, u32[]{:S(2)}) copy-start(bf16[512,512]{1,0:T(8,128)(2,1)} %param.21) | copy-start | bytes 1572868
  51.9 209.7 %all-to-all-start = ((bf16[24,16,24,2,256]{4,3,2,0,1:T(2,128)(2,1)}), bf16[24,16,24,2,256]{4,3,2,0,1:T(2,128)(2,1)}, u32[]{:S(2)}, u32[]{:S(2)}) async-start(bf16[24,16,24,2,256]{4,3,2,0,1:T(2,128)(2,1)} %copy.40), calls=%async_computation | async-start | bytes 18874368 | tf_op jit(solution)/shard_map/all_to_all | solution.py:75
  57.9 474.6 %all-gather.2.cloned.1.call-start = ((), (), s32[]{:S(2)}) async-start(), calls=%async_computation.4 | async-start | bytes 28311552 | tf_op jit(solution)/shard_map/all_gather | solution.py:86
  307.1 236.8 %copy-start.1 = (bf16[2,512,256]{2,1,0:T(8,128)(2,1)S(1)}, bf16[2,512,256]{2,1,0:T(8,128)(2,1)}, u32[]{:S(2)}) copy-start(bf16[2,512,256]{2,1,0:T(8,128)(2,1)} %param.14) | copy-start | bytes 1572868
  582.1 14.3 copy-start.4
  626.4 12.5 copy-start.2
  626.4 24.1 %copy-start.3 = (s32[9]{0:T(128)S(1)}, s32[9]{0:T(128)}, u32[]{:S(2)}) copy-start(s32[9]{0:T(128)} %param.18) | copy-start | bytes 112
  626.4 209.9 %all-to-all-start.1 = ((bf16[384,1,24,2,256]{4,2,3,1,0:T(8,128)(2,1)}), bf16[384,1,24,2,256]{4,2,3,1,0:T(8,128)(2,1)}, u32[]{:S(2)}, u32[]{:S(2)}) async-start(bf16[384,1,24,2,256]{4,2,3,1,0:T(8,128)(2,1)} %copy.44), calls=%async_computation.1 | async-start | bytes 18874368 | tf_op jit(solution)/shard_map/all_to_all | solution.py:100
  632.5 42.5 %copy-start.5 = (f32[9,256]{1,0:T(8,128)S(1)}, f32[9,256]{1,0:T(8,128)}, u32[]{:S(2)}) copy-start(f32[9,256]{1,0:T(8,128)} %param.16) | copy-start | bytes 27652
  634.5 63.5 %collective-permute-start.1 = (bf16[1,720,256]{2,1,0:T(8,128)(2,1)}, bf16[1,720,256]{2,1,0:T(8,128)(2,1)S(1)}, u32[]{:S(2)}, u32[]{:S(2)}) collective-permute-start(bf16[1,720,256]{2,1,0:T(8,128)(2,1)} %get-tuple-element.17), channel_id=1, source_target_pairs={{2,0},{4,2},{6,4},{8,6},{10,8},{12,10},{14,12},{16,14},{18,16},{20... | collective-permute-start | bytes 1105928 | tf_op jit(solution)/shard_map/ppermute | solution.py:20
  636.8 52.0 %collective-permute-start = (bf16[1,720,256]{2,1,0:T(8,128)(2,1)}, bf16[1,720,256]{2,1,0:T(8,128)(2,1)}, u32[]{:S(2)}, u32[]{:S(2)}) collective-permute-start(bf16[1,720,256]{2,1,0:T(8,128)(2,1)} %get-tuple-element.18), channel_id=1, source_target_pairs={{0,2},{2,4},{4,6},{6,8},{8,10},{10,12},{12,14},{14,16},{16,18},{18... | collective-permute-start | bytes 1105928 | tf_op jit(solution)/shard_map/ppermute | solution.py:19
  1359.3 13.3 copy-start.6
  1359.4 13.3 copy-start.7
Sparse Core Ops, SparseCore 0:
  307.2 225.2 all-gather.1
where the time goes:
time: 1550 us; the launch traced here: 1540 us
  waiting for transfers between devices  526 us (34%)
  other arithmetic  302 us (19%)
  local copies, waits for them, and re-layouts  240 us (15%)
  blocking collectives  225 us (15%)
  matrix products  203 us (13%)
  between operations  30.9 us (2%)
  starting transfers between devices  16.7 us (1%)
    all_gather x1, waiting for transfers between devices, on_device(): piece = lax.all_gather(coeff, 'chan', axis=3, tiled=True)  225 us
    all_to_all x1, waiting for transfers between devices, on_device(): lax.all_to_all(spec, 'lat', split_axis=1, concat_axis=0, tiled=True)  203 us
    reduce_sum x1, other arithmetic, on_device(): center = jnp.mean(rows, axis=-1, keepdims=True)  129 us
    reduce_sum x1, other arithmetic, on_device(): spread = jnp.mean((rows - center) ** 2, axis=-1, keepdims=True)  127 us
    all_to_all x1, blocking collectives, on_device(): lax.all_to_all(output.reshape(count, span, channels), 'chan', split_axis=...  115 us
    all_to_all x1, blocking collectives, on_device(): lax.all_to_all(summed, 'chan', split_axis=1, concat_axis=2, tiled=True)  110 us
    dot_general x1, matrix products, on_device(): jnp.einsum('tkc,kp->tpc', back, inv_table, preferred_element_type=jnp.flo...  90.5 us
    all_to_all x1, waiting for transfers between devices, on_device(): lax.all_to_all(back.reshape(nlat, 1, modes, 2, width), 'lat', split_axis=...  83.7 us
  transfers between devices with their start and end apart: 5, of which 4 were waited for; matrix products, arithmetic and copies ran while one was open for 6% of the time, Pallas kernels for 0%

commit v1 on v0

--- a/solution.py
+++ b/solution.py
@@ -1,12 +1,390 @@
+import functools
 import math
 
 import jax
 import jax.numpy as jnp
+import numpy as np
 from jax import lax
+from jax.experimental import pallas as pl
+from jax.experimental.pallas import tpu as pltpu
 from jax.sharding import PartitionSpec as P
 
 MMAX = 384
 L = 384
+STEP = 4
+LANES = 128
+NEAR = 1
+REACH = 3
+BF = jnp.bfloat16
+F32 = jnp.float32
+SWAP = [(0, 1), (1, 0)]
+
+
+def cycle_angle(rows, nlat):
+    return math.pi * (rows.astype(F32) + 0.5) / nlat
+
+
+def params(mib):
+    return pltpu.CompilerParams(vmem_limit_bytes=mib * 1024 * 1024)
+
+
+def cost(flops, nbytes):
+    return pl.CostEstimate(flops=int(flops), bytes_accessed=int(nbytes), transcendentals=0)
+
+
+def angle_table(nlon):
+    phase = np.arange(nlon)[:, None] * np.arange(MMAX)[None, :] % nlon
+    angle = (2.0 * math.pi * phase / nlon).astype(np.float32).astype(np.float64)
+    return np.cos(angle), np.sin(angle)
+
+
+def forward_kernel(scale, table_ref, grid_ref, out_ref, held):
+    cycles = grid_ref.shape[0]
+    rows = table_ref.shape[0]
+    for t in range(cycles):
+        value = jnp.dot(table_ref[...], grid_ref[t], preferred_element_type=F32)
+        value = value * scale
+        for at in range(held.shape[0]):
+            held[at, pl.ds(t, rows, stride=cycles), :] = value[:, at * LANES : (at + 1) * LANES]
+    for at in range(held.shape[0]):
+        lanes = slice(at * LANES, (at + 1) * LANES)
+        out_ref[:, :, lanes] = held[at].reshape(rows, cycles, LANES).astype(BF)
+
+
+def forward_part(grid, table):
+    cycles, nlon, width = grid.shape
+    rows = table.shape[0]
+    return pl.pallas_call(
+        functools.partial(forward_kernel, 1.0 / nlon),
+        out_shape=jax.ShapeDtypeStruct((rows, cycles, width), BF),
+        in_specs=[pl.BlockSpec(memory_space=pltpu.VMEM)] * 2,
+        out_specs=pl.BlockSpec(memory_space=pltpu.VMEM),
+        scratch_shapes=[pltpu.VMEM((width // LANES, rows * cycles, LANES), F32)],
+        compiler_params=params(40),
+        cost_estimate=cost(2 * rows * nlon * cycles * width, grid.size * 2),
+    )(table, grid)
+
+
+def middle_kernel(counts, at_ref, spec_ref, basis_ref, quad_ref, mix_ref, gain_ref, *rest):
+    outs, held = (rest[-len(counts) - 1 : -1], rest[-1])
+    mode = pl.program_id(0)
+    groups, sides, _, _, cycles, width = spec_ref.shape
+    nlat = groups * cycles
+    table = basis_ref[0]
+    forward = (table * quad_ref[...]).astype(BF)
+    pieces = []
+    for side in range(sides):
+        for part in range(2):
+            piece = spec_ref[:, side, 0, part, :, :].astype(F32)
+            pieces.append(piece.reshape(nlat, width).astype(BF))
+    spec = jnp.concatenate(pieces, axis=1)
+    coeff = jnp.dot(forward, spec, preferred_element_type=F32).astype(BF)
+    mixed = jnp.dot(coeff, mix_ref[...], preferred_element_type=F32) * gain_ref[...]
+    inverse = table.T.astype(BF)
+    back = jnp.dot(inverse, mixed.astype(BF), preferred_element_type=F32)
+    half = back.shape[1] // 2
+    slots = 2 * STEP
+    for part in range(2):
+        for where in range(STEP):
+
+            @pl.when(mode == where)
+            def _():
+                row = 2 * where + part
+                for at in range(half // LANES):
+                    low = part * half + at * LANES
+                    held[at, pl.ds(row, nlat, stride=slots), :] = back[:, low : low + LANES]
+
+    @pl.when(mode == STEP - 1)
+    def _():
+        for at in range(half // LANES):
+            whole = held[at].reshape(groups * sides, nlat // (groups * sides), slots, LANES)
+            start = 0
+            for out, count in zip(outs, counts):
+                part = whole[:, start : start + count].astype(BF)
+                out[:, 0, :, :, at * LANES : (at + 1) * LANES] = part
+                start += count
+
+
+def middle_part(part, spec, basis, quad, mix, gain, offset, counts, filled):
+    groups, sides, _, _, cycles, width = spec.shape
+    nlat = groups * cycles
+    modes = basis.shape[0]
+    parts = modes // sides // STEP
+    channels = sides * width
+    slots = 2 * STEP
+    everywhere = [
+        jax.ShapeDtypeStruct((groups * sides, parts, count, slots, channels), BF)
+        for count in counts
+    ]
+    fixed = lambda m, at: (0, 0)
+    specs = [
+        pl.BlockSpec((groups, sides, 1, 2, cycles, width), lambda m, at: (0, 0, m, 0, 0, 0)),
+        pl.BlockSpec((1, L, nlat), lambda m, at: (at[0] + m, 0, 0)),
+        pl.BlockSpec((1, nlat), fixed),
+        pl.BlockSpec(mix.shape, fixed),
+        pl.BlockSpec((L, 1), fixed),
+    ]
+    arguments = [spec, basis, quad, mix, gain]
+    aliases = {}
+    if filled is not None:
+        for at, value in enumerate(filled):
+            aliases[1 + len(arguments)] = at
+            specs.append(pl.BlockSpec(memory_space=pl.ANY))
+            arguments.append(value)
+    return pl.pallas_call(
+        functools.partial(middle_kernel, counts),
+        out_shape=everywhere,
+        grid_spec=pltpu.PrefetchScalarGridSpec(
+            num_scalar_prefetch=1,
+            grid=(STEP,),
+            in_specs=specs,
+            out_specs=[
+                pl.BlockSpec(
+                    (groups * sides, 1, count, slots, channels),
+                    lambda m, at: (0, part, 0, 0, 0),
+                )
+                for count in counts
+            ],
+            scratch_shapes=[pltpu.VMEM((channels // LANES, nlat * slots, LANES), F32)],
+        ),
+        input_output_aliases=aliases,
+        compiler_params=params(56),
+        cost_estimate=cost(
+            2 * STEP * (2 * L * nlat * 2 * channels + L * 4 * channels * channels),
+            STEP * (L * nlat * 4 + nlat * channels * 8) + mix.size * 2,
+        ),
+    )(offset, *arguments)
+
+
+def local_rows(ratio_ref, weight_ref, here_ref, after_ref, edge_ref, tail_ref, out_ref, held):
+    t = pl.program_id(0)
+    cycles = pl.num_programs(0)
+    _, nlon, width = out_ref.shape
+    near = weight_ref.shape[0] // 2
+    reach = weight_ref.shape[1] // 2
+    pad = 8
+    block = max(size for size in range(8, 73, 8) if nlon % size == 0)
+    wide = block + 2 * pad
+
+    def fill(slot, row):
+        held[slot, pl.ds(pad, nlon), :] = row
+        held[slot, pl.ds(0, pad), :] = row[nlon - pad :]
+        held[slot, pl.ds(pad + nlon, pad), :] = row[:pad]
+
+    @pl.when(t == 0)
+    def _():
+        fill(2, edge_ref[0].astype(F32))
+        fill(0, here_ref[0].astype(F32))
+
+    after = lax.rem(t + 1, 3)
+
+    @pl.when(t < cycles - 1)
+    def _():
+        fill(after, after_ref[0].astype(F32))
+
+    @pl.when(t == cycles - 1)
+    def _():
+        fill(after, tail_ref[0].astype(F32))
+
+    slots = [lax.rem(t + 2 + a, 3) for a in range(2 * near + 1)]
+    for low in range(0, width, LANES):
+        lanes = slice(low, low + LANES)
+        weights = [
+            [weight_ref[a, b : b + 1, lanes] * ratio_ref[t, a] for b in range(2 * reach + 1)]
+            for a in range(2 * near + 1)
+        ]
+
+        def body(at, carry):
+            start = pl.multiple_of(at * block, 8)
+            rows = [held[slot, pl.ds(start, wide), lanes] for slot in slots]
+            total = rows[near][pad : pad + block]
+            for b in range(2 * reach + 1):
+                value = rows[0] * weights[0][b]
+                for a in range(1, 2 * near + 1):
+                    value = value + rows[a] * weights[a][b]
+                if b != reach:
+                    value = pltpu.roll(value, (wide + reach - b) % wide, 0)
+                total = total + value[pad : pad + block]
+            out_ref[0, pl.ds(start, block), lanes] = total.astype(BF)
+            return carry
+
+        lax.fori_loop(0, nlon // block, body, 0)
+
+
+def local_part(grid, before, after, ratio, weight):
+    cycles, nlon, width = grid.shape
+    row = (1, nlon, width)
+    edge = lambda t, _: (0, 0, 0)
+    return pl.pallas_call(
+        local_rows,
+        out_shape=jax.ShapeDtypeStruct(grid.shape, BF),
+        grid_spec=pltpu.PrefetchScalarGridSpec(
+            num_scalar_prefetch=1,
+            grid=(cycles,),
+            in_specs=[
+                pl.BlockSpec(weight.shape, lambda t, _: (0, 0, 0)),
+                pl.BlockSpec(row, lambda t, _: (t, 0, 0)),
+                pl.BlockSpec(row, lambda t, _: (jnp.minimum(t + 1, cycles - 1), 0, 0)),
+                pl.BlockSpec(row, edge),
+                pl.BlockSpec(row, edge),
+            ],
+            out_specs=pl.BlockSpec(row, lambda t, _: (t, 0, 0)),
+            scratch_shapes=[pltpu.VMEM((3, nlon + 16, width), F32)],
+        ),
+        compiler_params=params(32),
+        cost_estimate=cost(grid.size * 400, grid.size * 6),
+    )(ratio, weight, grid, grid, before, after)
+
+
+def tail_kernel(place_ref, back_ref, own_ref, got_ref, table_ref, gain_ref, up_ref, down_ref, *rest):
+    mine_ref, theirs_ref = rest[-2:]
+    first = place_ref[1] == 0
+    channels = up_ref.shape[0]
+    width = own_ref.shape[2]
+    back = back_ref[:, :, 0].astype(F32).reshape(table_ref.shape[1], channels).astype(BF)
+    spectral = jnp.dot(table_ref[...], back, preferred_element_type=F32)
+    own = own_ref[0].astype(F32)
+    got = got_ref[0].astype(F32)
+    low = jnp.where(first, own, got)
+    high = jnp.where(first, got, own)
+    local = jnp.concatenate([low, high], axis=1)
+    rows = (spectral + local).astype(BF).astype(F32)
+    center = jnp.mean(rows, axis=-1, keepdims=True)
+    moved = rows - center
+    spread = jnp.mean(moved * moved, axis=-1, keepdims=True)
+    normed = (moved * lax.rsqrt(spread + 1e-05) * gain_ref[...]).astype(BF)
+    hidden = jax.nn.gelu(jnp.dot(normed, up_ref[...], preferred_element_type=F32), approximate=True)
+    output = jnp.dot(hidden.astype(BF), down_ref[...], preferred_element_type=F32) + rows
+    low = output[:, :width]
+    high = output[:, width:]
+    mine_ref[0] = jnp.where(first, low, high).astype(BF)
+    theirs_ref[0] = jnp.where(first, high, low).astype(BF)
+
+
+def tail_part(back, own, got, start, table, ln_gain, up_weight, down_weight, place, result, cycles):
+    devices, parts, count, slots, channels = back.shape
+    _, nlon, width = own.shape
+    fixed = lambda t, at: (0, 0)
+    row = (1, nlon, width)
+    specs = [
+        pl.BlockSpec((devices, parts, 1, slots, channels), lambda t, at: (0, 0, t, 0, 0)),
+        pl.BlockSpec(row, lambda t, at: (start + t, 0, 0)),
+        pl.BlockSpec(row, lambda t, at: (start + t, 0, 0)),
+        pl.BlockSpec(table.shape, fixed),
+        pl.BlockSpec(ln_gain.shape, fixed),
+        pl.BlockSpec(up_weight.shape, fixed),
+        pl.BlockSpec(down_weight.shape, fixed),
+    ]
+    arguments = [back, own, got, table, ln_gain, up_weight, down_weight]
+    aliases = {}
+    if result is not None:
+        aliases[1 + len(arguments)] = 0
+        specs.append(pl.BlockSpec(memory_space=pl.ANY))
+        arguments.append(result)
+    return pl.pallas_call(
+        tail_kernel,
+        out_shape=[
+            jax.ShapeDtypeStruct((cycles, nlon, width), BF),
+            jax.ShapeDtypeStruct((count, nlon, width), BF),
+        ],
+        grid_spec=pltpu.PrefetchScalarGridSpec(
+            num_scalar_prefetch=1,
+            grid=(count,),
+            in_specs=specs,
+            out_specs=[
+                pl.BlockSpec(row, lambda t, at: (at[0] + start + t, 0, 0)),
+                pl.BlockSpec(row, lambda t, at: (t, 0, 0)),
+            ],
+        ),
+        input_output_aliases=aliases,
+        compiler_params=params(56),
+        cost_estimate=cost(
+            2 * count * nlon * channels * (table.shape[1] + 2 * channels),
+            count * nlon * channels * 8,
+        ),
+    )(place, *arguments)
+
+
+def fast(grid, basis, mix_weight, spectral_gain, conv_weight, lat_offsets, lon_offsets, ln_gain, up_weight, down_weight):
+    cycles, nlon, width = grid.shape
+    groups = lax.axis_size("lat")
+    sides = lax.axis_size("chan")
+    rank = lax.axis_index("lat")
+    side = lax.axis_index("chan")
+    nlat = cycles * groups
+    modes = basis.shape[0]
+    few = modes // sides
+    parts = few // STEP
+    span = cycles // sides
+    counts = [span // 3] * 3 if span % 3 == 0 else [span]
+
+    cosine, sine = angle_table(nlon)
+    both = np.stack([cosine, -sine], axis=-1)
+    fwd_table = np.ascontiguousarray(
+        both.reshape(nlon, groups * sides, parts, STEP * 2).transpose(2, 1, 3, 0)
+    ).reshape(parts, groups * sides * STEP * 2, nlon)
+    weight_m = np.where(np.arange(MMAX) == 0, 1.0, 2.0)[None, :, None]
+    inv_table = jnp.asarray((both * weight_m).reshape(nlon, 2 * MMAX), BF)
+
+    gathered = []
+    for part in range(parts):
+        spec = forward_part(grid, jnp.asarray(fwd_table[part], BF))
+        spec = spec.reshape(groups * sides, STEP, 2, cycles, width)
+        spec = lax.all_to_all(spec, ("lat", "chan"), 0, 0, tiled=True)
+        gathered.append(spec.reshape(groups, sides, STEP, 2, cycles, width))
+
+    up = [(i, i + 1) for i in range(groups - 1)]
+    down = [(j, i) for i, j in up]
+    before = lax.ppermute(grid[-1:], "lat", up)
+    after = lax.ppermute(grid[:1], "lat", down)
+    own_cycles = rank * cycles + jnp.arange(cycles, dtype=jnp.int32)
+    moved = own_cycles[:, None] + jnp.arange(-NEAR, NEAR + 1, dtype=jnp.int32)[None, :]
+    ratio = jnp.sin(cycle_angle(moved, nlat)) / jnp.sin(cycle_angle(own_cycles, nlat))[:, None]
+    by_lat = lat_offsets[None, :] == jnp.arange(-NEAR, NEAR + 1, dtype=jnp.int32)[:, None]
+    by_lon = lon_offsets[None, :] == jnp.arange(-REACH, REACH + 1, dtype=jnp.int32)[:, None]
+    hit = (by_lat[:, None, :] & by_lon[None, :, :])[..., None]
+    weight = jnp.sum(jnp.where(hit, conv_weight[None, None], 0.0), axis=2)
+    local = local_part(grid, before, after, ratio, weight)
+    own = lax.dynamic_slice_in_dim(local, side * span, span, 0)
+    got = lax.ppermute(
+        lax.dynamic_slice_in_dim(local, (1 - side) * span, span, 0), "chan", SWAP
+    )
+
+    weights = lax.all_gather(mix_weight, "chan", axis=2, tiled=True)
+    real_w, imag_w = (weights[0], weights[1])
+    rows = []
+    for at in range(sides):
+        real_part = real_w[at * width : (at + 1) * width]
+        imag_part = imag_w[at * width : (at + 1) * width]
+        rows.append(jnp.concatenate([real_part, imag_part], axis=1))
+        rows.append(jnp.concatenate([-imag_part, real_part], axis=1))
+    mix = jnp.concatenate(rows, axis=0)
+    theta = cycle_angle(jnp.arange(nlat, dtype=jnp.int32), nlat)
+    quad = (math.pi / nlat * jnp.sin(theta))[None, :]
+    gain = spectral_gain[:, None]
+
+    filled = None
+    for part in range(parts):
+        offset = (side * few + part * STEP).astype(jnp.int32).reshape(1)
+        filled = middle_part(
+            part, gathered[part], basis, quad, mix, gain, offset, counts, filled
+        )
+
+    place = jnp.stack([side * span, side]).astype(jnp.int32)
+    result = None
+    start = 0
+    sent = []
+    for value, count in zip(filled, counts):
+        back = lax.all_to_all(value, ("lat", "chan"), 0, 0, tiled=True)
+        result, theirs = tail_part(
+            back, own, got, start, inv_table, ln_gain[None, :], up_weight, down_weight,
+            place, result, cycles,
+        )
+        sent.append((start, lax.ppermute(theirs, "chan", SWAP)))
+        start += count
+    for start, value in sent:
+        result = lax.dynamic_update_slice_in_dim(result, value, (1 - side) * span + start, 0)
+    return result
 
 
 def padded_2(value, sides, width):
@@ -22,10 +400,6 @@
     return value
 
 
-def cycle_angle(rows, nlat):
-    return math.pi * (rows.astype(jnp.float32) + 0.5) / nlat
-
-
 def complex_mix(real_in, imag_in, real_w, imag_w):
     real_out = jnp.dot(real_in, real_w, preferred_element_type=jnp.float32) - jnp.dot(
         imag_in, imag_w, preferred_element_type=jnp.float32
@@ -36,7 +410,7 @@
     return (real_out, imag_out)
 
 
-def on_device(
+def plain(
     grid,
     basis,
     mix_weight,
@@ -130,6 +504,21 @@
     )
 
 
+def on_device(*arguments):
+    grid, basis = arguments[:2]
+    cycles, nlon, width = grid.shape
+    sides = lax.axis_size("chan")
+    fits = (
+        sides == 2
+        and cycles % 8 == 0
+        and cycles % sides == 0
+        and basis.shape[0] % (sides * STEP) == 0
+        and nlon % 8 == 0
+        and width % 128 == 0
+    )
+    return (fast if fits else plain)(*arguments)
+
+
 def solution(mesh):
     return jax.shard_map(
         on_device,

time: 1550 us -> 705 us (0.45)
  other arithmetic: 302 us -> 16.4 us
  local copies, waits for them, and re-layouts: 240 us -> 32.7 us
  matrix products: 203 us -> 0 us
  blocking collectives: 225 us -> 74.1 us
  waiting for transfers between devices: 526 us -> 390 us
  Pallas kernels: 0 us -> 134 us
  starting transfers between devices: 16.7 us -> 39.8 us
  between operations: 30.9 us -> 13.6 us
    reduce_sum x2 -> x1, other arithmetic: 256 us -> 0.1 us  [fast(): weight = jnp.sum(jnp.where(hit, conv_weight[None, None], 0.0), axis=2)]
    dot_general x9 -> x0, matrix products: 203 us -> none  [the longest x1 90.5 us: on_device(): jnp.einsum('tkc,kp->tpc', back, inv_table, preferred_element_type=jnp.flo...]
    all_gather x1, waiting for transfers between devices: 225 us -> 40.2 us  [fast(): weights = lax.all_gather(mix_weight, 'chan', axis=2, tiled=True)]
    ppermute x2 -> x6, waiting for transfers between devices: 13 us -> 166 us  [the longest x1 99.6 us: fast(): lax.ppermute(lax.dynamic_slice_in_dim(local, (1 - side) * span, span, 0),...]
    all_to_all x2 -> x1, blocking collectives: 225 us -> 74.1 us  [fast(): back = lax.all_to_all(value, ('lat', 'chan'), 0, 0, tiled=True)]
    pallas_call x0 -> x10, Pallas kernels: none -> 134 us  [the longest x1 41.2 us: local_part(): pl.pallas_call(local_rows, out_shape=jax.ShapeDtypeStruct(grid.shape, BF)...]
    all_to_all x2 -> x5, waiting for transfers between devices: 287 us -> 183 us  [the longest x3 121 us: fast(): spec = lax.all_to_all(spec, ('lat', 'chan'), 0, 0, tiled=True)]
    reshape x7 -> x0, local copies, waits for them, and re-layouts: 88.8 us -> none  [the longest x2 24.5 us: on_device(): spec = spec.astype(jnp.bfloat16).reshape(cycles, groups, modes, 2, width)]
  transfers between devices with their start and end apart: 5 -> 12, of which waited for: 4 -> 8; matrix products, arithmetic and copies ran while one was open for 6% -> 4% of each run, Pallas kernels for 0% -> 16%
where the time goes in v1:
time: 705 us; the launch traced here: 701 us
  waiting for transfers between devices  390 us (55%)
  Pallas kernels  134 us (19%)
  blocking collectives  74.1 us (11%)
  starting transfers between devices  39.8 us (6%)
  local copies, waits for them, and re-layouts  32.7 us (5%)
  other arithmetic  16.4 us (2%)
  between operations  13.6 us (2%)
    all_to_all x3, waiting for transfers between devices, fast(): spec = lax.all_to_all(spec, ('lat', 'chan'), 0, 0, tiled=True)  121 us
    ppermute x1, waiting for transfers between devices, fast(): lax.ppermute(lax.dynamic_slice_in_dim(local, (1 - side) * span, span, 0),...  99.6 us
    all_to_all x1, blocking collectives, fast(): back = lax.all_to_all(value, ('lat', 'chan'), 0, 0, tiled=True)  74.1 us
    ppermute x3, waiting for transfers between devices, fast(): sent.append((start, lax.ppermute(theirs, 'chan', SWAP)))  66.7 us
    all_to_all x2, waiting for transfers between devices, fast(): back = lax.all_to_all(value, ('lat', 'chan'), 0, 0, tiled=True)  62.2 us
    pallas_call x1, Pallas kernels, local_part(): pl.pallas_call(local_rows, out_shape=jax.ShapeDtypeStruct(grid.shape, BF)...  41.2 us
    pallas_call x3, Pallas kernels, middle_part(): pl.pallas_call(functools.partial(middle_kernel, counts), out_shape=everyw...  40.5 us
    all_gather x1, waiting for transfers between devices, fast(): weights = lax.all_gather(mix_weight, 'chan', axis=2, tiled=True)  40.2 us
  transfers between devices with their start and end apart: 12, of which 8 were waited for; matrix products, arithmetic and copies ran while one was open for 4% of the time, Pallas kernels for 16%

profile of v1, /device:TPU:26, one launch (start us, length us, event | category | flops | bytes accessed | tf_op | source)
XLA Modules:
  0.0 700.5 jit_solution(10938686984234823558)
XLA Ops:
  11.0 5.3 shard_map.137
  16.3 5.9 all-to-all-start.1
  25.7 5.3 shard_map.138
  31.0 60.4 %all-to-all-done.1 = bf16[32,4,2,24,256]{4,3,2,1,0:T(8,128)(2,1)S(1)} async-done(((bf16[32,4,2,24,256]{4,3,2,1,0:T(8,128)(2,1)}), bf16[32,4,2,24,256]{4,3,2,1,0:T(8,128)(2,1)S(1)}, u32[]{:S(2)}, u32[]{:S(2)}) %all-to-all-start.1) | async-done | bytes 3145760 | tf_op jit(solution)/shard_map/all_to_all | solution.py:333
  93.0 5.7 all-to-all-start.2
  107.5 60.5 %all-to-all-done.2 = bf16[32,4,2,24,256]{4,3,2,1,0:T(8,128)(2,1)} async-done(((bf16[32,4,2,24,256]{4,3,2,1,0:T(8,128)(2,1)}), bf16[32,4,2,24,256]{4,3,2,1,0:T(8,128)(2,1)}, u32[]{:S(2)}, u32[]{:S(2)}) %all-to-all-start.2) | async-done | bytes 3145760 | tf_op jit(solution)/shard_map/all_to_all | solution.py:333
  168.0 5.7 all-to-all-start
  175.9 40.2 %all-gather.2.cloned.1.call-done = bf16[2,512,512]{2,1,0:T(8,128)(2,1)} async-done(((bf16[2,512,256]{2,1,0:T(8,128)(2,1)}), bf16[2,512,512]{2,1,0:T(8,128)(2,1)}) %all-gather.2.cloned.1.call-update) | async-done | bytes 1048592 | tf_op jit(solution)/shard_map/all_gather | solution.py:353
  218.4 13.5 %maximum_maximum_fusion.mix_ref = bf16[1024,1024]{1,0:T(8,128)(2,1)} fusion(bf16[256,512]{1,0:T(8,128)(2,1)S(1)} %get-tuple-element.41, bf16[256,512]{1,0:T(8,128)(2,1)S(1)} %get-tuple-element.44, bf16[256,512]{1,0:T(8,128)(2,1)S(1)} %get-tuple-element.40, bf16[256,512]{1,0:T(8,128)(2,1)S(1)} %get-tuple-element.42, bf16[256,512]{1,0:T(8,128)(2,1)S(1)} %get-tuple-element.43, ...), kind=kLoop, calls=%fused_computation | loop fusion | flops 16777216 | bytes 3670016 | tf_op jit(solution)/shard_map/concatenate | solution.py:361
  232.0 13.4 %shard_map.139 = (bf16[32,3,4,8,512]{4,3,2,1,0:T(8,128)(2,1)}, bf16[32,3,4,8,512]{4,3,2,1,0:T(8,128)(2,1)}, bf16[32,3,4,8,512]{4,3,2,1,0:T(8,128)(2,1)}) custom-call(s32[1]{0:T(128)} %bitcast.at_ref, bf16[16,2,4,2,24,256]{5,4,3,2,1,0:T(8,128)(2,1)} %bitcast.13.spec_ref, f32[24,384,384]{2,1,0:T(8,128)} %basis_ref.5, f32[1,384]{1,0:T(1,128)} %sine_multiply_fusion.quad_ref, ...), custom_call_target="tpu_custom_call" | custom-call | flops 5637144576 | bytes 10747904 | tf_op jit(solution)/shard_map/pallas_call | solution.py:134
  245.4 13.6 %shard_map.140 = (bf16[32,3,4,8,512]{4,3,2,1,0:T(8,128)(2,1)}, bf16[32,3,4,8,512]{4,3,2,1,0:T(8,128)(2,1)}, bf16[32,3,4,8,512]{4,3,2,1,0:T(8,128)(2,1)}) custom-call(s32[1]{0:T(128)} %bitcast.9.at_ref, bf16[16,2,4,2,24,256]{5,4,3,2,1,0:T(8,128)(2,1)} %bitcast.23, ...), custom_call_target="tpu_custom_call", output_to_operand_aliasing={{0}: (6, {}), {1}: (7, {}), {2}: (8, {})} | custom-call | flops 5637144576 | bytes 10747904 | tf_op jit(solution)/shard_map/pallas_call | solution.py:134
  260.7 13.4 %shard_map.141 = (bf16[32,3,4,8,512]{4,3,2,1,0:T(8,128)(2,1)}, bf16[32,3,4,8,512]{4,3,2,1,0:T(8,128)(2,1)}, bf16[32,3,4,8,512]{4,3,2,1,0:T(8,128)(2,1)}) custom-call(s32[1]{0:T(128)} %bitcast.2.at_ref, bf16[16,2,4,2,24,256]{5,4,3,2,1,0:T(8,128)(2,1)} %bitcast.24, ...), custom_call_target="tpu_custom_call", output_to_operand_aliasing={{0}: (6, {}), {1}: (7, {}), {2}: (8, {})} | custom-call | flops 5637144576 | bytes 10747904 | tf_op jit(solution)/shard_map/pallas_call | solution.py:134
  274.1 74.1 %all_to_all.30.back_ref = bf16[32,3,4,8,512]{4,3,2,1,0:T(8,128)(2,1)} all-to-all(bf16[32,3,4,8,512]{4,3,2,1,0:T(8,128)(2,1)} %get-tuple-element.27), channel_id=1, replica_groups=mesh['lat'=16,'chan'=2] {'lat','chan'}, dimensions={0} | all-to-all | bytes 6291456 | tf_op jit(solution)/shard_map/all_to_all | solution.py:378
  348.2 5.8 all-to-all-start.5
  361.2 62.2 %all-to-all-done.5.back_ref = bf16[32,3,4,8,512]{4,3,2,1,0:T(8,128)(2,1)} async-done(((bf16[32,3,4,8,512]{4,3,2,1,0:T(8,128)(2,1)}), bf16[32,3,4,8,512]{4,3,2,1,0:T(8,128)(2,1)}, u32[]{:S(2)}, u32[]{:S(2)}) %all-to-all-start.5) | async-done | bytes 3145760 | tf_op jit(solution)/shard_map/all_to_all | solution.py:378
  423.4 5.8 all-to-all-start.3
  432.8 41.2 %shard_map.142 = bf16[24,720,256]{2,1,0:T(8,128)(2,1)S(1)} custom-call(f32[24,3]{1,0:T(8,128)S(1)} %sine_divide_fusion.ratio_ref, f32[3,7,256]{2,1,0:T(8,128)S(1)} %select_reduce_fusion.weight_ref, bf16[24,720,256]{2,1,0:T(8,128)(2,1)S(1)} %copy-done.3, bf16[24,720,256]{2,1,0:T(8,128)(2,1)S(1)} %copy-done.3, ...), custom_call_target="tpu_custom_call" | custom-call | flops 1769472000 | bytes 26542080 | tf_op jit(solution)/shard_map/pallas_call | solution.py:218
  480.2 99.6 %collective-permute-done.2.got_ref = bf16[12,720,256]{2,1,0:T(8,128)(2,1)S(1)} collective-permute-done((bf16[12,720,256]{2,1,0:T(8,128)(2,1)}, bf16[12,720,256]{2,1,0:T(8,128)(2,1)S(1)}, u32[]{:S(2)}, u32[]{:S(2)}) %collective-permute-start.2) | collective-permute-done | bytes 4423712 | tf_op jit(solution)/shard_map/ppermute | solution.py:349
  581.9 12.1 %shard_map.143 = (bf16[24,720,256]{2,1,0:T(8,128)(2,1)}, bf16[4,720,256]{2,1,0:T(8,128)(2,1)}) custom-call(s32[2]{0:T(128)} %pad_add_fusion.place_ref, bf16[32,3,4,8,512]{4,3,2,1,0:T(8,128)(2,1)} %all-to-all-done.5.back_ref, bf16[12,720,256]{2,1,0:T(8,128)(2,1)} %get-tuple-element.36.own_ref, bf16[12,720,256]{2,1,0:T(8,128)(2,1)} %copy-done.7, ...), custom_call_target="tpu_custom_call" | custom-call | flops 5284823040 | bytes 11796480 | tf_op jit(solution)/shard_map/pallas_call | solution.py:284
  595.7 12.1 %shard_map.144 = (bf16[24,720,256]{2,1,0:T(8,128)(2,1)}, bf16[4,720,256]{2,1,0:T(8,128)(2,1)}) custom-call(s32[2]{0:T(128)} %pad_add_fusion.place_ref, bf16[32,3,4,8,512]{4,3,2,1,0:T(8,128)(2,1)} %all_to_all.30.back_ref, bf16[12,720,256]{2,1,0:T(8,128)(2,1)} %get-tuple-element.36.own_ref, ...), custom_call_target="tpu_custom_call", output_to_operand_aliasing={{0}: (8, {})} | custom-call | flops 5284823040 | bytes 11796480 | tf_op jit(solution)/shard_map/pallas_call | solution.py:284
  608.1 12.2 %shard_map.145 = (bf16[24,720,256]{2,1,0:T(8,128)(2,1)}, bf16[4,720,256]{2,1,0:T(8,128)(2,1)}) custom-call(s32[2]{0:T(128)} %pad_add_fusion.place_ref, bf16[32,3,4,8,512]{4,3,2,1,0:T(8,128)(2,1)} %all-to-all-done.3.back_ref, bf16[12,720,256]{2,1,0:T(8,128)(2,1)} %get-tuple-element.36.own_ref, ...), custom_call_target="tpu_custom_call", output_to_operand_aliasing={{0}: (8, {})} | custom-call | flops 5284823040 | bytes 11796480 | tf_op jit(solution)/shard_map/pallas_call | solution.py:284
  622.0 7.4 %collective-permute-done.3 = bf16[4,720,256]{2,1,0:T(8,128)(2,1)S(1)} collective-permute-done((bf16[4,720,256]{2,1,0:T(8,128)(2,1)}, bf16[4,720,256]{2,1,0:T(8,128)(2,1)S(1)}, u32[]{:S(2)}, u32[]{:S(2)}) %collective-permute-start.3) | collective-permute-done | bytes 1474592 | tf_op jit(solution)/shard_map/ppermute | solution.py:383
  630.6 30.4 %collective-permute-done.4 = bf16[4,720,256]{2,1,0:T(8,128)(2,1)S(1)} collective-permute-done((bf16[4,720,256]{2,1,0:T(8,128)(2,1)}, bf16[4,720,256]{2,1,0:T(8,128)(2,1)S(1)}, u32[]{:S(2)}, u32[]{:S(2)}) %collective-permute-start.4) | collective-permute-done | bytes 1474592 | tf_op jit(solution)/shard_map/ppermute | solution.py:383
  662.2 28.9 %collective-permute-done.5 = bf16[4,720,256]{2,1,0:T(8,128)(2,1)} collective-permute-done((bf16[4,720,256]{2,1,0:T(8,128)(2,1)}, bf16[4,720,256]{2,1,0:T(8,128)(2,1)}, u32[]{:S(2)}, u32[]{:S(2)}) %collective-permute-start.5) | collective-permute-done | bytes 1474592 | tf_op jit(solution)/shard_map/ppermute | solution.py:383
  (60 shorter events, 52.4 us)
Async XLA Ops:
  6.5 3.5 copy-start
  16.3 5.9 copy-start.6
  16.3 75.1 %all-to-all-start.1 = ((bf16[32,4,2,24,256]{4,3,2,1,0:T(8,128)(2,1)}), bf16[32,4,2,24,256]{4,3,2,1,0:T(8,128)(2,1)S(1)}, u32[]{:S(2)}, u32[]{:S(2)}) async-start(bf16[32,4,2,24,256]{4,3,2,1,0:T(8,128)(2,1)} %bitcast.10), calls=%async_computation.1 | async-start | bytes 6291456 | tf_op jit(solution)/shard_map/all_to_all | solution.py:333
  22.2 3.5 copy-start.1
  91.4 7.3 %copy-start.4 = (bf16[256,720]{1,0:T(8,128)(2,1)S(1)}, bf16[256,720]{1,0:T(8,128)(2,1)}, u32[]{:S(2)}) copy-start(bf16[256,720]{1,0:T(8,128)(2,1)} %constant.59.clone.table_ref) | copy-start | bytes 1105924
  93.0 75.0 %all-to-all-start.2 = ((bf16[32,4,2,24,256]{4,3,2,1,0:T(8,128)(2,1)}), bf16[32,4,2,24,256]{4,3,2,1,0:T(8,128)(2,1)}, u32[]{:S(2)}, u32[]{:S(2)}) async-start(bf16[32,4,2,24,256]{4,3,2,1,0:T(8,128)(2,1)} %bitcast.12), calls=%async_computation.2 | async-start | bytes 6291456 | tf_op jit(solution)/shard_map/all_to_all | solution.py:333
  98.8 3.5 copy-start.2
  168.0 6.4 copy-start.11
  168.0 91.0 %all-to-all-start = ((bf16[32,4,2,24,256]{4,3,2,1,0:T(8,128)(2,1)}), bf16[32,4,2,24,256]{4,3,2,1,0:T(8,128)(2,1)S(1)}, u32[]{:S(2)}, u32[]{:S(2)}) async-start(bf16[32,4,2,24,256]{4,3,2,1,0:T(8,128)(2,1)} %bitcast.3), calls=%async_computation | async-start | bytes 6291456 | tf_op jit(solution)/shard_map/all_to_all | solution.py:333
  173.7 42.4 %all-gather.2.cloned.1.call-start = ((), (), s32[]{:S(2)}) async-start(), calls=%async_computation.6 | async-start | bytes 1572864 | tf_op jit(solution)/shard_map/all_gather | solution.py:353
  259.0 1.7 copy-start.9
  348.2 12.6 %copy-start.13 = (s32[9]{0:T(128)S(1)}, s32[9]{0:T(128)}, u32[]{:S(2)}) copy-start(s32[9]{0:T(128)} %param.19) | copy-start | bytes 112
  348.2 12.7 %copy-start.12 = (s32[9]{0:T(128)S(1)}, s32[9]{0:T(128)}, u32[]{:S(2)}) copy-start(s32[9]{0:T(128)} %param.20) | copy-start | bytes 112
  348.2 12.9 %copy-start.10 = (f32[9,256]{1,0:T(8,128)S(1)}, f32[9,256]{1,0:T(8,128)}, u32[]{:S(2)}) copy-start(f32[9,256]{1,0:T(8,128)} %param.18) | copy-start | bytes 27652
  348.2 75.1 %all-to-all-start.5 = ((bf16[32,3,4,8,512]{4,3,2,1,0:T(8,128)(2,1)}), bf16[32,3,4,8,512]{4,3,2,1,0:T(8,128)(2,1)}, u32[]{:S(2)}, u32[]{:S(2)}) async-start(bf16[32,3,4,8,512]{4,3,2,1,0:T(8,128)(2,1)} %get-tuple-element.28), calls=%async_computation.5 | async-start | bytes 6291456 | tf_op jit(solution)/shard_map/all_to_all | solution.py:378
  355.2 74.1 %collective-permute-start = (bf16[1,720,256]{2,1,0:T(8,128)(2,1)S(1)}, bf16[1,720,256]{2,1,0:T(8,128)(2,1)S(1)}, u32[]{:S(2)}, u32[]{:S(2)}) collective-permute-start(bf16[1,720,256]{2,1,0:T(8,128)(2,1)S(1)} %get-tuple-element.38), channel_id=1, source_target_pairs={{0,2},{2,4},{4,6},{6,8},{8,10},{10,12},{12,14},{14,16},{16,18},{18... | collective-permute-start | bytes 1105928 | tf_op jit(solution)/shard_map/ppermute | solution.py:338
  357.2 72.0 %collective-permute-start.1 = (bf16[1,720,256]{2,1,0:T(8,128)(2,1)S(1)}, bf16[1,720,256]{2,1,0:T(8,128)(2,1)S(1)}, u32[]{:S(2)}, u32[]{:S(2)}) collective-permute-start(bf16[1,720,256]{2,1,0:T(8,128)(2,1)S(1)} %get-tuple-element.37), channel_id=1, source_target_pairs={{2,0},{4,2},{6,4},{8,6},{10,8},{12,10},{14,12},{16,14},{18,16},{20... | collective-permute-start | bytes 1105928 | tf_op jit(solution)/shard_map/ppermute | solution.py:339
  423.4 184.7 %all-to-all-start.3 = ((bf16[32,3,4,8,512]{4,3,2,1,0:T(8,128)(2,1)}), bf16[32,3,4,8,512]{4,3,2,1,0:T(8,128)(2,1)}, u32[]{:S(2)}, u32[]{:S(2)}) async-start(bf16[32,3,4,8,512]{4,3,2,1,0:T(8,128)(2,1)} %get-tuple-element.26), calls=%async_computation.3 | async-start | bytes 6291456 | tf_op jit(solution)/shard_map/all_to_all | solution.py:378
  429.3 3.5 copy-start.3
  478.1 101.7 %collective-permute-start.2 = (bf16[12,720,256]{2,1,0:T(8,128)(2,1)}, bf16[12,720,256]{2,1,0:T(8,128)(2,1)S(1)}, u32[]{:S(2)}, u32[]{:S(2)}) collective-permute-start(bf16[12,720,256]{2,1,0:T(8,128)(2,1)} %get-tuple-element.35), channel_id=1, source_target_pairs={{0,1},{1,0},{2,3},{3,2},{4,5},{5,4},{6,7},{7,6},{8,9},{9,8},{10,11... | collective-permute-start | bytes 13271048 | tf_op jit(solution)/shard_map/ppermute | solution.py:349
  579.8 2.1 copy-start.7
  593.9 35.4 %collective-permute-start.3 = (bf16[4,720,256]{2,1,0:T(8,128)(2,1)}, bf16[4,720,256]{2,1,0:T(8,128)(2,1)S(1)}, u32[]{:S(2)}, u32[]{:S(2)}) collective-permute-start(bf16[4,720,256]{2,1,0:T(8,128)(2,1)} %get-tuple-element.32), channel_id=1, source_target_pairs={{0,1},{1,0},{2,3},{3,2},{4,5},{5,4},{6,7},{7,6},{8,9},{9,8},{10,11... | collective-permute-start | bytes 4423688 | tf_op jit(solution)/shard_map/ppermute | solution.py:383
  607.8 53.1 %collective-permute-start.4 = (bf16[4,720,256]{2,1,0:T(8,128)(2,1)}, bf16[4,720,256]{2,1,0:T(8,128)(2,1)S(1)}, u32[]{:S(2)}, u32[]{:S(2)}) collective-permute-start(bf16[4,720,256]{2,1,0:T(8,128)(2,1)} %get-tuple-element.33), channel_id=1, source_target_pairs={{0,1},{1,0},{2,3},{3,2},{4,5},{5,4},{6,7},{7,6},{8,9},{9,8},{10,11... | collective-permute-start | bytes 4423688 | tf_op jit(solution)/shard_map/ppermute | solution.py:383
  620.3 70.8 %collective-permute-start.5 = (bf16[4,720,256]{2,1,0:T(8,128)(2,1)}, bf16[4,720,256]{2,1,0:T(8,128)(2,1)}, u32[]{:S(2)}, u32[]{:S(2)}) collective-permute-start(bf16[4,720,256]{2,1,0:T(8,128)(2,1)} %get-tuple-element.34), channel_id=1, source_target_pairs={{0,1},{1,0},{2,3},{3,2},{4,5},{5,4},{6,7},{7,6},{8,9},{9,8},{10,11... | collective-permute-start | bytes 4423688 | tf_op jit(solution)/shard_map/ppermute | solution.py:383
  (2 other events, 2.6 us)
Sparse Core Ops, SparseCore 0:
  176.1 39.9 all-gather.1

commit v2 on v1

--- a/solution.py
+++ b/solution.py
@@ -38,7 +38,8 @@
     return np.cos(angle), np.sin(angle)
 
 
-def forward_kernel(scale, table_ref, grid_ref, out_ref, held):
+def forward_kernel(scale, table_ref, grid_ref, *rest):
+    out_ref, held = rest[-2:]
     cycles = grid_ref.shape[0]
     rows = table_ref.shape[0]
     for t in range(cycles):
@@ -51,24 +52,44 @@
         out_ref[:, :, lanes] = held[at].reshape(rows, cycles, LANES).astype(BF)
 
 
-def forward_part(grid, table):
+def forward_part(grid, table, first):
     cycles, nlon, width = grid.shape
     rows = table.shape[0]
     return pl.pallas_call(
         functools.partial(forward_kernel, 1.0 / nlon),
         out_shape=jax.ShapeDtypeStruct((rows, cycles, width), BF),
-        in_specs=[pl.BlockSpec(memory_space=pltpu.VMEM)] * 2,
+        in_specs=[pl.BlockSpec(memory_space=pltpu.VMEM)] * 2
+        + [pl.BlockSpec(memory_space=pl.ANY)] * len(first),
         out_specs=pl.BlockSpec(memory_space=pltpu.VMEM),
         scratch_shapes=[pltpu.VMEM((width // LANES, rows * cycles, LANES), F32)],
         compiler_params=params(40),
         cost_estimate=cost(2 * rows * nlon * cycles * width, grid.size * 2),
-    )(table, grid)
-
-
-def middle_kernel(counts, at_ref, spec_ref, basis_ref, quad_ref, mix_ref, gain_ref, *rest):
-    outs, held = (rest[-len(counts) - 1 : -1], rest[-1])
+    )(table, grid, *first)
+
+
+def middle_kernel(counts, at_ref, spec_ref, basis_ref, quad_ref, own_ref, other_ref, gain_ref, *rest):
+    outs, mix_ref, held = (rest[-len(counts) - 2 : -2], rest[-2], rest[-1])
     mode = pl.program_id(0)
     groups, sides, _, _, cycles, width = spec_ref.shape
+
+    @pl.when(mode == 0)
+    def _():
+        first = at_ref[1] == 0
+        channels = sides * width
+        own = own_ref[...].astype(F32)
+        other = other_ref[...].astype(F32)
+        low = jnp.where(first, own, other)
+        high = jnp.where(first, other, own)
+        whole = jnp.concatenate([low, high], axis=2).astype(BF)
+        for at in range(sides):
+            block = whole[:, at * width : (at + 1) * width]
+            real = pl.ds(2 * at * width, width)
+            imag = pl.ds((2 * at + 1) * width, width)
+            mix_ref[real, 0:channels] = block[0]
+            mix_ref[real, channels : 2 * channels] = block[1]
+            mix_ref[imag, 0:channels] = -block[1]
+            mix_ref[imag, channels : 2 * channels] = block[0]
+
     nlat = groups * cycles
     table = basis_ref[0]
     forward = (table * quad_ref[...]).astype(BF)
@@ -105,7 +126,7 @@
                 start += count
 
 
-def middle_part(part, spec, basis, quad, mix, gain, offset, counts, filled):
+def middle_part(part, spec, basis, quad, mix, other, gain, offset, counts, filled, first):
     groups, sides, _, _, cycles, width = spec.shape
     nlat = groups * cycles
     modes = basis.shape[0]
@@ -121,16 +142,19 @@
         pl.BlockSpec((groups, sides, 1, 2, cycles, width), lambda m, at: (0, 0, m, 0, 0, 0)),
         pl.BlockSpec((1, L, nlat), lambda m, at: (at[0] + m, 0, 0)),
         pl.BlockSpec((1, nlat), fixed),
-        pl.BlockSpec(mix.shape, fixed),
+        pl.BlockSpec(mix.shape, lambda m, at: (0, 0, 0)),
+        pl.BlockSpec(mix.shape, lambda m, at: (0, 0, 0)),
         pl.BlockSpec((L, 1), fixed),
     ]
-    arguments = [spec, basis, quad, mix, gain]
+    arguments = [spec, basis, quad, mix, other, gain]
     aliases = {}
     if filled is not None:
         for at, value in enumerate(filled):
             aliases[1 + len(arguments)] = at
             specs.append(pl.BlockSpec(memory_space=pl.ANY))
             arguments.append(value)
+    specs += [pl.BlockSpec(memory_space=pl.ANY)] * len(first)
+    arguments += first
     return pl.pallas_call(
         functools.partial(middle_kernel, counts),
         out_shape=everywhere,
@@ -145,7 +169,10 @@
                 )
                 for count in counts
             ],
-            scratch_shapes=[pltpu.VMEM((channels // LANES, nlat * slots, LANES), F32)],
+            scratch_shapes=[
+                pltpu.VMEM((2 * channels, 2 * channels), BF),
+                pltpu.VMEM((channels // LANES, nlat * slots, LANES), F32),
+            ],
         ),
         input_output_aliases=aliases,
         compiler_params=params(56),
@@ -269,7 +296,7 @@
     specs = [
         pl.BlockSpec((devices, parts, 1, slots, channels), lambda t, at: (0, 0, t, 0, 0)),
         pl.BlockSpec(row, lambda t, at: (start + t, 0, 0)),
-        pl.BlockSpec(row, lambda t, at: (start + t, 0, 0)),
+        pl.BlockSpec(row, lambda t, at: (t, 0, 0)),
         pl.BlockSpec(table.shape, fixed),
         pl.BlockSpec(ln_gain.shape, fixed),
         pl.BlockSpec(up_weight.shape, fixed),
@@ -316,7 +343,7 @@
     few = modes // sides
     parts = few // STEP
     span = cycles // sides
-    counts = [span // 3] * 3 if span % 3 == 0 else [span]
+    counts = [span // 2, span // 3, span // 6] if span % 6 == 0 else [span]
 
     cosine, sine = angle_table(nlon)
     both = np.stack([cosine, -sine], axis=-1)
@@ -325,13 +352,6 @@
     ).reshape(parts, groups * sides * STEP * 2, nlon)
     weight_m = np.where(np.arange(MMAX) == 0, 1.0, 2.0)[None, :, None]
     inv_table = jnp.asarray((both * weight_m).reshape(nlon, 2 * MMAX), BF)
-
-    gathered = []
-    for part in range(parts):
-        spec = forward_part(grid, jnp.asarray(fwd_table[part], BF))
-        spec = spec.reshape(groups * sides, STEP, 2, cycles, width)
-        spec = lax.all_to_all(spec, ("lat", "chan"), 0, 0, tiled=True)
-        gathered.append(spec.reshape(groups, sides, STEP, 2, cycles, width))
 
     up = [(i, i + 1) for i in range(groups - 1)]
     down = [(j, i) for i, j in up]
@@ -346,44 +366,58 @@
     weight = jnp.sum(jnp.where(hit, conv_weight[None, None], 0.0), axis=2)
     local = local_part(grid, before, after, ratio, weight)
     own = lax.dynamic_slice_in_dim(local, side * span, span, 0)
-    got = lax.ppermute(
-        lax.dynamic_slice_in_dim(local, (1 - side) * span, span, 0), "chan", SWAP
-    )
-
-    weights = lax.all_gather(mix_weight, "chan", axis=2, tiled=True)
-    real_w, imag_w = (weights[0], weights[1])
-    rows = []
-    for at in range(sides):
-        real_part = real_w[at * width : (at + 1) * width]
-        imag_part = imag_w[at * width : (at + 1) * width]
-        rows.append(jnp.concatenate([real_part, imag_part], axis=1))
-        rows.append(jnp.concatenate([-imag_part, real_part], axis=1))
-    mix = jnp.concatenate(rows, axis=0)
+    got = []
+    start = 0
+    for count in counts:
+        piece = lax.dynamic_slice_in_dim(local, (1 - side) * span + start, count, 0)
+        got.append(lax.ppermute(piece, "chan", SWAP))
+        start += count
+
+    gathered = []
+    for part in range(parts):
+        first = [local] if part == min(1, parts - 1) else []
+        spec = forward_part(grid, jnp.asarray(fwd_table[part], BF), first)
+        spec = spec.reshape(groups * sides, STEP, 2, cycles, width)
+        if part == parts - 1:
+            spec, got[0] = lax.optimization_barrier((spec, got[0]))
+        spec = lax.all_to_all(spec, ("lat", "chan"), 0, 0, tiled=True)
+        gathered.append(spec.reshape(groups, sides, STEP, 2, cycles, width))
+
+    other = lax.ppermute(mix_weight, "chan", SWAP)
     theta = cycle_angle(jnp.arange(nlat, dtype=jnp.int32), nlat)
     quad = (math.pi / nlat * jnp.sin(theta))[None, :]
     gain = spectral_gain[:, None]
 
     filled = None
     for part in range(parts):
-        offset = (side * few + part * STEP).astype(jnp.int32).reshape(1)
+        offset = jnp.stack([side * few + part * STEP, side]).astype(jnp.int32)
         filled = middle_part(
-            part, gathered[part], basis, quad, mix, gain, offset, counts, filled
+            part, gathered[part], basis, quad, mix_weight, other, gain, offset, counts, filled,
+            got[1:] if part == parts - 1 else [],
         )
 
     place = jnp.stack([side * span, side]).astype(jnp.int32)
     result = None
     start = 0
     sent = []
+    back = None
     for value, count in zip(filled, counts):
+        if back is not None:
+            value, back = lax.optimization_barrier((value, back))
+        if len(sent) > 1:
+            value, last = lax.optimization_barrier((value, sent[-2]))
+            sent[-2] = last
         back = lax.all_to_all(value, ("lat", "chan"), 0, 0, tiled=True)
         result, theirs = tail_part(
-            back, own, got, start, inv_table, ln_gain[None, :], up_weight, down_weight,
+            back, own, got[len(sent)], start, inv_table, ln_gain[None, :], up_weight, down_weight,
             place, result, cycles,
         )
-        sent.append((start, lax.ppermute(theirs, "chan", SWAP)))
+        sent.append(lax.ppermute(theirs, "chan", SWAP))
         start += count
-    for start, value in sent:
+    start = 0
+    for value, count in zip(sent, counts):
         result = lax.dynamic_update_slice_in_dim(result, value, (1 - side) * span + start, 0)
+        start += count
     return result
 
 

time: 705 us -> 629 us (0.89)
  waiting for transfers between devices: 390 us -> 252 us
  starting transfers between devices: 39.8 us -> 89.3 us
  blocking collectives: 74.1 us -> 108 us
  other arithmetic: 16.4 us -> 2.9 us
  between operations: 13.6 us -> 0.2 us
    all_to_all x3, waiting for transfers between devices: 121 us -> 0.01 us  [fast(): spec = lax.all_to_all(spec, ('lat', 'chan'), 0, 0, tiled=True)]
    all_to_all x3, starting transfers between devices: 17.2 us -> 61.9 us  [fast(): spec = lax.all_to_all(spec, ('lat', 'chan'), 0, 0, tiled=True)]
    all_gather x1 -> x0, waiting for transfers between devices: 40.2 us -> none  [fast(): weights = lax.all_gather(mix_weight, 'chan', axis=2, tiled=True)]
    all_to_all x1, blocking collectives: 74.1 us -> 108 us  [fast(): back = lax.all_to_all(value, ('lat', 'chan'), 0, 0, tiled=True)]
    ppermute x1, waiting for transfers between devices: 0.01 us -> 16.3 us  [fast(): after = lax.ppermute(grid[:1], 'lat', down)]
    concatenate x1 -> x0, other arithmetic: 13.5 us -> none  [fast(): mix = jnp.concatenate(rows, axis=0)]
    ppermute x4 -> x7, waiting for transfers between devices: 166 us -> 162 us  [the longest x3 95.2 us: fast(): got.append(lax.ppermute(piece, 'chan', SWAP))]
    unnamed x28 -> x36, local copies, waits for them, and re-layouts: 20.4 us -> 20.3 us
  transfers between devices with their start and end apart: 12 -> 14, of which waited for: 8 -> 10; matrix products, arithmetic and copies ran while one was open for 4% -> 3% of each run, Pallas kernels for 16% -> 19%
where the time goes in v2:
time: 629 us; the launch traced here: 624 us
  waiting for transfers between devices  252 us (40%)
  Pallas kernels  135 us (21%)
  blocking collectives  108 us (17%)
  starting transfers between devices  89.3 us (14%)
  local copies, waits for them, and re-layouts  36.6 us (6%)
    all_to_all x1, blocking collectives, fast(): back = lax.all_to_all(value, ('lat', 'chan'), 0, 0, tiled=True)  108 us
    ppermute x3, waiting for transfers between devices, fast(): got.append(lax.ppermute(piece, 'chan', SWAP))  95.2 us
    all_to_all x2, waiting for transfers between devices, fast(): back = lax.all_to_all(value, ('lat', 'chan'), 0, 0, tiled=True)  68.6 us
    all_to_all x3, starting transfers between devices, fast(): spec = lax.all_to_all(spec, ('lat', 'chan'), 0, 0, tiled=True)  61.9 us
    pallas_call x3, Pallas kernels, middle_part(): pl.pallas_call(functools.partial(middle_kernel, counts), out_shape=everyw...  41.9 us
    pallas_call x1, Pallas kernels, local_part(): pl.pallas_call(local_rows, out_shape=jax.ShapeDtypeStruct(grid.shape, BF)...  41.2 us
    pallas_call x3, Pallas kernels, tail_part(): pl.pallas_call(tail_kernel, out_shape=[jax.ShapeDtypeStruct((cycles, nlon...  36.3 us
    ppermute x3, waiting for transfers between devices, fast(): sent.append(lax.ppermute(theirs, 'chan', SWAP))  34.5 us
  transfers between devices with their start and end apart: 14, of which 10 were waited for; matrix products, arithmetic and copies ran while one was open for 3% of the time, Pallas kernels for 19%

profile of v2, /device:TPU:26, one launch (start us, length us, event | category | flops | bytes accessed | tf_op | source)
XLA Modules:
  0.0 623.8 jit_solution(1283809237350170501)
XLA Ops:
  4.5 5.3 shard_map.139
  9.8 5.9 all-to-all-start.2
  21.8 16.3 %collective-permute-done.1.tail_ref = bf16[1,720,256]{2,1,0:T(8,128)(2,1)S(1)} collective-permute-done((bf16[1,720,256]{2,1,0:T(8,128)(2,1)S(1)}, bf16[1,720,256]{2,1,0:T(8,128)(2,1)S(1)}, u32[]{:S(2)}, u32[]{:S(2)}) %collective-permute-start.1) | collective-permute-done | bytes 368672 | tf_op jit(solution)/shard_map/ppermute | solution.py:359
  46.1 41.2 %shard_map.137.rest_0_ = bf16[24,720,256]{2,1,0:T(8,128)(2,1)S(1)} custom-call(f32[24,3]{1,0:T(8,128)S(1)} %sine_divide_fusion.ratio_ref, f32[3,7,256]{2,1,0:T(8,128)S(1)} %select_reduce_fusion.weight_ref, bf16[24,720,256]{2,1,0:T(8,128)(2,1)S(1)} %copy-done.1, bf16[24,720,256]{2,1,0:T(8,128)(2,1)S(1)} %copy-done.1, ...), custom_call_target="tpu_custom_call" | custom-call | flops 1769472000 | bytes 26542080 | tf_op jit(solution)/shard_map/pallas_call | solution.py:245
  90.9 5.2 shard_map.138
  96.2 51.0 %all-to-all-start.1 = ((bf16[32,4,2,24,256]{4,3,2,1,0:T(8,128)(2,1)}), bf16[32,4,2,24,256]{4,3,2,1,0:T(8,128)(2,1)S(1)}, u32[]{:S(2)}, u32[]{:S(2)}) async-start(bf16[32,4,2,24,256]{4,3,2,1,0:T(8,128)(2,1)} %bitcast.6), calls=%async_computation.1 | async-start | bytes 6291456 | tf_op jit(solution)/shard_map/all_to_all | solution.py:383
  154.1 5.3 shard_map.136
  159.4 71.4 %collective-permute-done.2.got_ref = bf16[6,720,256]{2,1,0:T(8,128)(2,1)S(1)} collective-permute-done((bf16[6,720,256]{2,1,0:T(8,128)(2,1)S(1)}, bf16[6,720,256]{2,1,0:T(8,128)(2,1)S(1)}, u32[]{:S(2)}, u32[]{:S(2)}) %collective-permute-start.2) | collective-permute-done | bytes 2211872 | tf_op jit(solution)/shard_map/ppermute | solution.py:373
  233.8 5.0 all-to-all-start
  248.3 32.6 %collective-permute-done.3.other_ref = bf16[2,512,256]{2,1,0:T(8,128)(2,1)S(1)} collective-permute-done((bf16[2,512,256]{2,1,0:T(8,128)(2,1)}, bf16[2,512,256]{2,1,0:T(8,128)(2,1)S(1)}, u32[]{:S(2)}, u32[]{:S(2)}) %collective-permute-start.3) | collective-permute-done | bytes 524320 | tf_op jit(solution)/shard_map/ppermute | solution.py:386
  281.8 14.0 %shard_map.140 = (bf16[32,3,6,8,512]{4,3,2,1,0:T(8,128)(2,1)}, bf16[32,3,4,8,512]{4,3,2,1,0:T(8,128)(2,1)}, bf16[32,3,2,8,512]{4,3,2,1,0:T(8,128)(2,1)}) custom-call(s32[2]{0:T(128)} %pad_add_fusion.at_ref.place_ref, bf16[16,2,4,2,24,256]{5,4,3,2,1,0:T(8,128)(2,1)} %bitcast.9.spec_ref, f32[24,384,384]{2,1,0:T(8,128)} %basis_ref.5, ...), custom_call_target="tpu_custom_call" | custom-call | flops 5637144576 | bytes 9175040 | tf_op jit(solution)/shard_map/pallas_call | solution.py:158
  295.8 13.9 %shard_map.141 = (bf16[32,3,6,8,512]{4,3,2,1,0:T(8,128)(2,1)}, bf16[32,3,4,8,512]{4,3,2,1,0:T(8,128)(2,1)}, bf16[32,3,2,8,512]{4,3,2,1,0:T(8,128)(2,1)}) custom-call(s32[2]{0:T(128)} %pad_add_fusion.2.at_ref, bf16[16,2,4,2,24,256]{5,4,3,2,1,0:T(8,128)(2,1)} %bitcast.11, ...), custom_call_target="tpu_custom_call", output_to_operand_aliasing={{0}: (7, {}), {1}: (8, {}), {2}: (9, {})} | custom-call | flops 5637144576 | bytes 9175040 | tf_op jit(solution)/shard_map/pallas_call | solution.py:158
  309.7 23.8 %collective-permute-done.5.rest_4_.got_ref = bf16[2,720,256]{2,1,0:T(8,128)(2,1)S(1)} collective-permute-done((bf16[2,720,256]{2,1,0:T(8,128)(2,1)S(1)}, bf16[2,720,256]{2,1,0:T(8,128)(2,1)S(1)}, u32[]{:S(2)}, u32[]{:S(2)}) %collective-permute-start.5) | collective-permute-done | bytes 737312 | tf_op jit(solution)/shard_map/ppermute | solution.py:373
  335.0 13.9 %shard_map.142 = (bf16[32,3,6,8,512]{4,3,2,1,0:T(8,128)(2,1)}, bf16[32,3,4,8,512]{4,3,2,1,0:T(8,128)(2,1)}, bf16[32,3,2,8,512]{4,3,2,1,0:T(8,128)(2,1)}) custom-call(s32[2]{0:T(128)} %pad_add_fusion.1.at_ref, bf16[16,2,4,2,24,256]{5,4,3,2,1,0:T(8,128)(2,1)} %bitcast.4.spec_ref, ...), custom_call_target="tpu_custom_call", output_to_operand_aliasing={{0}: (7, {}), {1}: (8, {}), {2}: (9, {})} | custom-call | flops 5637144576 | bytes 9175040 | tf_op jit(solution)/shard_map/pallas_call | solution.py:158
  348.9 107.9 %all_to_all.30.back_ref = bf16[32,3,6,8,512]{4,3,2,1,0:T(8,128)(2,1)} all-to-all(bf16[32,3,6,8,512]{4,3,2,1,0:T(8,128)(2,1)} %get-tuple-element.35), channel_id=1, replica_groups=mesh['lat'=16,'chan'=2] {'lat','chan'}, dimensions={0} | all-to-all | bytes 9437184 | tf_op jit(solution)/shard_map/all_to_all | solution.py:410
  456.8 5.8 all-to-all-start.4
  467.1 16.3 %shard_map.143 = (bf16[24,720,256]{2,1,0:T(8,128)(2,1)}, bf16[6,720,256]{2,1,0:T(8,128)(2,1)}) custom-call(s32[2]{0:T(128)} %pad_add_fusion.at_ref.place_ref, bf16[32,3,6,8,512]{4,3,2,1,0:T(8,128)(2,1)} %all_to_all.30.back_ref, bf16[12,720,256]{2,1,0:T(8,128)(2,1)} %constant_dynamic-slice_fusion.own_ref, bf16[6,720,256]{2,1,0:T(8,128)(2,1)} %copy-done.16, ...), custom_call_target="tpu_custom_call" | custom-call | flops 7927234560 | bytes 17694720 | tf_op jit(solution)/shard_map/pallas_call | solution.py:311
  484.9 46.8 %all-to-all-done.4.back_ref = bf16[32,3,4,8,512]{4,3,2,1,0:T(8,128)(2,1)S(1)} async-done(((bf16[32,3,4,8,512]{4,3,2,1,0:T(8,128)(2,1)}), bf16[32,3,4,8,512]{4,3,2,1,0:T(8,128)(2,1)S(1)}, u32[]{:S(2)}, u32[]{:S(2)}) %all-to-all-start.4) | async-done | bytes 3145760 | tf_op jit(solution)/shard_map/all_to_all | solution.py:410
  531.8 15.8 %collective-permute-done.6 = bf16[6,720,256]{2,1,0:T(8,128)(2,1)} collective-permute-done((bf16[6,720,256]{2,1,0:T(8,128)(2,1)}, bf16[6,720,256]{2,1,0:T(8,128)(2,1)}, u32[]{:S(2)}, u32[]{:S(2)}) %collective-permute-start.6) | collective-permute-done | bytes 2211872 | tf_op jit(solution)/shard_map/ppermute | solution.py:415
  547.6 7.6 %all-to-all-start.5 = ((bf16[32,3,2,8,512]{4,3,2,1,0:T(8,128)(2,1)}), bf16[32,3,2,8,512]{4,3,2,1,0:T(8,128)(2,1)}, u32[]{:S(2)}, u32[]{:S(2)}) async-start(bf16[32,3,2,8,512]{4,3,2,1,0:T(8,128)(2,1)} %get-tuple-element.40), calls=%async_computation.5 | async-start | bytes 3145728 | tf_op jit(solution)/shard_map/all_to_all | solution.py:410
  555.2 12.1 %shard_map.144 = (bf16[24,720,256]{2,1,0:T(8,128)(2,1)}, bf16[4,720,256]{2,1,0:T(8,128)(2,1)}) custom-call(s32[2]{0:T(128)} %pad_add_fusion.at_ref.place_ref, bf16[32,3,4,8,512]{4,3,2,1,0:T(8,128)(2,1)} %copy-done.8, bf16[12,720,256]{2,1,0:T(8,128)(2,1)} %constant_dynamic-slice_fusion.own_ref, ...), custom_call_target="tpu_custom_call", output_to_operand_aliasing={{0}: (8, {})} | custom-call | flops 5284823040 | bytes 11796480 | tf_op jit(solution)/shard_map/pallas_call | solution.py:311
  568.8 21.7 %all-to-all-done.5.back_ref = bf16[32,3,2,8,512]{4,3,2,1,0:T(8,128)(2,1)} async-done(((bf16[32,3,2,8,512]{4,3,2,1,0:T(8,128)(2,1)}), bf16[32,3,2,8,512]{4,3,2,1,0:T(8,128)(2,1)}, u32[]{:S(2)}, u32[]{:S(2)}) %all-to-all-start.5) | async-done | bytes 1572896 | tf_op jit(solution)/shard_map/all_to_all | solution.py:410
  590.5 7.9 %shard_map.145 = (bf16[24,720,256]{2,1,0:T(8,128)(2,1)}, bf16[2,720,256]{2,1,0:T(8,128)(2,1)}) custom-call(s32[2]{0:T(128)} %pad_add_fusion.at_ref.place_ref, bf16[32,3,2,8,512]{4,3,2,1,0:T(8,128)(2,1)} %all-to-all-done.5.back_ref, bf16[12,720,256]{2,1,0:T(8,128)(2,1)} %constant_dynamic-slice_fusion.own_ref, ...), custom_call_target="tpu_custom_call", output_to_operand_aliasing={{0}: (8, {})} | custom-call | flops 2642411520 | bytes 5898240 | tf_op jit(solution)/shard_map/pallas_call | solution.py:311
  609.0 13.9 %collective-permute-done.8 = bf16[2,720,256]{2,1,0:T(8,128)(2,1)S(1)} collective-permute-done((bf16[2,720,256]{2,1,0:T(8,128)(2,1)}, bf16[2,720,256]{2,1,0:T(8,128)(2,1)S(1)}, u32[]{:S(2)}, u32[]{:S(2)}) %collective-permute-start.8) | collective-permute-done | bytes 737312 | tf_op jit(solution)/shard_map/ppermute | solution.py:415
  (73 shorter events, 62.8 us)
Async XLA Ops:
  9.8 11.5 %copy-start.17 = (s32[9]{0:T(128)S(1)}, s32[9]{0:T(128)}, u32[]{:S(2)}) copy-start(s32[9]{0:T(128)} %param.19) | copy-start | bytes 112
  9.8 11.6 %copy-start.15 = (s32[9]{0:T(128)S(1)}, s32[9]{0:T(128)}, u32[]{:S(2)}) copy-start(s32[9]{0:T(128)} %param.20) | copy-start | bytes 112
  9.8 11.7 %copy-start.13 = (f32[9,256]{1,0:T(8,128)S(1)}, f32[9,256]{1,0:T(8,128)}, u32[]{:S(2)}) copy-start(f32[9,256]{1,0:T(8,128)} %param.18) | copy-start | bytes 27652
  9.8 86.4 %all-to-all-start.2 = ((bf16[32,4,2,24,256]{4,3,2,1,0:T(8,128)(2,1)}), bf16[32,4,2,24,256]{4,3,2,1,0:T(8,128)(2,1)}, u32[]{:S(2)}, u32[]{:S(2)}) async-start(bf16[32,4,2,24,256]{4,3,2,1,0:T(8,128)(2,1)} %bitcast.8), calls=%async_computation.2 | async-start | bytes 6291456 | tf_op jit(solution)/shard_map/all_to_all | solution.py:383
  16.9 21.3 %collective-permute-start.1 = (bf16[1,720,256]{2,1,0:T(8,128)(2,1)S(1)}, bf16[1,720,256]{2,1,0:T(8,128)(2,1)S(1)}, u32[]{:S(2)}, u32[]{:S(2)}) collective-permute-start(bf16[1,720,256]{2,1,0:T(8,128)(2,1)S(1)} %get-tuple-element.47), channel_id=1, source_target_pairs={{2,0},{4,2},{6,4},{8,6},{10,8},{12,10},{14,12},{16,14},{18,16},{20... | collective-permute-start | bytes 1105928 | tf_op jit(solution)/shard_map/ppermute | solution.py:359
  19.1 23.5 %collective-permute-start = (bf16[1,720,256]{2,1,0:T(8,128)(2,1)S(1)}, bf16[1,720,256]{2,1,0:T(8,128)(2,1)S(1)}, u32[]{:S(2)}, u32[]{:S(2)}) collective-permute-start(bf16[1,720,256]{2,1,0:T(8,128)(2,1)S(1)} %get-tuple-element.48), channel_id=1, source_target_pairs={{0,2},{2,4},{4,6},{6,8},{8,10},{10,12},{12,14},{14,16},{16,18},{18... | collective-permute-start | bytes 1105928 | tf_op jit(solution)/shard_map/ppermute | solution.py:358
  42.6 3.5 copy-start.1
  46.1 44.8 %copy-start.2 = (bf16[24,720,256]{2,1,0:T(8,128)(2,1)S(1)}, bf16[24,720,256]{2,1,0:T(8,128)(2,1)}, u32[]{:S(2)}) copy-start(bf16[24,720,256]{2,1,0:T(8,128)(2,1)} %grid_ref.5) | copy-start | bytes 26542084
  46.1 44.8 %copy-start.7 = (bf16[256,720]{1,0:T(8,128)(2,1)S(1)}, bf16[256,720]{1,0:T(8,128)(2,1)}, u32[]{:S(2)}) copy-start(bf16[256,720]{1,0:T(8,128)(2,1)} %constant.62.clone.table_ref) | copy-start | bytes 1105924
  87.4 3.6 copy-start.4
  96.2 136.0 %all-to-all-start.1 = ((bf16[32,4,2,24,256]{4,3,2,1,0:T(8,128)(2,1)}), bf16[32,4,2,24,256]{4,3,2,1,0:T(8,128)(2,1)S(1)}, u32[]{:S(2)}, u32[]{:S(2)}) async-start(bf16[32,4,2,24,256]{4,3,2,1,0:T(8,128)(2,1)} %bitcast.6), calls=%async_computation.1 | async-start | bytes 6291456 | tf_op jit(solution)/shard_map/all_to_all | solution.py:383
  149.0 81.8 %collective-permute-start.2 = (bf16[6,720,256]{2,1,0:T(8,128)(2,1)S(1)}, bf16[6,720,256]{2,1,0:T(8,128)(2,1)S(1)}, u32[]{:S(2)}, u32[]{:S(2)}) collective-permute-start(bf16[6,720,256]{2,1,0:T(8,128)(2,1)S(1)} %constant_dynamic-slice_fusion.3), channel_id=1, source_target_pairs={{0,1},{1,0},{2,3},{3,2},{4,5},{5,4},{6,7},{7,6},{8,9},{9,8},{10,11... | collective-permute-start | bytes 6635528 | tf_op jit(solution)/shard_map/ppermute | solution.py:373
  150.6 3.5 copy-start.3
  232.2 8.2 %copy-start.14 = (f32[384]{0:T(512)S(1)}, f32[384]{0:T(512)}, u32[]{:S(2)}) copy-start(f32[384]{0:T(512)} %param.17) | copy-start | bytes 4612
  233.8 99.8 %all-to-all-start = ((bf16[32,4,2,24,256]{4,3,2,1,0:T(8,128)(2,1)}), bf16[32,4,2,24,256]{4,3,2,1,0:T(8,128)(2,1)}, u32[]{:S(2)}, u32[]{:S(2)}) async-start(bf16[32,4,2,24,256]{4,3,2,1,0:T(8,128)(2,1)} %bitcast.3), calls=%async_computation | async-start | bytes 6291456 | tf_op jit(solution)/shard_map/all_to_all | solution.py:383
  238.8 42.2 %collective-permute-start.3 = (bf16[2,512,256]{2,1,0:T(8,128)(2,1)}, bf16[2,512,256]{2,1,0:T(8,128)(2,1)S(1)}, u32[]{:S(2)}, u32[]{:S(2)}) collective-permute-start(bf16[2,512,256]{2,1,0:T(8,128)(2,1)} %own_ref.5), channel_id=1, source_target_pairs={{0,1},{1,0},{2,3},{3,2},{4,5},{5,4},{6,7},{7,6},{8,9},{9,8},{10,11... | collective-permute-start | bytes 1572872 | tf_op jit(solution)/shard_map/ppermute | solution.py:386
  243.2 90.4 %collective-permute-start.4 = (bf16[4,720,256]{2,1,0:T(8,128)(2,1)S(1)}, bf16[4,720,256]{2,1,0:T(8,128)(2,1)S(1)}, u32[]{:S(2)}, u32[]{:S(2)}) collective-permute-start(bf16[4,720,256]{2,1,0:T(8,128)(2,1)S(1)} %constant_dynamic-slice_fusion.2), channel_id=1, source_target_pairs={{0,1},{1,0},{2,3},{3,2},{4,5},{5,4},{6,7},{7,6},{8,9},{9,8},{10,11... | collective-permute-start | bytes 4423688 | tf_op jit(solution)/shard_map/ppermute | solution.py:373
  246.8 86.8 %collective-permute-start.5 = (bf16[2,720,256]{2,1,0:T(8,128)(2,1)S(1)}, bf16[2,720,256]{2,1,0:T(8,128)(2,1)S(1)}, u32[]{:S(2)}, u32[]{:S(2)}) collective-permute-start(bf16[2,720,256]{2,1,0:T(8,128)(2,1)S(1)} %constant_dynamic-slice_fusion.1), channel_id=1, source_target_pairs={{0,1},{1,0},{2,3},{3,2},{4,5},{5,4},{6,7},{7,6},{8,9},{9,8},{10,11... | collective-permute-start | bytes 2211848 | tf_op jit(solution)/shard_map/ppermute | solution.py:373
  456.8 75.0 %all-to-all-start.4 = ((bf16[32,3,4,8,512]{4,3,2,1,0:T(8,128)(2,1)}), bf16[32,3,4,8,512]{4,3,2,1,0:T(8,128)(2,1)S(1)}, u32[]{:S(2)}, u32[]{:S(2)}) async-start(bf16[32,3,4,8,512]{4,3,2,1,0:T(8,128)(2,1)} %get-tuple-element.36), calls=%async_computation.4 | async-start | bytes 6291456 | tf_op jit(solution)/shard_map/all_to_all | solution.py:410
  483.4 64.2 %collective-permute-start.6 = (bf16[6,720,256]{2,1,0:T(8,128)(2,1)}, bf16[6,720,256]{2,1,0:T(8,128)(2,1)}, u32[]{:S(2)}, u32[]{:S(2)}) collective-permute-start(bf16[6,720,256]{2,1,0:T(8,128)(2,1)} %get-tuple-element.39), channel_id=1, source_target_pairs={{0,1},{1,0},{2,3},{3,2},{4,5},{5,4},{6,7},{7,6},{8,9},{9,8},{10,11... | collective-permute-start | bytes 6635528 | tf_op jit(solution)/shard_map/ppermute | solution.py:415
  531.8 23.4 %copy-start.8 = (bf16[32,3,4,8,512]{4,3,2,1,0:T(8,128)(2,1)}, bf16[32,3,4,8,512]{4,3,2,1,0:T(8,128)(2,1)S(1)}, u32[]{:S(2)}) copy-start(bf16[32,3,4,8,512]{4,3,2,1,0:T(8,128)(2,1)S(1)} %all-to-all-done.4.back_ref) | copy-start | bytes 9437188
  547.6 43.0 %all-to-all-start.5 = ((bf16[32,3,2,8,512]{4,3,2,1,0:T(8,128)(2,1)}), bf16[32,3,2,8,512]{4,3,2,1,0:T(8,128)(2,1)}, u32[]{:S(2)}, u32[]{:S(2)}) async-start(bf16[32,3,2,8,512]{4,3,2,1,0:T(8,128)(2,1)} %get-tuple-element.40), calls=%async_computation.5 | async-start | bytes 3145728 | tf_op jit(solution)/shard_map/all_to_all | solution.py:410
  567.3 40.5 %collective-permute-start.7 = (bf16[4,720,256]{2,1,0:T(8,128)(2,1)}, bf16[4,720,256]{2,1,0:T(8,128)(2,1)S(1)}, u32[]{:S(2)}, u32[]{:S(2)}) collective-permute-start(bf16[4,720,256]{2,1,0:T(8,128)(2,1)} %get-tuple-element.45), channel_id=1, source_target_pairs={{0,1},{1,0},{2,3},{3,2},{4,5},{5,4},{6,7},{7,6},{8,9},{9,8},{10,11... | collective-permute-start | bytes 4423688 | tf_op jit(solution)/shard_map/ppermute | solution.py:415
  598.4 24.5 %collective-permute-start.8 = (bf16[2,720,256]{2,1,0:T(8,128)(2,1)}, bf16[2,720,256]{2,1,0:T(8,128)(2,1)S(1)}, u32[]{:S(2)}, u32[]{:S(2)}) collective-permute-start(bf16[2,720,256]{2,1,0:T(8,128)(2,1)} %get-tuple-element.46), channel_id=1, source_target_pairs={{0,1},{1,0},{2,3},{3,2},{4,5},{5,4},{6,7},{7,6},{8,9},{9,8},{10,11... | collective-permute-start | bytes 2211848 | tf_op jit(solution)/shard_map/ppermute | solution.py:415
  (8 other events, 14.0 us)

commit v3 on v2

--- a/solution.py
+++ b/solution.py
@@ -40,29 +40,40 @@
 
 def forward_kernel(scale, table_ref, grid_ref, *rest):
     out_ref, held = rest[-2:]
-    cycles = grid_ref.shape[0]
+    few = grid_ref.shape[0]
+    cycles = out_ref.shape[1]
     rows = table_ref.shape[0]
-    for t in range(cycles):
+    step = pl.program_id(0)
+    for t in range(few):
         value = jnp.dot(table_ref[...], grid_ref[t], preferred_element_type=F32)
         value = value * scale
         for at in range(held.shape[0]):
-            held[at, pl.ds(t, rows, stride=cycles), :] = value[:, at * LANES : (at + 1) * LANES]
-    for at in range(held.shape[0]):
-        lanes = slice(at * LANES, (at + 1) * LANES)
-        out_ref[:, :, lanes] = held[at].reshape(rows, cycles, LANES).astype(BF)
+            part = value[:, at * LANES : (at + 1) * LANES]
+            held[at, pl.ds(step * few + t, rows, stride=cycles), :] = part
+
+    @pl.when(step == pl.num_programs(0) - 1)
+    def _():
+        for at in range(held.shape[0]):
+            lanes = slice(at * LANES, (at + 1) * LANES)
+            out_ref[:, :, lanes] = held[at].reshape(rows, cycles, LANES).astype(BF)
 
 
 def forward_part(grid, table, first):
     cycles, nlon, width = grid.shape
     rows = table.shape[0]
+    few = 4
     return pl.pallas_call(
         functools.partial(forward_kernel, 1.0 / nlon),
         out_shape=jax.ShapeDtypeStruct((rows, cycles, width), BF),
-        in_specs=[pl.BlockSpec(memory_space=pltpu.VMEM)] * 2
+        grid=(cycles // few,),
+        in_specs=[
+            pl.BlockSpec(table.shape, lambda t: (0, 0)),
+            pl.BlockSpec((few, nlon, width), lambda t: (t, 0, 0)),
+        ]
         + [pl.BlockSpec(memory_space=pl.ANY)] * len(first),
-        out_specs=pl.BlockSpec(memory_space=pltpu.VMEM),
+        out_specs=pl.BlockSpec((rows, cycles, width), lambda t: (0, 0, 0)),
         scratch_shapes=[pltpu.VMEM((width // LANES, rows * cycles, LANES), F32)],
-        compiler_params=params(40),
+        compiler_params=params(58),
         cost_estimate=cost(2 * rows * nlon * cycles * width, grid.size * 2),
     )(table, grid, *first)
 
@@ -175,7 +186,7 @@
             ],
         ),
         input_output_aliases=aliases,
-        compiler_params=params(56),
+        compiler_params=params(60),
         cost_estimate=cost(
             2 * STEP * (2 * L * nlat * 2 * channels + L * 4 * channels * channels),
             STEP * (L * nlat * 4 + nlat * channels * 8) + mix.size * 2,
@@ -183,9 +194,10 @@
     )(offset, *arguments)
 
 
-def local_rows(ratio_ref, weight_ref, here_ref, after_ref, edge_ref, tail_ref, out_ref, held):
+def local_rows(base_ref, ratio_ref, weight_ref, prev_ref, here_ref, after_ref, edge_ref, tail_ref, out_ref, held):
     t = pl.program_id(0)
-    cycles = pl.num_programs(0)
+    cycle = base_ref[0] + t
+    cycles = base_ref[1]
     _, nlon, width = out_ref.shape
     near = weight_ref.shape[0] // 2
     reach = weight_ref.shape[1] // 2
@@ -200,16 +212,23 @@
 
     @pl.when(t == 0)
     def _():
-        fill(2, edge_ref[0].astype(F32))
         fill(0, here_ref[0].astype(F32))
 
+        @pl.when(cycle == 0)
+        def _():
+            fill(2, edge_ref[0].astype(F32))
+
+        @pl.when(cycle > 0)
+        def _():
+            fill(2, prev_ref[0].astype(F32))
+
     after = lax.rem(t + 1, 3)
 
-    @pl.when(t < cycles - 1)
+    @pl.when(cycle < cycles - 1)
     def _():
         fill(after, after_ref[0].astype(F32))
 
-    @pl.when(t == cycles - 1)
+    @pl.when(cycle == cycles - 1)
     def _():
         fill(after, tail_ref[0].astype(F32))
 
@@ -217,7 +236,7 @@
     for low in range(0, width, LANES):
         lanes = slice(low, low + LANES)
         weights = [
-            [weight_ref[a, b : b + 1, lanes] * ratio_ref[t, a] for b in range(2 * reach + 1)]
+            [weight_ref[a, b : b + 1, lanes] * ratio_ref[cycle, a] for b in range(2 * reach + 1)]
             for a in range(2 * near + 1)
         ]
 
@@ -238,29 +257,40 @@
         lax.fori_loop(0, nlon // block, body, 0)
 
 
-def local_part(grid, before, after, ratio, weight):
+def local_part(grid, before, after, ratio, weight, base, span):
     cycles, nlon, width = grid.shape
     row = (1, nlon, width)
-    edge = lambda t, _: (0, 0, 0)
+    edge = lambda t, *_: (0, 0, 0)
     return pl.pallas_call(
         local_rows,
-        out_shape=jax.ShapeDtypeStruct(grid.shape, BF),
+        out_shape=jax.ShapeDtypeStruct((span, nlon, width), BF),
         grid_spec=pltpu.PrefetchScalarGridSpec(
-            num_scalar_prefetch=1,
-            grid=(cycles,),
+            num_scalar_prefetch=2,
+            grid=(span,),
             in_specs=[
-                pl.BlockSpec(weight.shape, lambda t, _: (0, 0, 0)),
-                pl.BlockSpec(row, lambda t, _: (t, 0, 0)),
-                pl.BlockSpec(row, lambda t, _: (jnp.minimum(t + 1, cycles - 1), 0, 0)),
+                pl.BlockSpec(weight.shape, edge),
+                pl.BlockSpec(row, lambda t, at, _: (jnp.maximum(at[0] - 1, 0), 0, 0)),
+                pl.BlockSpec(row, lambda t, at, _: (at[0] + t, 0, 0)),
+                pl.BlockSpec(row, lambda t, at, _: (jnp.minimum(at[0] + t + 1, cycles - 1), 0, 0)),
                 pl.BlockSpec(row, edge),
                 pl.BlockSpec(row, edge),
             ],
-            out_specs=pl.BlockSpec(row, lambda t, _: (t, 0, 0)),
+            out_specs=pl.BlockSpec(row, lambda t, *_: (t, 0, 0)),
             scratch_shapes=[pltpu.VMEM((3, nlon + 16, width), F32)],
         ),
-        compiler_params=params(32),
-        cost_estimate=cost(grid.size * 400, grid.size * 6),
-    )(ratio, weight, grid, grid, before, after)
+        compiler_params=params(58),
+        cost_estimate=cost(span * nlon * width * 400, span * nlon * width * 6),
+    )(jnp.stack([base, cycles]).astype(jnp.int32), ratio, weight, grid, grid, grid, before, after)
+
+
+def exchanged(value, counts):
+    got = []
+    start = 0
+    for count in counts:
+        piece = lax.slice_in_dim(value, start, start + count, axis=0)
+        got.append(lax.ppermute(piece, "chan", SWAP))
+        start += count
+    return got
 
 
 def tail_kernel(place_ref, back_ref, own_ref, got_ref, table_ref, gain_ref, up_ref, down_ref, *rest):
@@ -324,7 +354,7 @@
             ],
         ),
         input_output_aliases=aliases,
-        compiler_params=params(56),
+        compiler_params=params(60),
         cost_estimate=cost(
             2 * count * nlon * channels * (table.shape[1] + 2 * channels),
             count * nlon * channels * 8,
@@ -343,7 +373,7 @@
     few = modes // sides
     parts = few // STEP
     span = cycles // sides
-    counts = [span // 2, span // 3, span // 6] if span % 6 == 0 else [span]
+    counts = [span // 4] * 4
 
     cosine, sine = angle_table(nlon)
     both = np.stack([cosine, -sine], axis=-1)
@@ -364,26 +394,24 @@
     by_lon = lon_offsets[None, :] == jnp.arange(-REACH, REACH + 1, dtype=jnp.int32)[:, None]
     hit = (by_lat[:, None, :] & by_lon[None, :, :])[..., None]
     weight = jnp.sum(jnp.where(hit, conv_weight[None, None], 0.0), axis=2)
-    local = local_part(grid, before, after, ratio, weight)
-    own = lax.dynamic_slice_in_dim(local, side * span, span, 0)
-    got = []
-    start = 0
-    for count in counts:
-        piece = lax.dynamic_slice_in_dim(local, (1 - side) * span + start, count, 0)
-        got.append(lax.ppermute(piece, "chan", SWAP))
-        start += count
-
+
+    other = lax.ppermute(mix_weight, "chan", SWAP)
     gathered = []
     for part in range(parts):
-        first = [local] if part == min(1, parts - 1) else []
-        spec = forward_part(grid, jnp.asarray(fwd_table[part], BF), first)
+        spec = forward_part(grid, jnp.asarray(fwd_table[part], BF), [])
         spec = spec.reshape(groups * sides, STEP, 2, cycles, width)
-        if part == parts - 1:
-            spec, got[0] = lax.optimization_barrier((spec, got[0]))
+        if part == 0:
+            spec, before, after = lax.optimization_barrier((spec, before, after))
+            asked = local_part(grid, before, after, ratio, weight, (1 - side) * span, span)
+            got = exchanged(asked, counts)
+        elif part == 1:
+            spec, other, got[0] = lax.optimization_barrier((spec, other, got[0]))
+            own = local_part(grid, before, after, ratio, weight, side * span, span)
+        elif part == 2:
+            spec, got[1], own = lax.optimization_barrier((spec, got[1], own))
         spec = lax.all_to_all(spec, ("lat", "chan"), 0, 0, tiled=True)
         gathered.append(spec.reshape(groups, sides, STEP, 2, cycles, width))
 
-    other = lax.ppermute(mix_weight, "chan", SWAP)
     theta = cycle_angle(jnp.arange(nlat, dtype=jnp.int32), nlat)
     quad = (math.pi / nlat * jnp.sin(theta))[None, :]
     gain = spectral_gain[:, None]
@@ -393,7 +421,7 @@
         offset = jnp.stack([side * few + part * STEP, side]).astype(jnp.int32)
         filled = middle_part(
             part, gathered[part], basis, quad, mix_weight, other, gain, offset, counts, filled,
-            got[1:] if part == parts - 1 else [],
+            got[2:3] if part == parts - 1 else [],
         )
 
     place = jnp.stack([side * span, side]).astype(jnp.int32)
@@ -401,15 +429,16 @@
     start = 0
     sent = []
     back = None
-    for value, count in zip(filled, counts):
-        if back is not None:
+    for at, (value, count) in enumerate(zip(filled, counts)):
+        if at > 0:
             value, back = lax.optimization_barrier((value, back))
-        if len(sent) > 1:
-            value, last = lax.optimization_barrier((value, sent[-2]))
-            sent[-2] = last
+        if at == 1:
+            value, got[3] = lax.optimization_barrier((value, got[3]))
+        if at > 1:
+            value, sent[at - 2] = lax.optimization_barrier((value, sent[at - 2]))
         back = lax.all_to_all(value, ("lat", "chan"), 0, 0, tiled=True)
         result, theirs = tail_part(
-            back, own, got[len(sent)], start, inv_table, ln_gain[None, :], up_weight, down_weight,
+            back, own, got[at], start, inv_table, ln_gain[None, :], up_weight, down_weight,
             place, result, cycles,
         )
         sent.append(lax.ppermute(theirs, "chan", SWAP))
@@ -546,6 +575,8 @@
         sides == 2
         and cycles % 8 == 0
         and cycles % sides == 0
+        and cycles // sides % 4 == 0
+        and basis.shape[0] // (sides * STEP) == 3
         and basis.shape[0] % (sides * STEP) == 0
         and nlon % 8 == 0
         and width % 128 == 0

time: 629 us -> 550 us (0.87)
  blocking collectives: 108 us -> 0 us
  waiting for transfers between devices: 252 us -> 300 us
  starting transfers between devices: 89.3 us -> 59.7 us
  Pallas kernels: 135 us -> 157 us
  local copies, waits for them, and re-layouts: 36.6 us -> 22.9 us
    all_to_all x1 -> x0, blocking collectives: 108 us -> none  [fast(): back = lax.all_to_all(value, ('lat', 'chan'), 0, 0, tiled=True)]
    all_to_all x2 -> x4, waiting for transfers between devices: 68.6 us -> 173 us  [fast(): back = lax.all_to_all(value, ('lat', 'chan'), 0, 0, tiled=True)]
    ppermute x3 -> x4, waiting for transfers between devices: 95.2 us -> 47.9 us  [exchanged(): got.append(lax.ppermute(piece, 'chan', SWAP))]
    all_to_all x3, starting transfers between devices: 61.9 us -> 18.9 us  [fast(): spec = lax.all_to_all(spec, ('lat', 'chan'), 0, 0, tiled=True)]
    all_to_all x3, waiting for transfers between devices: 0.01 us -> 22.6 us  [fast(): spec = lax.all_to_all(spec, ('lat', 'chan'), 0, 0, tiled=True)]
    ppermute x1, waiting for transfers between devices: 16.3 us -> 0.01 us  [fast(): after = lax.ppermute(grid[:1], 'lat', down)]
    ppermute x3 -> x4, waiting for transfers between devices: 34.5 us -> 20.8 us  [fast(): sent.append(lax.ppermute(theirs, 'chan', SWAP))]
    pallas_call x3, Pallas kernels: 15.9 us -> 27.5 us  [forward_part(): pl.pallas_call(functools.partial(forward_kernel, 1.0 / nlon), out_shape=j...]
  transfers between devices with their start and end apart: 14 -> 18, of which waited for: 10 -> 10; matrix products, arithmetic and copies ran while one was open for 3% -> 3% of each run, Pallas kernels for 19% -> 26%
where the time goes in v3:
time: 550 us; the launch traced here: 546 us
  waiting for transfers between devices  300 us (55%)
  Pallas kernels  157 us (29%)
  starting transfers between devices  59.7 us (11%)
  local copies, waits for them, and re-layouts  22.9 us (4%)
    all_to_all x4, waiting for transfers between devices, fast(): back = lax.all_to_all(value, ('lat', 'chan'), 0, 0, tiled=True)  173 us
    ppermute x4, waiting for transfers between devices, exchanged(): got.append(lax.ppermute(piece, 'chan', SWAP))  47.9 us
    pallas_call x2, Pallas kernels, local_part(): pl.pallas_call(local_rows, out_shape=jax.ShapeDtypeStruct((span, nlon, wi...  47.9 us
    pallas_call x3, Pallas kernels, middle_part(): pl.pallas_call(functools.partial(middle_kernel, counts), out_shape=everyw...  42 us
    pallas_call x4, Pallas kernels, tail_part(): pl.pallas_call(tail_kernel, out_shape=[jax.ShapeDtypeStruct((cycles, nlon...  40.1 us
    ppermute x1, waiting for transfers between devices, fast(): other = lax.ppermute(mix_weight, 'chan', SWAP)  35.6 us
    pallas_call x3, Pallas kernels, forward_part(): pl.pallas_call(functools.partial(forward_kernel, 1.0 / nlon), out_shape=j...  27.5 us
    all_to_all x4, starting transfers between devices, fast(): back = lax.all_to_all(value, ('lat', 'chan'), 0, 0, tiled=True)  22.8 us
  transfers between devices with their start and end apart: 18, of which 10 were waited for; matrix products, arithmetic and copies ran while one was open for 3% of the time, Pallas kernels for 26%

profile of v3, /device:TPU:26, one launch (start us, length us, event | category | flops | bytes accessed | tf_op | source)
XLA Modules:
  0.0 545.8 jit_solution(7105073399057749042)
XLA Ops:
  6.7 9.1 %shard_map.137 = bf16[256,24,256]{2,1,0:T(8,128)(2,1)} custom-call(bf16[256,720]{1,0:T(8,128)(2,1)} %constant.67.clone.table_ref, bf16[24,720,256]{2,1,0:T(8,128)(2,1)} %grid_ref.5), custom_call_target="tpu_custom_call" | custom-call | flops 2264924160 | bytes 8847360 | tf_op jit(solution)/shard_map/pallas_call | solution.py:65
  16.6 5.9 %all-to-all-start.2 = ((bf16[32,4,2,24,256]{4,3,2,1,0:T(8,128)(2,1)}), bf16[32,4,2,24,256]{4,3,2,1,0:T(8,128)(2,1)S(1)}, u32[]{:S(2)}, u32[]{:S(2)}) async-start(bf16[32,4,2,24,256]{4,3,2,1,0:T(8,128)(2,1)} %bitcast.13), calls=%async_computation.2 | async-start | bytes 6291456 | tf_op jit(solution)/shard_map/all_to_all | solution.py:412
  24.9 23.9 %shard_map.138 = bf16[12,720,256]{2,1,0:T(8,128)(2,1)} custom-call(s32[2]{0:T(128)} %pad_add_fusion.1.base_ref, f32[24,3]{1,0:T(8,128)} %sine_divide_fusion.ratio_ref, f32[3,7,256]{2,1,0:T(8,128)} %select_reduce_fusion.weight_ref, bf16[24,720,256]{2,1,0:T(8,128)(2,1)} %grid_ref.5, bf16[24,720,256]{2,1,0:T(8,128)(2,1)} %grid_ref.5, ...), custom_call_target="tpu_custom_call" | custom-call | flops 884736000 | bytes 13271040 | tf_op jit(solution)/shard_map/pallas_call | solution.py:264
  54.9 9.2 %shard_map.140 = bf16[256,24,256]{2,1,0:T(8,128)(2,1)} custom-call(bf16[256,720]{1,0:T(8,128)(2,1)} %constant.68.clone.table_ref, bf16[24,720,256]{2,1,0:T(8,128)(2,1)} %grid_ref.5), custom_call_target="tpu_custom_call" | custom-call | flops 2264924160 | bytes 8847360 | tf_op jit(solution)/shard_map/pallas_call | solution.py:65
  64.1 35.6 %collective-permute-done.3.other_ref = bf16[2,512,256]{2,1,0:T(8,128)(2,1)S(1)} collective-permute-done((bf16[2,512,256]{2,1,0:T(8,128)(2,1)S(1)}, bf16[2,512,256]{2,1,0:T(8,128)(2,1)S(1)}, u32[]{:S(2)}, u32[]{:S(2)}) %collective-permute-start.3) | collective-permute-done | bytes 524320 | tf_op jit(solution)/shard_map/ppermute | solution.py:398
  102.2 7.4 %all-to-all-start.1 = ((bf16[32,4,2,24,256]{4,3,2,1,0:T(8,128)(2,1)}), bf16[32,4,2,24,256]{4,3,2,1,0:T(8,128)(2,1)S(1)}, u32[]{:S(2)}, u32[]{:S(2)}) async-start(bf16[32,4,2,24,256]{4,3,2,1,0:T(8,128)(2,1)} %bitcast.15), calls=%async_computation.1 | async-start | bytes 6291456 | tf_op jit(solution)/shard_map/all_to_all | solution.py:412
  111.7 9.1 %shard_map.136 = bf16[256,24,256]{2,1,0:T(8,128)(2,1)} custom-call(bf16[256,720]{1,0:T(8,128)(2,1)} %constant.69.clone.table_ref, bf16[24,720,256]{2,1,0:T(8,128)(2,1)} %grid_ref.5), custom_call_target="tpu_custom_call" | custom-call | flops 2264924160 | bytes 8847360 | tf_op jit(solution)/shard_map/pallas_call | solution.py:65
  120.8 23.9 %shard_map.139.own_ref = bf16[12,720,256]{2,1,0:T(8,128)(2,1)} custom-call(s32[2]{0:T(128)} %pad_add_fusion.base_ref, f32[24,3]{1,0:T(8,128)} %sine_divide_fusion.ratio_ref, f32[3,7,256]{2,1,0:T(8,128)} %select_reduce_fusion.weight_ref, bf16[24,720,256]{2,1,0:T(8,128)(2,1)} %grid_ref.5, bf16[24,720,256]{2,1,0:T(8,128)(2,1)} %grid_ref.5, ...), custom_call_target="tpu_custom_call" | custom-call | flops 884736000 | bytes 13271040 | tf_op jit(solution)/shard_map/pallas_call | solution.py:264
  144.8 22.7 %collective-permute-done.2.got_ref = bf16[3,720,256]{2,1,0:T(8,128)(2,1)} collective-permute-done((bf16[3,720,256]{2,1,0:T(8,128)(2,1)}, bf16[3,720,256]{2,1,0:T(8,128)(2,1)}, u32[]{:S(2)}, u32[]{:S(2)}) %collective-permute-start.2) | collective-permute-done | bytes 1105952 | tf_op jit(solution)/shard_map/ppermute | solution.py:291
  167.5 11.3 %all-to-all-done.1 = bf16[32,4,2,24,256]{4,3,2,1,0:T(8,128)(2,1)S(1)} async-done(((bf16[32,4,2,24,256]{4,3,2,1,0:T(8,128)(2,1)}), bf16[32,4,2,24,256]{4,3,2,1,0:T(8,128)(2,1)S(1)}, u32[]{:S(2)}, u32[]{:S(2)}) %all-to-all-start.1) | async-done | bytes 3145760 | tf_op jit(solution)/shard_map/all_to_all | solution.py:412
  191.0 14.0 %shard_map.141 = (bf16[32,3,3,8,512]{4,3,2,1,0:T(8,128)(2,1)}, bf16[32,3,3,8,512]{4,3,2,1,0:T(8,128)(2,1)}, bf16[32,3,3,8,512]{4,3,2,1,0:T(8,128)(2,1)}, bf16[32,3,3,8,512]{4,3,2,1,0:T(8,128)(2,1)}) custom-call(s32[2]{0:T(128)} %pad_add_fusion.4.at_ref.place_ref, bf16[16,2,4,2,24,256]{5,4,3,2,1,0:T(8,128)(2,1)} %bitcast.17, f32[24,384,384]{2,1,0:T(8,128)} %basis_ref.5, ...), custom_call_target="tpu_custom_call" | custom-call | flops 5637144576 | bytes 9175040 | tf_op jit(solution)/shard_map/pallas_call | solution.py:169
  205.0 14.0 %shard_map.142 = (bf16[32,3,3,8,512]{4,3,2,1,0:T(8,128)(2,1)}, bf16[32,3,3,8,512]{4,3,2,1,0:T(8,128)(2,1)}, bf16[32,3,3,8,512]{4,3,2,1,0:T(8,128)(2,1)}, bf16[32,3,3,8,512]{4,3,2,1,0:T(8,128)(2,1)}) custom-call(s32[2]{0:T(128)} %pad_add_fusion.3.at_ref, ...), custom_call_target="tpu_custom_call", output_to_operand_aliasing={{0}: (7, {}), {1}: (8, {}), {2}: (9, {}), {3}: (10, {})} | custom-call | flops 5637144576 | bytes 9175040 | tf_op jit(solution)/shard_map/pallas_call | solution.py:169
  219.0 25.2 %collective-permute-done.5.rest_4_.got_ref = bf16[3,720,256]{2,1,0:T(8,128)(2,1)} collective-permute-done((bf16[3,720,256]{2,1,0:T(8,128)(2,1)}, bf16[3,720,256]{2,1,0:T(8,128)(2,1)}, u32[]{:S(2)}, u32[]{:S(2)}) %collective-permute-start.5) | collective-permute-done | bytes 1105952 | tf_op jit(solution)/shard_map/ppermute | solution.py:291
  244.2 11.3 %all-to-all-done = bf16[32,4,2,24,256]{4,3,2,1,0:T(8,128)(2,1)S(1)} async-done(((bf16[32,4,2,24,256]{4,3,2,1,0:T(8,128)(2,1)}), bf16[32,4,2,24,256]{4,3,2,1,0:T(8,128)(2,1)S(1)}, u32[]{:S(2)}, u32[]{:S(2)}) %all-to-all-start) | async-done | bytes 3145760 | tf_op jit(solution)/shard_map/all_to_all | solution.py:412
  257.2 14.0 %shard_map.143 = (bf16[32,3,3,8,512]{4,3,2,1,0:T(8,128)(2,1)}, bf16[32,3,3,8,512]{4,3,2,1,0:T(8,128)(2,1)}, bf16[32,3,3,8,512]{4,3,2,1,0:T(8,128)(2,1)}, bf16[32,3,3,8,512]{4,3,2,1,0:T(8,128)(2,1)}) custom-call(s32[2]{0:T(128)} %pad_add_fusion.2.at_ref, ...), custom_call_target="tpu_custom_call", output_to_operand_aliasing={{0}: (7, {}), {1}: (8, {}), {2}: (9, {}), {3}: (10, {})} | custom-call | flops 5637144576 | bytes 9175040 | tf_op jit(solution)/shard_map/pallas_call | solution.py:169
  278.4 50.8 %all-to-all-done.3.back_ref = bf16[32,3,3,8,512]{4,3,2,1,0:T(8,128)(2,1)S(1)} async-done(((bf16[32,3,3,8,512]{4,3,2,1,0:T(8,128)(2,1)}), bf16[32,3,3,8,512]{4,3,2,1,0:T(8,128)(2,1)S(1)}, u32[]{:S(2)}, u32[]{:S(2)}) %all-to-all-start.3) | async-done | bytes 2359328 | tf_op jit(solution)/shard_map/all_to_all | solution.py:439
  336.7 10.0 %shard_map.144 = (bf16[24,720,256]{2,1,0:T(8,128)(2,1)}, bf16[3,720,256]{2,1,0:T(8,128)(2,1)}) custom-call(s32[2]{0:T(128)} %pad_add_fusion.4.at_ref.place_ref, bf16[32,3,3,8,512]{4,3,2,1,0:T(8,128)(2,1)} %copy-done.5, bf16[12,720,256]{2,1,0:T(8,128)(2,1)} %shard_map.139.own_ref, bf16[3,720,256]{2,1,0:T(8,128)(2,1)} %collective-permute-done.4.got_ref, ...), custom_call_target="tpu_custom_call" | custom-call | flops 3963617280 | bytes 8847360 | tf_op jit(solution)/shard_map/pallas_call | solution.py:341
  348.3 40.8 %all-to-all-done.4.back_ref = bf16[32,3,3,8,512]{4,3,2,1,0:T(8,128)(2,1)S(1)} async-done(((bf16[32,3,3,8,512]{4,3,2,1,0:T(8,128)(2,1)}), bf16[32,3,3,8,512]{4,3,2,1,0:T(8,128)(2,1)S(1)}, u32[]{:S(2)}, u32[]{:S(2)}) %all-to-all-start.4) | async-done | bytes 2359328 | tf_op jit(solution)/shard_map/all_to_all | solution.py:439
  396.2 10.0 %shard_map.145 = (bf16[24,720,256]{2,1,0:T(8,128)(2,1)}, bf16[3,720,256]{2,1,0:T(8,128)(2,1)}) custom-call(s32[2]{0:T(128)} %pad_add_fusion.4.at_ref.place_ref, bf16[32,3,3,8,512]{4,3,2,1,0:T(8,128)(2,1)} %copy-done.3, bf16[12,720,256]{2,1,0:T(8,128)(2,1)} %shard_map.139.own_ref, ...), custom_call_target="tpu_custom_call", output_to_operand_aliasing={{0}: (8, {})} | custom-call | flops 3963617280 | bytes 8847360 | tf_op jit(solution)/shard_map/pallas_call | solution.py:341
  407.7 40.8 %all-to-all-done.5.back_ref = bf16[32,3,3,8,512]{4,3,2,1,0:T(8,128)(2,1)S(1)} async-done(((bf16[32,3,3,8,512]{4,3,2,1,0:T(8,128)(2,1)}), bf16[32,3,3,8,512]{4,3,2,1,0:T(8,128)(2,1)S(1)}, u32[]{:S(2)}, u32[]{:S(2)}) %all-to-all-start.5) | async-done | bytes 2359328 | tf_op jit(solution)/shard_map/all_to_all | solution.py:439
  455.7 10.0 %shard_map.146 = (bf16[24,720,256]{2,1,0:T(8,128)(2,1)}, bf16[3,720,256]{2,1,0:T(8,128)(2,1)}) custom-call(s32[2]{0:T(128)} %pad_add_fusion.4.at_ref.place_ref, bf16[32,3,3,8,512]{4,3,2,1,0:T(8,128)(2,1)} %copy-done.2, bf16[12,720,256]{2,1,0:T(8,128)(2,1)} %shard_map.139.own_ref, ...), custom_call_target="tpu_custom_call", output_to_operand_aliasing={{0}: (8, {})} | custom-call | flops 3963617280 | bytes 8847360 | tf_op jit(solution)/shard_map/pallas_call | solution.py:341
  467.2 40.9 %all-to-all-done.6.back_ref = bf16[32,3,3,8,512]{4,3,2,1,0:T(8,128)(2,1)} async-done(((bf16[32,3,3,8,512]{4,3,2,1,0:T(8,128)(2,1)}), bf16[32,3,3,8,512]{4,3,2,1,0:T(8,128)(2,1)}, u32[]{:S(2)}, u32[]{:S(2)}) %all-to-all-start.6) | async-done | bytes 2359328 | tf_op jit(solution)/shard_map/all_to_all | solution.py:439
  508.1 10.1 %shard_map.147 = (bf16[24,720,256]{2,1,0:T(8,128)(2,1)}, bf16[3,720,256]{2,1,0:T(8,128)(2,1)}) custom-call(s32[2]{0:T(128)} %pad_add_fusion.4.at_ref.place_ref, bf16[32,3,3,8,512]{4,3,2,1,0:T(8,128)(2,1)} %all-to-all-done.6.back_ref, bf16[12,720,256]{2,1,0:T(8,128)(2,1)} %shard_map.139.own_ref, ...), custom_call_target="tpu_custom_call", output_to_operand_aliasing={{0}: (8, {})} | custom-call | flops 3963617280 | bytes 8847360 | tf_op jit(solution)/shard_map/pallas_call | solution.py:341
  523.9 20.8 %collective-permute-done.10 = bf16[3,720,256]{2,1,0:T(8,128)(2,1)S(1)} collective-permute-done((bf16[3,720,256]{2,1,0:T(8,128)(2,1)}, bf16[3,720,256]{2,1,0:T(8,128)(2,1)S(1)}, u32[]{:S(2)}, u32[]{:S(2)}) %collective-permute-start.10) | collective-permute-done | bytes 1105952 | tf_op jit(solution)/shard_map/ppermute | solution.py:444
  (74 shorter events, 74.8 us)
Async XLA Ops:
  1.1 14.7 %collective-permute-start = (bf16[1,720,256]{2,1,0:T(8,128)(2,1)S(1)}, bf16[1,720,256]{2,1,0:T(8,128)(2,1)S(1)}, u32[]{:S(2)}, u32[]{:S(2)}) collective-permute-start(bf16[1,720,256]{2,1,0:T(8,128)(2,1)S(1)} %get-tuple-element.82), channel_id=1, source_target_pairs={{0,2},{2,4},{4,6},{6,8},{8,10},{10,12},{12,14},{14,16},{16,18},{18... | collective-permute-start | bytes 1105928 | tf_op jit(solution)/shard_map/ppermute | solution.py:388
  3.1 12.8 %collective-permute-start.1 = (bf16[1,720,256]{2,1,0:T(8,128)(2,1)S(1)}, bf16[1,720,256]{2,1,0:T(8,128)(2,1)}, u32[]{:S(2)}, u32[]{:S(2)}) collective-permute-start(bf16[1,720,256]{2,1,0:T(8,128)(2,1)S(1)} %get-tuple-element.81), channel_id=1, source_target_pairs={{2,0},{4,2},{6,4},{8,6},{10,8},{12,10},{14,12},{16,14},{18,16},{20... | collective-permute-start | bytes 1105928 | tf_op jit(solution)/shard_map/ppermute | solution.py:389
  15.9 7.3 %copy-start.13 = (s32[9]{0:T(128)S(1)}, s32[9]{0:T(128)}, u32[]{:S(2)}) copy-start(s32[9]{0:T(128)} %param.19) | copy-start | bytes 112
  15.9 7.4 %copy-start.12 = (s32[9]{0:T(128)S(1)}, s32[9]{0:T(128)}, u32[]{:S(2)}) copy-start(s32[9]{0:T(128)} %param.20) | copy-start | bytes 112
  15.9 7.6 %copy-start.10 = (f32[9,256]{1,0:T(8,128)S(1)}, f32[9,256]{1,0:T(8,128)}, u32[]{:S(2)}) copy-start(f32[9,256]{1,0:T(8,128)} %param.18) | copy-start | bytes 27652
  16.6 83.9 %all-to-all-start.2 = ((bf16[32,4,2,24,256]{4,3,2,1,0:T(8,128)(2,1)}), bf16[32,4,2,24,256]{4,3,2,1,0:T(8,128)(2,1)S(1)}, u32[]{:S(2)}, u32[]{:S(2)}) async-start(bf16[32,4,2,24,256]{4,3,2,1,0:T(8,128)(2,1)} %bitcast.13), calls=%async_computation.2 | async-start | bytes 6291456 | tf_op jit(solution)/shard_map/all_to_all | solution.py:412
  48.8 5.6 %copy-start.6 = (bf16[2,512,256]{2,1,0:T(8,128)(2,1)S(1)}, bf16[2,512,256]{2,1,0:T(8,128)(2,1)}, u32[]{:S(2)}) copy-start(bf16[2,512,256]{2,1,0:T(8,128)(2,1)} %own_ref.5) | copy-start | bytes 1572868
  52.9 46.9 %collective-permute-start.4 = (bf16[3,720,256]{2,1,0:T(8,128)(2,1)S(1)}, bf16[3,720,256]{2,1,0:T(8,128)(2,1)}, u32[]{:S(2)}, u32[]{:S(2)}) collective-permute-start(bf16[3,720,256]{2,1,0:T(8,128)(2,1)S(1)} %get-tuple-element.85), channel_id=1, source_target_pairs={{0,1},{1,0},{2,3},{3,2},{4,5},{5,4},{6,7},{7,6},{8,9},{9,8},{10,11... | collective-permute-start | bytes 3317768 | tf_op jit(solution)/shard_map/ppermute | solution.py:291
  54.4 45.3 %collective-permute-start.3 = (bf16[2,512,256]{2,1,0:T(8,128)(2,1)S(1)}, bf16[2,512,256]{2,1,0:T(8,128)(2,1)S(1)}, u32[]{:S(2)}, u32[]{:S(2)}) collective-permute-start(bf16[2,512,256]{2,1,0:T(8,128)(2,1)S(1)} %copy-done.6), channel_id=1, source_target_pairs={{0,1},{1,0},{2,3},{3,2},{4,5},{5,4},{6,7},{7,6},{8,9},{9,8},{10,11... | collective-permute-start | bytes 1572872 | tf_op jit(solution)/shard_map/ppermute | solution.py:398
  102.2 76.6 %all-to-all-start.1 = ((bf16[32,4,2,24,256]{4,3,2,1,0:T(8,128)(2,1)}), bf16[32,4,2,24,256]{4,3,2,1,0:T(8,128)(2,1)S(1)}, u32[]{:S(2)}, u32[]{:S(2)}) async-start(bf16[32,4,2,24,256]{4,3,2,1,0:T(8,128)(2,1)} %bitcast.15), calls=%async_computation.1 | async-start | bytes 6291456 | tf_op jit(solution)/shard_map/all_to_all | solution.py:412
  109.6 57.9 %collective-permute-start.2 = (bf16[3,720,256]{2,1,0:T(8,128)(2,1)}, bf16[3,720,256]{2,1,0:T(8,128)(2,1)}, u32[]{:S(2)}, u32[]{:S(2)}) collective-permute-start(bf16[3,720,256]{2,1,0:T(8,128)(2,1)} %get-tuple-element.86), channel_id=1, source_target_pairs={{0,1},{1,0},{2,3},{3,2},{4,5},{5,4},{6,7},{7,6},{8,9},{9,8},{10,11... | collective-permute-start | bytes 3317768 | tf_op jit(solution)/shard_map/ppermute | solution.py:291
  167.5 22.7 %copy-start.11 = (f32[384]{0:T(512)S(1)}, f32[384]{0:T(512)}, u32[]{:S(2)}) copy-start(f32[384]{0:T(512)} %param.17) | copy-start | bytes 4612
  180.6 75.0 %all-to-all-start = ((bf16[32,4,2,24,256]{4,3,2,1,0:T(8,128)(2,1)}), bf16[32,4,2,24,256]{4,3,2,1,0:T(8,128)(2,1)S(1)}, u32[]{:S(2)}, u32[]{:S(2)}) async-start(bf16[32,4,2,24,256]{4,3,2,1,0:T(8,128)(2,1)} %bitcast.14), calls=%async_computation | async-start | bytes 6291456 | tf_op jit(solution)/shard_map/all_to_all | solution.py:412
  188.1 56.1 %collective-permute-start.5 = (bf16[3,720,256]{2,1,0:T(8,128)(2,1)}, bf16[3,720,256]{2,1,0:T(8,128)(2,1)}, u32[]{:S(2)}, u32[]{:S(2)}) collective-permute-start(bf16[3,720,256]{2,1,0:T(8,128)(2,1)} %get-tuple-element.84), channel_id=1, source_target_pairs={{0,1},{1,0},{2,3},{3,2},{4,5},{5,4},{6,7},{7,6},{8,9},{9,8},{10,11... | collective-permute-start | bytes 3317768 | tf_op jit(solution)/shard_map/ppermute | solution.py:291
  271.2 58.0 %all-to-all-start.3 = ((bf16[32,3,3,8,512]{4,3,2,1,0:T(8,128)(2,1)}), bf16[32,3,3,8,512]{4,3,2,1,0:T(8,128)(2,1)S(1)}, u32[]{:S(2)}, u32[]{:S(2)}) async-start(bf16[32,3,3,8,512]{4,3,2,1,0:T(8,128)(2,1)} %get-tuple-element.60), calls=%async_computation.3 | async-start | bytes 4718592 | tf_op jit(solution)/shard_map/all_to_all | solution.py:439
  276.9 52.3 %collective-permute-start.6 = (bf16[3,720,256]{2,1,0:T(8,128)(2,1)}, bf16[3,720,256]{2,1,0:T(8,128)(2,1)S(1)}, u32[]{:S(2)}, u32[]{:S(2)}) collective-permute-start(bf16[3,720,256]{2,1,0:T(8,128)(2,1)} %get-tuple-element.83), channel_id=1, source_target_pairs={{0,1},{1,0},{2,3},{3,2},{4,5},{5,4},{6,7},{7,6},{8,9},{9,8},{10,11... | collective-permute-start | bytes 3317768 | tf_op jit(solution)/shard_map/ppermute | solution.py:291
  329.2 1.8 copy-start.9
  331.0 58.0 %all-to-all-start.4 = ((bf16[32,3,3,8,512]{4,3,2,1,0:T(8,128)(2,1)}), bf16[32,3,3,8,512]{4,3,2,1,0:T(8,128)(2,1)S(1)}, u32[]{:S(2)}, u32[]{:S(2)}) async-start(bf16[32,3,3,8,512]{4,3,2,1,0:T(8,128)(2,1)} %get-tuple-element.62), calls=%async_computation.4 | async-start | bytes 4718592 | tf_op jit(solution)/shard_map/all_to_all | solution.py:439
  346.8 42.3 %collective-permute-start.7 = (bf16[3,720,256]{2,1,0:T(8,128)(2,1)}, bf16[3,720,256]{2,1,0:T(8,128)(2,1)S(1)}, u32[]{:S(2)}, u32[]{:S(2)}) collective-permute-start(bf16[3,720,256]{2,1,0:T(8,128)(2,1)} %get-tuple-element.66), channel_id=1, source_target_pairs={{0,1},{1,0},{2,3},{3,2},{4,5},{5,4},{6,7},{7,6},{8,9},{9,8},{10,11... | collective-permute-start | bytes 3317768 | tf_op jit(solution)/shard_map/ppermute | solution.py:444
  390.5 58.0 %all-to-all-start.5 = ((bf16[32,3,3,8,512]{4,3,2,1,0:T(8,128)(2,1)}), bf16[32,3,3,8,512]{4,3,2,1,0:T(8,128)(2,1)S(1)}, u32[]{:S(2)}, u32[]{:S(2)}) async-start(bf16[32,3,3,8,512]{4,3,2,1,0:T(8,128)(2,1)} %get-tuple-element.67), calls=%async_computation.5 | async-start | bytes 4718592 | tf_op jit(solution)/shard_map/all_to_all | solution.py:439
  406.2 42.3 %collective-permute-start.8 = (bf16[3,720,256]{2,1,0:T(8,128)(2,1)}, bf16[3,720,256]{2,1,0:T(8,128)(2,1)}, u32[]{:S(2)}, u32[]{:S(2)}) collective-permute-start(bf16[3,720,256]{2,1,0:T(8,128)(2,1)} %get-tuple-element.71), channel_id=1, source_target_pairs={{0,1},{1,0},{2,3},{3,2},{4,5},{5,4},{6,7},{7,6},{8,9},{9,8},{10,11... | collective-permute-start | bytes 3317768 | tf_op jit(solution)/shard_map/ppermute | solution.py:444
  450.0 58.1 %all-to-all-start.6 = ((bf16[32,3,3,8,512]{4,3,2,1,0:T(8,128)(2,1)}), bf16[32,3,3,8,512]{4,3,2,1,0:T(8,128)(2,1)}, u32[]{:S(2)}, u32[]{:S(2)}) async-start(bf16[32,3,3,8,512]{4,3,2,1,0:T(8,128)(2,1)} %get-tuple-element.72), calls=%async_computation.6 | async-start | bytes 4718592 | tf_op jit(solution)/shard_map/all_to_all | solution.py:439
  465.7 57.1 %collective-permute-start.9 = (bf16[3,720,256]{2,1,0:T(8,128)(2,1)}, bf16[3,720,256]{2,1,0:T(8,128)(2,1)S(1)}, u32[]{:S(2)}, u32[]{:S(2)}) collective-permute-start(bf16[3,720,256]{2,1,0:T(8,128)(2,1)} %get-tuple-element.79), channel_id=1, source_target_pairs={{0,1},{1,0},{2,3},{3,2},{4,5},{5,4},{6,7},{7,6},{8,9},{9,8},{10,11... | collective-permute-start | bytes 3317768 | tf_op jit(solution)/shard_map/ppermute | solution.py:444
  518.1 26.6 %collective-permute-start.10 = (bf16[3,720,256]{2,1,0:T(8,128)(2,1)}, bf16[3,720,256]{2,1,0:T(8,128)(2,1)S(1)}, u32[]{:S(2)}, u32[]{:S(2)}) collective-permute-start(bf16[3,720,256]{2,1,0:T(8,128)(2,1)} %get-tuple-element.80), channel_id=1, source_target_pairs={{0,1},{1,0},{2,3},{3,2},{4,5},{5,4},{6,7},{7,6},{8,9},{9,8},{10,11... | collective-permute-start | bytes 3317768 | tf_op jit(solution)/shard_map/ppermute | solution.py:444
  (8 other events, 11.0 us)

commit v4 on v3

--- a/solution.py
+++ b/solution.py
@@ -73,13 +73,13 @@
         + [pl.BlockSpec(memory_space=pl.ANY)] * len(first),
         out_specs=pl.BlockSpec((rows, cycles, width), lambda t: (0, 0, 0)),
         scratch_shapes=[pltpu.VMEM((width // LANES, rows * cycles, LANES), F32)],
-        compiler_params=params(58),
+        compiler_params=params(60),
         cost_estimate=cost(2 * rows * nlon * cycles * width, grid.size * 2),
     )(table, grid, *first)
 
 
-def middle_kernel(counts, at_ref, spec_ref, basis_ref, quad_ref, own_ref, other_ref, gain_ref, *rest):
-    outs, mix_ref, held = (rest[-len(counts) - 2 : -2], rest[-2], rest[-1])
+def middle_kernel(plan, at_ref, spec_ref, basis_ref, quad_ref, own_ref, other_ref, gain_ref, *rest):
+    outs, mix_ref, held = (rest[-len(plan) - 2 : -2], rest[-2], rest[-1])
     mode = pl.program_id(0)
     groups, sides, _, _, cycles, width = spec_ref.shape
 
@@ -131,23 +131,17 @@
         for at in range(half // LANES):
             whole = held[at].reshape(groups * sides, nlat // (groups * sides), slots, LANES)
             start = 0
-            for out, count in zip(outs, counts):
+            for out, (_, _, count) in zip(outs, plan):
                 part = whole[:, start : start + count].astype(BF)
                 out[:, 0, :, :, at * LANES : (at + 1) * LANES] = part
                 start += count
 
 
-def middle_part(part, spec, basis, quad, mix, other, gain, offset, counts, filled, first):
+def middle_part(spec, basis, quad, mix, other, gain, offset, plan, filled):
     groups, sides, _, _, cycles, width = spec.shape
     nlat = groups * cycles
-    modes = basis.shape[0]
-    parts = modes // sides // STEP
     channels = sides * width
     slots = 2 * STEP
-    everywhere = [
-        jax.ShapeDtypeStruct((groups * sides, parts, count, slots, channels), BF)
-        for count in counts
-    ]
     fixed = lambda m, at: (0, 0)
     specs = [
         pl.BlockSpec((groups, sides, 1, 2, cycles, width), lambda m, at: (0, 0, m, 0, 0, 0)),
@@ -159,16 +153,17 @@
     ]
     arguments = [spec, basis, quad, mix, other, gain]
     aliases = {}
-    if filled is not None:
-        for at, value in enumerate(filled):
+    for at, value in enumerate(filled):
+        if value is not None:
             aliases[1 + len(arguments)] = at
             specs.append(pl.BlockSpec(memory_space=pl.ANY))
             arguments.append(value)
-    specs += [pl.BlockSpec(memory_space=pl.ANY)] * len(first)
-    arguments += first
     return pl.pallas_call(
-        functools.partial(middle_kernel, counts),
-        out_shape=everywhere,
+        functools.partial(middle_kernel, plan),
+        out_shape=[
+            jax.ShapeDtypeStruct((groups * sides, total, count, slots, channels), BF)
+            for total, _, count in plan
+        ],
         grid_spec=pltpu.PrefetchScalarGridSpec(
             num_scalar_prefetch=1,
             grid=(STEP,),
@@ -176,9 +171,9 @@
             out_specs=[
                 pl.BlockSpec(
                     (groups * sides, 1, count, slots, channels),
-                    lambda m, at: (0, part, 0, 0, 0),
+                    functools.partial(lambda slot, m, at: (0, slot, 0, 0, 0), slot),
                 )
-                for count in counts
+                for _, slot, count in plan
             ],
             scratch_shapes=[
                 pltpu.VMEM((2 * channels, 2 * channels), BF),
@@ -278,7 +273,7 @@
             out_specs=pl.BlockSpec(row, lambda t, *_: (t, 0, 0)),
             scratch_shapes=[pltpu.VMEM((3, nlon + 16, width), F32)],
         ),
-        compiler_params=params(58),
+        compiler_params=params(60),
         cost_estimate=cost(span * nlon * width * 400, span * nlon * width * 6),
     )(jnp.stack([base, cycles]).astype(jnp.int32), ratio, weight, grid, grid, grid, before, after)
 
@@ -293,13 +288,15 @@
     return got
 
 
-def tail_kernel(place_ref, back_ref, own_ref, got_ref, table_ref, gain_ref, up_ref, down_ref, *rest):
+def tail_kernel(pieces, place_ref, own_ref, got_ref, gain_ref, up_ref, down_ref, *rest):
     mine_ref, theirs_ref = rest[-2:]
     first = place_ref[1] == 0
     channels = up_ref.shape[0]
     width = own_ref.shape[2]
-    back = back_ref[:, :, 0].astype(F32).reshape(table_ref.shape[1], channels).astype(BF)
-    spectral = jnp.dot(table_ref[...], back, preferred_element_type=F32)
+    spectral = 0.0
+    for back_ref, table_ref in zip(rest[:pieces], rest[pieces : 2 * pieces]):
+        back = back_ref[:, :, 0].astype(F32).reshape(table_ref.shape[1], channels).astype(BF)
+        spectral += jnp.dot(table_ref[...], back, preferred_element_type=F32)
     own = own_ref[0].astype(F32)
     got = got_ref[0].astype(F32)
     low = jnp.where(first, own, got)
@@ -318,28 +315,31 @@
     theirs_ref[0] = jnp.where(first, high, low).astype(BF)
 
 
-def tail_part(back, own, got, start, table, ln_gain, up_weight, down_weight, place, result, cycles):
-    devices, parts, count, slots, channels = back.shape
+def tail_part(backs, tables, own, got, start, ln_gain, up_weight, down_weight, place, result, cycles):
+    count = backs[0].shape[2]
+    channels = backs[0].shape[4]
     _, nlon, width = own.shape
     fixed = lambda t, at: (0, 0)
     row = (1, nlon, width)
     specs = [
-        pl.BlockSpec((devices, parts, 1, slots, channels), lambda t, at: (0, 0, t, 0, 0)),
         pl.BlockSpec(row, lambda t, at: (start + t, 0, 0)),
         pl.BlockSpec(row, lambda t, at: (t, 0, 0)),
-        pl.BlockSpec(table.shape, fixed),
         pl.BlockSpec(ln_gain.shape, fixed),
         pl.BlockSpec(up_weight.shape, fixed),
         pl.BlockSpec(down_weight.shape, fixed),
     ]
-    arguments = [back, own, got, table, ln_gain, up_weight, down_weight]
+    for back in backs:
+        block = back.shape[:2] + (1,) + back.shape[3:]
+        specs.append(pl.BlockSpec(block, lambda t, at: (0, 0, t, 0, 0)))
+    specs += [pl.BlockSpec(table.shape, fixed) for table in tables]
+    arguments = [own, got, ln_gain, up_weight, down_weight, *backs, *tables]
     aliases = {}
     if result is not None:
         aliases[1 + len(arguments)] = 0
         specs.append(pl.BlockSpec(memory_space=pl.ANY))
         arguments.append(result)
     return pl.pallas_call(
-        tail_kernel,
+        functools.partial(tail_kernel, len(backs)),
         out_shape=[
             jax.ShapeDtypeStruct((cycles, nlon, width), BF),
             jax.ShapeDtypeStruct((count, nlon, width), BF),
@@ -356,7 +356,7 @@
         input_output_aliases=aliases,
         compiler_params=params(60),
         cost_estimate=cost(
-            2 * count * nlon * channels * (table.shape[1] + 2 * channels),
+            2 * count * nlon * channels * (sum(table.shape[1] for table in tables) + 2 * channels),
             count * nlon * channels * 8,
         ),
     )(place, *arguments)
@@ -373,7 +373,8 @@
     few = modes // sides
     parts = few // STEP
     span = cycles // sides
-    counts = [span // 4] * 4
+    third = span // 3
+    counts = [third + 1, third, span - 2 * third - 1]
 
     cosine, sine = angle_table(nlon)
     both = np.stack([cosine, -sine], axis=-1)
@@ -381,7 +382,11 @@
         both.reshape(nlon, groups * sides, parts, STEP * 2).transpose(2, 1, 3, 0)
     ).reshape(parts, groups * sides * STEP * 2, nlon)
     weight_m = np.where(np.arange(MMAX) == 0, 1.0, 2.0)[None, :, None]
-    inv_table = jnp.asarray((both * weight_m).reshape(nlon, 2 * MMAX), BF)
+    inv_table = (both * weight_m).reshape(nlon, groups * sides, parts, STEP * 2)
+
+    def inverse(low, high):
+        return jnp.asarray(inv_table[:, :, low:high].reshape(nlon, -1), BF)
+
 
     up = [(i, i + 1) for i in range(groups - 1)]
     down = [(j, i) for i, j in up]
@@ -401,11 +406,11 @@
         spec = forward_part(grid, jnp.asarray(fwd_table[part], BF), [])
         spec = spec.reshape(groups * sides, STEP, 2, cycles, width)
         if part == 0:
-            spec, before, after = lax.optimization_barrier((spec, before, after))
+            spec, before, after, other = lax.optimization_barrier((spec, before, after, other))
             asked = local_part(grid, before, after, ratio, weight, (1 - side) * span, span)
             got = exchanged(asked, counts)
         elif part == 1:
-            spec, other, got[0] = lax.optimization_barrier((spec, other, got[0]))
+            spec, got[2] = lax.optimization_barrier((spec, got[2]))
             own = local_part(grid, before, after, ratio, weight, side * span, span)
         elif part == 2:
             spec, got[1], own = lax.optimization_barrier((spec, got[1], own))
@@ -416,35 +421,55 @@
     quad = (math.pi / nlat * jnp.sin(theta))[None, :]
     gain = spectral_gain[:, None]
 
-    filled = None
+    begin, filled = (None, [None] * 2)
     for part in range(parts):
         offset = jnp.stack([side * few + part * STEP, side]).astype(jnp.int32)
-        filled = middle_part(
-            part, gathered[part], basis, quad, mix_weight, other, gain, offset, counts, filled,
-            got[2:3] if part == parts - 1 else [],
+        late = part == parts - 1
+        plan = [(1, 0, counts[0]) if late else (parts - 1, part, counts[0])]
+        plan += [(parts, part, count) for count in counts[1:]]
+        value = None if late else begin
+        ready = middle_part(
+            gathered[part], basis, quad, mix_weight, other, gain, offset, plan, [value] + filled
         )
+        if late:
+            end = ready[0]
+        else:
+            begin = ready[0]
+        filled = list(ready[1:])
+
+    def shuffled(value):
+        return lax.all_to_all(value, ("lat", "chan"), 0, 0, tiled=True)
 
     place = jnp.stack([side * span, side]).astype(jnp.int32)
-    result = None
+
+    def finished(at, backs, tables, result):
+        result, theirs = tail_part(
+            backs, tables, own, got[at], sum(counts[:at]), ln_gain[None, :], up_weight,
+            down_weight, place, result, cycles,
+        )
+        return (result, theirs)
+
+    begin, _ = lax.optimization_barrier((begin, gathered[-1]))
+    begin = shuffled(begin)
+    end, begin, got[0] = lax.optimization_barrier((end, begin, got[0]))
+    end = shuffled(end)
+    second, end = lax.optimization_barrier((filled[0], end))
+    second = shuffled(second)
+    result, theirs = finished(
+        0, [begin, end], [inverse(0, parts - 1), inverse(parts - 1, parts)], None
+    )
+    sent = [lax.ppermute(theirs[: counts[2]], "chan", SWAP)]
+    rest = lax.ppermute(theirs[counts[2] :], "chan", SWAP)
+    third, second, _ = lax.optimization_barrier((filled[1], second, sent[0]))
+    third = shuffled(third)
+    result, theirs = finished(1, [second], [inverse(0, parts)], result)
+    sent += [rest, lax.ppermute(theirs, "chan", SWAP)]
+    third, sent[1] = lax.optimization_barrier((third, sent[1]))
+    result, theirs = finished(2, [third], [inverse(0, parts)], result)
+    sent.append(lax.ppermute(theirs, "chan", SWAP))
     start = 0
-    sent = []
-    back = None
-    for at, (value, count) in enumerate(zip(filled, counts)):
-        if at > 0:
-            value, back = lax.optimization_barrier((value, back))
-        if at == 1:
-            value, got[3] = lax.optimization_barrier((value, got[3]))
-        if at > 1:
-            value, sent[at - 2] = lax.optimization_barrier((value, sent[at - 2]))
-        back = lax.all_to_all(value, ("lat", "chan"), 0, 0, tiled=True)
-        result, theirs = tail_part(
-            back, own, got[at], start, inv_table, ln_gain[None, :], up_weight, down_weight,
-            place, result, cycles,
-        )
-        sent.append(lax.ppermute(theirs, "chan", SWAP))
-        start += count
-    start = 0
-    for value, count in zip(sent, counts):
+    for value in sent:
+        count = value.shape[0]
         result = lax.dynamic_update_slice_in_dim(result, value, (1 - side) * span + start, 0)
         start += count
     return result
@@ -575,7 +600,7 @@
         sides == 2
         and cycles % 8 == 0
         and cycles % sides == 0
-        and cycles // sides % 4 == 0
+        and cycles // sides >= 6
         and basis.shape[0] // (sides * STEP) == 3
         and basis.shape[0] % (sides * STEP) == 0
         and nlon % 8 == 0

time: 550 us -> 539 us (0.980)
  blocking collectives: 0 us -> 35 us
  waiting for transfers between devices: 300 us -> 269 us
  starting transfers between devices: 59.7 us -> 48.9 us
    all_to_all x4 -> x3, waiting for transfers between devices: 173 us -> 23.1 us  [shuffled(): return lax.all_to_all(value, ('lat', 'chan'), 0, 0, tiled=True)]
    ppermute x0 -> x3, waiting for transfers between devices: none -> 72.3 us  [the longest x1 40.7 us: fast(): sent = [lax.ppermute(theirs[:counts[2]], 'chan', SWAP)]]
    ppermute x4 -> x3, waiting for transfers between devices: 47.9 us -> 105 us  [exchanged(): got.append(lax.ppermute(piece, 'chan', SWAP))]
    ppermute x1, waiting for transfers between devices: 35.6 us -> 0.01 us  [fast(): other = lax.ppermute(mix_weight, 'chan', SWAP)]
    all_to_all x0 -> x1, blocking collectives: none -> 35 us  [shuffled(): return lax.all_to_all(value, ('lat', 'chan'), 0, 0, tiled=True)]
    all_to_all x3, waiting for transfers between devices: 22.6 us -> 46.3 us  [fast(): spec = lax.all_to_all(spec, ('lat', 'chan'), 0, 0, tiled=True)]
    unnamed x28 -> x18, local copies, waits for them, and re-layouts: 11.4 us -> 4.15 us
    all_to_all x4 -> x3, starting transfers between devices: 22.8 us -> 17 us  [shuffled(): return lax.all_to_all(value, ('lat', 'chan'), 0, 0, tiled=True)]
  transfers between devices with their start and end apart: 18 -> 16, of which waited for: 10 -> 12; matrix products, arithmetic and copies ran while one was open for 3% -> 5% of each run, Pallas kernels for 26% -> 29%
where the time goes in v4:
time: 539 us; the launch traced here: 536 us
  waiting for transfers between devices  269 us (50%)
  Pallas kernels  154 us (29%)
  starting transfers between devices  48.9 us (9%)
  blocking collectives  35 us (6%)
  local copies, waits for them, and re-layouts  23.9 us (4%)
  other arithmetic  5.44 us (1%)
    ppermute x3, waiting for transfers between devices, exchanged(): got.append(lax.ppermute(piece, 'chan', SWAP))  105 us
    pallas_call x2, Pallas kernels, local_part(): pl.pallas_call(local_rows, out_shape=jax.ShapeDtypeStruct((span, nlon, wi...  47.8 us
    all_to_all x3, waiting for transfers between devices, fast(): spec = lax.all_to_all(spec, ('lat', 'chan'), 0, 0, tiled=True)  46.3 us
    pallas_call x3, Pallas kernels, middle_part(): pl.pallas_call(functools.partial(middle_kernel, plan), out_shape=[jax.Sha...  41.9 us
    ppermute x1, waiting for transfers between devices, fast(): sent = [lax.ppermute(theirs[:counts[2]], 'chan', SWAP)]  40.7 us
    pallas_call x3, Pallas kernels, tail_part(): pl.pallas_call(functools.partial(tail_kernel, len(backs)), out_shape=[jax...  36.4 us
    all_to_all x1, blocking collectives, shuffled(): return lax.all_to_all(value, ('lat', 'chan'), 0, 0, tiled=True)  35 us
    pallas_call x3, Pallas kernels, forward_part(): pl.pallas_call(functools.partial(forward_kernel, 1.0 / nlon), out_shape=j...  27.4 us
  transfers between devices with their start and end apart: 16, of which 12 were waited for; matrix products, arithmetic and copies ran while one was open for 5% of the time, Pallas kernels for 29%

profile of v4, /device:TPU:26, one launch (start us, length us, event | category | flops | bytes accessed | tf_op | source)
XLA Modules:
  0.0 535.9 jit_solution(5052492705200448157)
XLA Ops:
  7.0 9.1 %shard_map.164 = bf16[256,24,256]{2,1,0:T(8,128)(2,1)} custom-call(bf16[256,720]{1,0:T(8,128)(2,1)} %constant.70.clone.table_ref, bf16[24,720,256]{2,1,0:T(8,128)(2,1)} %grid_ref.5), custom_call_target="tpu_custom_call" | custom-call | flops 2264924160 | bytes 8847360 | tf_op jit(solution)/shard_map/pallas_call | solution.py:65
  24.4 23.9 %shard_map.165 = bf16[12,720,256]{2,1,0:T(8,128)(2,1)} custom-call(s32[2]{0:T(128)} %pad_add_fusion.1.base_ref, f32[24,3]{1,0:T(8,128)} %sine_divide_fusion.ratio_ref, f32[3,7,256]{2,1,0:T(8,128)} %select_reduce_fusion.weight_ref, bf16[24,720,256]{2,1,0:T(8,128)(2,1)} %grid_ref.5, bf16[24,720,256]{2,1,0:T(8,128)(2,1)} %grid_ref.5, ...), custom_call_target="tpu_custom_call" | custom-call | flops 884736000 | bytes 13271040 | tf_op jit(solution)/shard_map/pallas_call | solution.py:259
  52.2 9.2 %shard_map.167 = bf16[256,24,256]{2,1,0:T(8,128)(2,1)} custom-call(bf16[256,720]{1,0:T(8,128)(2,1)} %constant.71.clone.table_ref, bf16[24,720,256]{2,1,0:T(8,128)(2,1)} %grid_ref.5), custom_call_target="tpu_custom_call" | custom-call | flops 2264924160 | bytes 8847360 | tf_op jit(solution)/shard_map/pallas_call | solution.py:65
  61.4 24.1 %collective-permute-done.4.got_ref = bf16[3,720,256]{2,1,0:T(8,128)(2,1)} collective-permute-done((bf16[3,720,256]{2,1,0:T(8,128)(2,1)}, bf16[3,720,256]{2,1,0:T(8,128)(2,1)}, u32[]{:S(2)}, u32[]{:S(2)}) %collective-permute-start.4) | collective-permute-done | bytes 1105952 | tf_op jit(solution)/shard_map/ppermute | solution.py:286
  103.4 9.1 %shard_map.163 = bf16[256,24,256]{2,1,0:T(8,128)(2,1)} custom-call(bf16[256,720]{1,0:T(8,128)(2,1)} %constant.72.clone.table_ref, bf16[24,720,256]{2,1,0:T(8,128)(2,1)} %grid_ref.5), custom_call_target="tpu_custom_call" | custom-call | flops 2264924160 | bytes 8847360 | tf_op jit(solution)/shard_map/pallas_call | solution.py:65
  112.5 23.9 %shard_map.166.own_ref = bf16[12,720,256]{2,1,0:T(8,128)(2,1)} custom-call(s32[2]{0:T(128)} %pad_add_fusion.base_ref, f32[24,3]{1,0:T(8,128)} %sine_divide_fusion.ratio_ref, f32[3,7,256]{2,1,0:T(8,128)} %select_reduce_fusion.weight_ref, bf16[24,720,256]{2,1,0:T(8,128)(2,1)} %grid_ref.5, bf16[24,720,256]{2,1,0:T(8,128)(2,1)} %grid_ref.5, ...), custom_call_target="tpu_custom_call" | custom-call | flops 884736000 | bytes 13271040 | tf_op jit(solution)/shard_map/pallas_call | solution.py:259
  136.5 29.5 %collective-permute-done.3.got_ref = bf16[4,720,256]{2,1,0:T(8,128)(2,1)} collective-permute-done((bf16[4,720,256]{2,1,0:T(8,128)(2,1)}, bf16[4,720,256]{2,1,0:T(8,128)(2,1)}, u32[]{:S(2)}, u32[]{:S(2)}) %collective-permute-start.3) | collective-permute-done | bytes 1474592 | tf_op jit(solution)/shard_map/ppermute | solution.py:286
  178.0 14.0 %shard_map.168 = (bf16[32,2,5,8,512]{4,3,2,1,0:T(8,128)(2,1)}, bf16[32,3,4,8,512]{4,3,2,1,0:T(8,128)(2,1)}, bf16[32,3,3,8,512]{4,3,2,1,0:T(8,128)(2,1)}) custom-call(s32[2]{0:T(128)} %pad_add_fusion.4.at_ref.place_ref, bf16[16,2,4,2,24,256]{5,4,3,2,1,0:T(8,128)(2,1)} %bitcast.17, f32[24,384,384]{2,1,0:T(8,128)} %basis_ref.5, ...), custom_call_target="tpu_custom_call" | custom-call | flops 5637144576 | bytes 9175040 | tf_op jit(solution)/shard_map/pallas_call | solution.py:161
  192.0 14.0 %shard_map.169 = (bf16[32,2,5,8,512]{4,3,2,1,0:T(8,128)(2,1)}, bf16[32,3,4,8,512]{4,3,2,1,0:T(8,128)(2,1)}, bf16[32,3,3,8,512]{4,3,2,1,0:T(8,128)(2,1)}) custom-call(s32[2]{0:T(128)} %pad_add_fusion.3.at_ref, bf16[16,2,4,2,24,256]{5,4,3,2,1,0:T(8,128)(2,1)} %bitcast.16, ...), custom_call_target="tpu_custom_call", output_to_operand_aliasing={{0}: (7, {}), {1}: (8, {}), {2}: (9, {})} | custom-call | flops 5637144576 | bytes 9175040 | tf_op jit(solution)/shard_map/pallas_call | solution.py:161
  206.0 38.6 %all-to-all-done = bf16[32,4,2,24,256]{4,3,2,1,0:T(8,128)(2,1)S(1)} async-done(((bf16[32,4,2,24,256]{4,3,2,1,0:T(8,128)(2,1)}), bf16[32,4,2,24,256]{4,3,2,1,0:T(8,128)(2,1)S(1)}, u32[]{:S(2)}, u32[]{:S(2)}) %all-to-all-start) | async-done | bytes 3145760 | tf_op jit(solution)/shard_map/all_to_all | solution.py:417
  244.6 5.8 %all-to-all-start.3 = ((bf16[32,2,5,8,512]{4,3,2,1,0:T(8,128)(2,1)}), bf16[32,2,5,8,512]{4,3,2,1,0:T(8,128)(2,1)}, u32[]{:S(2)}, u32[]{:S(2)}) async-start(bf16[32,2,5,8,512]{4,3,2,1,0:T(8,128)(2,1)} %get-tuple-element.56), calls=%async_computation.3 | async-start | bytes 5242880 | tf_op jit(solution)/shard_map/all_to_all | solution.py:441
  255.4 13.9 %shard_map.170 = (bf16[32,1,5,8,512]{4,3,2,1,0:T(8,128)(2,1)}, bf16[32,3,4,8,512]{4,3,2,1,0:T(8,128)(2,1)}, bf16[32,3,3,8,512]{4,3,2,1,0:T(8,128)(2,1)}) custom-call(s32[2]{0:T(128)} %pad_add_fusion.2.at_ref, bf16[16,2,4,2,24,256]{5,4,3,2,1,0:T(8,128)(2,1)} %bitcast.12, f32[24,384,384]{2,1,0:T(8,128)} %basis_ref.5, ...), custom_call_target="tpu_custom_call", output_to_operand_aliasing={{1}: (7, {}), {2}: (8, {})} | custom-call | flops 5637144576 | bytes 9175040 | tf_op jit(solution)/shard_map/pallas_call | solution.py:161
  269.3 51.2 %collective-permute-done.5.got_ref = bf16[5,720,256]{2,1,0:T(8,128)(2,1)} collective-permute-done((bf16[5,720,256]{2,1,0:T(8,128)(2,1)}, bf16[5,720,256]{2,1,0:T(8,128)(2,1)}, u32[]{:S(2)}, u32[]{:S(2)}) %collective-permute-start.5) | collective-permute-done | bytes 1843232 | tf_op jit(solution)/shard_map/ppermute | solution.py:286
  320.5 35.0 %all_to_all.35.rest_1_ = bf16[32,1,5,8,512]{4,3,2,1,0:T(8,128)(2,1)} all-to-all(bf16[32,1,5,8,512]{4,3,2,1,0:T(8,128)(2,1)} %get-tuple-element.57), channel_id=1, replica_groups=mesh['lat'=16,'chan'=2] {'lat','chan'}, dimensions={0} | all-to-all | bytes 2621440 | tf_op jit(solution)/shard_map/all_to_all | solution.py:441
  361.0 14.3 %shard_map.171 = (bf16[24,720,256]{2,1,0:T(8,128)(2,1)}, bf16[5,720,256]{2,1,0:T(8,128)(2,1)}) custom-call(s32[2]{0:T(128)} %pad_add_fusion.4.at_ref.place_ref, bf16[12,720,256]{2,1,0:T(8,128)(2,1)} %shard_map.166.own_ref, bf16[5,720,256]{2,1,0:T(8,128)(2,1)} %collective-permute-done.5.got_ref, f32[1,512]{1,0:T(1,128)} %bitcast.18, bf16[512,512]{1,0:T(8,128)(2,1)} %up_ref.5, ...), custom_call_target="tpu_custom_call" | custom-call | flops 6606028800 | bytes 14745600 | tf_op jit(solution)/shard_map/pallas_call | solution.py:341
  378.2 40.7 %collective-permute-done.6 = bf16[3,720,256]{2,1,0:T(8,128)(2,1)} collective-permute-done((bf16[3,720,256]{2,1,0:T(8,128)(2,1)S(1)}, bf16[3,720,256]{2,1,0:T(8,128)(2,1)}, u32[]{:S(2)}, u32[]{:S(2)}) %collective-permute-start.6) | collective-permute-done | bytes 1105952 | tf_op jit(solution)/shard_map/ppermute | solution.py:461
  418.9 11.3 %all-to-all-done.5.rest_0_ = bf16[32,3,4,8,512]{4,3,2,1,0:T(8,128)(2,1)S(1)} async-done(((bf16[32,3,4,8,512]{4,3,2,1,0:T(8,128)(2,1)}), bf16[32,3,4,8,512]{4,3,2,1,0:T(8,128)(2,1)S(1)}, u32[]{:S(2)}, u32[]{:S(2)}) %all-to-all-start.5) | async-done | bytes 3145760 | tf_op jit(solution)/shard_map/all_to_all | solution.py:441
  430.3 5.7 %all-to-all-start.6 = ((bf16[32,3,3,8,512]{4,3,2,1,0:T(8,128)(2,1)}), bf16[32,3,3,8,512]{4,3,2,1,0:T(8,128)(2,1)}, u32[]{:S(2)}, u32[]{:S(2)}) async-start(bf16[32,3,3,8,512]{4,3,2,1,0:T(8,128)(2,1)} %get-tuple-element.63), calls=%async_computation.6 | async-start | bytes 4718592 | tf_op jit(solution)/shard_map/all_to_all | solution.py:441
  439.6 12.1 %shard_map.172 = (bf16[24,720,256]{2,1,0:T(8,128)(2,1)}, bf16[4,720,256]{2,1,0:T(8,128)(2,1)}) custom-call(s32[2]{0:T(128)} %pad_add_fusion.4.at_ref.place_ref, bf16[12,720,256]{2,1,0:T(8,128)(2,1)} %shard_map.166.own_ref, bf16[4,720,256]{2,1,0:T(8,128)(2,1)} %collective-permute-done.3.got_ref, f32[1,512]{1,0:T(1,128)} %bitcast.19, ...), custom_call_target="tpu_custom_call", output_to_operand_aliasing={{0}: (8, {})} | custom-call | flops 5284823040 | bytes 11796480 | tf_op jit(solution)/shard_map/pallas_call | solution.py:341
  452.2 24.4 %collective-permute-done.7 = bf16[2,720,256]{2,1,0:T(8,128)(2,1)} collective-permute-done((bf16[2,720,256]{2,1,0:T(8,128)(2,1)}, bf16[2,720,256]{2,1,0:T(8,128)(2,1)}, u32[]{:S(2)}, u32[]{:S(2)}) %collective-permute-start.7) | collective-permute-done | bytes 737312 | tf_op jit(solution)/shard_map/ppermute | solution.py:462
  476.7 11.7 %all-to-all-done.6.rest_0_ = bf16[32,3,3,8,512]{4,3,2,1,0:T(8,128)(2,1)} async-done(((bf16[32,3,3,8,512]{4,3,2,1,0:T(8,128)(2,1)}), bf16[32,3,3,8,512]{4,3,2,1,0:T(8,128)(2,1)}, u32[]{:S(2)}, u32[]{:S(2)}) %all-to-all-start.6) | async-done | bytes 2359328 | tf_op jit(solution)/shard_map/all_to_all | solution.py:441
  488.4 10.0 %shard_map.173 = (bf16[24,720,256]{2,1,0:T(8,128)(2,1)}, bf16[3,720,256]{2,1,0:T(8,128)(2,1)}) custom-call(s32[2]{0:T(128)} %pad_add_fusion.4.at_ref.place_ref, bf16[12,720,256]{2,1,0:T(8,128)(2,1)} %shard_map.166.own_ref, bf16[3,720,256]{2,1,0:T(8,128)(2,1)} %collective-permute-done.4.got_ref, f32[1,512]{1,0:T(1,128)} %bitcast.20, ...), custom_call_target="tpu_custom_call", output_to_operand_aliasing={{0}: (8, {})} | custom-call | flops 3963617280 | bytes 8847360 | tf_op jit(solution)/shard_map/pallas_call | solution.py:341
  504.1 7.1 %collective-permute-done.8 = bf16[4,720,256]{2,1,0:T(8,128)(2,1)S(1)} collective-permute-done((bf16[4,720,256]{2,1,0:T(8,128)(2,1)}, bf16[4,720,256]{2,1,0:T(8,128)(2,1)S(1)}, u32[]{:S(2)}, u32[]{:S(2)}) %collective-permute-start.8) | collective-permute-done | bytes 1474592 | tf_op jit(solution)/shard_map/ppermute | solution.py:466
  512.4 22.4 %collective-permute-done.9 = bf16[3,720,256]{2,1,0:T(8,128)(2,1)S(1)} collective-permute-done((bf16[3,720,256]{2,1,0:T(8,128)(2,1)}, bf16[3,720,256]{2,1,0:T(8,128)(2,1)S(1)}, u32[]{:S(2)}, u32[]{:S(2)}) %collective-permute-start.9) | collective-permute-done | bytes 1105952 | tf_op jit(solution)/shard_map/ppermute | solution.py:469
  (64 shorter events, 74.3 us)
Async XLA Ops:
  0.0 16.1 %collective-permute-start.2 = (bf16[2,512,256]{2,1,0:T(8,128)(2,1)}, bf16[2,512,256]{2,1,0:T(8,128)(2,1)}, u32[]{:S(2)}, u32[]{:S(2)}) collective-permute-start(bf16[2,512,256]{2,1,0:T(8,128)(2,1)} %own_ref.5), channel_id=1, source_target_pairs={{0,1},{1,0},{2,3},{3,2},{4,5},{5,4},{6,7},{7,6},{8,9},{9,8},{10,11... | collective-permute-start | bytes 1572872 | tf_op jit(solution)/shard_map/ppermute | solution.py:403
  2.7 13.4 %collective-permute-start.1 = (bf16[1,720,256]{2,1,0:T(8,128)(2,1)S(1)}, bf16[1,720,256]{2,1,0:T(8,128)(2,1)S(1)}, u32[]{:S(2)}, u32[]{:S(2)}) collective-permute-start(bf16[1,720,256]{2,1,0:T(8,128)(2,1)S(1)} %get-tuple-element.73), channel_id=1, source_target_pairs={{2,0},{4,2},{6,4},{8,6},{10,8},{12,10},{14,12},{16,14},{18,16},{20... | collective-permute-start | bytes 1105928 | tf_op jit(solution)/shard_map/ppermute | solution.py:394
  4.6 11.5 %collective-permute-start = (bf16[1,720,256]{2,1,0:T(8,128)(2,1)S(1)}, bf16[1,720,256]{2,1,0:T(8,128)(2,1)}, u32[]{:S(2)}, u32[]{:S(2)}) collective-permute-start(bf16[1,720,256]{2,1,0:T(8,128)(2,1)S(1)} %get-tuple-element.74), channel_id=1, source_target_pairs={{0,2},{2,4},{4,6},{6,8},{8,10},{10,12},{12,14},{14,16},{16,18},{18... | collective-permute-start | bytes 1105928 | tf_op jit(solution)/shard_map/ppermute | solution.py:393
  16.1 6.7 %copy-start.8 = (s32[9]{0:T(128)S(1)}, s32[9]{0:T(128)}, u32[]{:S(2)}) copy-start(s32[9]{0:T(128)} %param.22) | copy-start | bytes 112
  16.1 6.7 %copy-start.7 = (s32[9]{0:T(128)S(1)}, s32[9]{0:T(128)}, u32[]{:S(2)}) copy-start(s32[9]{0:T(128)} %param.23) | copy-start | bytes 112
  16.2 6.9 %copy-start.5 = (f32[9,256]{1,0:T(8,128)S(1)}, f32[9,256]{1,0:T(8,128)}, u32[]{:S(2)}) copy-start(f32[9,256]{1,0:T(8,128)} %param.21) | copy-start | bytes 27652
  16.9 74.4 %all-to-all-start.2 = ((bf16[32,4,2,24,256]{4,3,2,1,0:T(8,128)(2,1)}), bf16[32,4,2,24,256]{4,3,2,1,0:T(8,128)(2,1)S(1)}, u32[]{:S(2)}, u32[]{:S(2)}) async-start(bf16[32,4,2,24,256]{4,3,2,1,0:T(8,128)(2,1)} %bitcast.13), calls=%async_computation.2 | async-start | bytes 6291456 | tf_op jit(solution)/shard_map/all_to_all | solution.py:417
  50.7 34.8 %collective-permute-start.4 = (bf16[3,720,256]{2,1,0:T(8,128)(2,1)}, bf16[3,720,256]{2,1,0:T(8,128)(2,1)}, u32[]{:S(2)}, u32[]{:S(2)}) collective-permute-start(bf16[3,720,256]{2,1,0:T(8,128)(2,1)} %slice.29), channel_id=1, source_target_pairs={{0,1},{1,0},{2,3},{3,2},{4,5},{5,4},{6,7},{7,6},{8,9},{9,8},{10,11... | collective-permute-start | bytes 3317768 | tf_op jit(solution)/shard_map/ppermute | solution.py:286
  91.3 1.7 copy-start.3
  93.0 74.9 %all-to-all-start.1 = ((bf16[32,4,2,24,256]{4,3,2,1,0:T(8,128)(2,1)}), bf16[32,4,2,24,256]{4,3,2,1,0:T(8,128)(2,1)S(1)}, u32[]{:S(2)}, u32[]{:S(2)}) async-start(bf16[32,4,2,24,256]{4,3,2,1,0:T(8,128)(2,1)} %bitcast.15), calls=%async_computation.1 | async-start | bytes 6291456 | tf_op jit(solution)/shard_map/all_to_all | solution.py:417
  101.3 64.7 %collective-permute-start.3 = (bf16[4,720,256]{2,1,0:T(8,128)(2,1)}, bf16[4,720,256]{2,1,0:T(8,128)(2,1)}, u32[]{:S(2)}, u32[]{:S(2)}) collective-permute-start(bf16[4,720,256]{2,1,0:T(8,128)(2,1)} %slice.28), channel_id=1, source_target_pairs={{0,1},{1,0},{2,3},{3,2},{4,5},{5,4},{6,7},{7,6},{8,9},{9,8},{10,11... | collective-permute-start | bytes 4423688 | tf_op jit(solution)/shard_map/ppermute | solution.py:286
  166.0 9.3 %copy-start.6 = (f32[384]{0:T(512)S(1)}, f32[384]{0:T(512)}, u32[]{:S(2)}) copy-start(f32[384]{0:T(512)} %param.20) | copy-start | bytes 4612
  167.9 1.7 copy-start.2
  169.6 74.9 %all-to-all-start = ((bf16[32,4,2,24,256]{4,3,2,1,0:T(8,128)(2,1)}), bf16[32,4,2,24,256]{4,3,2,1,0:T(8,128)(2,1)S(1)}, u32[]{:S(2)}, u32[]{:S(2)}) async-start(bf16[32,4,2,24,256]{4,3,2,1,0:T(8,128)(2,1)} %bitcast.14), calls=%async_computation | async-start | bytes 6291456 | tf_op jit(solution)/shard_map/all_to_all | solution.py:417
  244.6 8.7 %copy-start = (bf16[32,4,2,24,256]{4,3,2,1,0:T(8,128)(2,1)}, bf16[32,4,2,24,256]{4,3,2,1,0:T(8,128)(2,1)S(1)}, u32[]{:S(2)}) copy-start(bf16[32,4,2,24,256]{4,3,2,1,0:T(8,128)(2,1)S(1)} %all-to-all-done) | copy-start | bytes 9437188
  244.6 75.9 %all-to-all-start.3 = ((bf16[32,2,5,8,512]{4,3,2,1,0:T(8,128)(2,1)}), bf16[32,2,5,8,512]{4,3,2,1,0:T(8,128)(2,1)}, u32[]{:S(2)}, u32[]{:S(2)}) async-start(bf16[32,2,5,8,512]{4,3,2,1,0:T(8,128)(2,1)} %get-tuple-element.56), calls=%async_computation.3 | async-start | bytes 5242880 | tf_op jit(solution)/shard_map/all_to_all | solution.py:441
  253.3 67.2 %collective-permute-start.5 = (bf16[5,720,256]{2,1,0:T(8,128)(2,1)}, bf16[5,720,256]{2,1,0:T(8,128)(2,1)}, u32[]{:S(2)}, u32[]{:S(2)}) collective-permute-start(bf16[5,720,256]{2,1,0:T(8,128)(2,1)} %slice.30), channel_id=1, source_target_pairs={{0,1},{1,0},{2,3},{3,2},{4,5},{5,4},{6,7},{7,6},{8,9},{9,8},{10,11... | collective-permute-start | bytes 5529608 | tf_op jit(solution)/shard_map/ppermute | solution.py:286
  355.5 74.7 %all-to-all-start.5 = ((bf16[32,3,4,8,512]{4,3,2,1,0:T(8,128)(2,1)}), bf16[32,3,4,8,512]{4,3,2,1,0:T(8,128)(2,1)S(1)}, u32[]{:S(2)}, u32[]{:S(2)}) async-start(bf16[32,3,4,8,512]{4,3,2,1,0:T(8,128)(2,1)} %get-tuple-element.58), calls=%async_computation.5 | async-start | bytes 6291456 | tf_op jit(solution)/shard_map/all_to_all | solution.py:441
  376.6 42.3 %collective-permute-start.6 = (bf16[3,720,256]{2,1,0:T(8,128)(2,1)S(1)}, bf16[3,720,256]{2,1,0:T(8,128)(2,1)}, u32[]{:S(2)}, u32[]{:S(2)}) collective-permute-start(bf16[3,720,256]{2,1,0:T(8,128)(2,1)S(1)} %slice.26), channel_id=1, source_target_pairs={{0,1},{1,0},{2,3},{3,2},{4,5},{5,4},{6,7},{7,6},{8,9},{9,8},{10,11... | collective-permute-start | bytes 3317768 | tf_op jit(solution)/shard_map/ppermute | solution.py:461
  430.3 9.3 %copy-start.1 = (bf16[32,3,4,8,512]{4,3,2,1,0:T(8,128)(2,1)}, bf16[32,3,4,8,512]{4,3,2,1,0:T(8,128)(2,1)S(1)}, u32[]{:S(2)}) copy-start(bf16[32,3,4,8,512]{4,3,2,1,0:T(8,128)(2,1)S(1)} %all-to-all-done.5.rest_0_) | copy-start | bytes 9437188
  430.3 58.1 %all-to-all-start.6 = ((bf16[32,3,3,8,512]{4,3,2,1,0:T(8,128)(2,1)}), bf16[32,3,3,8,512]{4,3,2,1,0:T(8,128)(2,1)}, u32[]{:S(2)}, u32[]{:S(2)}) async-start(bf16[32,3,3,8,512]{4,3,2,1,0:T(8,128)(2,1)} %get-tuple-element.63), calls=%async_computation.6 | async-start | bytes 4718592 | tf_op jit(solution)/shard_map/all_to_all | solution.py:441
  438.1 38.6 %collective-permute-start.7 = (bf16[2,720,256]{2,1,0:T(8,128)(2,1)}, bf16[2,720,256]{2,1,0:T(8,128)(2,1)}, u32[]{:S(2)}, u32[]{:S(2)}) collective-permute-start(bf16[2,720,256]{2,1,0:T(8,128)(2,1)} %slice.27), channel_id=1, source_target_pairs={{0,1},{1,0},{2,3},{3,2},{4,5},{5,4},{6,7},{7,6},{8,9},{9,8},{10,11... | collective-permute-start | bytes 2211848 | tf_op jit(solution)/shard_map/ppermute | solution.py:462
  451.7 59.5 %collective-permute-start.8 = (bf16[4,720,256]{2,1,0:T(8,128)(2,1)}, bf16[4,720,256]{2,1,0:T(8,128)(2,1)S(1)}, u32[]{:S(2)}, u32[]{:S(2)}) collective-permute-start(bf16[4,720,256]{2,1,0:T(8,128)(2,1)} %get-tuple-element.71), channel_id=1, source_target_pairs={{0,1},{1,0},{2,3},{3,2},{4,5},{5,4},{6,7},{7,6},{8,9},{9,8},{10,11... | collective-permute-start | bytes 4423688 | tf_op jit(solution)/shard_map/ppermute | solution.py:466
  498.4 36.4 %collective-permute-start.9 = (bf16[3,720,256]{2,1,0:T(8,128)(2,1)}, bf16[3,720,256]{2,1,0:T(8,128)(2,1)S(1)}, u32[]{:S(2)}, u32[]{:S(2)}) collective-permute-start(bf16[3,720,256]{2,1,0:T(8,128)(2,1)} %get-tuple-element.72), channel_id=1, source_target_pairs={{0,1},{1,0},{2,3},{3,2},{4,5},{5,4},{6,7},{7,6},{8,9},{9,8},{10,11... | collective-permute-start | bytes 3317768 | tf_op jit(solution)/shard_map/ppermute | solution.py:469
  (1 other events, 0.8 us)

commit v5 on v4

--- a/solution.py
+++ b/solution.py
@@ -38,8 +38,7 @@
     return np.cos(angle), np.sin(angle)
 
 
-def forward_kernel(scale, table_ref, grid_ref, *rest):
-    out_ref, held = rest[-2:]
+def forward_kernel(scale, table_ref, grid_ref, out_ref, held):
     few = grid_ref.shape[0]
     cycles = out_ref.shape[1]
     rows = table_ref.shape[0]
@@ -58,7 +57,7 @@
             out_ref[:, :, lanes] = held[at].reshape(rows, cycles, LANES).astype(BF)
 
 
-def forward_part(grid, table, first):
+def forward_part(grid, table):
     cycles, nlon, width = grid.shape
     rows = table.shape[0]
     few = 4
@@ -69,13 +68,12 @@
         in_specs=[
             pl.BlockSpec(table.shape, lambda t: (0, 0)),
             pl.BlockSpec((few, nlon, width), lambda t: (t, 0, 0)),
-        ]
-        + [pl.BlockSpec(memory_space=pl.ANY)] * len(first),
+        ],
         out_specs=pl.BlockSpec((rows, cycles, width), lambda t: (0, 0, 0)),
         scratch_shapes=[pltpu.VMEM((width // LANES, rows * cycles, LANES), F32)],
         compiler_params=params(60),
         cost_estimate=cost(2 * rows * nlon * cycles * width, grid.size * 2),
-    )(table, grid, *first)
+    )(table, grid)
 
 
 def middle_kernel(plan, at_ref, spec_ref, basis_ref, quad_ref, own_ref, other_ref, gain_ref, *rest):
@@ -137,14 +135,14 @@
                 start += count
 
 
-def middle_part(spec, basis, quad, mix, other, gain, offset, plan, filled):
+def middle_part(spec, skip, basis, quad, mix, other, gain, offset, plan, filled):
     groups, sides, _, _, cycles, width = spec.shape
     nlat = groups * cycles
     channels = sides * width
     slots = 2 * STEP
     fixed = lambda m, at: (0, 0)
     specs = [
-        pl.BlockSpec((groups, sides, 1, 2, cycles, width), lambda m, at: (0, 0, m, 0, 0, 0)),
+        pl.BlockSpec((groups, sides, 1, 2, cycles, width), lambda m, at: (0, 0, skip + m, 0, 0, 0)),
         pl.BlockSpec((1, L, nlat), lambda m, at: (at[0] + m, 0, 0)),
         pl.BlockSpec((1, nlat), fixed),
         pl.BlockSpec(mix.shape, lambda m, at: (0, 0, 0)),
@@ -374,13 +372,11 @@
     parts = few // STEP
     span = cycles // sides
     third = span // 3
-    counts = [third + 1, third, span - 2 * third - 1]
+    counts = [third, third, span - 2 * third - 1, 1]
 
     cosine, sine = angle_table(nlon)
     both = np.stack([cosine, -sine], axis=-1)
-    fwd_table = np.ascontiguousarray(
-        both.reshape(nlon, groups * sides, parts, STEP * 2).transpose(2, 1, 3, 0)
-    ).reshape(parts, groups * sides * STEP * 2, nlon)
+    fwd_table = both.reshape(nlon, groups * sides, few, 2).transpose(1, 2, 3, 0)
     weight_m = np.where(np.arange(MMAX) == 0, 1.0, 2.0)[None, :, None]
     inv_table = (both * weight_m).reshape(nlon, groups * sides, parts, STEP * 2)
 
@@ -402,39 +398,37 @@
 
     other = lax.ppermute(mix_weight, "chan", SWAP)
     gathered = []
-    for part in range(parts):
-        spec = forward_part(grid, jnp.asarray(fwd_table[part], BF), [])
-        spec = spec.reshape(groups * sides, STEP, 2, cycles, width)
+    bounds = [(0, STEP), (STEP, few)]
+    for part, (low, high) in enumerate(bounds):
+        table = jnp.asarray(fwd_table[:, low:high].reshape(-1, nlon), BF)
+        spec = forward_part(grid, table)
+        spec = spec.reshape(groups * sides, high - low, 2, cycles, width)
         if part == 0:
             spec, before, after, other = lax.optimization_barrier((spec, before, after, other))
             asked = local_part(grid, before, after, ratio, weight, (1 - side) * span, span)
             got = exchanged(asked, counts)
-        elif part == 1:
+        else:
             spec, got[2] = lax.optimization_barrier((spec, got[2]))
             own = local_part(grid, before, after, ratio, weight, side * span, span)
-        elif part == 2:
-            spec, got[1], own = lax.optimization_barrier((spec, got[1], own))
         spec = lax.all_to_all(spec, ("lat", "chan"), 0, 0, tiled=True)
-        gathered.append(spec.reshape(groups, sides, STEP, 2, cycles, width))
+        gathered.append(spec.reshape(groups, sides, high - low, 2, cycles, width))
 
     theta = cycle_angle(jnp.arange(nlat, dtype=jnp.int32), nlat)
     quad = (math.pi / nlat * jnp.sin(theta))[None, :]
     gain = spectral_gain[:, None]
 
-    begin, filled = (None, [None] * 2)
+    filled = [None] * (len(counts) - 1)
+    heads = []
     for part in range(parts):
         offset = jnp.stack([side * few + part * STEP, side]).astype(jnp.int32)
-        late = part == parts - 1
-        plan = [(1, 0, counts[0]) if late else (parts - 1, part, counts[0])]
+        plan = [(parts - 1, part - 1, counts[0]) if part else (1, 0, counts[0])]
         plan += [(parts, part, count) for count in counts[1:]]
-        value = None if late else begin
+        head = heads[-1] if part > 1 else None
         ready = middle_part(
-            gathered[part], basis, quad, mix_weight, other, gain, offset, plan, [value] + filled
+            gathered[min(part, 1)], max(part - 1, 0) * STEP, basis, quad, mix_weight, other, gain,
+            offset, plan, [head] + filled,
         )
-        if late:
-            end = ready[0]
-        else:
-            begin = ready[0]
+        heads.append(ready[0])
         filled = list(ready[1:])
 
     def shuffled(value):
@@ -447,26 +441,40 @@
             backs, tables, own, got[at], sum(counts[:at]), ln_gain[None, :], up_weight,
             down_weight, place, result, cycles,
         )
-        return (result, theirs)
-
-    begin, _ = lax.optimization_barrier((begin, gathered[-1]))
+        cut = theirs.shape[0] * 3 // 4 if at == 1 else theirs.shape[0]
+        pieces = [theirs[:cut], theirs[cut:]] if cut < theirs.shape[0] else [theirs]
+        return (result, [lax.ppermute(piece, "chan", SWAP) for piece in pieces])
+
+    begin, end = (heads[0], heads[-1])
+    begin, _, own, got[0], got[1] = lax.optimization_barrier(
+        (begin, gathered[1], own, got[0], got[1])
+    )
     begin = shuffled(begin)
-    end, begin, got[0] = lax.optimization_barrier((end, begin, got[0]))
+    end, begin = lax.optimization_barrier((end, begin))
     end = shuffled(end)
-    second, end = lax.optimization_barrier((filled[0], end))
-    second = shuffled(second)
-    result, theirs = finished(
-        0, [begin, end], [inverse(0, parts - 1), inverse(parts - 1, parts)], None
-    )
-    sent = [lax.ppermute(theirs[: counts[2]], "chan", SWAP)]
-    rest = lax.ppermute(theirs[counts[2] :], "chan", SWAP)
-    third, second, _ = lax.optimization_barrier((filled[1], second, sent[0]))
-    third = shuffled(third)
-    result, theirs = finished(1, [second], [inverse(0, parts)], result)
-    sent += [rest, lax.ppermute(theirs, "chan", SWAP)]
-    third, sent[1] = lax.optimization_barrier((third, sent[1]))
-    result, theirs = finished(2, [third], [inverse(0, parts)], result)
-    sent.append(lax.ppermute(theirs, "chan", SWAP))
+    backs = [[begin, end]]
+    tables = [[inverse(0, 1), inverse(1, parts)]] + [[inverse(0, parts)]] * 3
+    last = end
+    result = None
+    sent = []
+    for at, value in enumerate(filled):
+        if at == 0:
+            value, last = lax.optimization_barrier((value, last))
+            backs[0][1] = last
+        else:
+            value, last = lax.optimization_barrier((value, last))
+            backs[-1] = [last]
+        if at == 1:
+            value, sent[0], got[3] = lax.optimization_barrier((value, sent[0], got[3]))
+        if at > 1:
+            value, sent[1] = lax.optimization_barrier((value, sent[1]))
+        last = shuffled(value)
+        result, values = finished(at, backs[-1], tables[at], result)
+        sent += values
+        backs.append([last])
+    last, sent[2] = lax.optimization_barrier((last, sent[2]))
+    result, values = finished(len(filled), [last], tables[-1], result)
+    sent += values
     start = 0
     for value in sent:
         count = value.shape[0]

time: 539 us -> 535 us (level)
  waiting for transfers between devices: 269 us -> 250 us
  blocking collectives: 35 us -> 52.4 us
    all_to_all x3 -> x4, waiting for transfers between devices: 23.1 us -> 90.7 us  [shuffled(): return lax.all_to_all(value, ('lat', 'chan'), 0, 0, tiled=True)]
    ppermute x4 -> x5, waiting for transfers between devices: 94.8 us -> 35.7 us  [finished(): return (result, [lax.ppermute(piece, 'chan', SWAP) for piece in pieces])]
    all_to_all x3 -> x2, waiting for transfers between devices: 46.3 us -> 10.4 us  [fast(): spec = lax.all_to_all(spec, ('lat', 'chan'), 0, 0, tiled=True)]
    all_to_all x1, blocking collectives: 35 us -> 52.4 us  [shuffled(): return lax.all_to_all(value, ('lat', 'chan'), 0, 0, tiled=True)]
    ppermute x3 -> x4, waiting for transfers between devices: 105 us -> 113 us  [exchanged(): got.append(lax.ppermute(piece, 'chan', SWAP))]
    all_to_all x3 -> x4, starting transfers between devices: 17 us -> 23.6 us  [shuffled(): return lax.all_to_all(value, ('lat', 'chan'), 0, 0, tiled=True)]
    pallas_call x3 -> x2, Pallas kernels: 27.4 us -> 21.6 us  [forward_part(): pl.pallas_call(functools.partial(forward_kernel, 1.0 / nlon), out_shape=j...]
    all_to_all x3 -> x2, starting transfers between devices: 16.6 us -> 10.9 us  [fast(): spec = lax.all_to_all(spec, ('lat', 'chan'), 0, 0, tiled=True)]
  transfers between devices with their start and end apart: 16 -> 18, of which waited for: 12 -> 10; matrix products, arithmetic and copies ran while one was open for 5% -> 4% of each run, Pallas kernels for 29% -> 28%
where the time goes in v5:
time: 535 us; the launch traced here: 532 us
  waiting for transfers between devices  250 us (47%)
  Pallas kernels  151 us (28%)
  blocking collectives  52.4 us (10%)
  starting transfers between devices  50.8 us (9%)
  local copies, waits for them, and re-layouts  21.8 us (4%)
    ppermute x4, waiting for transfers between devices, exchanged(): got.append(lax.ppermute(piece, 'chan', SWAP))  113 us
    all_to_all x4, waiting for transfers between devices, shuffled(): return lax.all_to_all(value, ('lat', 'chan'), 0, 0, tiled=True)  90.7 us
    all_to_all x1, blocking collectives, shuffled(): return lax.all_to_all(value, ('lat', 'chan'), 0, 0, tiled=True)  52.4 us
    pallas_call x2, Pallas kernels, local_part(): pl.pallas_call(local_rows, out_shape=jax.ShapeDtypeStruct((span, nlon, wi...  47.9 us
    pallas_call x3, Pallas kernels, middle_part(): pl.pallas_call(functools.partial(middle_kernel, plan), out_shape=[jax.Sha...  42 us
    pallas_call x4, Pallas kernels, tail_part(): pl.pallas_call(functools.partial(tail_kernel, len(backs)), out_shape=[jax...  40 us
    ppermute x5, waiting for transfers between devices, finished(): return (result, [lax.ppermute(piece, 'chan', SWAP) for piece in pieces])  35.7 us
    all_to_all x4, starting transfers between devices, shuffled(): return lax.all_to_all(value, ('lat', 'chan'), 0, 0, tiled=True)  23.6 us
  transfers between devices with their start and end apart: 18, of which 10 were waited for; matrix products, arithmetic and copies ran while one was open for 4% of the time, Pallas kernels for 28%

profile of v5, /device:TPU:26, one launch (start us, length us, event | category | flops | bytes accessed | tf_op | source)
XLA Modules:
  0.0 531.8 jit_solution(17359847661996725694)
XLA Ops:
  7.0 9.1 %shard_map.145 = bf16[256,24,256]{2,1,0:T(8,128)(2,1)} custom-call(bf16[256,720]{1,0:T(8,128)(2,1)} %constant.68.clone.table_ref, bf16[24,720,256]{2,1,0:T(8,128)(2,1)} %after_ref.3), custom_call_target="tpu_custom_call" | custom-call | flops 2264924160 | bytes 8847360 | tf_op jit(solution)/shard_map/pallas_call | solution.py:64
  24.4 23.9 %shard_map.148 = bf16[12,720,256]{2,1,0:T(8,128)(2,1)} custom-call(s32[2]{0:T(128)} %pad_add_fusion.1.base_ref, f32[24,3]{1,0:T(8,128)} %sine_divide_fusion.ratio_ref, f32[3,7,256]{2,1,0:T(8,128)} %select_reduce_fusion.weight_ref, bf16[24,720,256]{2,1,0:T(8,128)(2,1)} %after_ref.3, bf16[24,720,256]{2,1,0:T(8,128)(2,1)} %after_ref.3, ...), custom_call_target="tpu_custom_call" | custom-call | flops 884736000 | bytes 13271040 | tf_op jit(solution)/shard_map/pallas_call | solution.py:257
  52.2 12.5 %shard_map.147 = bf16[512,24,256]{2,1,0:T(8,128)(2,1)} custom-call(bf16[512,720]{1,0:T(8,128)(2,1)} %constant.69.clone.table_ref, bf16[24,720,256]{2,1,0:T(8,128)(2,1)} %after_ref.3), custom_call_target="tpu_custom_call" | custom-call | flops 4529848320 | bytes 8847360 | tf_op jit(solution)/shard_map/pallas_call | solution.py:64
  64.7 20.9 %collective-permute-done.3.got_ref = bf16[3,720,256]{2,1,0:T(8,128)(2,1)} collective-permute-done((bf16[3,720,256]{2,1,0:T(8,128)(2,1)}, bf16[3,720,256]{2,1,0:T(8,128)(2,1)}, u32[]{:S(2)}, u32[]{:S(2)}) %collective-permute-start.3) | collective-permute-done | bytes 1105952 | tf_op jit(solution)/shard_map/ppermute | solution.py:284
  85.5 5.8 %all-to-all-done = bf16[32,4,2,24,256]{4,3,2,1,0:T(8,128)(2,1)S(1)} async-done(((bf16[32,4,2,24,256]{4,3,2,1,0:T(8,128)(2,1)}), bf16[32,4,2,24,256]{4,3,2,1,0:T(8,128)(2,1)S(1)}, u32[]{:S(2)}, u32[]{:S(2)}) %all-to-all-start) | async-done | bytes 3145760 | tf_op jit(solution)/shard_map/all_to_all | solution.py:413
  93.0 5.8 %all-to-all-start.1 = ((bf16[32,8,2,24,256]{4,3,2,1,0:T(8,128)(2,1)}), bf16[32,8,2,24,256]{4,3,2,1,0:T(8,128)(2,1)}, u32[]{:S(2)}, u32[]{:S(2)}) async-start(bf16[32,8,2,24,256]{4,3,2,1,0:T(8,128)(2,1)} %bitcast.11), calls=%async_computation.1 | async-start | bytes 12582912 | tf_op jit(solution)/shard_map/all_to_all | solution.py:413
  106.6 23.9 %shard_map.149.own_ref = bf16[12,720,256]{2,1,0:T(8,128)(2,1)} custom-call(s32[2]{0:T(128)} %pad_add_fusion.base_ref, f32[24,3]{1,0:T(8,128)} %sine_divide_fusion.ratio_ref, f32[3,7,256]{2,1,0:T(8,128)} %select_reduce_fusion.weight_ref, bf16[24,720,256]{2,1,0:T(8,128)(2,1)} %after_ref.3, bf16[24,720,256]{2,1,0:T(8,128)(2,1)} %after_ref.3, ...), custom_call_target="tpu_custom_call" | custom-call | flops 884736000 | bytes 13271040 | tf_op jit(solution)/shard_map/pallas_call | solution.py:257
  130.5 14.0 %shard_map.146 = (bf16[32,1,4,8,512]{4,3,2,1,0:T(8,128)(2,1)}, bf16[32,3,4,8,512]{4,3,2,1,0:T(8,128)(2,1)}, bf16[32,3,3,8,512]{4,3,2,1,0:T(8,128)(2,1)}, bf16[32,3,1,8,512]{4,3,2,1,0:T(8,128)(2,1)}) custom-call(s32[2]{0:T(128)} %pad_add_fusion.4.at_ref.place_ref, bf16[16,2,4,2,24,256]{5,4,3,2,1,0:T(8,128)(2,1)} %bitcast.12, f32[24,384,384]{2,1,0:T(8,128)} %basis_ref.5, ...), custom_call_target="tpu_custom_call" | custom-call | flops 5637144576 | bytes 9175040 | tf_op jit(solution)/shard_map/pallas_call | solution.py:159
  144.6 45.2 %collective-permute-done.5.got_ref = bf16[4,720,256]{2,1,0:T(8,128)(2,1)S(1)} collective-permute-done((bf16[4,720,256]{2,1,0:T(8,128)(2,1)}, bf16[4,720,256]{2,1,0:T(8,128)(2,1)S(1)}, u32[]{:S(2)}, u32[]{:S(2)}) %collective-permute-start.5) | collective-permute-done | bytes 1474592 | tf_op jit(solution)/shard_map/ppermute | solution.py:284
  189.8 40.9 %collective-permute-done.4.got_ref = bf16[4,720,256]{2,1,0:T(8,128)(2,1)} collective-permute-done((bf16[4,720,256]{2,1,0:T(8,128)(2,1)S(1)}, bf16[4,720,256]{2,1,0:T(8,128)(2,1)}, u32[]{:S(2)}, u32[]{:S(2)}) %collective-permute-start.4) | collective-permute-done | bytes 1474592 | tf_op jit(solution)/shard_map/ppermute | solution.py:284
  235.3 7.2 %all-to-all-start.2 = ((bf16[32,1,4,8,512]{4,3,2,1,0:T(8,128)(2,1)}), bf16[32,1,4,8,512]{4,3,2,1,0:T(8,128)(2,1)S(1)}, u32[]{:S(2)}, u32[]{:S(2)}) async-start(bf16[32,1,4,8,512]{4,3,2,1,0:T(8,128)(2,1)} %get-tuple-element.67), calls=%async_computation.2 | async-start | bytes 2097152 | tf_op jit(solution)/shard_map/all_to_all | solution.py:435
  243.2 14.0 %shard_map.150 = (bf16[32,2,4,8,512]{4,3,2,1,0:T(8,128)(2,1)}, bf16[32,3,4,8,512]{4,3,2,1,0:T(8,128)(2,1)}, bf16[32,3,3,8,512]{4,3,2,1,0:T(8,128)(2,1)}, bf16[32,3,1,8,512]{4,3,2,1,0:T(8,128)(2,1)}) custom-call(s32[2]{0:T(128)} %get-tuple-element.100.at_ref, ...), custom_call_target="tpu_custom_call", output_to_operand_aliasing={{1}: (7, {}), {2}: (8, {}), {3}: (9, {})} | custom-call | flops 5637144576 | bytes 9175040 | tf_op jit(solution)/shard_map/pallas_call | solution.py:159
  257.2 14.0 %shard_map.151 = (bf16[32,2,4,8,512]{4,3,2,1,0:T(8,128)(2,1)}, bf16[32,3,4,8,512]{4,3,2,1,0:T(8,128)(2,1)}, bf16[32,3,3,8,512]{4,3,2,1,0:T(8,128)(2,1)}, bf16[32,3,1,8,512]{4,3,2,1,0:T(8,128)(2,1)}) custom-call(s32[2]{0:T(128)} %get-tuple-element.99.at_ref, ...), custom_call_target="tpu_custom_call", output_to_operand_aliasing={{0}: (7, {}), {1}: (8, {}), {2}: (9, {}), {3}: (10, {})} | custom-call | flops 5637144576 | bytes 9175040 | tf_op jit(solution)/shard_map/pallas_call | solution.py:159
  271.2 52.4 %all_to_all.35.rest_1_ = bf16[32,2,4,8,512]{4,3,2,1,0:T(8,128)(2,1)} all-to-all(bf16[32,2,4,8,512]{4,3,2,1,0:T(8,128)(2,1)} %get-tuple-element.68), channel_id=1, replica_groups=mesh['lat'=16,'chan'=2] {'lat','chan'}, dimensions={0} | all-to-all | bytes 4194304 | tf_op jit(solution)/shard_map/all_to_all | solution.py:435
  323.7 5.8 %all-to-all-start.4 = ((bf16[32,3,4,8,512]{4,3,2,1,0:T(8,128)(2,1)}), bf16[32,3,4,8,512]{4,3,2,1,0:T(8,128)(2,1)S(1)}, u32[]{:S(2)}, u32[]{:S(2)}) async-start(bf16[32,3,4,8,512]{4,3,2,1,0:T(8,128)(2,1)} %get-tuple-element.69), calls=%async_computation.4 | async-start | bytes 6291456 | tf_op jit(solution)/shard_map/all_to_all | solution.py:435
  329.5 12.1 %shard_map.152 = (bf16[24,720,256]{2,1,0:T(8,128)(2,1)}, bf16[4,720,256]{2,1,0:T(8,128)(2,1)}) custom-call(s32[2]{0:T(128)} %pad_add_fusion.4.at_ref.place_ref, bf16[12,720,256]{2,1,0:T(8,128)(2,1)} %shard_map.149.own_ref, bf16[4,720,256]{2,1,0:T(8,128)(2,1)} %collective-permute-done.4.got_ref, f32[1,512]{1,0:T(1,128)} %bitcast.13, bf16[512,512]{1,0:T(8,128)(2,1)} %up_ref.7, ...), custom_call_target="tpu_custom_call" | custom-call | flops 5284823040 | bytes 11796480 | tf_op jit(solution)/shard_map/pallas_call | solution.py:339
  345.4 53.3 %all-to-all-done.4.rest_0_ = bf16[32,3,4,8,512]{4,3,2,1,0:T(8,128)(2,1)S(1)} async-done(((bf16[32,3,4,8,512]{4,3,2,1,0:T(8,128)(2,1)}), bf16[32,3,4,8,512]{4,3,2,1,0:T(8,128)(2,1)S(1)}, u32[]{:S(2)}, u32[]{:S(2)}) %all-to-all-start.4) | async-done | bytes 3145760 | tf_op jit(solution)/shard_map/all_to_all | solution.py:435
  398.7 6.5 %collective-permute-done.7.got_ref = bf16[1,720,256]{2,1,0:T(8,128)(2,1)S(1)} collective-permute-done((bf16[1,720,256]{2,1,0:T(8,128)(2,1)}, bf16[1,720,256]{2,1,0:T(8,128)(2,1)S(1)}, u32[]{:S(2)}, u32[]{:S(2)}) %collective-permute-start.7) | collective-permute-done | bytes 368672 | tf_op jit(solution)/shard_map/ppermute | solution.py:284
  410.2 12.2 %shard_map.153 = (bf16[24,720,256]{2,1,0:T(8,128)(2,1)}, bf16[4,720,256]{2,1,0:T(8,128)(2,1)}) custom-call(s32[2]{0:T(128)} %pad_add_fusion.4.at_ref.place_ref, bf16[12,720,256]{2,1,0:T(8,128)(2,1)} %shard_map.149.own_ref, bf16[4,720,256]{2,1,0:T(8,128)(2,1)} %copy-done.4, f32[1,512]{1,0:T(1,128)} %bitcast.14, ...), custom_call_target="tpu_custom_call", output_to_operand_aliasing={{0}: (8, {})} | custom-call | flops 5284823040 | bytes 11796480 | tf_op jit(solution)/shard_map/pallas_call | solution.py:339
  425.2 37.3 %all-to-all-done.5.rest_0_ = bf16[32,3,3,8,512]{4,3,2,1,0:T(8,128)(2,1)} async-done(((bf16[32,3,3,8,512]{4,3,2,1,0:T(8,128)(2,1)}), bf16[32,3,3,8,512]{4,3,2,1,0:T(8,128)(2,1)}, u32[]{:S(2)}, u32[]{:S(2)}) %all-to-all-start.5) | async-done | bytes 2359328 | tf_op jit(solution)/shard_map/all_to_all | solution.py:435
  462.6 5.7 %all-to-all-start.6 = ((bf16[32,3,1,8,512]{4,3,2,1,0:T(8,128)(2,1)}), bf16[32,3,1,8,512]{4,3,2,1,0:T(8,128)(2,1)S(1)}, u32[]{:S(2)}, u32[]{:S(2)}) async-start(bf16[32,3,1,8,512]{4,3,2,1,0:T(8,128)(2,1)} %get-tuple-element.83), calls=%async_computation.6 | async-start | bytes 1572864 | tf_op jit(solution)/shard_map/all_to_all | solution.py:435
  468.3 10.0 %shard_map.154 = (bf16[24,720,256]{2,1,0:T(8,128)(2,1)}, bf16[3,720,256]{2,1,0:T(8,128)(2,1)}) custom-call(s32[2]{0:T(128)} %pad_add_fusion.4.at_ref.place_ref, bf16[12,720,256]{2,1,0:T(8,128)(2,1)} %shard_map.149.own_ref, bf16[3,720,256]{2,1,0:T(8,128)(2,1)} %collective-permute-done.3.got_ref, f32[1,512]{1,0:T(1,128)} %bitcast.15, ...), custom_call_target="tpu_custom_call", output_to_operand_aliasing={{0}: (8, {})} | custom-call | flops 3963617280 | bytes 8847360 | tf_op jit(solution)/shard_map/pallas_call | solution.py:339
  482.1 32.1 %collective-permute-done.9 = bf16[1,720,256]{2,1,0:T(8,128)(2,1)S(1)} collective-permute-done((bf16[1,720,256]{2,1,0:T(8,128)(2,1)}, bf16[1,720,256]{2,1,0:T(8,128)(2,1)S(1)}, u32[]{:S(2)}, u32[]{:S(2)}) %collective-permute-start.9) | collective-permute-done | bytes 368672 | tf_op jit(solution)/shard_map/ppermute | solution.py:446
  515.1 5.6 %shard_map.155 = (bf16[24,720,256]{2,1,0:T(8,128)(2,1)}, bf16[1,720,256]{2,1,0:T(8,128)(2,1)}) custom-call(s32[2]{0:T(128)} %pad_add_fusion.4.at_ref.place_ref, bf16[12,720,256]{2,1,0:T(8,128)(2,1)} %shard_map.149.own_ref, bf16[1,720,256]{2,1,0:T(8,128)(2,1)} %copy-done.6, f32[1,512]{1,0:T(1,128)} %bitcast.16, ...), custom_call_target="tpu_custom_call", output_to_operand_aliasing={{0}: (8, {})} | custom-call | flops 1321205760 | bytes 2949120 | tf_op jit(solution)/shard_map/pallas_call | solution.py:339
  (72 shorter events, 61.2 us)
Async XLA Ops:
  0.0 16.2 %collective-permute-start.2 = (bf16[2,512,256]{2,1,0:T(8,128)(2,1)}, bf16[2,512,256]{2,1,0:T(8,128)(2,1)}, u32[]{:S(2)}, u32[]{:S(2)}) collective-permute-start(bf16[2,512,256]{2,1,0:T(8,128)(2,1)} %own_ref.5), channel_id=1, source_target_pairs={{0,1},{1,0},{2,3},{3,2},{4,5},{5,4},{6,7},{7,6},{8,9},{9,8},{10,11... | collective-permute-start | bytes 1572872 | tf_op jit(solution)/shard_map/ppermute | solution.py:399
  2.7 13.5 %collective-permute-start.1 = (bf16[1,720,256]{2,1,0:T(8,128)(2,1)S(1)}, bf16[1,720,256]{2,1,0:T(8,128)(2,1)S(1)}, u32[]{:S(2)}, u32[]{:S(2)}) collective-permute-start(bf16[1,720,256]{2,1,0:T(8,128)(2,1)S(1)} %get-tuple-element.95), channel_id=1, source_target_pairs={{2,0},{4,2},{6,4},{8,6},{10,8},{12,10},{14,12},{16,14},{18,16},{20... | collective-permute-start | bytes 1105928 | tf_op jit(solution)/shard_map/ppermute | solution.py:390
  4.6 11.6 %collective-permute-start = (bf16[1,720,256]{2,1,0:T(8,128)(2,1)S(1)}, bf16[1,720,256]{2,1,0:T(8,128)(2,1)}, u32[]{:S(2)}, u32[]{:S(2)}) collective-permute-start(bf16[1,720,256]{2,1,0:T(8,128)(2,1)S(1)} %get-tuple-element.96), channel_id=1, source_target_pairs={{0,2},{2,4},{4,6},{6,8},{8,10},{10,12},{12,14},{14,16},{16,18},{18... | collective-permute-start | bytes 1105928 | tf_op jit(solution)/shard_map/ppermute | solution.py:389
  16.2 6.6 %copy-start.9 = (s32[9]{0:T(128)S(1)}, s32[9]{0:T(128)}, u32[]{:S(2)}) copy-start(s32[9]{0:T(128)} %param.21) | copy-start | bytes 112
  16.2 6.8 %copy-start.7 = (f32[9,256]{1,0:T(8,128)S(1)}, f32[9,256]{1,0:T(8,128)}, u32[]{:S(2)}) copy-start(f32[9,256]{1,0:T(8,128)} %param.19) | copy-start | bytes 27652
  16.9 74.4 %all-to-all-start = ((bf16[32,4,2,24,256]{4,3,2,1,0:T(8,128)(2,1)}), bf16[32,4,2,24,256]{4,3,2,1,0:T(8,128)(2,1)S(1)}, u32[]{:S(2)}, u32[]{:S(2)}) async-start(bf16[32,4,2,24,256]{4,3,2,1,0:T(8,128)(2,1)} %bitcast.10), calls=%async_computation | async-start | bytes 6291456 | tf_op jit(solution)/shard_map/all_to_all | solution.py:413
  50.7 34.8 %collective-permute-start.3 = (bf16[3,720,256]{2,1,0:T(8,128)(2,1)}, bf16[3,720,256]{2,1,0:T(8,128)(2,1)}, u32[]{:S(2)}, u32[]{:S(2)}) collective-permute-start(bf16[3,720,256]{2,1,0:T(8,128)(2,1)} %slice.32), channel_id=1, source_target_pairs={{0,1},{1,0},{2,3},{3,2},{4,5},{5,4},{6,7},{7,6},{8,9},{9,8},{10,11... | collective-permute-start | bytes 3317768 | tf_op jit(solution)/shard_map/ppermute | solution.py:284
  93.0 142.3 %all-to-all-start.1 = ((bf16[32,8,2,24,256]{4,3,2,1,0:T(8,128)(2,1)}), bf16[32,8,2,24,256]{4,3,2,1,0:T(8,128)(2,1)}, u32[]{:S(2)}, u32[]{:S(2)}) async-start(bf16[32,8,2,24,256]{4,3,2,1,0:T(8,128)(2,1)} %bitcast.11), calls=%async_computation.1 | async-start | bytes 12582912 | tf_op jit(solution)/shard_map/all_to_all | solution.py:413
  101.9 87.9 %collective-permute-start.5 = (bf16[4,720,256]{2,1,0:T(8,128)(2,1)}, bf16[4,720,256]{2,1,0:T(8,128)(2,1)S(1)}, u32[]{:S(2)}, u32[]{:S(2)}) collective-permute-start(bf16[4,720,256]{2,1,0:T(8,128)(2,1)} %get-tuple-element.97), channel_id=1, source_target_pairs={{0,1},{1,0},{2,3},{3,2},{4,5},{5,4},{6,7},{7,6},{8,9},{9,8},{10,11... | collective-permute-start | bytes 4423688 | tf_op jit(solution)/shard_map/ppermute | solution.py:284
  103.4 127.3 %collective-permute-start.4 = (bf16[4,720,256]{2,1,0:T(8,128)(2,1)S(1)}, bf16[4,720,256]{2,1,0:T(8,128)(2,1)}, u32[]{:S(2)}, u32[]{:S(2)}) collective-permute-start(bf16[4,720,256]{2,1,0:T(8,128)(2,1)S(1)} %get-tuple-element.98), channel_id=1, source_target_pairs={{0,1},{1,0},{2,3},{3,2},{4,5},{5,4},{6,7},{7,6},{8,9},{9,8},{10,11... | collective-permute-start | bytes 4423688 | tf_op jit(solution)/shard_map/ppermute | solution.py:284
  189.8 67.4 %copy-start.4 = (bf16[4,720,256]{2,1,0:T(8,128)(2,1)}, bf16[4,720,256]{2,1,0:T(8,128)(2,1)S(1)}, u32[]{:S(2)}) copy-start(bf16[4,720,256]{2,1,0:T(8,128)(2,1)S(1)} %collective-permute-done.5.got_ref) | copy-start | bytes 4423684
  235.3 35.9 %all-to-all-start.2 = ((bf16[32,1,4,8,512]{4,3,2,1,0:T(8,128)(2,1)}), bf16[32,1,4,8,512]{4,3,2,1,0:T(8,128)(2,1)S(1)}, u32[]{:S(2)}, u32[]{:S(2)}) async-start(bf16[32,1,4,8,512]{4,3,2,1,0:T(8,128)(2,1)} %get-tuple-element.67), calls=%async_computation.2 | async-start | bytes 2097152 | tf_op jit(solution)/shard_map/all_to_all | solution.py:435
  271.2 52.5 %copy-start.5 = (bf16[32,1,4,8,512]{4,3,2,1,0:T(8,128)(2,1)}, bf16[32,1,4,8,512]{4,3,2,1,0:T(8,128)(2,1)S(1)}, u32[]{:S(2)}) copy-start(bf16[32,1,4,8,512]{4,3,2,1,0:T(8,128)(2,1)S(1)} %all-to-all-done.2.rest_0_) | copy-start | bytes 3145732
  323.7 75.1 %all-to-all-start.4 = ((bf16[32,3,4,8,512]{4,3,2,1,0:T(8,128)(2,1)}), bf16[32,3,4,8,512]{4,3,2,1,0:T(8,128)(2,1)S(1)}, u32[]{:S(2)}, u32[]{:S(2)}) async-start(bf16[32,3,4,8,512]{4,3,2,1,0:T(8,128)(2,1)} %get-tuple-element.69), calls=%async_computation.4 | async-start | bytes 6291456 | tf_op jit(solution)/shard_map/all_to_all | solution.py:435
  341.6 63.6 %collective-permute-start.6 = (bf16[4,720,256]{2,1,0:T(8,128)(2,1)}, bf16[4,720,256]{2,1,0:T(8,128)(2,1)}, u32[]{:S(2)}, u32[]{:S(2)}) collective-permute-start(bf16[4,720,256]{2,1,0:T(8,128)(2,1)} %get-tuple-element.74), channel_id=1, source_target_pairs={{0,1},{1,0},{2,3},{3,2},{4,5},{5,4},{6,7},{7,6},{8,9},{9,8},{10,11... | collective-permute-start | bytes 4423688 | tf_op jit(solution)/shard_map/ppermute | solution.py:446
  344.9 60.4 %collective-permute-start.7 = (bf16[1,720,256]{2,1,0:T(8,128)(2,1)}, bf16[1,720,256]{2,1,0:T(8,128)(2,1)S(1)}, u32[]{:S(2)}, u32[]{:S(2)}) collective-permute-start(bf16[1,720,256]{2,1,0:T(8,128)(2,1)} %slice.35), channel_id=1, source_target_pairs={{0,1},{1,0},{2,3},{3,2},{4,5},{5,4},{6,7},{7,6},{8,9},{9,8},{10,11... | collective-permute-start | bytes 1105928 | tf_op jit(solution)/shard_map/ppermute | solution.py:284
  398.7 11.4 %copy-start = (bf16[32,3,4,8,512]{4,3,2,1,0:T(8,128)(2,1)}, bf16[32,3,4,8,512]{4,3,2,1,0:T(8,128)(2,1)S(1)}, u32[]{:S(2)}) copy-start(bf16[32,3,4,8,512]{4,3,2,1,0:T(8,128)(2,1)S(1)} %all-to-all-done.4.rest_0_) | copy-start | bytes 9437188
  405.2 17.1 %copy-start.6 = (bf16[1,720,256]{2,1,0:T(8,128)(2,1)}, bf16[1,720,256]{2,1,0:T(8,128)(2,1)S(1)}, u32[]{:S(2)}) copy-start(bf16[1,720,256]{2,1,0:T(8,128)(2,1)S(1)} %collective-permute-done.7.got_ref) | copy-start | bytes 1105924
  405.2 57.3 %all-to-all-start.5 = ((bf16[32,3,3,8,512]{4,3,2,1,0:T(8,128)(2,1)}), bf16[32,3,3,8,512]{4,3,2,1,0:T(8,128)(2,1)}, u32[]{:S(2)}, u32[]{:S(2)}) async-start(bf16[32,3,3,8,512]{4,3,2,1,0:T(8,128)(2,1)} %get-tuple-element.77), calls=%async_computation.5 | async-start | bytes 4718592 | tf_op jit(solution)/shard_map/all_to_all | solution.py:435
  423.7 38.9 %collective-permute-start.8 = (bf16[3,720,256]{2,1,0:T(8,128)(2,1)S(1)}, bf16[3,720,256]{2,1,0:T(8,128)(2,1)S(1)}, u32[]{:S(2)}, u32[]{:S(2)}) collective-permute-start(bf16[3,720,256]{2,1,0:T(8,128)(2,1)S(1)} %slice.30), channel_id=1, source_target_pairs={{0,1},{1,0},{2,3},{3,2},{4,5},{5,4},{6,7},{7,6},{8,9},{9,8},{10,11... | collective-permute-start | bytes 3317768 | tf_op jit(solution)/shard_map/ppermute | solution.py:446
  462.6 51.6 %all-to-all-start.6 = ((bf16[32,3,1,8,512]{4,3,2,1,0:T(8,128)(2,1)}), bf16[32,3,1,8,512]{4,3,2,1,0:T(8,128)(2,1)S(1)}, u32[]{:S(2)}, u32[]{:S(2)}) async-start(bf16[32,3,1,8,512]{4,3,2,1,0:T(8,128)(2,1)} %get-tuple-element.83), calls=%async_computation.6 | async-start | bytes 1572864 | tf_op jit(solution)/shard_map/all_to_all | solution.py:435
  478.3 48.1 %collective-permute-start.10 = (bf16[3,720,256]{2,1,0:T(8,128)(2,1)}, bf16[3,720,256]{2,1,0:T(8,128)(2,1)S(1)}, u32[]{:S(2)}, u32[]{:S(2)}) collective-permute-start(bf16[3,720,256]{2,1,0:T(8,128)(2,1)} %get-tuple-element.93), channel_id=1, source_target_pairs={{0,1},{1,0},{2,3},{3,2},{4,5},{5,4},{6,7},{7,6},{8,9},{9,8},{10,11... | collective-permute-start | bytes 3317768 | tf_op jit(solution)/shard_map/ppermute | solution.py:446
  481.5 32.6 %collective-permute-start.9 = (bf16[1,720,256]{2,1,0:T(8,128)(2,1)}, bf16[1,720,256]{2,1,0:T(8,128)(2,1)S(1)}, u32[]{:S(2)}, u32[]{:S(2)}) collective-permute-start(bf16[1,720,256]{2,1,0:T(8,128)(2,1)} %slice.31), channel_id=1, source_target_pairs={{0,1},{1,0},{2,3},{3,2},{4,5},{5,4},{6,7},{7,6},{8,9},{9,8},{10,11... | collective-permute-start | bytes 1105928 | tf_op jit(solution)/shard_map/ppermute | solution.py:446
  520.7 10.3 %collective-permute-start.11 = (bf16[1,720,256]{2,1,0:T(8,128)(2,1)}, bf16[1,720,256]{2,1,0:T(8,128)(2,1)S(1)}, u32[]{:S(2)}, u32[]{:S(2)}) collective-permute-start(bf16[1,720,256]{2,1,0:T(8,128)(2,1)} %get-tuple-element.94), channel_id=1, source_target_pairs={{0,1},{1,0},{2,3},{3,2},{4,5},{5,4},{6,7},{7,6},{8,9},{9,8},{10,11... | collective-permute-start | bytes 1105928 | tf_op jit(solution)/shard_map/ppermute | solution.py:446
  (5 other events, 15.1 us)

commit v6 on v5

--- a/solution.py
+++ b/solution.py
@@ -372,7 +372,7 @@
     parts = few // STEP
     span = cycles // sides
     third = span // 3
-    counts = [third, third, span - 2 * third - 1, 1]
+    counts = [third - 1, third, third - 1, span - 3 * third + 2]
 
     cosine, sine = angle_table(nlon)
     both = np.stack([cosine, -sine], axis=-1)
@@ -398,18 +398,18 @@
 
     other = lax.ppermute(mix_weight, "chan", SWAP)
     gathered = []
-    bounds = [(0, STEP), (STEP, few)]
+    bounds = [(0, few - STEP), (few - STEP, few)]
     for part, (low, high) in enumerate(bounds):
         table = jnp.asarray(fwd_table[:, low:high].reshape(-1, nlon), BF)
         spec = forward_part(grid, table)
         spec = spec.reshape(groups * sides, high - low, 2, cycles, width)
         if part == 0:
-            spec, before, after, other = lax.optimization_barrier((spec, before, after, other))
+            spec, before, after = lax.optimization_barrier((spec, before, after))
             asked = local_part(grid, before, after, ratio, weight, (1 - side) * span, span)
             got = exchanged(asked, counts)
         else:
-            spec, got[2] = lax.optimization_barrier((spec, got[2]))
             own = local_part(grid, before, after, ratio, weight, side * span, span)
+            spec, own, other, got[1] = lax.optimization_barrier((spec, own, other, got[1]))
         spec = lax.all_to_all(spec, ("lat", "chan"), 0, 0, tiled=True)
         gathered.append(spec.reshape(groups, sides, high - low, 2, cycles, width))
 
@@ -421,11 +421,12 @@
     heads = []
     for part in range(parts):
         offset = jnp.stack([side * few + part * STEP, side]).astype(jnp.int32)
-        plan = [(parts - 1, part - 1, counts[0]) if part else (1, 0, counts[0])]
+        late = part == parts - 1
+        plan = [(1, 0, counts[0]) if late else (parts - 1, part, counts[0])]
         plan += [(parts, part, count) for count in counts[1:]]
-        head = heads[-1] if part > 1 else None
+        head = heads[-1] if heads and not late else None
         ready = middle_part(
-            gathered[min(part, 1)], max(part - 1, 0) * STEP, basis, quad, mix_weight, other, gain,
+            gathered[int(late)], 0 if late else part * STEP, basis, quad, mix_weight, other, gain,
             offset, plan, [head] + filled,
         )
         heads.append(ready[0])
@@ -435,25 +436,29 @@
         return lax.all_to_all(value, ("lat", "chan"), 0, 0, tiled=True)
 
     place = jnp.stack([side * span, side]).astype(jnp.int32)
+
+    kept = []
 
     def finished(at, backs, tables, result):
         result, theirs = tail_part(
             backs, tables, own, got[at], sum(counts[:at]), ln_gain[None, :], up_weight,
             down_weight, place, result, cycles,
         )
-        cut = theirs.shape[0] * 3 // 4 if at == 1 else theirs.shape[0]
-        pieces = [theirs[:cut], theirs[cut:]] if cut < theirs.shape[0] else [theirs]
-        return (result, [lax.ppermute(piece, "chan", SWAP) for piece in pieces])
-
-    begin, end = (heads[0], heads[-1])
-    begin, _, own, got[0], got[1] = lax.optimization_barrier(
-        (begin, gathered[1], own, got[0], got[1])
-    )
+        if at == 1:
+            cut = max(theirs.shape[0] - 1, 1)
+            kept.append(theirs[cut:])
+            theirs = theirs[:cut]
+        elif at == 2:
+            theirs = jnp.concatenate([kept[0], theirs], axis=0)
+        return (result, lax.ppermute(theirs, "chan", SWAP))
+
+    begin, end = heads[-2:]
+    begin, _, got[2], got[3] = lax.optimization_barrier((begin, gathered[1], got[2], got[3]))
     begin = shuffled(begin)
-    end, begin = lax.optimization_barrier((end, begin))
+    end, begin, got[0] = lax.optimization_barrier((end, begin, got[0]))
     end = shuffled(end)
     backs = [[begin, end]]
-    tables = [[inverse(0, 1), inverse(1, parts)]] + [[inverse(0, parts)]] * 3
+    tables = [[inverse(0, parts - 1), inverse(parts - 1, parts)]] + [[inverse(0, parts)]] * 3
     last = end
     result = None
     sent = []
@@ -465,16 +470,15 @@
             value, last = lax.optimization_barrier((value, last))
             backs[-1] = [last]
         if at == 1:
-            value, sent[0], got[3] = lax.optimization_barrier((value, sent[0], got[3]))
+            value, sent[0] = lax.optimization_barrier((value, sent[0]))
         if at > 1:
             value, sent[1] = lax.optimization_barrier((value, sent[1]))
         last = shuffled(value)
-        result, values = finished(at, backs[-1], tables[at], result)
-        sent += values
+        result, value = finished(at, backs[-1], tables[at], result)
+        sent.append(value)
         backs.append([last])
-    last, sent[2] = lax.optimization_barrier((last, sent[2]))
-    result, values = finished(len(filled), [last], tables[-1], result)
-    sent += values
+    result, value = finished(len(filled), [last], tables[-1], result)
+    sent.append(value)
     start = 0
     for value in sent:
         count = value.shape[0]
@@ -609,7 +613,7 @@
         and cycles % 8 == 0
         and cycles % sides == 0
         and cycles // sides >= 6
-        and basis.shape[0] // (sides * STEP) == 3
+        and basis.shape[0] // (sides * STEP) >= 2
         and basis.shape[0] % (sides * STEP) == 0
         and nlon % 8 == 0
         and width % 128 == 0

time: 535 us -> 534 us (level)
  blocking collectives: 52.4 us -> 23.5 us
  waiting for transfers between devices: 250 us -> 271 us
    ppermute x4, waiting for transfers between devices: 113 us -> 65.7 us  [exchanged(): got.append(lax.ppermute(piece, 'chan', SWAP))]
    ppermute x1, waiting for transfers between devices: 0.01 us -> 39.7 us  [fast(): other = lax.ppermute(mix_weight, 'chan', SWAP)]
    all_to_all x1, blocking collectives: 52.4 us -> 23.5 us  [shuffled(): return lax.all_to_all(value, ('lat', 'chan'), 0, 0, tiled=True)]
    all_to_all x4, waiting for transfers between devices: 90.7 us -> 115 us  [shuffled(): return lax.all_to_all(value, ('lat', 'chan'), 0, 0, tiled=True)]
    all_to_all x2, waiting for transfers between devices: 10.4 us -> 32.3 us  [fast(): spec = lax.all_to_all(spec, ('lat', 'chan'), 0, 0, tiled=True)]
    ppermute x5 -> x4, waiting for transfers between devices: 35.7 us -> 18.4 us  [finished(): return (result, lax.ppermute(theirs, 'chan', SWAP))]
  transfers between devices with their start and end apart: 18 -> 17, of which waited for: 10 -> 9; matrix products, arithmetic and copies ran while one was open for 4% -> 4% of each run, Pallas kernels for 28% -> 29%
where the time goes in v6:
time: 534 us; the launch traced here: 529 us
  waiting for transfers between devices  271 us (51%)
  Pallas kernels  152 us (28%)
  starting transfers between devices  51.7 us (10%)
  blocking collectives  23.5 us (4%)
  local copies, waits for them, and re-layouts  23.4 us (4%)
  other arithmetic  7.13 us (1%)
    all_to_all x4, waiting for transfers between devices, shuffled(): return lax.all_to_all(value, ('lat', 'chan'), 0, 0, tiled=True)  115 us
    ppermute x4, waiting for transfers between devices, exchanged(): got.append(lax.ppermute(piece, 'chan', SWAP))  65.7 us
    pallas_call x2, Pallas kernels, local_part(): pl.pallas_call(local_rows, out_shape=jax.ShapeDtypeStruct((span, nlon, wi...  47.9 us
    pallas_call x3, Pallas kernels, middle_part(): pl.pallas_call(functools.partial(middle_kernel, plan), out_shape=[jax.Sha...  42 us
    pallas_call x4, Pallas kernels, tail_part(): pl.pallas_call(functools.partial(tail_kernel, len(backs)), out_shape=[jax...  40.2 us
    ppermute x1, waiting for transfers between devices, fast(): other = lax.ppermute(mix_weight, 'chan', SWAP)  39.7 us
    all_to_all x2, waiting for transfers between devices, fast(): spec = lax.all_to_all(spec, ('lat', 'chan'), 0, 0, tiled=True)  32.3 us
    all_to_all x1, blocking collectives, shuffled(): return lax.all_to_all(value, ('lat', 'chan'), 0, 0, tiled=True)  23.5 us
  transfers between devices with their start and end apart: 17, of which 9 were waited for; matrix products, arithmetic and copies ran while one was open for 4% of the time, Pallas kernels for 29%

profile of v6, /device:TPU:26, one launch (start us, length us, event | category | flops | bytes accessed | tf_op | source)
XLA Modules:
  0.0 528.9 jit_solution(3469753065103147571)
XLA Ops:
  5.5 12.5 %shard_map.146 = bf16[512,24,256]{2,1,0:T(8,128)(2,1)} custom-call(bf16[512,720]{1,0:T(8,128)(2,1)} %constant.68.clone.table_ref, bf16[24,720,256]{2,1,0:T(8,128)(2,1)} %after_ref.3), custom_call_target="tpu_custom_call" | custom-call | flops 4529848320 | bytes 8847360 | tf_op jit(solution)/shard_map/pallas_call | solution.py:64
  18.9 6.4 %all-to-all-start = ((bf16[32,8,2,24,256]{4,3,2,1,0:T(8,128)(2,1)}), bf16[32,8,2,24,256]{4,3,2,1,0:T(8,128)(2,1)}, u32[]{:S(2)}, u32[]{:S(2)}) async-start(bf16[32,8,2,24,256]{4,3,2,1,0:T(8,128)(2,1)} %bitcast.12), calls=%async_computation | async-start | bytes 12582912 | tf_op jit(solution)/shard_map/all_to_all | solution.py:413
  27.7 23.9 %shard_map.148 = bf16[12,720,256]{2,1,0:T(8,128)(2,1)} custom-call(s32[2]{0:T(128)} %pad_add_fusion.base_ref, f32[24,3]{1,0:T(8,128)} %sine_divide_fusion.ratio_ref, f32[3,7,256]{2,1,0:T(8,128)} %select_reduce_fusion.weight_ref, bf16[24,720,256]{2,1,0:T(8,128)(2,1)} %after_ref.3, bf16[24,720,256]{2,1,0:T(8,128)(2,1)} %after_ref.3, ...), custom_call_target="tpu_custom_call" | custom-call | flops 884736000 | bytes 13271040 | tf_op jit(solution)/shard_map/pallas_call | solution.py:257
  56.9 9.1 %shard_map.145 = bf16[256,24,256]{2,1,0:T(8,128)(2,1)} custom-call(bf16[256,720]{1,0:T(8,128)(2,1)} %constant.69.clone.table_ref, bf16[24,720,256]{2,1,0:T(8,128)(2,1)} %after_ref.3), custom_call_target="tpu_custom_call" | custom-call | flops 2264924160 | bytes 8847360 | tf_op jit(solution)/shard_map/pallas_call | solution.py:64
  66.0 24.0 %shard_map.147.own_ref = bf16[12,720,256]{2,1,0:T(8,128)(2,1)} custom-call(s32[2]{0:T(128)} %pad_add_fusion.1.base_ref, f32[24,3]{1,0:T(8,128)} %sine_divide_fusion.ratio_ref, f32[3,7,256]{2,1,0:T(8,128)} %select_reduce_fusion.weight_ref, bf16[24,720,256]{2,1,0:T(8,128)(2,1)} %after_ref.3, bf16[24,720,256]{2,1,0:T(8,128)(2,1)} %after_ref.3, ...), custom_call_target="tpu_custom_call" | custom-call | flops 884736000 | bytes 13271040 | tf_op jit(solution)/shard_map/pallas_call | solution.py:257
  90.0 39.7 %collective-permute-done.2.other_ref = bf16[2,512,256]{2,1,0:T(8,128)(2,1)S(1)} collective-permute-done((bf16[2,512,256]{2,1,0:T(8,128)(2,1)S(1)}, bf16[2,512,256]{2,1,0:T(8,128)(2,1)S(1)}, u32[]{:S(2)}, u32[]{:S(2)}) %collective-permute-start.2) | collective-permute-done | bytes 524320 | tf_op jit(solution)/shard_map/ppermute | solution.py:399
  129.6 32.3 %all-to-all-done = bf16[32,8,2,24,256]{4,3,2,1,0:T(8,128)(2,1)} async-done(((bf16[32,8,2,24,256]{4,3,2,1,0:T(8,128)(2,1)}), bf16[32,8,2,24,256]{4,3,2,1,0:T(8,128)(2,1)}, u32[]{:S(2)}, u32[]{:S(2)}) %all-to-all-start) | async-done | bytes 6291488 | tf_op jit(solution)/shard_map/all_to_all | solution.py:413
  161.9 7.1 %all-to-all-start.1 = ((bf16[32,4,2,24,256]{4,3,2,1,0:T(8,128)(2,1)}), bf16[32,4,2,24,256]{4,3,2,1,0:T(8,128)(2,1)S(1)}, u32[]{:S(2)}, u32[]{:S(2)}) async-start(bf16[32,4,2,24,256]{4,3,2,1,0:T(8,128)(2,1)} %bitcast.11), calls=%async_computation.1 | async-start | bytes 6291456 | tf_op jit(solution)/shard_map/all_to_all | solution.py:413
  178.2 14.0 %shard_map.149 = (bf16[32,2,3,8,512]{4,3,2,1,0:T(8,128)(2,1)}, bf16[32,3,4,8,512]{4,3,2,1,0:T(8,128)(2,1)}, bf16[32,3,3,8,512]{4,3,2,1,0:T(8,128)(2,1)}, bf16[32,3,2,8,512]{4,3,2,1,0:T(8,128)(2,1)}) custom-call(s32[2]{0:T(128)} %get-tuple-element.96.at_ref.place_ref, bf16[16,2,8,2,24,256]{5,4,3,2,1,0:T(8,128)(2,1)} %bitcast.6.spec_ref, ...), custom_call_target="tpu_custom_call" | custom-call | flops 5637144576 | bytes 9175040 | tf_op jit(solution)/shard_map/pallas_call | solution.py:159
  192.2 14.0 %shard_map.150 = (bf16[32,2,3,8,512]{4,3,2,1,0:T(8,128)(2,1)}, bf16[32,3,4,8,512]{4,3,2,1,0:T(8,128)(2,1)}, bf16[32,3,3,8,512]{4,3,2,1,0:T(8,128)(2,1)}, bf16[32,3,2,8,512]{4,3,2,1,0:T(8,128)(2,1)}) custom-call(s32[2]{0:T(128)} %get-tuple-element.95.at_ref, ...), custom_call_target="tpu_custom_call", output_to_operand_aliasing={{0}: (7, {}), {1}: (8, {}), {2}: (9, {}), {3}: (10, {})} | custom-call | flops 5637144576 | bytes 9175040 | tf_op jit(solution)/shard_map/pallas_call | solution.py:159
  206.3 38.6 %collective-permute-done.5.got_ref = bf16[2,720,256]{2,1,0:T(8,128)(2,1)} collective-permute-done((bf16[2,720,256]{2,1,0:T(8,128)(2,1)}, bf16[2,720,256]{2,1,0:T(8,128)(2,1)}, u32[]{:S(2)}, u32[]{:S(2)}) %collective-permute-start.5) | collective-permute-done | bytes 737312 | tf_op jit(solution)/shard_map/ppermute | solution.py:284
  252.0 14.0 %shard_map.151 = (bf16[32,1,3,8,512]{4,3,2,1,0:T(8,128)(2,1)}, bf16[32,3,4,8,512]{4,3,2,1,0:T(8,128)(2,1)}, bf16[32,3,3,8,512]{4,3,2,1,0:T(8,128)(2,1)}, bf16[32,3,2,8,512]{4,3,2,1,0:T(8,128)(2,1)}) custom-call(s32[2]{0:T(128)} %pad_add_fusion.3.at_ref, ...), custom_call_target="tpu_custom_call", output_to_operand_aliasing={{1}: (7, {}), {2}: (8, {}), {3}: (9, {})} | custom-call | flops 5637144576 | bytes 9175040 | tf_op jit(solution)/shard_map/pallas_call | solution.py:159
  266.0 27.0 %collective-permute-done.6.got_ref = bf16[3,720,256]{2,1,0:T(8,128)(2,1)} collective-permute-done((bf16[3,720,256]{2,1,0:T(8,128)(2,1)}, bf16[3,720,256]{2,1,0:T(8,128)(2,1)}, u32[]{:S(2)}, u32[]{:S(2)}) %collective-permute-start.6) | collective-permute-done | bytes 1105952 | tf_op jit(solution)/shard_map/ppermute | solution.py:284
  293.0 23.5 %all_to_all.35.rest_1_ = bf16[32,1,3,8,512]{4,3,2,1,0:T(8,128)(2,1)} all-to-all(bf16[32,1,3,8,512]{4,3,2,1,0:T(8,128)(2,1)} %get-tuple-element.68), channel_id=1, replica_groups=mesh['lat'=16,'chan'=2] {'lat','chan'}, dimensions={0} | all-to-all | bytes 1572864 | tf_op jit(solution)/shard_map/all_to_all | solution.py:436
  316.4 5.8 %all-to-all-start.4 = ((bf16[32,3,4,8,512]{4,3,2,1,0:T(8,128)(2,1)}), bf16[32,3,4,8,512]{4,3,2,1,0:T(8,128)(2,1)S(1)}, u32[]{:S(2)}, u32[]{:S(2)}) async-start(bf16[32,3,4,8,512]{4,3,2,1,0:T(8,128)(2,1)} %get-tuple-element.69), calls=%async_computation.4 | async-start | bytes 6291456 | tf_op jit(solution)/shard_map/all_to_all | solution.py:436
  322.3 10.0 %shard_map.152 = (bf16[24,720,256]{2,1,0:T(8,128)(2,1)}, bf16[3,720,256]{2,1,0:T(8,128)(2,1)}) custom-call(s32[2]{0:T(128)} %get-tuple-element.96.at_ref.place_ref, bf16[12,720,256]{2,1,0:T(8,128)(2,1)} %shard_map.147.own_ref, bf16[3,720,256]{2,1,0:T(8,128)(2,1)} %collective-permute-done.6.got_ref, f32[1,512]{1,0:T(1,128)} %bitcast.13, ...), custom_call_target="tpu_custom_call" | custom-call | flops 3963617280 | bytes 8847360 | tf_op jit(solution)/shard_map/pallas_call | solution.py:339
  333.8 57.7 %all-to-all-done.4.rest_0_ = bf16[32,3,4,8,512]{4,3,2,1,0:T(8,128)(2,1)S(1)} async-done(((bf16[32,3,4,8,512]{4,3,2,1,0:T(8,128)(2,1)}), bf16[32,3,4,8,512]{4,3,2,1,0:T(8,128)(2,1)S(1)}, u32[]{:S(2)}, u32[]{:S(2)}) %all-to-all-start.4) | async-done | bytes 3145760 | tf_op jit(solution)/shard_map/all_to_all | solution.py:436
  393.1 5.8 %all-to-all-start.5 = ((bf16[32,3,3,8,512]{4,3,2,1,0:T(8,128)(2,1)}), bf16[32,3,3,8,512]{4,3,2,1,0:T(8,128)(2,1)}, u32[]{:S(2)}, u32[]{:S(2)}) async-start(bf16[32,3,3,8,512]{4,3,2,1,0:T(8,128)(2,1)} %get-tuple-element.75), calls=%async_computation.5 | async-start | bytes 4718592 | tf_op jit(solution)/shard_map/all_to_all | solution.py:436
  398.9 12.2 %shard_map.153 = (bf16[24,720,256]{2,1,0:T(8,128)(2,1)}, bf16[4,720,256]{2,1,0:T(8,128)(2,1)}) custom-call(s32[2]{0:T(128)} %get-tuple-element.96.at_ref.place_ref, bf16[12,720,256]{2,1,0:T(8,128)(2,1)} %shard_map.147.own_ref, bf16[4,720,256]{2,1,0:T(8,128)(2,1)} %copy-done.7, f32[1,512]{1,0:T(1,128)} %bitcast.14, ...), custom_call_target="tpu_custom_call", output_to_operand_aliasing={{0}: (8, {})} | custom-call | flops 5284823040 | bytes 11796480 | tf_op jit(solution)/shard_map/pallas_call | solution.py:339
  413.9 37.3 %all-to-all-done.5.rest_0_ = bf16[32,3,3,8,512]{4,3,2,1,0:T(8,128)(2,1)} async-done(((bf16[32,3,3,8,512]{4,3,2,1,0:T(8,128)(2,1)}), bf16[32,3,3,8,512]{4,3,2,1,0:T(8,128)(2,1)}, u32[]{:S(2)}, u32[]{:S(2)}) %all-to-all-start.5) | async-done | bytes 2359328 | tf_op jit(solution)/shard_map/all_to_all | solution.py:436
  459.1 10.0 %shard_map.154 = (bf16[24,720,256]{2,1,0:T(8,128)(2,1)}, bf16[3,720,256]{2,1,0:T(8,128)(2,1)}) custom-call(s32[2]{0:T(128)} %get-tuple-element.96.at_ref.place_ref, bf16[12,720,256]{2,1,0:T(8,128)(2,1)} %shard_map.147.own_ref, bf16[3,720,256]{2,1,0:T(8,128)(2,1)} %collective-permute-done.4.got_ref, ...), custom_call_target="tpu_custom_call", output_to_operand_aliasing={{0}: (8, {})} | custom-call | flops 3963617280 | bytes 8847360 | tf_op jit(solution)/shard_map/pallas_call | solution.py:339
  473.1 20.3 %all-to-all-done.6.rest_0_ = bf16[32,3,2,8,512]{4,3,2,1,0:T(8,128)(2,1)S(1)} async-done(((bf16[32,3,2,8,512]{4,3,2,1,0:T(8,128)(2,1)}), bf16[32,3,2,8,512]{4,3,2,1,0:T(8,128)(2,1)S(1)}, u32[]{:S(2)}, u32[]{:S(2)}) %all-to-all-start.6) | async-done | bytes 1572896 | tf_op jit(solution)/shard_map/all_to_all | solution.py:436
  494.5 7.9 %shard_map.155 = (bf16[24,720,256]{2,1,0:T(8,128)(2,1)}, bf16[2,720,256]{2,1,0:T(8,128)(2,1)}) custom-call(s32[2]{0:T(128)} %get-tuple-element.96.at_ref.place_ref, bf16[12,720,256]{2,1,0:T(8,128)(2,1)} %shard_map.147.own_ref, bf16[2,720,256]{2,1,0:T(8,128)(2,1)} %collective-permute-done.5.got_ref, ...), custom_call_target="tpu_custom_call", output_to_operand_aliasing={{0}: (8, {})} | custom-call | flops 2642411520 | bytes 5898240 | tf_op jit(solution)/shard_map/pallas_call | solution.py:339
  512.7 14.2 %collective-permute-done.10 = bf16[2,720,256]{2,1,0:T(8,128)(2,1)} collective-permute-done((bf16[2,720,256]{2,1,0:T(8,128)(2,1)}, bf16[2,720,256]{2,1,0:T(8,128)(2,1)}, u32[]{:S(2)}, u32[]{:S(2)}) %collective-permute-start.10) | collective-permute-done | bytes 737312 | tf_op jit(solution)/shard_map/ppermute | solution.py:453
  (76 shorter events, 61.4 us)
Async XLA Ops:
  1.1 16.9 %collective-permute-start.1 = (bf16[1,720,256]{2,1,0:T(8,128)(2,1)S(1)}, bf16[1,720,256]{2,1,0:T(8,128)(2,1)S(1)}, u32[]{:S(2)}, u32[]{:S(2)}) collective-permute-start(bf16[1,720,256]{2,1,0:T(8,128)(2,1)S(1)} %get-tuple-element.91), channel_id=1, source_target_pairs={{2,0},{4,2},{6,4},{8,6},{10,8},{12,10},{14,12},{16,14},{18,16},{20... | collective-permute-start | bytes 1105928 | tf_op jit(solution)/shard_map/ppermute | solution.py:390
  3.1 14.9 %collective-permute-start = (bf16[1,720,256]{2,1,0:T(8,128)(2,1)S(1)}, bf16[1,720,256]{2,1,0:T(8,128)(2,1)S(1)}, u32[]{:S(2)}, u32[]{:S(2)}) collective-permute-start(bf16[1,720,256]{2,1,0:T(8,128)(2,1)S(1)} %get-tuple-element.92), channel_id=1, source_target_pairs={{0,2},{2,4},{4,6},{6,8},{8,10},{10,12},{12,14},{14,16},{16,18},{18... | collective-permute-start | bytes 1105928 | tf_op jit(solution)/shard_map/ppermute | solution.py:389
  18.0 8.0 %copy-start.13 = (s32[9]{0:T(128)S(1)}, s32[9]{0:T(128)}, u32[]{:S(2)}) copy-start(s32[9]{0:T(128)} %param.20) | copy-start | bytes 112
  18.0 8.1 %copy-start.12 = (s32[9]{0:T(128)S(1)}, s32[9]{0:T(128)}, u32[]{:S(2)}) copy-start(s32[9]{0:T(128)} %param.21) | copy-start | bytes 112
  18.1 8.2 %copy-start.10 = (f32[9,256]{1,0:T(8,128)S(1)}, f32[9,256]{1,0:T(8,128)}, u32[]{:S(2)}) copy-start(f32[9,256]{1,0:T(8,128)} %param.19) | copy-start | bytes 27652
  18.9 143.0 %all-to-all-start = ((bf16[32,8,2,24,256]{4,3,2,1,0:T(8,128)(2,1)}), bf16[32,8,2,24,256]{4,3,2,1,0:T(8,128)(2,1)}, u32[]{:S(2)}, u32[]{:S(2)}) async-start(bf16[32,8,2,24,256]{4,3,2,1,0:T(8,128)(2,1)} %bitcast.12), calls=%async_computation | async-start | bytes 12582912 | tf_op jit(solution)/shard_map/all_to_all | solution.py:413
  54.3 75.4 %collective-permute-start.3 = (bf16[4,720,256]{2,1,0:T(8,128)(2,1)}, bf16[4,720,256]{2,1,0:T(8,128)(2,1)S(1)}, u32[]{:S(2)}, u32[]{:S(2)}) collective-permute-start(bf16[4,720,256]{2,1,0:T(8,128)(2,1)} %slice.32), channel_id=1, source_target_pairs={{0,1},{1,0},{2,3},{3,2},{4,5},{5,4},{6,7},{7,6},{8,9},{9,8},{10,11... | collective-permute-start | bytes 4423688 | tf_op jit(solution)/shard_map/ppermute | solution.py:284
  55.8 73.8 %collective-permute-start.2 = (bf16[2,512,256]{2,1,0:T(8,128)(2,1)S(1)}, bf16[2,512,256]{2,1,0:T(8,128)(2,1)S(1)}, u32[]{:S(2)}, u32[]{:S(2)}) collective-permute-start(bf16[2,512,256]{2,1,0:T(8,128)(2,1)S(1)} %copy-done.3), channel_id=1, source_target_pairs={{0,1},{1,0},{2,3},{3,2},{4,5},{5,4},{6,7},{7,6},{8,9},{9,8},{10,11... | collective-permute-start | bytes 1572872 | tf_op jit(solution)/shard_map/ppermute | solution.py:399
  129.6 32.3 %copy-start.4 = (bf16[2,512,256]{2,1,0:T(8,128)(2,1)}, bf16[2,512,256]{2,1,0:T(8,128)(2,1)S(1)}, u32[]{:S(2)}) copy-start(bf16[2,512,256]{2,1,0:T(8,128)(2,1)S(1)} %collective-permute-done.2.other_ref) | copy-start | bytes 1572868
  129.6 32.3 %copy-start.7 = (bf16[4,720,256]{2,1,0:T(8,128)(2,1)}, bf16[4,720,256]{2,1,0:T(8,128)(2,1)S(1)}, u32[]{:S(2)}) copy-start(bf16[4,720,256]{2,1,0:T(8,128)(2,1)S(1)} %collective-permute-done.3.got_ref) | copy-start | bytes 4423684
  161.9 83.0 %all-to-all-start.1 = ((bf16[32,4,2,24,256]{4,3,2,1,0:T(8,128)(2,1)}), bf16[32,4,2,24,256]{4,3,2,1,0:T(8,128)(2,1)S(1)}, u32[]{:S(2)}, u32[]{:S(2)}) async-start(bf16[32,4,2,24,256]{4,3,2,1,0:T(8,128)(2,1)} %bitcast.11), calls=%async_computation.1 | async-start | bytes 6291456 | tf_op jit(solution)/shard_map/all_to_all | solution.py:413
  169.1 5.8 %copy-start.11 = (f32[384]{0:T(512)S(1)}, f32[384]{0:T(512)}, u32[]{:S(2)}) copy-start(f32[384]{0:T(512)} %param.18) | copy-start | bytes 4612
  172.8 72.1 %collective-permute-start.4 = (bf16[3,720,256]{2,1,0:T(8,128)(2,1)}, bf16[3,720,256]{2,1,0:T(8,128)(2,1)}, u32[]{:S(2)}, u32[]{:S(2)}) collective-permute-start(bf16[3,720,256]{2,1,0:T(8,128)(2,1)} %get-tuple-element.94), channel_id=1, source_target_pairs={{0,1},{1,0},{2,3},{3,2},{4,5},{5,4},{6,7},{7,6},{8,9},{9,8},{10,11... | collective-permute-start | bytes 3317768 | tf_op jit(solution)/shard_map/ppermute | solution.py:284
  177.7 67.2 %collective-permute-start.5 = (bf16[2,720,256]{2,1,0:T(8,128)(2,1)}, bf16[2,720,256]{2,1,0:T(8,128)(2,1)}, u32[]{:S(2)}, u32[]{:S(2)}) collective-permute-start(bf16[2,720,256]{2,1,0:T(8,128)(2,1)} %slice.34), channel_id=1, source_target_pairs={{0,1},{1,0},{2,3},{3,2},{4,5},{5,4},{6,7},{7,6},{8,9},{9,8},{10,11... | collective-permute-start | bytes 2211848 | tf_op jit(solution)/shard_map/ppermute | solution.py:284
  244.9 7.1 %copy-start = (bf16[32,4,2,24,256]{4,3,2,1,0:T(8,128)(2,1)}, bf16[32,4,2,24,256]{4,3,2,1,0:T(8,128)(2,1)S(1)}, u32[]{:S(2)}) copy-start(bf16[32,4,2,24,256]{4,3,2,1,0:T(8,128)(2,1)S(1)} %all-to-all-done.1) | copy-start | bytes 9437188
  244.9 48.1 %all-to-all-start.2 = ((bf16[32,2,3,8,512]{4,3,2,1,0:T(8,128)(2,1)}), bf16[32,2,3,8,512]{4,3,2,1,0:T(8,128)(2,1)}, u32[]{:S(2)}, u32[]{:S(2)}) async-start(bf16[32,2,3,8,512]{4,3,2,1,0:T(8,128)(2,1)} %get-tuple-element.67), calls=%async_computation.2 | async-start | bytes 3145728 | tf_op jit(solution)/shard_map/all_to_all | solution.py:436
  249.9 43.1 %collective-permute-start.6 = (bf16[3,720,256]{2,1,0:T(8,128)(2,1)}, bf16[3,720,256]{2,1,0:T(8,128)(2,1)}, u32[]{:S(2)}, u32[]{:S(2)}) collective-permute-start(bf16[3,720,256]{2,1,0:T(8,128)(2,1)} %get-tuple-element.93), channel_id=1, source_target_pairs={{0,1},{1,0},{2,3},{3,2},{4,5},{5,4},{6,7},{7,6},{8,9},{9,8},{10,11... | collective-permute-start | bytes 3317768 | tf_op jit(solution)/shard_map/ppermute | solution.py:284
  316.4 75.0 %all-to-all-start.4 = ((bf16[32,3,4,8,512]{4,3,2,1,0:T(8,128)(2,1)}), bf16[32,3,4,8,512]{4,3,2,1,0:T(8,128)(2,1)S(1)}, u32[]{:S(2)}, u32[]{:S(2)}) async-start(bf16[32,3,4,8,512]{4,3,2,1,0:T(8,128)(2,1)} %get-tuple-element.69), calls=%async_computation.4 | async-start | bytes 6291456 | tf_op jit(solution)/shard_map/all_to_all | solution.py:436
  332.3 59.2 %collective-permute-start.7 = (bf16[3,720,256]{2,1,0:T(8,128)(2,1)}, bf16[3,720,256]{2,1,0:T(8,128)(2,1)}, u32[]{:S(2)}, u32[]{:S(2)}) collective-permute-start(bf16[3,720,256]{2,1,0:T(8,128)(2,1)} %get-tuple-element.74), channel_id=1, source_target_pairs={{0,1},{1,0},{2,3},{3,2},{4,5},{5,4},{6,7},{7,6},{8,9},{9,8},{10,11... | collective-permute-start | bytes 3317768 | tf_op jit(solution)/shard_map/ppermute | solution.py:453
  393.1 58.1 %all-to-all-start.5 = ((bf16[32,3,3,8,512]{4,3,2,1,0:T(8,128)(2,1)}), bf16[32,3,3,8,512]{4,3,2,1,0:T(8,128)(2,1)}, u32[]{:S(2)}, u32[]{:S(2)}) async-start(bf16[32,3,3,8,512]{4,3,2,1,0:T(8,128)(2,1)} %get-tuple-element.75), calls=%async_computation.5 | async-start | bytes 4718592 | tf_op jit(solution)/shard_map/all_to_all | solution.py:436
  412.4 38.9 %collective-permute-start.8 = (bf16[3,720,256]{2,1,0:T(8,128)(2,1)S(1)}, bf16[3,720,256]{2,1,0:T(8,128)(2,1)S(1)}, u32[]{:S(2)}, u32[]{:S(2)}) collective-permute-start(bf16[3,720,256]{2,1,0:T(8,128)(2,1)S(1)} %slice.30), channel_id=1, source_target_pairs={{0,1},{1,0},{2,3},{3,2},{4,5},{5,4},{6,7},{7,6},{8,9},{9,8},{10,11... | collective-permute-start | bytes 3317768 | tf_op jit(solution)/shard_map/ppermute | solution.py:453
  452.4 41.0 %all-to-all-start.6 = ((bf16[32,3,2,8,512]{4,3,2,1,0:T(8,128)(2,1)}), bf16[32,3,2,8,512]{4,3,2,1,0:T(8,128)(2,1)S(1)}, u32[]{:S(2)}, u32[]{:S(2)}) async-start(bf16[32,3,2,8,512]{4,3,2,1,0:T(8,128)(2,1)} %get-tuple-element.81), calls=%async_computation.6 | async-start | bytes 3145728 | tf_op jit(solution)/shard_map/all_to_all | solution.py:436
  471.6 39.9 %collective-permute-start.9 = (bf16[4,720,256]{2,1,0:T(8,128)(2,1)}, bf16[4,720,256]{2,1,0:T(8,128)(2,1)S(1)}, u32[]{:S(2)}, u32[]{:S(2)}) collective-permute-start(bf16[4,720,256]{2,1,0:T(8,128)(2,1)} %pad_maximum_fusion), channel_id=1, source_target_pairs={{0,1},{1,0},{2,3},{3,2},{4,5},{5,4},{6,7},{7,6},{8,9},{9,8},{10,11... | collective-permute-start | bytes 4423688 | tf_op jit(solution)/shard_map/ppermute | solution.py:453
  502.5 24.4 %collective-permute-start.10 = (bf16[2,720,256]{2,1,0:T(8,128)(2,1)}, bf16[2,720,256]{2,1,0:T(8,128)(2,1)}, u32[]{:S(2)}, u32[]{:S(2)}) collective-permute-start(bf16[2,720,256]{2,1,0:T(8,128)(2,1)} %get-tuple-element.90), channel_id=1, source_target_pairs={{0,1},{1,0},{2,3},{3,2},{4,5},{5,4},{6,7},{7,6},{8,9},{9,8},{10,11... | collective-permute-start | bytes 2211848 | tf_op jit(solution)/shard_map/ppermute | solution.py:453
  (7 other events, 13.5 us)

commit v7 on v6

--- a/solution.py
+++ b/solution.py
@@ -38,51 +38,45 @@
     return np.cos(angle), np.sin(angle)
 
 
-def forward_kernel(scale, table_ref, grid_ref, out_ref, held):
-    few = grid_ref.shape[0]
-    cycles = out_ref.shape[1]
-    rows = table_ref.shape[0]
-    step = pl.program_id(0)
+def forward_kernel(scale, table_ref, grid_ref, out_ref):
+    places, blocks, few, slots, width = out_ref.shape
     for t in range(few):
-        value = jnp.dot(table_ref[...], grid_ref[t], preferred_element_type=F32)
-        value = value * scale
-        for at in range(held.shape[0]):
-            part = value[:, at * LANES : (at + 1) * LANES]
-            held[at, pl.ds(step * few + t, rows, stride=cycles), :] = part
-
-    @pl.when(step == pl.num_programs(0) - 1)
-    def _():
-        for at in range(held.shape[0]):
-            lanes = slice(at * LANES, (at + 1) * LANES)
-            out_ref[:, :, lanes] = held[at].reshape(rows, cycles, LANES).astype(BF)
-
-
-def forward_part(grid, table):
+        value = jnp.dot(table_ref[...], grid_ref[t], preferred_element_type=F32) * scale
+        out_ref[:, :, t] = value.reshape(places, blocks, slots, width).astype(BF)
+
+
+def forward_part(grid, table, places):
     cycles, nlon, width = grid.shape
     rows = table.shape[0]
+    slots = 2 * STEP
+    blocks = rows // places // slots
     few = 4
     return pl.pallas_call(
         functools.partial(forward_kernel, 1.0 / nlon),
-        out_shape=jax.ShapeDtypeStruct((rows, cycles, width), BF),
+        out_shape=jax.ShapeDtypeStruct((places, blocks, cycles, slots, width), BF),
         grid=(cycles // few,),
         in_specs=[
             pl.BlockSpec(table.shape, lambda t: (0, 0)),
             pl.BlockSpec((few, nlon, width), lambda t: (t, 0, 0)),
         ],
-        out_specs=pl.BlockSpec((rows, cycles, width), lambda t: (0, 0, 0)),
-        scratch_shapes=[pltpu.VMEM((width // LANES, rows * cycles, LANES), F32)],
+        out_specs=pl.BlockSpec((places, blocks, few, slots, width), lambda t: (0, 0, t, 0, 0)),
         compiler_params=params(60),
         cost_estimate=cost(2 * rows * nlon * cycles * width, grid.size * 2),
     )(table, grid)
 
 
 def middle_kernel(plan, at_ref, spec_ref, basis_ref, quad_ref, own_ref, other_ref, gain_ref, *rest):
-    outs, mix_ref, held = (rest[-len(plan) - 2 : -2], rest[-2], rest[-1])
+    outs, mix_ref, held, loose = (rest[-len(plan) - 3 : -3], *rest[-3:])
     mode = pl.program_id(0)
-    groups, sides, _, _, cycles, width = spec_ref.shape
+    groups, sides, _, cycles, slots, width = spec_ref.shape
+    lanes = width // LANES
 
     @pl.when(mode == 0)
     def _():
+        for at in range(sides * lanes):
+            low = at % lanes * LANES
+            piece = spec_ref[:, at // lanes, 0, :, :, low : low + LANES].astype(F32)
+            loose[at] = piece.reshape(groups * cycles * slots, LANES)
         first = at_ref[1] == 0
         channels = sides * width
         own = own_ref[...].astype(F32)
@@ -105,15 +99,15 @@
     pieces = []
     for side in range(sides):
         for part in range(2):
-            piece = spec_ref[:, side, 0, part, :, :].astype(F32)
-            pieces.append(piece.reshape(nlat, width).astype(BF))
+            for at in range(side * lanes, (side + 1) * lanes):
+                rows = pl.ds(2 * mode + part, nlat, stride=slots)
+                pieces.append(loose[at, rows, :].astype(BF))
     spec = jnp.concatenate(pieces, axis=1)
     coeff = jnp.dot(forward, spec, preferred_element_type=F32).astype(BF)
     mixed = jnp.dot(coeff, mix_ref[...], preferred_element_type=F32) * gain_ref[...]
     inverse = table.T.astype(BF)
     back = jnp.dot(inverse, mixed.astype(BF), preferred_element_type=F32)
     half = back.shape[1] // 2
-    slots = 2 * STEP
     for part in range(2):
         for where in range(STEP):
 
@@ -136,13 +130,12 @@
 
 
 def middle_part(spec, skip, basis, quad, mix, other, gain, offset, plan, filled):
-    groups, sides, _, _, cycles, width = spec.shape
+    groups, sides, _, cycles, slots, width = spec.shape
     nlat = groups * cycles
     channels = sides * width
-    slots = 2 * STEP
     fixed = lambda m, at: (0, 0)
     specs = [
-        pl.BlockSpec((groups, sides, 1, 2, cycles, width), lambda m, at: (0, 0, skip + m, 0, 0, 0)),
+        pl.BlockSpec((groups, sides, 1, cycles, slots, width), lambda m, at: (0, 0, skip, 0, 0, 0)),
         pl.BlockSpec((1, L, nlat), lambda m, at: (at[0] + m, 0, 0)),
         pl.BlockSpec((1, nlat), fixed),
         pl.BlockSpec(mix.shape, lambda m, at: (0, 0, 0)),
@@ -175,6 +168,7 @@
             ],
             scratch_shapes=[
                 pltpu.VMEM((2 * channels, 2 * channels), BF),
+                pltpu.VMEM((channels // LANES, nlat * slots, LANES), F32),
                 pltpu.VMEM((channels // LANES, nlat * slots, LANES), F32),
             ],
         ),
@@ -401,17 +395,16 @@
     bounds = [(0, few - STEP), (few - STEP, few)]
     for part, (low, high) in enumerate(bounds):
         table = jnp.asarray(fwd_table[:, low:high].reshape(-1, nlon), BF)
-        spec = forward_part(grid, table)
-        spec = spec.reshape(groups * sides, high - low, 2, cycles, width)
+        spec = forward_part(grid, table, groups * sides)
         if part == 0:
-            spec, before, after = lax.optimization_barrier((spec, before, after))
+            spec, before, after, other = lax.optimization_barrier((spec, before, after, other))
             asked = local_part(grid, before, after, ratio, weight, (1 - side) * span, span)
             got = exchanged(asked, counts)
         else:
             own = local_part(grid, before, after, ratio, weight, side * span, span)
-            spec, own, other, got[1] = lax.optimization_barrier((spec, own, other, got[1]))
+            spec, own, got[1], got[3] = lax.optimization_barrier((spec, own, got[1], got[3]))
         spec = lax.all_to_all(spec, ("lat", "chan"), 0, 0, tiled=True)
-        gathered.append(spec.reshape(groups, sides, high - low, 2, cycles, width))
+        gathered.append(spec.reshape((groups, sides) + spec.shape[1:]))
 
     theta = cycle_angle(jnp.arange(nlat, dtype=jnp.int32), nlat)
     quad = (math.pi / nlat * jnp.sin(theta))[None, :]
@@ -426,7 +419,7 @@
         plan += [(parts, part, count) for count in counts[1:]]
         head = heads[-1] if heads and not late else None
         ready = middle_part(
-            gathered[int(late)], 0 if late else part * STEP, basis, quad, mix_weight, other, gain,
+            gathered[int(late)], 0 if late else part, basis, quad, mix_weight, other, gain,
             offset, plan, [head] + filled,
         )
         heads.append(ready[0])
@@ -453,7 +446,7 @@
         return (result, lax.ppermute(theirs, "chan", SWAP))
 
     begin, end = heads[-2:]
-    begin, _, got[2], got[3] = lax.optimization_barrier((begin, gathered[1], got[2], got[3]))
+    begin, _, got[2] = lax.optimization_barrier((begin, gathered[1], got[2]))
     begin = shuffled(begin)
     end, begin, got[0] = lax.optimization_barrier((end, begin, got[0]))
     end = shuffled(end)

time: 534 us -> 527 us (0.987)
  waiting for transfers between devices: 271 us -> 263 us
    ppermute x1, waiting for transfers between devices: 39.7 us -> 0.01 us  [fast(): other = lax.ppermute(mix_weight, 'chan', SWAP)]
    ppermute x4, waiting for transfers between devices: 65.7 us -> 94.5 us  [exchanged(): got.append(lax.ppermute(piece, 'chan', SWAP))]
  transfers between devices with their start and end apart: 17 -> 17, of which waited for: 9 -> 10; matrix products, arithmetic and copies ran while one was open for 4% -> 4% of each run, Pallas kernels for 29% -> 29%
where the time goes in v7:
time: 527 us; the launch traced here: 522 us
  waiting for transfers between devices  263 us (50%)
  Pallas kernels  152 us (29%)
  starting transfers between devices  53.4 us (10%)
  blocking collectives  23.5 us (4%)
  local copies, waits for them, and re-layouts  22.1 us (4%)
  other arithmetic  7.41 us (1%)
    all_to_all x4, waiting for transfers between devices, shuffled(): return lax.all_to_all(value, ('lat', 'chan'), 0, 0, tiled=True)  115 us
    ppermute x4, waiting for transfers between devices, exchanged(): got.append(lax.ppermute(piece, 'chan', SWAP))  94.5 us
    pallas_call x2, Pallas kernels, local_part(): pl.pallas_call(local_rows, out_shape=jax.ShapeDtypeStruct((span, nlon, wi...  47.9 us
    pallas_call x3, Pallas kernels, middle_part(): pl.pallas_call(functools.partial(middle_kernel, plan), out_shape=[jax.Sha...  46 us
    pallas_call x4, Pallas kernels, tail_part(): pl.pallas_call(functools.partial(tail_kernel, len(backs)), out_shape=[jax...  40.1 us
    all_to_all x2, waiting for transfers between devices, fast(): spec = lax.all_to_all(spec, ('lat', 'chan'), 0, 0, tiled=True)  35.1 us
    all_to_all x1, blocking collectives, shuffled(): return lax.all_to_all(value, ('lat', 'chan'), 0, 0, tiled=True)  23.5 us
    all_to_all x4, starting transfers between devices, shuffled(): return lax.all_to_all(value, ('lat', 'chan'), 0, 0, tiled=True)  23 us
  transfers between devices with their start and end apart: 17, of which 10 were waited for; matrix products, arithmetic and copies ran while one was open for 4% of the time, Pallas kernels for 29%

profile of v7, /device:TPU:26, one launch (start us, length us, event | category | flops | bytes accessed | tf_op | source)
XLA Modules:
  0.0 522.1 jit_solution(10317380962351256412)
XLA Ops:
  8.2 10.3 %shard_map.146 = bf16[32,2,24,8,256]{4,3,2,1,0:T(8,128)(2,1)} custom-call(bf16[512,720]{1,0:T(8,128)(2,1)} %constant.68.clone.table_ref, bf16[24,720,256]{2,1,0:T(8,128)(2,1)} %after_ref.3), custom_call_target="tpu_custom_call" | custom-call | flops 4529848320 | bytes 8847360 | tf_op jit(solution)/shard_map/pallas_call | solution.py:54
  26.8 23.9 %shard_map.148 = bf16[12,720,256]{2,1,0:T(8,128)(2,1)} custom-call(s32[2]{0:T(128)} %pad_add_fusion.base_ref, f32[24,3]{1,0:T(8,128)} %sine_divide_fusion.ratio_ref, f32[3,7,256]{2,1,0:T(8,128)} %select_reduce_fusion.weight_ref, bf16[24,720,256]{2,1,0:T(8,128)(2,1)} %after_ref.3, bf16[24,720,256]{2,1,0:T(8,128)(2,1)} %after_ref.3, ...), custom_call_target="tpu_custom_call" | custom-call | flops 884736000 | bytes 13271040 | tf_op jit(solution)/shard_map/pallas_call | solution.py:251
  57.0 8.0 %shard_map.145 = bf16[32,1,24,8,256]{4,3,2,1,0:T(8,128)(2,1)} custom-call(bf16[256,720]{1,0:T(8,128)(2,1)} %constant.69.clone.table_ref, bf16[24,720,256]{2,1,0:T(8,128)(2,1)} %after_ref.3), custom_call_target="tpu_custom_call" | custom-call | flops 2264924160 | bytes 8847360 | tf_op jit(solution)/shard_map/pallas_call | solution.py:54
  64.9 23.9 %shard_map.147.own_ref = bf16[12,720,256]{2,1,0:T(8,128)(2,1)} custom-call(s32[2]{0:T(128)} %pad_add_fusion.1.base_ref, f32[24,3]{1,0:T(8,128)} %sine_divide_fusion.ratio_ref, f32[3,7,256]{2,1,0:T(8,128)} %select_reduce_fusion.weight_ref, bf16[24,720,256]{2,1,0:T(8,128)(2,1)} %after_ref.3, bf16[24,720,256]{2,1,0:T(8,128)(2,1)} %after_ref.3, ...), custom_call_target="tpu_custom_call" | custom-call | flops 884736000 | bytes 13271040 | tf_op jit(solution)/shard_map/pallas_call | solution.py:251
  88.9 48.3 %collective-permute-done.4.got_ref = bf16[2,720,256]{2,1,0:T(8,128)(2,1)} collective-permute-done((bf16[2,720,256]{2,1,0:T(8,128)(2,1)}, bf16[2,720,256]{2,1,0:T(8,128)(2,1)}, u32[]{:S(2)}, u32[]{:S(2)}) %collective-permute-start.4) | collective-permute-done | bytes 737312 | tf_op jit(solution)/shard_map/ppermute | solution.py:278
  137.2 23.8 %all-to-all-done.1 = bf16[32,2,24,8,256]{4,3,2,1,0:T(8,128)(2,1)} async-done(((bf16[32,2,24,8,256]{4,3,2,1,0:T(8,128)(2,1)}), bf16[32,2,24,8,256]{4,3,2,1,0:T(8,128)(2,1)}, u32[]{:S(2)}, u32[]{:S(2)}) %all-to-all-start.1) | async-done | bytes 6291488 | tf_op jit(solution)/shard_map/all_to_all | solution.py:406
  160.9 7.2 %all-to-all-start = ((bf16[32,1,24,8,256]{4,3,2,1,0:T(8,128)(2,1)}), bf16[32,1,24,8,256]{4,3,2,1,0:T(8,128)(2,1)S(1)}, u32[]{:S(2)}, u32[]{:S(2)}) async-start(bf16[32,1,24,8,256]{4,3,2,1,0:T(8,128)(2,1)} %shard_map.145), calls=%async_computation | async-start | bytes 6291456 | tf_op jit(solution)/shard_map/all_to_all | solution.py:406
  174.8 15.4 %shard_map.149 = (bf16[32,2,3,8,512]{4,3,2,1,0:T(8,128)(2,1)}, bf16[32,3,4,8,512]{4,3,2,1,0:T(8,128)(2,1)}, bf16[32,3,3,8,512]{4,3,2,1,0:T(8,128)(2,1)}, bf16[32,3,2,8,512]{4,3,2,1,0:T(8,128)(2,1)}) custom-call(s32[2]{0:T(128)} %get-tuple-element.96.at_ref.place_ref, bf16[16,2,2,24,8,256]{5,4,3,2,1,0:T(8,128)(2,1)} %bitcast.7.spec_ref, ...), custom_call_target="tpu_custom_call" | custom-call | flops 5637144576 | bytes 9175040 | tf_op jit(solution)/shard_map/pallas_call | solution.py:152
  190.2 15.4 %shard_map.150 = (bf16[32,2,3,8,512]{4,3,2,1,0:T(8,128)(2,1)}, bf16[32,3,4,8,512]{4,3,2,1,0:T(8,128)(2,1)}, bf16[32,3,3,8,512]{4,3,2,1,0:T(8,128)(2,1)}, bf16[32,3,2,8,512]{4,3,2,1,0:T(8,128)(2,1)}) custom-call(s32[2]{0:T(128)} %get-tuple-element.95.at_ref, ...), custom_call_target="tpu_custom_call", output_to_operand_aliasing={{0}: (7, {}), {1}: (8, {}), {2}: (9, {}), {3}: (10, {})} | custom-call | flops 5637144576 | bytes 9175040 | tf_op jit(solution)/shard_map/pallas_call | solution.py:152
  205.6 20.5 %collective-permute-done.5.got_ref = bf16[3,720,256]{2,1,0:T(8,128)(2,1)} collective-permute-done((bf16[3,720,256]{2,1,0:T(8,128)(2,1)}, bf16[3,720,256]{2,1,0:T(8,128)(2,1)}, u32[]{:S(2)}, u32[]{:S(2)}) %collective-permute-start.5) | collective-permute-done | bytes 1105952 | tf_op jit(solution)/shard_map/ppermute | solution.py:278
  226.0 11.3 %all-to-all-done = bf16[32,1,24,8,256]{4,3,2,1,0:T(8,128)(2,1)S(1)} async-done(((bf16[32,1,24,8,256]{4,3,2,1,0:T(8,128)(2,1)}), bf16[32,1,24,8,256]{4,3,2,1,0:T(8,128)(2,1)S(1)}, u32[]{:S(2)}, u32[]{:S(2)}) %all-to-all-start) | async-done | bytes 3145760 | tf_op jit(solution)/shard_map/all_to_all | solution.py:406
  237.4 5.8 %all-to-all-start.2 = ((bf16[32,2,3,8,512]{4,3,2,1,0:T(8,128)(2,1)}), bf16[32,2,3,8,512]{4,3,2,1,0:T(8,128)(2,1)}, u32[]{:S(2)}, u32[]{:S(2)}) async-start(bf16[32,2,3,8,512]{4,3,2,1,0:T(8,128)(2,1)} %get-tuple-element.67), calls=%async_computation.2 | async-start | bytes 3145728 | tf_op jit(solution)/shard_map/all_to_all | solution.py:429
  245.3 15.3 %shard_map.151 = (bf16[32,1,3,8,512]{4,3,2,1,0:T(8,128)(2,1)}, bf16[32,3,4,8,512]{4,3,2,1,0:T(8,128)(2,1)}, bf16[32,3,3,8,512]{4,3,2,1,0:T(8,128)(2,1)}, bf16[32,3,2,8,512]{4,3,2,1,0:T(8,128)(2,1)}) custom-call(s32[2]{0:T(128)} %pad_add_fusion.2.at_ref, ...), custom_call_target="tpu_custom_call", output_to_operand_aliasing={{1}: (7, {}), {2}: (8, {}), {3}: (9, {})} | custom-call | flops 5637144576 | bytes 9175040 | tf_op jit(solution)/shard_map/pallas_call | solution.py:152
  260.5 25.7 %collective-permute-done.6.got_ref = bf16[3,720,256]{2,1,0:T(8,128)(2,1)} collective-permute-done((bf16[3,720,256]{2,1,0:T(8,128)(2,1)}, bf16[3,720,256]{2,1,0:T(8,128)(2,1)}, u32[]{:S(2)}, u32[]{:S(2)}) %collective-permute-start.6) | collective-permute-done | bytes 1105952 | tf_op jit(solution)/shard_map/ppermute | solution.py:278
  286.2 23.5 %all_to_all.35.rest_1_ = bf16[32,1,3,8,512]{4,3,2,1,0:T(8,128)(2,1)} all-to-all(bf16[32,1,3,8,512]{4,3,2,1,0:T(8,128)(2,1)} %get-tuple-element.68), channel_id=1, replica_groups=mesh['lat'=16,'chan'=2] {'lat','chan'}, dimensions={0} | all-to-all | bytes 1572864 | tf_op jit(solution)/shard_map/all_to_all | solution.py:429
  309.7 5.8 %all-to-all-start.4 = ((bf16[32,3,4,8,512]{4,3,2,1,0:T(8,128)(2,1)}), bf16[32,3,4,8,512]{4,3,2,1,0:T(8,128)(2,1)S(1)}, u32[]{:S(2)}, u32[]{:S(2)}) async-start(bf16[32,3,4,8,512]{4,3,2,1,0:T(8,128)(2,1)} %get-tuple-element.69), calls=%async_computation.4 | async-start | bytes 6291456 | tf_op jit(solution)/shard_map/all_to_all | solution.py:429
  315.5 10.0 %shard_map.152 = (bf16[24,720,256]{2,1,0:T(8,128)(2,1)}, bf16[3,720,256]{2,1,0:T(8,128)(2,1)}) custom-call(s32[2]{0:T(128)} %get-tuple-element.96.at_ref.place_ref, bf16[12,720,256]{2,1,0:T(8,128)(2,1)} %shard_map.147.own_ref, bf16[3,720,256]{2,1,0:T(8,128)(2,1)} %collective-permute-done.6.got_ref, f32[1,512]{1,0:T(1,128)} %bitcast.9, ...), custom_call_target="tpu_custom_call" | custom-call | flops 3963617280 | bytes 8847360 | tf_op jit(solution)/shard_map/pallas_call | solution.py:333
  327.0 57.7 %all-to-all-done.4.rest_0_ = bf16[32,3,4,8,512]{4,3,2,1,0:T(8,128)(2,1)S(1)} async-done(((bf16[32,3,4,8,512]{4,3,2,1,0:T(8,128)(2,1)}), bf16[32,3,4,8,512]{4,3,2,1,0:T(8,128)(2,1)S(1)}, u32[]{:S(2)}, u32[]{:S(2)}) %all-to-all-start.4) | async-done | bytes 3145760 | tf_op jit(solution)/shard_map/all_to_all | solution.py:429
  392.1 12.2 %shard_map.153 = (bf16[24,720,256]{2,1,0:T(8,128)(2,1)}, bf16[4,720,256]{2,1,0:T(8,128)(2,1)}) custom-call(s32[2]{0:T(128)} %get-tuple-element.96.at_ref.place_ref, bf16[12,720,256]{2,1,0:T(8,128)(2,1)} %shard_map.147.own_ref, bf16[4,720,256]{2,1,0:T(8,128)(2,1)} %copy-done.5, f32[1,512]{1,0:T(1,128)} %bitcast.10, ...), custom_call_target="tpu_custom_call", output_to_operand_aliasing={{0}: (8, {})} | custom-call | flops 5284823040 | bytes 11796480 | tf_op jit(solution)/shard_map/pallas_call | solution.py:333
  407.2 37.3 %all-to-all-done.5.rest_0_ = bf16[32,3,3,8,512]{4,3,2,1,0:T(8,128)(2,1)} async-done(((bf16[32,3,3,8,512]{4,3,2,1,0:T(8,128)(2,1)}), bf16[32,3,3,8,512]{4,3,2,1,0:T(8,128)(2,1)}, u32[]{:S(2)}, u32[]{:S(2)}) %all-to-all-start.5) | async-done | bytes 2359328 | tf_op jit(solution)/shard_map/all_to_all | solution.py:429
  452.2 10.0 %shard_map.154 = (bf16[24,720,256]{2,1,0:T(8,128)(2,1)}, bf16[3,720,256]{2,1,0:T(8,128)(2,1)}) custom-call(s32[2]{0:T(128)} %get-tuple-element.96.at_ref.place_ref, bf16[12,720,256]{2,1,0:T(8,128)(2,1)} %shard_map.147.own_ref, bf16[3,720,256]{2,1,0:T(8,128)(2,1)} %collective-permute-done.5.got_ref, ...), custom_call_target="tpu_custom_call", output_to_operand_aliasing={{0}: (8, {})} | custom-call | flops 3963617280 | bytes 8847360 | tf_op jit(solution)/shard_map/pallas_call | solution.py:333
  466.3 20.2 %all-to-all-done.6.rest_0_ = bf16[32,3,2,8,512]{4,3,2,1,0:T(8,128)(2,1)S(1)} async-done(((bf16[32,3,2,8,512]{4,3,2,1,0:T(8,128)(2,1)}), bf16[32,3,2,8,512]{4,3,2,1,0:T(8,128)(2,1)S(1)}, u32[]{:S(2)}, u32[]{:S(2)}) %all-to-all-start.6) | async-done | bytes 1572896 | tf_op jit(solution)/shard_map/all_to_all | solution.py:429
  487.7 7.9 %shard_map.155 = (bf16[24,720,256]{2,1,0:T(8,128)(2,1)}, bf16[2,720,256]{2,1,0:T(8,128)(2,1)}) custom-call(s32[2]{0:T(128)} %get-tuple-element.96.at_ref.place_ref, bf16[12,720,256]{2,1,0:T(8,128)(2,1)} %shard_map.147.own_ref, bf16[2,720,256]{2,1,0:T(8,128)(2,1)} %collective-permute-done.4.got_ref, ...), custom_call_target="tpu_custom_call", output_to_operand_aliasing={{0}: (8, {})} | custom-call | flops 2642411520 | bytes 5898240 | tf_op jit(solution)/shard_map/pallas_call | solution.py:333
  505.9 14.2 %collective-permute-done.10 = bf16[2,720,256]{2,1,0:T(8,128)(2,1)} collective-permute-done((bf16[2,720,256]{2,1,0:T(8,128)(2,1)}, bf16[2,720,256]{2,1,0:T(8,128)(2,1)}, u32[]{:S(2)}, u32[]{:S(2)}) %collective-permute-start.10) | collective-permute-done | bytes 737312 | tf_op jit(solution)/shard_map/ppermute | solution.py:446
  (72 shorter events, 68.4 us)
Async XLA Ops:
  0.0 18.6 %collective-permute-start.2 = (bf16[2,512,256]{2,1,0:T(8,128)(2,1)}, bf16[2,512,256]{2,1,0:T(8,128)(2,1)}, u32[]{:S(2)}, u32[]{:S(2)}) collective-permute-start(bf16[2,512,256]{2,1,0:T(8,128)(2,1)} %own_ref.5), channel_id=1, source_target_pairs={{0,1},{1,0},{2,3},{3,2},{4,5},{5,4},{6,7},{7,6},{8,9},{9,8},{10,11... | collective-permute-start | bytes 1572872 | tf_op jit(solution)/shard_map/ppermute | solution.py:393
  2.7 15.9 %collective-permute-start = (bf16[1,720,256]{2,1,0:T(8,128)(2,1)S(1)}, bf16[1,720,256]{2,1,0:T(8,128)(2,1)S(1)}, u32[]{:S(2)}, u32[]{:S(2)}) collective-permute-start(bf16[1,720,256]{2,1,0:T(8,128)(2,1)S(1)} %get-tuple-element.92), channel_id=1, source_target_pairs={{0,2},{2,4},{4,6},{6,8},{8,10},{10,12},{12,14},{14,16},{16,18},{18... | collective-permute-start | bytes 1105928 | tf_op jit(solution)/shard_map/ppermute | solution.py:383
  4.6 13.9 %collective-permute-start.1 = (bf16[1,720,256]{2,1,0:T(8,128)(2,1)S(1)}, bf16[1,720,256]{2,1,0:T(8,128)(2,1)S(1)}, u32[]{:S(2)}, u32[]{:S(2)}) collective-permute-start(bf16[1,720,256]{2,1,0:T(8,128)(2,1)S(1)} %get-tuple-element.91), channel_id=1, source_target_pairs={{2,0},{4,2},{6,4},{8,6},{10,8},{12,10},{14,12},{16,14},{18,16},{20... | collective-permute-start | bytes 1105928 | tf_op jit(solution)/shard_map/ppermute | solution.py:384
  18.5 6.6 %copy-start.11 = (s32[9]{0:T(128)S(1)}, s32[9]{0:T(128)}, u32[]{:S(2)}) copy-start(s32[9]{0:T(128)} %param.20) | copy-start | bytes 112
  18.5 6.7 %copy-start.10 = (s32[9]{0:T(128)S(1)}, s32[9]{0:T(128)}, u32[]{:S(2)}) copy-start(s32[9]{0:T(128)} %param.21) | copy-start | bytes 112
  18.5 6.8 %copy-start.8 = (f32[9,256]{1,0:T(8,128)S(1)}, f32[9,256]{1,0:T(8,128)}, u32[]{:S(2)}) copy-start(f32[9,256]{1,0:T(8,128)} %param.19) | copy-start | bytes 27652
  19.4 141.5 %all-to-all-start.1 = ((bf16[32,2,24,8,256]{4,3,2,1,0:T(8,128)(2,1)}), bf16[32,2,24,8,256]{4,3,2,1,0:T(8,128)(2,1)}, u32[]{:S(2)}, u32[]{:S(2)}) async-start(bf16[32,2,24,8,256]{4,3,2,1,0:T(8,128)(2,1)} %shard_map.146), calls=%async_computation.1 | async-start | bytes 12582912 | tf_op jit(solution)/shard_map/all_to_all | solution.py:406
  52.2 85.0 %collective-permute-start.3 = (bf16[4,720,256]{2,1,0:T(8,128)(2,1)S(1)}, bf16[4,720,256]{2,1,0:T(8,128)(2,1)S(1)}, u32[]{:S(2)}, u32[]{:S(2)}) collective-permute-start(bf16[4,720,256]{2,1,0:T(8,128)(2,1)S(1)} %slice.32), channel_id=1, source_target_pairs={{0,1},{1,0},{2,3},{3,2},{4,5},{5,4},{6,7},{7,6},{8,9},{9,8},{10,11... | collective-permute-start | bytes 4423688 | tf_op jit(solution)/shard_map/ppermute | solution.py:278
  55.8 81.3 %collective-permute-start.4 = (bf16[2,720,256]{2,1,0:T(8,128)(2,1)}, bf16[2,720,256]{2,1,0:T(8,128)(2,1)}, u32[]{:S(2)}, u32[]{:S(2)}) collective-permute-start(bf16[2,720,256]{2,1,0:T(8,128)(2,1)} %slice.33), channel_id=1, source_target_pairs={{0,1},{1,0},{2,3},{3,2},{4,5},{5,4},{6,7},{7,6},{8,9},{9,8},{10,11... | collective-permute-start | bytes 2211848 | tf_op jit(solution)/shard_map/ppermute | solution.py:278
  137.2 23.8 %copy-start.5 = (bf16[4,720,256]{2,1,0:T(8,128)(2,1)}, bf16[4,720,256]{2,1,0:T(8,128)(2,1)S(1)}, u32[]{:S(2)}) copy-start(bf16[4,720,256]{2,1,0:T(8,128)(2,1)S(1)} %collective-permute-done.3.got_ref) | copy-start | bytes 4423684
  160.9 76.4 %all-to-all-start = ((bf16[32,1,24,8,256]{4,3,2,1,0:T(8,128)(2,1)}), bf16[32,1,24,8,256]{4,3,2,1,0:T(8,128)(2,1)S(1)}, u32[]{:S(2)}, u32[]{:S(2)}) async-start(bf16[32,1,24,8,256]{4,3,2,1,0:T(8,128)(2,1)} %shard_map.145), calls=%async_computation | async-start | bytes 6291456 | tf_op jit(solution)/shard_map/all_to_all | solution.py:406
  168.1 5.9 %copy-start.9 = (f32[384]{0:T(512)S(1)}, f32[384]{0:T(512)}, u32[]{:S(2)}) copy-start(f32[384]{0:T(512)} %param.18) | copy-start | bytes 4612
  171.9 54.2 %collective-permute-start.5 = (bf16[3,720,256]{2,1,0:T(8,128)(2,1)}, bf16[3,720,256]{2,1,0:T(8,128)(2,1)}, u32[]{:S(2)}, u32[]{:S(2)}) collective-permute-start(bf16[3,720,256]{2,1,0:T(8,128)(2,1)} %get-tuple-element.94), channel_id=1, source_target_pairs={{0,1},{1,0},{2,3},{3,2},{4,5},{5,4},{6,7},{7,6},{8,9},{9,8},{10,11... | collective-permute-start | bytes 3317768 | tf_op jit(solution)/shard_map/ppermute | solution.py:278
  237.4 7.9 %copy-start = (bf16[32,1,24,8,256]{4,3,2,1,0:T(8,128)(2,1)}, bf16[32,1,24,8,256]{4,3,2,1,0:T(8,128)(2,1)S(1)}, u32[]{:S(2)}) copy-start(bf16[32,1,24,8,256]{4,3,2,1,0:T(8,128)(2,1)S(1)} %all-to-all-done) | copy-start | bytes 9437188
  237.4 48.9 %all-to-all-start.2 = ((bf16[32,2,3,8,512]{4,3,2,1,0:T(8,128)(2,1)}), bf16[32,2,3,8,512]{4,3,2,1,0:T(8,128)(2,1)}, u32[]{:S(2)}, u32[]{:S(2)}) async-start(bf16[32,2,3,8,512]{4,3,2,1,0:T(8,128)(2,1)} %get-tuple-element.67), calls=%async_computation.2 | async-start | bytes 3145728 | tf_op jit(solution)/shard_map/all_to_all | solution.py:429
  243.1 43.1 %collective-permute-start.6 = (bf16[3,720,256]{2,1,0:T(8,128)(2,1)}, bf16[3,720,256]{2,1,0:T(8,128)(2,1)}, u32[]{:S(2)}, u32[]{:S(2)}) collective-permute-start(bf16[3,720,256]{2,1,0:T(8,128)(2,1)} %get-tuple-element.93), channel_id=1, source_target_pairs={{0,1},{1,0},{2,3},{3,2},{4,5},{5,4},{6,7},{7,6},{8,9},{9,8},{10,11... | collective-permute-start | bytes 3317768 | tf_op jit(solution)/shard_map/ppermute | solution.py:278
  309.7 75.0 %all-to-all-start.4 = ((bf16[32,3,4,8,512]{4,3,2,1,0:T(8,128)(2,1)}), bf16[32,3,4,8,512]{4,3,2,1,0:T(8,128)(2,1)S(1)}, u32[]{:S(2)}, u32[]{:S(2)}) async-start(bf16[32,3,4,8,512]{4,3,2,1,0:T(8,128)(2,1)} %get-tuple-element.69), calls=%async_computation.4 | async-start | bytes 6291456 | tf_op jit(solution)/shard_map/all_to_all | solution.py:429
  325.5 59.2 %collective-permute-start.7 = (bf16[3,720,256]{2,1,0:T(8,128)(2,1)}, bf16[3,720,256]{2,1,0:T(8,128)(2,1)}, u32[]{:S(2)}, u32[]{:S(2)}) collective-permute-start(bf16[3,720,256]{2,1,0:T(8,128)(2,1)} %get-tuple-element.74), channel_id=1, source_target_pairs={{0,1},{1,0},{2,3},{3,2},{4,5},{5,4},{6,7},{7,6},{8,9},{9,8},{10,11... | collective-permute-start | bytes 3317768 | tf_op jit(solution)/shard_map/ppermute | solution.py:446
  386.4 58.1 %all-to-all-start.5 = ((bf16[32,3,3,8,512]{4,3,2,1,0:T(8,128)(2,1)}), bf16[32,3,3,8,512]{4,3,2,1,0:T(8,128)(2,1)}, u32[]{:S(2)}, u32[]{:S(2)}) async-start(bf16[32,3,3,8,512]{4,3,2,1,0:T(8,128)(2,1)} %get-tuple-element.75), calls=%async_computation.5 | async-start | bytes 4718592 | tf_op jit(solution)/shard_map/all_to_all | solution.py:429
  405.6 38.9 %collective-permute-start.8 = (bf16[3,720,256]{2,1,0:T(8,128)(2,1)S(1)}, bf16[3,720,256]{2,1,0:T(8,128)(2,1)S(1)}, u32[]{:S(2)}, u32[]{:S(2)}) collective-permute-start(bf16[3,720,256]{2,1,0:T(8,128)(2,1)S(1)} %slice.30), channel_id=1, source_target_pairs={{0,1},{1,0},{2,3},{3,2},{4,5},{5,4},{6,7},{7,6},{8,9},{9,8},{10,11... | collective-permute-start | bytes 3317768 | tf_op jit(solution)/shard_map/ppermute | solution.py:446
  445.5 41.0 %all-to-all-start.6 = ((bf16[32,3,2,8,512]{4,3,2,1,0:T(8,128)(2,1)}), bf16[32,3,2,8,512]{4,3,2,1,0:T(8,128)(2,1)S(1)}, u32[]{:S(2)}, u32[]{:S(2)}) async-start(bf16[32,3,2,8,512]{4,3,2,1,0:T(8,128)(2,1)} %get-tuple-element.81), calls=%async_computation.6 | async-start | bytes 3145728 | tf_op jit(solution)/shard_map/all_to_all | solution.py:429
  464.8 39.9 %collective-permute-start.9 = (bf16[4,720,256]{2,1,0:T(8,128)(2,1)}, bf16[4,720,256]{2,1,0:T(8,128)(2,1)S(1)}, u32[]{:S(2)}, u32[]{:S(2)}) collective-permute-start(bf16[4,720,256]{2,1,0:T(8,128)(2,1)} %pad_maximum_fusion), channel_id=1, source_target_pairs={{0,1},{1,0},{2,3},{3,2},{4,5},{5,4},{6,7},{7,6},{8,9},{9,8},{10,11... | collective-permute-start | bytes 4423688 | tf_op jit(solution)/shard_map/ppermute | solution.py:446
  495.6 3.8 copy-start.7
  495.6 24.4 %collective-permute-start.10 = (bf16[2,720,256]{2,1,0:T(8,128)(2,1)}, bf16[2,720,256]{2,1,0:T(8,128)(2,1)}, u32[]{:S(2)}, u32[]{:S(2)}) collective-permute-start(bf16[2,720,256]{2,1,0:T(8,128)(2,1)} %get-tuple-element.90), channel_id=1, source_target_pairs={{0,1},{1,0},{2,3},{3,2},{4,5},{5,4},{6,7},{7,6},{8,9},{9,8},{10,11... | collective-permute-start | bytes 2211848 | tf_op jit(solution)/shard_map/ppermute | solution.py:446
  (5 other events, 5.4 us)

commit v8 on v7

--- a/solution.py
+++ b/solution.py
@@ -366,7 +366,7 @@
     parts = few // STEP
     span = cycles // sides
     third = span // 3
-    counts = [third - 1, third, third - 1, span - 3 * third + 2]
+    counts = [third, third - 1, third - 1, span - 3 * third + 2]
 
     cosine, sine = angle_table(nlon)
     both = np.stack([cosine, -sine], axis=-1)
@@ -397,12 +397,12 @@
         table = jnp.asarray(fwd_table[:, low:high].reshape(-1, nlon), BF)
         spec = forward_part(grid, table, groups * sides)
         if part == 0:
-            spec, before, after, other = lax.optimization_barrier((spec, before, after, other))
+            spec, before, after = lax.optimization_barrier((spec, before, after))
             asked = local_part(grid, before, after, ratio, weight, (1 - side) * span, span)
             got = exchanged(asked, counts)
         else:
             own = local_part(grid, before, after, ratio, weight, side * span, span)
-            spec, own, got[1], got[3] = lax.optimization_barrier((spec, own, got[1], got[3]))
+            spec, own, got[0], got[1] = lax.optimization_barrier((spec, own, got[0], got[1]))
         spec = lax.all_to_all(spec, ("lat", "chan"), 0, 0, tiled=True)
         gathered.append(spec.reshape((groups, sides) + spec.shape[1:]))
 
@@ -430,31 +430,30 @@
 
     place = jnp.stack([side * span, side]).astype(jnp.int32)
 
-    kept = []
+    sent = []
 
     def finished(at, backs, tables, result):
+        early = at < 2
         result, theirs = tail_part(
             backs, tables, own, got[at], sum(counts[:at]), ln_gain[None, :], up_weight,
             down_weight, place, result, cycles,
         )
-        if at == 1:
-            cut = max(theirs.shape[0] - 1, 1)
-            kept.append(theirs[cut:])
-            theirs = theirs[:cut]
-        elif at == 2:
-            theirs = jnp.concatenate([kept[0], theirs], axis=0)
-        return (result, lax.ppermute(theirs, "chan", SWAP))
+        if sent and at < 3:
+            theirs, sent[-1] = lax.optimization_barrier((theirs, sent[-1]))
+        cut = max(theirs.shape[0] - 1, 1) if early else theirs.shape[0]
+        pieces = [theirs[:cut], theirs[cut:]] if cut < theirs.shape[0] else [theirs]
+        sent.extend(lax.ppermute(piece, "chan", SWAP) for piece in pieces)
+        return (result, sent[-len(pieces)])
 
     begin, end = heads[-2:]
     begin, _, got[2] = lax.optimization_barrier((begin, gathered[1], got[2]))
     begin = shuffled(begin)
-    end, begin, got[0] = lax.optimization_barrier((end, begin, got[0]))
+    end, begin, got[3] = lax.optimization_barrier((end, begin, got[3]))
     end = shuffled(end)
     backs = [[begin, end]]
     tables = [[inverse(0, parts - 1), inverse(parts - 1, parts)]] + [[inverse(0, parts)]] * 3
     last = end
     result = None
-    sent = []
     for at, value in enumerate(filled):
         if at == 0:
             value, last = lax.optimization_barrier((value, last))
@@ -462,16 +461,12 @@
         else:
             value, last = lax.optimization_barrier((value, last))
             backs[-1] = [last]
-        if at == 1:
-            value, sent[0] = lax.optimization_barrier((value, sent[0]))
-        if at > 1:
-            value, sent[1] = lax.optimization_barrier((value, sent[1]))
+        if at > 0:
+            value, _ = lax.optimization_barrier((value, tied))
         last = shuffled(value)
-        result, value = finished(at, backs[-1], tables[at], result)
-        sent.append(value)
+        result, tied = finished(at, backs[-1], tables[at], result)
         backs.append([last])
-    result, value = finished(len(filled), [last], tables[-1], result)
-    sent.append(value)
+    result, _ = finished(len(filled), [last], tables[-1], result)
     start = 0
     for value in sent:
         count = value.shape[0]

time: 527 us -> 522 us (level)
  waiting for transfers between devices: 263 us -> 253 us
  blocking collectives: 23.5 us -> 29.9 us
    all_to_all x4, waiting for transfers between devices: 115 us -> 71.2 us  [shuffled(): return lax.all_to_all(value, ('lat', 'chan'), 0, 0, tiled=True)]
    ppermute x1, waiting for transfers between devices: 0.01 us -> 38.2 us  [fast(): other = lax.ppermute(mix_weight, 'chan', SWAP)]
    ppermute x4 -> x6, waiting for transfers between devices: 18.4 us -> 53 us  [finished(): sent.extend((lax.ppermute(piece, 'chan', SWAP) for piece in pieces))]
    all_to_all x2, waiting for transfers between devices: 35.1 us -> 15.6 us  [fast(): spec = lax.all_to_all(spec, ('lat', 'chan'), 0, 0, tiled=True)]
    ppermute x4, waiting for transfers between devices: 94.5 us -> 75.4 us  [exchanged(): got.append(lax.ppermute(piece, 'chan', SWAP))]
    all_to_all x1, blocking collectives: 23.5 us -> 29.9 us  [shuffled(): return lax.all_to_all(value, ('lat', 'chan'), 0, 0, tiled=True)]
    slice x2 -> x4, local copies, waits for them, and re-layouts: 2.33 us -> 8.05 us  [finished(): pieces = [theirs[:cut], theirs[cut:]] if cut < theirs.shape[0] else [theirs]]
  transfers between devices with their start and end apart: 17 -> 19, of which waited for: 10 -> 13; matrix products, arithmetic and copies ran while one was open for 4% -> 5% of each run, Pallas kernels for 29% -> 29%
where the time goes in v8:
time: 522 us; the launch traced here: 519 us
  waiting for transfers between devices  253 us (48%)
  Pallas kernels  153 us (29%)
  starting transfers between devices  52.1 us (10%)
  blocking collectives  29.9 us (6%)
  local copies, waits for them, and re-layouts  26.3 us (5%)
    ppermute x4, waiting for transfers between devices, exchanged(): got.append(lax.ppermute(piece, 'chan', SWAP))  75.4 us
    all_to_all x4, waiting for transfers between devices, shuffled(): return lax.all_to_all(value, ('lat', 'chan'), 0, 0, tiled=True)  71.2 us
    ppermute x6, waiting for transfers between devices, finished(): sent.extend((lax.ppermute(piece, 'chan', SWAP) for piece in pieces))  53 us
    pallas_call x2, Pallas kernels, local_part(): pl.pallas_call(local_rows, out_shape=jax.ShapeDtypeStruct((span, nlon, wi...  47.9 us
    pallas_call x3, Pallas kernels, middle_part(): pl.pallas_call(functools.partial(middle_kernel, plan), out_shape=[jax.Sha...  46.2 us
    pallas_call x4, Pallas kernels, tail_part(): pl.pallas_call(functools.partial(tail_kernel, len(backs)), out_shape=[jax...  40.2 us
    ppermute x1, waiting for transfers between devices, fast(): other = lax.ppermute(mix_weight, 'chan', SWAP)  38.2 us
    all_to_all x1, blocking collectives, shuffled(): return lax.all_to_all(value, ('lat', 'chan'), 0, 0, tiled=True)  29.9 us
  transfers between devices with their start and end apart: 19, of which 13 were waited for; matrix products, arithmetic and copies ran while one was open for 5% of the time, Pallas kernels for 29%

profile of v8, /device:TPU:26, one launch (start us, length us, event | category | flops | bytes accessed | tf_op | source)
XLA Modules:
  0.0 519.3 jit_solution(267481323395158083)
XLA Ops:
  6.7 10.3 %shard_map.146 = bf16[32,2,24,8,256]{4,3,2,1,0:T(8,128)(2,1)} custom-call(bf16[512,720]{1,0:T(8,128)(2,1)} %constant.74.clone.table_ref, bf16[24,720,256]{2,1,0:T(8,128)(2,1)} %after_ref.3), custom_call_target="tpu_custom_call" | custom-call | flops 4529848320 | bytes 8847360 | tf_op jit(solution)/shard_map/pallas_call | solution.py:54
  26.1 23.9 %shard_map.148 = bf16[12,720,256]{2,1,0:T(8,128)(2,1)} custom-call(s32[2]{0:T(128)} %pad_add_fusion.base_ref, f32[24,3]{1,0:T(8,128)} %sine_divide_fusion.ratio_ref, f32[3,7,256]{2,1,0:T(8,128)} %select_reduce_fusion.weight_ref, bf16[24,720,256]{2,1,0:T(8,128)(2,1)} %after_ref.3, bf16[24,720,256]{2,1,0:T(8,128)(2,1)} %after_ref.3, ...), custom_call_target="tpu_custom_call" | custom-call | flops 884736000 | bytes 13271040 | tf_op jit(solution)/shard_map/pallas_call | solution.py:251
  57.3 8.0 %shard_map.145 = bf16[32,1,24,8,256]{4,3,2,1,0:T(8,128)(2,1)} custom-call(bf16[256,720]{1,0:T(8,128)(2,1)} %constant.75.clone.table_ref, bf16[24,720,256]{2,1,0:T(8,128)(2,1)} %after_ref.3), custom_call_target="tpu_custom_call" | custom-call | flops 2264924160 | bytes 8847360 | tf_op jit(solution)/shard_map/pallas_call | solution.py:54
  65.3 23.9 %shard_map.147.own_ref = bf16[12,720,256]{2,1,0:T(8,128)(2,1)} custom-call(s32[2]{0:T(128)} %pad_add_fusion.1.base_ref, f32[24,3]{1,0:T(8,128)} %sine_divide_fusion.ratio_ref, f32[3,7,256]{2,1,0:T(8,128)} %select_reduce_fusion.weight_ref, bf16[24,720,256]{2,1,0:T(8,128)(2,1)} %after_ref.3, bf16[24,720,256]{2,1,0:T(8,128)(2,1)} %after_ref.3, ...), custom_call_target="tpu_custom_call" | custom-call | flops 884736000 | bytes 13271040 | tf_op jit(solution)/shard_map/pallas_call | solution.py:251
  89.3 55.5 %collective-permute-done.3.got_ref = bf16[3,720,256]{2,1,0:T(8,128)(2,1)S(1)} collective-permute-done((bf16[3,720,256]{2,1,0:T(8,128)(2,1)}, bf16[3,720,256]{2,1,0:T(8,128)(2,1)S(1)}, u32[]{:S(2)}, u32[]{:S(2)}) %collective-permute-start.3) | collective-permute-done | bytes 1105952 | tf_op jit(solution)/shard_map/ppermute | solution.py:278
  144.8 15.6 %all-to-all-done.1 = bf16[32,2,24,8,256]{4,3,2,1,0:T(8,128)(2,1)} async-done(((bf16[32,2,24,8,256]{4,3,2,1,0:T(8,128)(2,1)}), bf16[32,2,24,8,256]{4,3,2,1,0:T(8,128)(2,1)}, u32[]{:S(2)}, u32[]{:S(2)}) %all-to-all-start.1) | async-done | bytes 6291488 | tf_op jit(solution)/shard_map/all_to_all | solution.py:406
  160.4 7.2 %all-to-all-start = ((bf16[32,1,24,8,256]{4,3,2,1,0:T(8,128)(2,1)}), bf16[32,1,24,8,256]{4,3,2,1,0:T(8,128)(2,1)S(1)}, u32[]{:S(2)}, u32[]{:S(2)}) async-start(bf16[32,1,24,8,256]{4,3,2,1,0:T(8,128)(2,1)} %shard_map.145), calls=%async_computation | async-start | bytes 6291456 | tf_op jit(solution)/shard_map/all_to_all | solution.py:406
  171.7 38.2 %collective-permute-done.4.other_ref = bf16[2,512,256]{2,1,0:T(8,128)(2,1)} collective-permute-done((bf16[2,512,256]{2,1,0:T(8,128)(2,1)}, bf16[2,512,256]{2,1,0:T(8,128)(2,1)}, u32[]{:S(2)}, u32[]{:S(2)}) %collective-permute-start.4) | collective-permute-done | bytes 524320 | tf_op jit(solution)/shard_map/ppermute | solution.py:393
  209.9 15.4 %shard_map.149 = (bf16[32,2,4,8,512]{4,3,2,1,0:T(8,128)(2,1)}, bf16[32,3,3,8,512]{4,3,2,1,0:T(8,128)(2,1)}, bf16[32,3,3,8,512]{4,3,2,1,0:T(8,128)(2,1)}, bf16[32,3,2,8,512]{4,3,2,1,0:T(8,128)(2,1)}) custom-call(s32[2]{0:T(128)} %get-tuple-element.98.at_ref.place_ref, bf16[16,2,2,24,8,256]{5,4,3,2,1,0:T(8,128)(2,1)} %bitcast.6.spec_ref, ...), custom_call_target="tpu_custom_call" | custom-call | flops 5637144576 | bytes 9175040 | tf_op jit(solution)/shard_map/pallas_call | solution.py:152
  225.3 15.5 %shard_map.150 = (bf16[32,2,4,8,512]{4,3,2,1,0:T(8,128)(2,1)}, bf16[32,3,3,8,512]{4,3,2,1,0:T(8,128)(2,1)}, bf16[32,3,3,8,512]{4,3,2,1,0:T(8,128)(2,1)}, bf16[32,3,2,8,512]{4,3,2,1,0:T(8,128)(2,1)}) custom-call(s32[2]{0:T(128)} %get-tuple-element.97.at_ref, ...), custom_call_target="tpu_custom_call", output_to_operand_aliasing={{0}: (7, {}), {1}: (8, {}), {2}: (9, {}), {3}: (10, {})} | custom-call | flops 5637144576 | bytes 9175040 | tf_op jit(solution)/shard_map/pallas_call | solution.py:152
  249.9 15.3 %shard_map.151 = (bf16[32,1,4,8,512]{4,3,2,1,0:T(8,128)(2,1)}, bf16[32,3,3,8,512]{4,3,2,1,0:T(8,128)(2,1)}, bf16[32,3,3,8,512]{4,3,2,1,0:T(8,128)(2,1)}, bf16[32,3,2,8,512]{4,3,2,1,0:T(8,128)(2,1)}) custom-call(s32[2]{0:T(128)} %pad_add_fusion.2.at_ref, ...), custom_call_target="tpu_custom_call", output_to_operand_aliasing={{1}: (7, {}), {2}: (8, {}), {3}: (9, {})} | custom-call | flops 5637144576 | bytes 9175040 | tf_op jit(solution)/shard_map/pallas_call | solution.py:152
  265.3 19.9 %collective-permute-done.6.got_ref = bf16[2,720,256]{2,1,0:T(8,128)(2,1)} collective-permute-done((bf16[2,720,256]{2,1,0:T(8,128)(2,1)}, bf16[2,720,256]{2,1,0:T(8,128)(2,1)}, u32[]{:S(2)}, u32[]{:S(2)}) %collective-permute-start.6) | collective-permute-done | bytes 737312 | tf_op jit(solution)/shard_map/ppermute | solution.py:278
  285.2 7.3 %all-to-all-done.2.rest_0_ = bf16[32,2,4,8,512]{4,3,2,1,0:T(8,128)(2,1)} async-done(((bf16[32,2,4,8,512]{4,3,2,1,0:T(8,128)(2,1)}), bf16[32,2,4,8,512]{4,3,2,1,0:T(8,128)(2,1)}, u32[]{:S(2)}, u32[]{:S(2)}) %all-to-all-start.2) | async-done | bytes 2097184 | tf_op jit(solution)/shard_map/all_to_all | solution.py:429
  292.5 29.9 %all_to_all.35.rest_1_ = bf16[32,1,4,8,512]{4,3,2,1,0:T(8,128)(2,1)} all-to-all(bf16[32,1,4,8,512]{4,3,2,1,0:T(8,128)(2,1)} %get-tuple-element.68), channel_id=1, replica_groups=mesh['lat'=16,'chan'=2] {'lat','chan'}, dimensions={0} | all-to-all | bytes 2097152 | tf_op jit(solution)/shard_map/all_to_all | solution.py:429
  328.2 12.2 %shard_map.152 = (bf16[24,720,256]{2,1,0:T(8,128)(2,1)}, bf16[4,720,256]{2,1,0:T(8,128)(2,1)}) custom-call(s32[2]{0:T(128)} %get-tuple-element.98.at_ref.place_ref, bf16[12,720,256]{2,1,0:T(8,128)(2,1)} %shard_map.147.own_ref, bf16[4,720,256]{2,1,0:T(8,128)(2,1)} %collective-permute-done.2.got_ref, f32[1,512]{1,0:T(1,128)} %bitcast.9, ...), custom_call_target="tpu_custom_call" | custom-call | flops 5284823040 | bytes 11796480 | tf_op jit(solution)/shard_map/pallas_call | solution.py:333
  344.2 36.3 %all-to-all-done.4.rest_0_ = bf16[32,3,3,8,512]{4,3,2,1,0:T(8,128)(2,1)S(1)} async-done(((bf16[32,3,3,8,512]{4,3,2,1,0:T(8,128)(2,1)}), bf16[32,3,3,8,512]{4,3,2,1,0:T(8,128)(2,1)S(1)}, u32[]{:S(2)}, u32[]{:S(2)}) %all-to-all-start.4) | async-done | bytes 2359328 | tf_op jit(solution)/shard_map/all_to_all | solution.py:429
  390.9 10.0 %shard_map.153 = (bf16[24,720,256]{2,1,0:T(8,128)(2,1)}, bf16[3,720,256]{2,1,0:T(8,128)(2,1)}) custom-call(s32[2]{0:T(128)} %get-tuple-element.98.at_ref.place_ref, bf16[12,720,256]{2,1,0:T(8,128)(2,1)} %shard_map.147.own_ref, bf16[3,720,256]{2,1,0:T(8,128)(2,1)} %copy-done.5, f32[1,512]{1,0:T(1,128)} %bitcast.10, ...), custom_call_target="tpu_custom_call", output_to_operand_aliasing={{0}: (8, {})} | custom-call | flops 3963617280 | bytes 8847360 | tf_op jit(solution)/shard_map/pallas_call | solution.py:333
  400.9 18.4 %collective-permute-done.8 = bf16[1,720,256]{2,1,0:T(8,128)(2,1)S(1)} collective-permute-done((bf16[1,720,256]{2,1,0:T(8,128)(2,1)}, bf16[1,720,256]{2,1,0:T(8,128)(2,1)S(1)}, u32[]{:S(2)}, u32[]{:S(2)}) %collective-permute-start.8) | collective-permute-done | bytes 368672 | tf_op jit(solution)/shard_map/ppermute | solution.py:445
  421.5 18.4 %all-to-all-done.5.rest_0_ = bf16[32,3,3,8,512]{4,3,2,1,0:T(8,128)(2,1)S(1)} async-done(((bf16[32,3,3,8,512]{4,3,2,1,0:T(8,128)(2,1)}), bf16[32,3,3,8,512]{4,3,2,1,0:T(8,128)(2,1)S(1)}, u32[]{:S(2)}, u32[]{:S(2)}) %all-to-all-start.5) | async-done | bytes 2359328 | tf_op jit(solution)/shard_map/all_to_all | solution.py:429
  451.8 10.0 %shard_map.154 = (bf16[24,720,256]{2,1,0:T(8,128)(2,1)}, bf16[3,720,256]{2,1,0:T(8,128)(2,1)}) custom-call(s32[2]{0:T(128)} %get-tuple-element.98.at_ref.place_ref, bf16[12,720,256]{2,1,0:T(8,128)(2,1)} %shard_map.147.own_ref, bf16[3,720,256]{2,1,0:T(8,128)(2,1)} %collective-permute-done.5.got_ref, ...), custom_call_target="tpu_custom_call", output_to_operand_aliasing={{0}: (8, {})} | custom-call | flops 3963617280 | bytes 8847360 | tf_op jit(solution)/shard_map/pallas_call | solution.py:333
  461.9 11.7 %collective-permute-done.10 = bf16[1,720,256]{2,1,0:T(8,128)(2,1)S(1)} collective-permute-done((bf16[1,720,256]{2,1,0:T(8,128)(2,1)}, bf16[1,720,256]{2,1,0:T(8,128)(2,1)S(1)}, u32[]{:S(2)}, u32[]{:S(2)}) %collective-permute-start.10) | collective-permute-done | bytes 368672 | tf_op jit(solution)/shard_map/ppermute | solution.py:445
  474.8 9.2 %all-to-all-done.6.rest_0_ = bf16[32,3,2,8,512]{4,3,2,1,0:T(8,128)(2,1)} async-done(((bf16[32,3,2,8,512]{4,3,2,1,0:T(8,128)(2,1)}), bf16[32,3,2,8,512]{4,3,2,1,0:T(8,128)(2,1)}, u32[]{:S(2)}, u32[]{:S(2)}) %all-to-all-start.6) | async-done | bytes 1572896 | tf_op jit(solution)/shard_map/all_to_all | solution.py:429
  484.0 8.0 %shard_map.155 = (bf16[24,720,256]{2,1,0:T(8,128)(2,1)}, bf16[2,720,256]{2,1,0:T(8,128)(2,1)}) custom-call(s32[2]{0:T(128)} %get-tuple-element.98.at_ref.place_ref, bf16[12,720,256]{2,1,0:T(8,128)(2,1)} %shard_map.147.own_ref, bf16[2,720,256]{2,1,0:T(8,128)(2,1)} %collective-permute-done.6.got_ref, ...), custom_call_target="tpu_custom_call", output_to_operand_aliasing={{0}: (8, {})} | custom-call | flops 2642411520 | bytes 5898240 | tf_op jit(solution)/shard_map/pallas_call | solution.py:333
  504.0 14.4 %collective-permute-done.12 = bf16[2,720,256]{2,1,0:T(8,128)(2,1)S(1)} collective-permute-done((bf16[2,720,256]{2,1,0:T(8,128)(2,1)}, bf16[2,720,256]{2,1,0:T(8,128)(2,1)S(1)}, u32[]{:S(2)}, u32[]{:S(2)}) %collective-permute-start.12) | collective-permute-done | bytes 737312 | tf_op jit(solution)/shard_map/ppermute | solution.py:445
  (83 shorter events, 84.5 us)
Async XLA Ops:
  1.1 15.9 %collective-permute-start = (bf16[1,720,256]{2,1,0:T(8,128)(2,1)S(1)}, bf16[1,720,256]{2,1,0:T(8,128)(2,1)S(1)}, u32[]{:S(2)}, u32[]{:S(2)}) collective-permute-start(bf16[1,720,256]{2,1,0:T(8,128)(2,1)S(1)} %get-tuple-element.94), channel_id=1, source_target_pairs={{0,2},{2,4},{4,6},{6,8},{8,10},{10,12},{12,14},{14,16},{16,18},{18... | collective-permute-start | bytes 1105928 | tf_op jit(solution)/shard_map/ppermute | solution.py:383
  3.1 13.9 %collective-permute-start.1 = (bf16[1,720,256]{2,1,0:T(8,128)(2,1)S(1)}, bf16[1,720,256]{2,1,0:T(8,128)(2,1)S(1)}, u32[]{:S(2)}, u32[]{:S(2)}) collective-permute-start(bf16[1,720,256]{2,1,0:T(8,128)(2,1)S(1)} %get-tuple-element.93), channel_id=1, source_target_pairs={{2,0},{4,2},{6,4},{8,6},{10,8},{12,10},{14,12},{16,14},{18,16},{20... | collective-permute-start | bytes 1105928 | tf_op jit(solution)/shard_map/ppermute | solution.py:384
  17.9 142.5 %all-to-all-start.1 = ((bf16[32,2,24,8,256]{4,3,2,1,0:T(8,128)(2,1)}), bf16[32,2,24,8,256]{4,3,2,1,0:T(8,128)(2,1)}, u32[]{:S(2)}, u32[]{:S(2)}) async-start(bf16[32,2,24,8,256]{4,3,2,1,0:T(8,128)(2,1)} %shard_map.146), calls=%async_computation.1 | async-start | bytes 12582912 | tf_op jit(solution)/shard_map/all_to_all | solution.py:406
  51.5 93.2 %collective-permute-start.2 = (bf16[4,720,256]{2,1,0:T(8,128)(2,1)S(1)}, bf16[4,720,256]{2,1,0:T(8,128)(2,1)}, u32[]{:S(2)}, u32[]{:S(2)}) collective-permute-start(bf16[4,720,256]{2,1,0:T(8,128)(2,1)S(1)} %slice.40), channel_id=1, source_target_pairs={{0,1},{1,0},{2,3},{3,2},{4,5},{5,4},{6,7},{7,6},{8,9},{9,8},{10,11... | collective-permute-start | bytes 4423688 | tf_op jit(solution)/shard_map/ppermute | solution.py:278
  56.2 88.6 %collective-permute-start.3 = (bf16[3,720,256]{2,1,0:T(8,128)(2,1)}, bf16[3,720,256]{2,1,0:T(8,128)(2,1)S(1)}, u32[]{:S(2)}, u32[]{:S(2)}) collective-permute-start(bf16[3,720,256]{2,1,0:T(8,128)(2,1)} %get-tuple-element.96), channel_id=1, source_target_pairs={{0,1},{1,0},{2,3},{3,2},{4,5},{5,4},{6,7},{7,6},{8,9},{9,8},{10,11... | collective-permute-start | bytes 3317768 | tf_op jit(solution)/shard_map/ppermute | solution.py:278
  89.3 81.6 %copy-start.11 = (f32[384]{0:T(512)S(1)}, f32[384]{0:T(512)}, u32[]{:S(2)}) copy-start(f32[384]{0:T(512)} %param.18) | copy-start | bytes 4612
  144.8 15.6 %copy-start.5 = (bf16[3,720,256]{2,1,0:T(8,128)(2,1)}, bf16[3,720,256]{2,1,0:T(8,128)(2,1)S(1)}, u32[]{:S(2)}) copy-start(bf16[3,720,256]{2,1,0:T(8,128)(2,1)S(1)} %collective-permute-done.3.got_ref) | copy-start | bytes 3317764
  160.4 80.4 %all-to-all-start = ((bf16[32,1,24,8,256]{4,3,2,1,0:T(8,128)(2,1)}), bf16[32,1,24,8,256]{4,3,2,1,0:T(8,128)(2,1)S(1)}, u32[]{:S(2)}, u32[]{:S(2)}) async-start(bf16[32,1,24,8,256]{4,3,2,1,0:T(8,128)(2,1)} %shard_map.145), calls=%async_computation | async-start | bytes 6291456 | tf_op jit(solution)/shard_map/all_to_all | solution.py:406
  167.6 42.3 %collective-permute-start.4 = (bf16[2,512,256]{2,1,0:T(8,128)(2,1)}, bf16[2,512,256]{2,1,0:T(8,128)(2,1)}, u32[]{:S(2)}, u32[]{:S(2)}) collective-permute-start(bf16[2,512,256]{2,1,0:T(8,128)(2,1)} %own_ref.5), channel_id=1, source_target_pairs={{0,1},{1,0},{2,3},{3,2},{4,5},{5,4},{6,7},{7,6},{8,9},{9,8},{10,11... | collective-permute-start | bytes 1572872 | tf_op jit(solution)/shard_map/ppermute | solution.py:393
  169.8 71.0 %collective-permute-start.5 = (bf16[3,720,256]{2,1,0:T(8,128)(2,1)}, bf16[3,720,256]{2,1,0:T(8,128)(2,1)}, u32[]{:S(2)}, u32[]{:S(2)}) collective-permute-start(bf16[3,720,256]{2,1,0:T(8,128)(2,1)} %get-tuple-element.95), channel_id=1, source_target_pairs={{0,1},{1,0},{2,3},{3,2},{4,5},{5,4},{6,7},{7,6},{8,9},{9,8},{10,11... | collective-permute-start | bytes 3317768 | tf_op jit(solution)/shard_map/ppermute | solution.py:278
  240.8 9.2 %copy-start = (bf16[32,1,24,8,256]{4,3,2,1,0:T(8,128)(2,1)}, bf16[32,1,24,8,256]{4,3,2,1,0:T(8,128)(2,1)S(1)}, u32[]{:S(2)}) copy-start(bf16[32,1,24,8,256]{4,3,2,1,0:T(8,128)(2,1)S(1)} %all-to-all-done) | copy-start | bytes 9437188
  240.8 51.7 %all-to-all-start.2 = ((bf16[32,2,4,8,512]{4,3,2,1,0:T(8,128)(2,1)}), bf16[32,2,4,8,512]{4,3,2,1,0:T(8,128)(2,1)}, u32[]{:S(2)}, u32[]{:S(2)}) async-start(bf16[32,2,4,8,512]{4,3,2,1,0:T(8,128)(2,1)} %get-tuple-element.63), calls=%async_computation.2 | async-start | bytes 4194304 | tf_op jit(solution)/shard_map/all_to_all | solution.py:429
  247.9 37.3 %collective-permute-start.6 = (bf16[2,720,256]{2,1,0:T(8,128)(2,1)}, bf16[2,720,256]{2,1,0:T(8,128)(2,1)}, u32[]{:S(2)}, u32[]{:S(2)}) collective-permute-start(bf16[2,720,256]{2,1,0:T(8,128)(2,1)} %slice.43), channel_id=1, source_target_pairs={{0,1},{1,0},{2,3},{3,2},{4,5},{5,4},{6,7},{7,6},{8,9},{9,8},{10,11... | collective-permute-start | bytes 2211848 | tf_op jit(solution)/shard_map/ppermute | solution.py:278
  322.4 58.1 %all-to-all-start.4 = ((bf16[32,3,3,8,512]{4,3,2,1,0:T(8,128)(2,1)}), bf16[32,3,3,8,512]{4,3,2,1,0:T(8,128)(2,1)S(1)}, u32[]{:S(2)}, u32[]{:S(2)}) async-start(bf16[32,3,3,8,512]{4,3,2,1,0:T(8,128)(2,1)} %get-tuple-element.69), calls=%async_computation.4 | async-start | bytes 4718592 | tf_op jit(solution)/shard_map/all_to_all | solution.py:429
  342.7 37.8 %collective-permute-start.7 = (bf16[3,720,256]{2,1,0:T(8,128)(2,1)}, bf16[3,720,256]{2,1,0:T(8,128)(2,1)S(1)}, u32[]{:S(2)}, u32[]{:S(2)}) collective-permute-start(bf16[3,720,256]{2,1,0:T(8,128)(2,1)} %slice.36), channel_id=1, source_target_pairs={{0,1},{1,0},{2,3},{3,2},{4,5},{5,4},{6,7},{7,6},{8,9},{9,8},{10,11... | collective-permute-start | bytes 3317768 | tf_op jit(solution)/shard_map/ppermute | solution.py:445
  381.9 58.0 %all-to-all-start.5 = ((bf16[32,3,3,8,512]{4,3,2,1,0:T(8,128)(2,1)}), bf16[32,3,3,8,512]{4,3,2,1,0:T(8,128)(2,1)S(1)}, u32[]{:S(2)}, u32[]{:S(2)}) async-start(bf16[32,3,3,8,512]{4,3,2,1,0:T(8,128)(2,1)} %get-tuple-element.75), calls=%async_computation.5 | async-start | bytes 4718592 | tf_op jit(solution)/shard_map/all_to_all | solution.py:429
  389.4 29.9 %collective-permute-start.8 = (bf16[1,720,256]{2,1,0:T(8,128)(2,1)}, bf16[1,720,256]{2,1,0:T(8,128)(2,1)S(1)}, u32[]{:S(2)}, u32[]{:S(2)}) collective-permute-start(bf16[1,720,256]{2,1,0:T(8,128)(2,1)} %slice.37), channel_id=1, source_target_pairs={{0,1},{1,0},{2,3},{3,2},{4,5},{5,4},{6,7},{7,6},{8,9},{9,8},{10,11... | collective-permute-start | bytes 1105928 | tf_op jit(solution)/shard_map/ppermute | solution.py:445
  421.5 22.1 %collective-permute-start.9 = (bf16[2,720,256]{2,1,0:T(8,128)(2,1)}, bf16[2,720,256]{2,1,0:T(8,128)(2,1)}, u32[]{:S(2)}, u32[]{:S(2)}) collective-permute-start(bf16[2,720,256]{2,1,0:T(8,128)(2,1)} %slice.38), channel_id=1, source_target_pairs={{0,1},{1,0},{2,3},{3,2},{4,5},{5,4},{6,7},{7,6},{8,9},{9,8},{10,11... | collective-permute-start | bytes 2211848 | tf_op jit(solution)/shard_map/ppermute | solution.py:445
  439.9 11.9 %copy-start.1 = (bf16[32,3,3,8,512]{4,3,2,1,0:T(8,128)(2,1)}, bf16[32,3,3,8,512]{4,3,2,1,0:T(8,128)(2,1)S(1)}, u32[]{:S(2)}) copy-start(bf16[32,3,3,8,512]{4,3,2,1,0:T(8,128)(2,1)S(1)} %all-to-all-done.5.rest_0_) | copy-start | bytes 7077892
  443.6 40.3 %all-to-all-start.6 = ((bf16[32,3,2,8,512]{4,3,2,1,0:T(8,128)(2,1)}), bf16[32,3,2,8,512]{4,3,2,1,0:T(8,128)(2,1)}, u32[]{:S(2)}, u32[]{:S(2)}) async-start(bf16[32,3,2,8,512]{4,3,2,1,0:T(8,128)(2,1)} %get-tuple-element.82), calls=%async_computation.6 | async-start | bytes 3145728 | tf_op jit(solution)/shard_map/all_to_all | solution.py:429
  450.3 23.2 %collective-permute-start.10 = (bf16[1,720,256]{2,1,0:T(8,128)(2,1)}, bf16[1,720,256]{2,1,0:T(8,128)(2,1)S(1)}, u32[]{:S(2)}, u32[]{:S(2)}) collective-permute-start(bf16[1,720,256]{2,1,0:T(8,128)(2,1)} %slice.39), channel_id=1, source_target_pairs={{0,1},{1,0},{2,3},{3,2},{4,5},{5,4},{6,7},{7,6},{8,9},{9,8},{10,11... | collective-permute-start | bytes 1105928 | tf_op jit(solution)/shard_map/ppermute | solution.py:445
  474.3 28.7 %collective-permute-start.11 = (bf16[3,720,256]{2,1,0:T(8,128)(2,1)}, bf16[3,720,256]{2,1,0:T(8,128)(2,1)S(1)}, u32[]{:S(2)}, u32[]{:S(2)}) collective-permute-start(bf16[3,720,256]{2,1,0:T(8,128)(2,1)} %get-tuple-element.91), channel_id=1, source_target_pairs={{0,1},{1,0},{2,3},{3,2},{4,5},{5,4},{6,7},{7,6},{8,9},{9,8},{10,11... | collective-permute-start | bytes 3317768 | tf_op jit(solution)/shard_map/ppermute | solution.py:445
  484.0 10.6 %copy-start.7 = (bf16[1,720,256]{2,1,0:T(8,128)(2,1)S(1)}, bf16[1,720,256]{2,1,0:T(8,128)(2,1)}, u32[]{:S(2)}) copy-start(bf16[1,720,256]{2,1,0:T(8,128)(2,1)} %copy-done.6) | copy-start | bytes 1105924
  492.0 26.4 %collective-permute-start.12 = (bf16[2,720,256]{2,1,0:T(8,128)(2,1)}, bf16[2,720,256]{2,1,0:T(8,128)(2,1)S(1)}, u32[]{:S(2)}, u32[]{:S(2)}) collective-permute-start(bf16[2,720,256]{2,1,0:T(8,128)(2,1)} %get-tuple-element.92), channel_id=1, source_target_pairs={{0,1},{1,0},{2,3},{3,2},{4,5},{5,4},{6,7},{7,6},{8,9},{9,8},{10,11... | collective-permute-start | bytes 2211848 | tf_op jit(solution)/shard_map/ppermute | solution.py:445
  (9 other events, 32.6 us)

commit v9 on v8

--- a/solution.py
+++ b/solution.py
@@ -50,7 +50,7 @@
     rows = table.shape[0]
     slots = 2 * STEP
     blocks = rows // places // slots
-    few = 4
+    few = 8
     return pl.pallas_call(
         functools.partial(forward_kernel, 1.0 / nlon),
         out_shape=jax.ShapeDtypeStruct((places, blocks, cycles, slots, width), BF),
@@ -307,22 +307,21 @@
     theirs_ref[0] = jnp.where(first, high, low).astype(BF)
 
 
-def tail_part(backs, tables, own, got, start, ln_gain, up_weight, down_weight, place, result, cycles):
-    count = backs[0].shape[2]
+def tail_part(backs, tables, own, got, start, low, count, ln_gain, up_weight, down_weight, place, result, cycles):
     channels = backs[0].shape[4]
     _, nlon, width = own.shape
     fixed = lambda t, at: (0, 0)
     row = (1, nlon, width)
     specs = [
-        pl.BlockSpec(row, lambda t, at: (start + t, 0, 0)),
-        pl.BlockSpec(row, lambda t, at: (t, 0, 0)),
+        pl.BlockSpec(row, lambda t, at: (start + low + t, 0, 0)),
+        pl.BlockSpec(row, lambda t, at: (low + t, 0, 0)),
         pl.BlockSpec(ln_gain.shape, fixed),
         pl.BlockSpec(up_weight.shape, fixed),
         pl.BlockSpec(down_weight.shape, fixed),
     ]
     for back in backs:
         block = back.shape[:2] + (1,) + back.shape[3:]
-        specs.append(pl.BlockSpec(block, lambda t, at: (0, 0, t, 0, 0)))
+        specs.append(pl.BlockSpec(block, lambda t, at: (0, 0, low + t, 0, 0)))
     specs += [pl.BlockSpec(table.shape, fixed) for table in tables]
     arguments = [own, got, ln_gain, up_weight, down_weight, *backs, *tables]
     aliases = {}
@@ -341,7 +340,7 @@
             grid=(count,),
             in_specs=specs,
             out_specs=[
-                pl.BlockSpec(row, lambda t, at: (at[0] + start + t, 0, 0)),
+                pl.BlockSpec(row, lambda t, at: (at[0] + start + low + t, 0, 0)),
                 pl.BlockSpec(row, lambda t, at: (t, 0, 0)),
             ],
         ),
@@ -433,17 +432,18 @@
     sent = []
 
     def finished(at, backs, tables, result):
-        early = at < 2
-        result, theirs = tail_part(
-            backs, tables, own, got[at], sum(counts[:at]), ln_gain[None, :], up_weight,
-            down_weight, place, result, cycles,
-        )
-        if sent and at < 3:
-            theirs, sent[-1] = lax.optimization_barrier((theirs, sent[-1]))
-        cut = max(theirs.shape[0] - 1, 1) if early else theirs.shape[0]
-        pieces = [theirs[:cut], theirs[cut:]] if cut < theirs.shape[0] else [theirs]
-        sent.extend(lax.ppermute(piece, "chan", SWAP) for piece in pieces)
-        return (result, sent[-len(pieces)])
+        pieces = [counts[at]]
+        low = 0
+        needed = []
+        for count in pieces:
+            result, theirs = tail_part(
+                backs, tables, own, got[at], sum(counts[:at]), low, count, ln_gain[None, :],
+                up_weight, down_weight, place, result, cycles,
+            )
+            sent.append(lax.ppermute(theirs, "chan", SWAP))
+            needed.append(theirs if low else sent[-1])
+            low += count
+        return (result, needed)
 
     begin, end = heads[-2:]
     begin, _, got[2] = lax.optimization_barrier((begin, gathered[1], got[2]))
@@ -462,7 +462,7 @@
             value, last = lax.optimization_barrier((value, last))
             backs[-1] = [last]
         if at > 0:
-            value, _ = lax.optimization_barrier((value, tied))
+            value, *_ = lax.optimization_barrier((value, *tied))
         last = shuffled(value)
         result, tied = finished(at, backs[-1], tables[at], result)
         backs.append([last])

time: 522 us -> 519 us (level)
  local copies, waits for them, and re-layouts: 26.3 us -> 17.5 us
  waiting for transfers between devices: 253 us -> 259 us
    all_to_all x4, waiting for transfers between devices: 71.2 us -> 111 us  [shuffled(): return lax.all_to_all(value, ('lat', 'chan'), 0, 0, tiled=True)]
    ppermute x6 -> x4, waiting for transfers between devices: 53 us -> 18.5 us  [finished(): sent.append(lax.ppermute(theirs, 'chan', SWAP))]
    slice x4 -> x0, local copies, waits for them, and re-layouts: 8.05 us -> none  [finished(): pieces = [theirs[:cut], theirs[cut:]] if cut < theirs.shape[0] else [theirs]]
  transfers between devices with their start and end apart: 19 -> 17, of which waited for: 13 -> 10; matrix products, arithmetic and copies ran while one was open for 5% -> 4% of each run, Pallas kernels for 29% -> 29%
where the time goes in v9:
time: 519 us; the launch traced here: 515 us
  waiting for transfers between devices  259 us (50%)
  Pallas kernels  151 us (29%)
  starting transfers between devices  52.7 us (10%)
  blocking collectives  29.9 us (6%)
  local copies, waits for them, and re-layouts  17.5 us (3%)
    all_to_all x4, waiting for transfers between devices, shuffled(): return lax.all_to_all(value, ('lat', 'chan'), 0, 0, tiled=True)  111 us
    ppermute x4, waiting for transfers between devices, exchanged(): got.append(lax.ppermute(piece, 'chan', SWAP))  75.8 us
    pallas_call x2, Pallas kernels, local_part(): pl.pallas_call(local_rows, out_shape=jax.ShapeDtypeStruct((span, nlon, wi...  47.9 us
    pallas_call x3, Pallas kernels, middle_part(): pl.pallas_call(functools.partial(middle_kernel, plan), out_shape=[jax.Sha...  46.2 us
    pallas_call x4, Pallas kernels, tail_part(): pl.pallas_call(functools.partial(tail_kernel, len(backs)), out_shape=[jax...  40.1 us
    ppermute x1, waiting for transfers between devices, fast(): other = lax.ppermute(mix_weight, 'chan', SWAP)  38.1 us
    all_to_all x1, blocking collectives, shuffled(): return lax.all_to_all(value, ('lat', 'chan'), 0, 0, tiled=True)  29.9 us
    all_to_all x4, starting transfers between devices, shuffled(): return lax.all_to_all(value, ('lat', 'chan'), 0, 0, tiled=True)  22.4 us
  transfers between devices with their start and end apart: 17, of which 10 were waited for; matrix products, arithmetic and copies ran while one was open for 4% of the time, Pallas kernels for 29%

profile of v9, /device:TPU:26, one launch (start us, length us, event | category | flops | bytes accessed | tf_op | source)
XLA Modules:
  0.0 515.0 jit_solution(5958923021939323379)
XLA Ops:
  6.7 9.6 %shard_map.146 = bf16[32,2,24,8,256]{4,3,2,1,0:T(8,128)(2,1)} custom-call(bf16[512,720]{1,0:T(8,128)(2,1)} %constant.66.clone.table_ref, bf16[24,720,256]{2,1,0:T(8,128)(2,1)} %after_ref.3), custom_call_target="tpu_custom_call" | custom-call | flops 4529848320 | bytes 8847360 | tf_op jit(solution)/shard_map/pallas_call | solution.py:54
  25.5 23.9 %shard_map.148 = bf16[12,720,256]{2,1,0:T(8,128)(2,1)} custom-call(s32[2]{0:T(128)} %pad_add_fusion.base_ref, f32[24,3]{1,0:T(8,128)} %sine_divide_fusion.ratio_ref, f32[3,7,256]{2,1,0:T(8,128)} %select_reduce_fusion.weight_ref, bf16[24,720,256]{2,1,0:T(8,128)(2,1)} %after_ref.3, bf16[24,720,256]{2,1,0:T(8,128)(2,1)} %after_ref.3, ...), custom_call_target="tpu_custom_call" | custom-call | flops 884736000 | bytes 13271040 | tf_op jit(solution)/shard_map/pallas_call | solution.py:251
  56.7 7.5 %shard_map.145 = bf16[32,1,24,8,256]{4,3,2,1,0:T(8,128)(2,1)} custom-call(bf16[256,720]{1,0:T(8,128)(2,1)} %constant.67.clone.table_ref, bf16[24,720,256]{2,1,0:T(8,128)(2,1)} %after_ref.3), custom_call_target="tpu_custom_call" | custom-call | flops 2264924160 | bytes 8847360 | tf_op jit(solution)/shard_map/pallas_call | solution.py:54
  64.2 23.9 %shard_map.147.own_ref = bf16[12,720,256]{2,1,0:T(8,128)(2,1)} custom-call(s32[2]{0:T(128)} %pad_add_fusion.1.base_ref, f32[24,3]{1,0:T(8,128)} %sine_divide_fusion.ratio_ref, f32[3,7,256]{2,1,0:T(8,128)} %select_reduce_fusion.weight_ref, bf16[24,720,256]{2,1,0:T(8,128)(2,1)} %after_ref.3, bf16[24,720,256]{2,1,0:T(8,128)(2,1)} %after_ref.3, ...), custom_call_target="tpu_custom_call" | custom-call | flops 884736000 | bytes 13271040 | tf_op jit(solution)/shard_map/pallas_call | solution.py:251
  88.1 56.0 %collective-permute-done.3.got_ref = bf16[3,720,256]{2,1,0:T(8,128)(2,1)S(1)} collective-permute-done((bf16[3,720,256]{2,1,0:T(8,128)(2,1)}, bf16[3,720,256]{2,1,0:T(8,128)(2,1)S(1)}, u32[]{:S(2)}, u32[]{:S(2)}) %collective-permute-start.3) | collective-permute-done | bytes 1105952 | tf_op jit(solution)/shard_map/ppermute | solution.py:278
  144.1 15.6 %all-to-all-done.1 = bf16[32,2,24,8,256]{4,3,2,1,0:T(8,128)(2,1)} async-done(((bf16[32,2,24,8,256]{4,3,2,1,0:T(8,128)(2,1)}), bf16[32,2,24,8,256]{4,3,2,1,0:T(8,128)(2,1)}, u32[]{:S(2)}, u32[]{:S(2)}) %all-to-all-start.1) | async-done | bytes 6291488 | tf_op jit(solution)/shard_map/all_to_all | solution.py:405
  159.7 7.2 %all-to-all-start = ((bf16[32,1,24,8,256]{4,3,2,1,0:T(8,128)(2,1)}), bf16[32,1,24,8,256]{4,3,2,1,0:T(8,128)(2,1)S(1)}, u32[]{:S(2)}, u32[]{:S(2)}) async-start(bf16[32,1,24,8,256]{4,3,2,1,0:T(8,128)(2,1)} %shard_map.145), calls=%async_computation | async-start | bytes 6291456 | tf_op jit(solution)/shard_map/all_to_all | solution.py:405
  171.1 38.1 %collective-permute-done.4.other_ref = bf16[2,512,256]{2,1,0:T(8,128)(2,1)} collective-permute-done((bf16[2,512,256]{2,1,0:T(8,128)(2,1)}, bf16[2,512,256]{2,1,0:T(8,128)(2,1)}, u32[]{:S(2)}, u32[]{:S(2)}) %collective-permute-start.4) | collective-permute-done | bytes 524320 | tf_op jit(solution)/shard_map/ppermute | solution.py:392
  209.2 15.3 %shard_map.149 = (bf16[32,2,4,8,512]{4,3,2,1,0:T(8,128)(2,1)}, bf16[32,3,3,8,512]{4,3,2,1,0:T(8,128)(2,1)}, bf16[32,3,3,8,512]{4,3,2,1,0:T(8,128)(2,1)}, bf16[32,3,2,8,512]{4,3,2,1,0:T(8,128)(2,1)}) custom-call(s32[2]{0:T(128)} %get-tuple-element.90.at_ref.place_ref, bf16[16,2,2,24,8,256]{5,4,3,2,1,0:T(8,128)(2,1)} %bitcast.6.spec_ref, ...), custom_call_target="tpu_custom_call" | custom-call | flops 5637144576 | bytes 9175040 | tf_op jit(solution)/shard_map/pallas_call | solution.py:152
  224.6 15.4 %shard_map.150 = (bf16[32,2,4,8,512]{4,3,2,1,0:T(8,128)(2,1)}, bf16[32,3,3,8,512]{4,3,2,1,0:T(8,128)(2,1)}, bf16[32,3,3,8,512]{4,3,2,1,0:T(8,128)(2,1)}, bf16[32,3,2,8,512]{4,3,2,1,0:T(8,128)(2,1)}) custom-call(s32[2]{0:T(128)} %get-tuple-element.89.at_ref, ...), custom_call_target="tpu_custom_call", output_to_operand_aliasing={{0}: (7, {}), {1}: (8, {}), {2}: (9, {}), {3}: (10, {})} | custom-call | flops 5637144576 | bytes 9175040 | tf_op jit(solution)/shard_map/pallas_call | solution.py:152
  249.1 15.4 %shard_map.151 = (bf16[32,1,4,8,512]{4,3,2,1,0:T(8,128)(2,1)}, bf16[32,3,3,8,512]{4,3,2,1,0:T(8,128)(2,1)}, bf16[32,3,3,8,512]{4,3,2,1,0:T(8,128)(2,1)}, bf16[32,3,2,8,512]{4,3,2,1,0:T(8,128)(2,1)}) custom-call(s32[2]{0:T(128)} %pad_add_fusion.2.at_ref, ...), custom_call_target="tpu_custom_call", output_to_operand_aliasing={{1}: (7, {}), {2}: (8, {}), {3}: (9, {})} | custom-call | flops 5637144576 | bytes 9175040 | tf_op jit(solution)/shard_map/pallas_call | solution.py:152
  264.5 19.8 %collective-permute-done.6.got_ref = bf16[2,720,256]{2,1,0:T(8,128)(2,1)} collective-permute-done((bf16[2,720,256]{2,1,0:T(8,128)(2,1)}, bf16[2,720,256]{2,1,0:T(8,128)(2,1)}, u32[]{:S(2)}, u32[]{:S(2)}) %collective-permute-start.6) | collective-permute-done | bytes 737312 | tf_op jit(solution)/shard_map/ppermute | solution.py:278
  284.4 7.3 %all-to-all-done.2.rest_0_ = bf16[32,2,4,8,512]{4,3,2,1,0:T(8,128)(2,1)} async-done(((bf16[32,2,4,8,512]{4,3,2,1,0:T(8,128)(2,1)}), bf16[32,2,4,8,512]{4,3,2,1,0:T(8,128)(2,1)}, u32[]{:S(2)}, u32[]{:S(2)}) %all-to-all-start.2) | async-done | bytes 2097184 | tf_op jit(solution)/shard_map/all_to_all | solution.py:428
  291.7 29.9 %all_to_all.35.rest_1_ = bf16[32,1,4,8,512]{4,3,2,1,0:T(8,128)(2,1)} all-to-all(bf16[32,1,4,8,512]{4,3,2,1,0:T(8,128)(2,1)} %get-tuple-element.64), channel_id=1, replica_groups=mesh['lat'=16,'chan'=2] {'lat','chan'}, dimensions={0} | all-to-all | bytes 2097152 | tf_op jit(solution)/shard_map/all_to_all | solution.py:428
  327.3 12.1 %shard_map.152 = (bf16[24,720,256]{2,1,0:T(8,128)(2,1)}, bf16[4,720,256]{2,1,0:T(8,128)(2,1)}) custom-call(s32[2]{0:T(128)} %get-tuple-element.90.at_ref.place_ref, bf16[12,720,256]{2,1,0:T(8,128)(2,1)} %shard_map.147.own_ref, bf16[4,720,256]{2,1,0:T(8,128)(2,1)} %collective-permute-done.2.got_ref, f32[1,512]{1,0:T(1,128)} %bitcast.9, ...), custom_call_target="tpu_custom_call" | custom-call | flops 5284823040 | bytes 11796480 | tf_op jit(solution)/shard_map/pallas_call | solution.py:332
  341.0 38.7 %all-to-all-done.4.rest_0_ = bf16[32,3,3,8,512]{4,3,2,1,0:T(8,128)(2,1)S(1)} async-done(((bf16[32,3,3,8,512]{4,3,2,1,0:T(8,128)(2,1)}), bf16[32,3,3,8,512]{4,3,2,1,0:T(8,128)(2,1)S(1)}, u32[]{:S(2)}, u32[]{:S(2)}) %all-to-all-start.4) | async-done | bytes 2359328 | tf_op jit(solution)/shard_map/all_to_all | solution.py:428
  379.7 7.2 %collective-permute-done.7 = bf16[4,720,256]{2,1,0:T(8,128)(2,1)} collective-permute-done((bf16[4,720,256]{2,1,0:T(8,128)(2,1)}, bf16[4,720,256]{2,1,0:T(8,128)(2,1)}, u32[]{:S(2)}, u32[]{:S(2)}) %collective-permute-start.7) | collective-permute-done | bytes 1474592 | tf_op jit(solution)/shard_map/ppermute | solution.py:443
  386.8 6.0 %all-to-all-start.5 = ((bf16[32,3,3,8,512]{4,3,2,1,0:T(8,128)(2,1)}), bf16[32,3,3,8,512]{4,3,2,1,0:T(8,128)(2,1)}, u32[]{:S(2)}, u32[]{:S(2)}) async-start(bf16[32,3,3,8,512]{4,3,2,1,0:T(8,128)(2,1)} %get-tuple-element.71), calls=%async_computation.5 | async-start | bytes 4718592 | tf_op jit(solution)/shard_map/all_to_all | solution.py:428
  392.8 10.0 %shard_map.153 = (bf16[24,720,256]{2,1,0:T(8,128)(2,1)}, bf16[3,720,256]{2,1,0:T(8,128)(2,1)}) custom-call(s32[2]{0:T(128)} %get-tuple-element.90.at_ref.place_ref, bf16[12,720,256]{2,1,0:T(8,128)(2,1)} %shard_map.147.own_ref, bf16[3,720,256]{2,1,0:T(8,128)(2,1)} %copy-done.5, f32[1,512]{1,0:T(1,128)} %bitcast.10, ...), custom_call_target="tpu_custom_call", output_to_operand_aliasing={{0}: (8, {})} | custom-call | flops 3963617280 | bytes 8847360 | tf_op jit(solution)/shard_map/pallas_call | solution.py:332
  404.4 40.8 %all-to-all-done.5.rest_0_ = bf16[32,3,3,8,512]{4,3,2,1,0:T(8,128)(2,1)} async-done(((bf16[32,3,3,8,512]{4,3,2,1,0:T(8,128)(2,1)}), bf16[32,3,3,8,512]{4,3,2,1,0:T(8,128)(2,1)}, u32[]{:S(2)}, u32[]{:S(2)}) %all-to-all-start.5) | async-done | bytes 2359328 | tf_op jit(solution)/shard_map/all_to_all | solution.py:428
  450.9 10.0 %shard_map.154 = (bf16[24,720,256]{2,1,0:T(8,128)(2,1)}, bf16[3,720,256]{2,1,0:T(8,128)(2,1)}) custom-call(s32[2]{0:T(128)} %get-tuple-element.90.at_ref.place_ref, bf16[12,720,256]{2,1,0:T(8,128)(2,1)} %shard_map.147.own_ref, bf16[3,720,256]{2,1,0:T(8,128)(2,1)} %collective-permute-done.5.got_ref, ...), custom_call_target="tpu_custom_call", output_to_operand_aliasing={{0}: (8, {})} | custom-call | flops 3963617280 | bytes 8847360 | tf_op jit(solution)/shard_map/pallas_call | solution.py:332
  462.4 23.8 %all-to-all-done.6.rest_0_ = bf16[32,3,2,8,512]{4,3,2,1,0:T(8,128)(2,1)S(1)} async-done(((bf16[32,3,2,8,512]{4,3,2,1,0:T(8,128)(2,1)}), bf16[32,3,2,8,512]{4,3,2,1,0:T(8,128)(2,1)S(1)}, u32[]{:S(2)}, u32[]{:S(2)}) %all-to-all-start.6) | async-done | bytes 1572896 | tf_op jit(solution)/shard_map/all_to_all | solution.py:428
  487.4 7.9 %shard_map.155 = (bf16[24,720,256]{2,1,0:T(8,128)(2,1)}, bf16[2,720,256]{2,1,0:T(8,128)(2,1)}) custom-call(s32[2]{0:T(128)} %get-tuple-element.90.at_ref.place_ref, bf16[12,720,256]{2,1,0:T(8,128)(2,1)} %shard_map.147.own_ref, bf16[2,720,256]{2,1,0:T(8,128)(2,1)} %collective-permute-done.6.got_ref, ...), custom_call_target="tpu_custom_call", output_to_operand_aliasing={{0}: (8, {})} | custom-call | flops 2642411520 | bytes 5898240 | tf_op jit(solution)/shard_map/pallas_call | solution.py:332
  502.7 11.4 %collective-permute-done.10 = bf16[2,720,256]{2,1,0:T(8,128)(2,1)S(1)} collective-permute-done((bf16[2,720,256]{2,1,0:T(8,128)(2,1)}, bf16[2,720,256]{2,1,0:T(8,128)(2,1)S(1)}, u32[]{:S(2)}, u32[]{:S(2)}) %collective-permute-start.10) | collective-permute-done | bytes 737312 | tf_op jit(solution)/shard_map/ppermute | solution.py:443
  (65 shorter events, 62.0 us)
Async XLA Ops:
  1.1 15.1 %collective-permute-start = (bf16[1,720,256]{2,1,0:T(8,128)(2,1)S(1)}, bf16[1,720,256]{2,1,0:T(8,128)(2,1)S(1)}, u32[]{:S(2)}, u32[]{:S(2)}) collective-permute-start(bf16[1,720,256]{2,1,0:T(8,128)(2,1)S(1)} %get-tuple-element.86), channel_id=1, source_target_pairs={{0,2},{2,4},{4,6},{6,8},{8,10},{10,12},{12,14},{14,16},{16,18},{18... | collective-permute-start | bytes 1105928 | tf_op jit(solution)/shard_map/ppermute | solution.py:382
  3.1 13.2 %collective-permute-start.1 = (bf16[1,720,256]{2,1,0:T(8,128)(2,1)S(1)}, bf16[1,720,256]{2,1,0:T(8,128)(2,1)S(1)}, u32[]{:S(2)}, u32[]{:S(2)}) collective-permute-start(bf16[1,720,256]{2,1,0:T(8,128)(2,1)S(1)} %get-tuple-element.85), channel_id=1, source_target_pairs={{2,0},{4,2},{6,4},{8,6},{10,8},{12,10},{14,12},{16,14},{18,16},{20... | collective-permute-start | bytes 1105928 | tf_op jit(solution)/shard_map/ppermute | solution.py:383
  16.3 7.5 %copy-start.9 = (s32[9]{0:T(128)S(1)}, s32[9]{0:T(128)}, u32[]{:S(2)}) copy-start(s32[9]{0:T(128)} %param.20) | copy-start | bytes 112
  16.3 7.6 %copy-start.8 = (s32[9]{0:T(128)S(1)}, s32[9]{0:T(128)}, u32[]{:S(2)}) copy-start(s32[9]{0:T(128)} %param.21) | copy-start | bytes 112
  16.3 7.8 %copy-start.6 = (f32[9,256]{1,0:T(8,128)S(1)}, f32[9,256]{1,0:T(8,128)}, u32[]{:S(2)}) copy-start(f32[9,256]{1,0:T(8,128)} %param.19) | copy-start | bytes 27652
  17.2 142.5 %all-to-all-start.1 = ((bf16[32,2,24,8,256]{4,3,2,1,0:T(8,128)(2,1)}), bf16[32,2,24,8,256]{4,3,2,1,0:T(8,128)(2,1)}, u32[]{:S(2)}, u32[]{:S(2)}) async-start(bf16[32,2,24,8,256]{4,3,2,1,0:T(8,128)(2,1)} %shard_map.146), calls=%async_computation.1 | async-start | bytes 12582912 | tf_op jit(solution)/shard_map/all_to_all | solution.py:405
  50.9 93.2 %collective-permute-start.2 = (bf16[4,720,256]{2,1,0:T(8,128)(2,1)S(1)}, bf16[4,720,256]{2,1,0:T(8,128)(2,1)}, u32[]{:S(2)}, u32[]{:S(2)}) collective-permute-start(bf16[4,720,256]{2,1,0:T(8,128)(2,1)S(1)} %slice.24), channel_id=1, source_target_pairs={{0,1},{1,0},{2,3},{3,2},{4,5},{5,4},{6,7},{7,6},{8,9},{9,8},{10,11... | collective-permute-start | bytes 4423688 | tf_op jit(solution)/shard_map/ppermute | solution.py:278
  55.6 88.5 %collective-permute-start.3 = (bf16[3,720,256]{2,1,0:T(8,128)(2,1)}, bf16[3,720,256]{2,1,0:T(8,128)(2,1)S(1)}, u32[]{:S(2)}, u32[]{:S(2)}) collective-permute-start(bf16[3,720,256]{2,1,0:T(8,128)(2,1)} %get-tuple-element.88), channel_id=1, source_target_pairs={{0,1},{1,0},{2,3},{3,2},{4,5},{5,4},{6,7},{7,6},{8,9},{9,8},{10,11... | collective-permute-start | bytes 3317768 | tf_op jit(solution)/shard_map/ppermute | solution.py:278
  88.1 82.2 %copy-start.7 = (f32[384]{0:T(512)S(1)}, f32[384]{0:T(512)}, u32[]{:S(2)}) copy-start(f32[384]{0:T(512)} %param.18) | copy-start | bytes 4612
  144.1 15.6 %copy-start.5 = (bf16[3,720,256]{2,1,0:T(8,128)(2,1)}, bf16[3,720,256]{2,1,0:T(8,128)(2,1)S(1)}, u32[]{:S(2)}) copy-start(bf16[3,720,256]{2,1,0:T(8,128)(2,1)S(1)} %collective-permute-done.3.got_ref) | copy-start | bytes 3317764
  159.7 80.3 %all-to-all-start = ((bf16[32,1,24,8,256]{4,3,2,1,0:T(8,128)(2,1)}), bf16[32,1,24,8,256]{4,3,2,1,0:T(8,128)(2,1)S(1)}, u32[]{:S(2)}, u32[]{:S(2)}) async-start(bf16[32,1,24,8,256]{4,3,2,1,0:T(8,128)(2,1)} %shard_map.145), calls=%async_computation | async-start | bytes 6291456 | tf_op jit(solution)/shard_map/all_to_all | solution.py:405
  166.9 42.3 %collective-permute-start.4 = (bf16[2,512,256]{2,1,0:T(8,128)(2,1)}, bf16[2,512,256]{2,1,0:T(8,128)(2,1)}, u32[]{:S(2)}, u32[]{:S(2)}) collective-permute-start(bf16[2,512,256]{2,1,0:T(8,128)(2,1)} %own_ref.5), channel_id=1, source_target_pairs={{0,1},{1,0},{2,3},{3,2},{4,5},{5,4},{6,7},{7,6},{8,9},{9,8},{10,11... | collective-permute-start | bytes 1572872 | tf_op jit(solution)/shard_map/ppermute | solution.py:392
  169.1 70.9 %collective-permute-start.5 = (bf16[3,720,256]{2,1,0:T(8,128)(2,1)}, bf16[3,720,256]{2,1,0:T(8,128)(2,1)}, u32[]{:S(2)}, u32[]{:S(2)}) collective-permute-start(bf16[3,720,256]{2,1,0:T(8,128)(2,1)} %get-tuple-element.87), channel_id=1, source_target_pairs={{0,1},{1,0},{2,3},{3,2},{4,5},{5,4},{6,7},{7,6},{8,9},{9,8},{10,11... | collective-permute-start | bytes 3317768 | tf_op jit(solution)/shard_map/ppermute | solution.py:278
  240.0 7.0 %copy-start = (bf16[32,1,24,8,256]{4,3,2,1,0:T(8,128)(2,1)}, bf16[32,1,24,8,256]{4,3,2,1,0:T(8,128)(2,1)S(1)}, u32[]{:S(2)}) copy-start(bf16[32,1,24,8,256]{4,3,2,1,0:T(8,128)(2,1)S(1)} %all-to-all-done) | copy-start | bytes 9437188
  240.0 51.7 %all-to-all-start.2 = ((bf16[32,2,4,8,512]{4,3,2,1,0:T(8,128)(2,1)}), bf16[32,2,4,8,512]{4,3,2,1,0:T(8,128)(2,1)}, u32[]{:S(2)}, u32[]{:S(2)}) async-start(bf16[32,2,4,8,512]{4,3,2,1,0:T(8,128)(2,1)} %get-tuple-element.59), calls=%async_computation.2 | async-start | bytes 4194304 | tf_op jit(solution)/shard_map/all_to_all | solution.py:428
  247.0 37.4 %collective-permute-start.6 = (bf16[2,720,256]{2,1,0:T(8,128)(2,1)}, bf16[2,720,256]{2,1,0:T(8,128)(2,1)}, u32[]{:S(2)}, u32[]{:S(2)}) collective-permute-start(bf16[2,720,256]{2,1,0:T(8,128)(2,1)} %slice.27), channel_id=1, source_target_pairs={{0,1},{1,0},{2,3},{3,2},{4,5},{5,4},{6,7},{7,6},{8,9},{9,8},{10,11... | collective-permute-start | bytes 2211848 | tf_op jit(solution)/shard_map/ppermute | solution.py:278
  321.6 58.1 %all-to-all-start.4 = ((bf16[32,3,3,8,512]{4,3,2,1,0:T(8,128)(2,1)}), bf16[32,3,3,8,512]{4,3,2,1,0:T(8,128)(2,1)S(1)}, u32[]{:S(2)}, u32[]{:S(2)}) async-start(bf16[32,3,3,8,512]{4,3,2,1,0:T(8,128)(2,1)} %get-tuple-element.65), calls=%async_computation.4 | async-start | bytes 4718592 | tf_op jit(solution)/shard_map/all_to_all | solution.py:428
  339.5 47.3 %collective-permute-start.7 = (bf16[4,720,256]{2,1,0:T(8,128)(2,1)}, bf16[4,720,256]{2,1,0:T(8,128)(2,1)}, u32[]{:S(2)}, u32[]{:S(2)}) collective-permute-start(bf16[4,720,256]{2,1,0:T(8,128)(2,1)} %get-tuple-element.70), channel_id=1, source_target_pairs={{0,1},{1,0},{2,3},{3,2},{4,5},{5,4},{6,7},{7,6},{8,9},{9,8},{10,11... | collective-permute-start | bytes 4423688 | tf_op jit(solution)/shard_map/ppermute | solution.py:443
  379.7 7.2 %copy-start.1 = (bf16[32,3,3,8,512]{4,3,2,1,0:T(8,128)(2,1)}, bf16[32,3,3,8,512]{4,3,2,1,0:T(8,128)(2,1)S(1)}, u32[]{:S(2)}) copy-start(bf16[32,3,3,8,512]{4,3,2,1,0:T(8,128)(2,1)S(1)} %all-to-all-done.4.rest_0_) | copy-start | bytes 7077892
  386.8 58.4 %all-to-all-start.5 = ((bf16[32,3,3,8,512]{4,3,2,1,0:T(8,128)(2,1)}), bf16[32,3,3,8,512]{4,3,2,1,0:T(8,128)(2,1)}, u32[]{:S(2)}, u32[]{:S(2)}) async-start(bf16[32,3,3,8,512]{4,3,2,1,0:T(8,128)(2,1)} %get-tuple-element.71), calls=%async_computation.5 | async-start | bytes 4718592 | tf_op jit(solution)/shard_map/all_to_all | solution.py:428
  402.9 42.4 %collective-permute-start.8 = (bf16[3,720,256]{2,1,0:T(8,128)(2,1)}, bf16[3,720,256]{2,1,0:T(8,128)(2,1)S(1)}, u32[]{:S(2)}, u32[]{:S(2)}) collective-permute-start(bf16[3,720,256]{2,1,0:T(8,128)(2,1)} %get-tuple-element.76), channel_id=1, source_target_pairs={{0,1},{1,0},{2,3},{3,2},{4,5},{5,4},{6,7},{7,6},{8,9},{9,8},{10,11... | collective-permute-start | bytes 3317768 | tf_op jit(solution)/shard_map/ppermute | solution.py:443
  445.2 41.0 %all-to-all-start.6 = ((bf16[32,3,2,8,512]{4,3,2,1,0:T(8,128)(2,1)}), bf16[32,3,2,8,512]{4,3,2,1,0:T(8,128)(2,1)S(1)}, u32[]{:S(2)}, u32[]{:S(2)}) async-start(bf16[32,3,2,8,512]{4,3,2,1,0:T(8,128)(2,1)} %get-tuple-element.77), calls=%async_computation.6 | async-start | bytes 3145728 | tf_op jit(solution)/shard_map/all_to_all | solution.py:428
  460.9 39.5 %collective-permute-start.9 = (bf16[3,720,256]{2,1,0:T(8,128)(2,1)}, bf16[3,720,256]{2,1,0:T(8,128)(2,1)}, u32[]{:S(2)}, u32[]{:S(2)}) collective-permute-start(bf16[3,720,256]{2,1,0:T(8,128)(2,1)} %get-tuple-element.83), channel_id=1, source_target_pairs={{0,1},{1,0},{2,3},{3,2},{4,5},{5,4},{6,7},{7,6},{8,9},{9,8},{10,11... | collective-permute-start | bytes 3317768 | tf_op jit(solution)/shard_map/ppermute | solution.py:443
  495.3 18.8 %collective-permute-start.10 = (bf16[2,720,256]{2,1,0:T(8,128)(2,1)}, bf16[2,720,256]{2,1,0:T(8,128)(2,1)S(1)}, u32[]{:S(2)}, u32[]{:S(2)}) collective-permute-start(bf16[2,720,256]{2,1,0:T(8,128)(2,1)} %get-tuple-element.84), channel_id=1, source_target_pairs={{0,1},{1,0},{2,3},{3,2},{4,5},{5,4},{6,7},{7,6},{8,9},{9,8},{10,11... | collective-permute-start | bytes 2211848 | tf_op jit(solution)/shard_map/ppermute | solution.py:443
  (3 other events, 2.9 us)

commit v10 on v9

--- a/solution.py
+++ b/solution.py
@@ -401,7 +401,9 @@
             got = exchanged(asked, counts)
         else:
             own = local_part(grid, before, after, ratio, weight, side * span, span)
-            spec, own, got[0], got[1] = lax.optimization_barrier((spec, own, got[0], got[1]))
+            spec, own, other, got[0], got[1] = lax.optimization_barrier(
+                (spec, own, other, got[0], got[1])
+            )
         spec = lax.all_to_all(spec, ("lat", "chan"), 0, 0, tiled=True)
         gathered.append(spec.reshape((groups, sides) + spec.shape[1:]))
 

time: 519 us -> 515 us (level)
    ppermute x4, waiting for transfers between devices: 75.8 us -> 43.5 us  [exchanged(): got.append(lax.ppermute(piece, 'chan', SWAP))]
    ppermute x1, waiting for transfers between devices: 38.1 us -> 70 us  [fast(): other = lax.ppermute(mix_weight, 'chan', SWAP)]
  transfers between devices with their start and end apart: 17 -> 17, of which waited for: 10 -> 11; matrix products, arithmetic and copies ran while one was open for 4% -> 4% of each run, Pallas kernels for 29% -> 30%
where the time goes in v10:
time: 515 us; the launch traced here: 511 us
  waiting for transfers between devices  254 us (49%)
  Pallas kernels  151 us (29%)
  starting transfers between devices  53.1 us (10%)
  blocking collectives  29.9 us (6%)
  local copies, waits for them, and re-layouts  18.1 us (4%)
    all_to_all x4, waiting for transfers between devices, shuffled(): return lax.all_to_all(value, ('lat', 'chan'), 0, 0, tiled=True)  111 us
    ppermute x1, waiting for transfers between devices, fast(): other = lax.ppermute(mix_weight, 'chan', SWAP)  70 us
    pallas_call x2, Pallas kernels, local_part(): pl.pallas_call(local_rows, out_shape=jax.ShapeDtypeStruct((span, nlon, wi...  47.9 us
    pallas_call x3, Pallas kernels, middle_part(): pl.pallas_call(functools.partial(middle_kernel, plan), out_shape=[jax.Sha...  46.1 us
    ppermute x4, waiting for transfers between devices, exchanged(): got.append(lax.ppermute(piece, 'chan', SWAP))  43.5 us
    pallas_call x4, Pallas kernels, tail_part(): pl.pallas_call(functools.partial(tail_kernel, len(backs)), out_shape=[jax...  40.1 us
    all_to_all x1, blocking collectives, shuffled(): return lax.all_to_all(value, ('lat', 'chan'), 0, 0, tiled=True)  29.9 us
    all_to_all x4, starting transfers between devices, shuffled(): return lax.all_to_all(value, ('lat', 'chan'), 0, 0, tiled=True)  23.2 us
  transfers between devices with their start and end apart: 17, of which 11 were waited for; matrix products, arithmetic and copies ran while one was open for 4% of the time, Pallas kernels for 30%

profile of v10, /device:TPU:26, one launch (start us, length us, event | category | flops | bytes accessed | tf_op | source)
XLA Modules:
  0.0 511.3 jit_solution(1899759673127973636)
XLA Ops:
  5.5 9.6 %shard_map.146 = bf16[32,2,24,8,256]{4,3,2,1,0:T(8,128)(2,1)} custom-call(bf16[512,720]{1,0:T(8,128)(2,1)} %constant.66.clone.table_ref, bf16[24,720,256]{2,1,0:T(8,128)(2,1)} %after_ref.3), custom_call_target="tpu_custom_call" | custom-call | flops 4529848320 | bytes 8847360 | tf_op jit(solution)/shard_map/pallas_call | solution.py:54
  16.0 6.4 %all-to-all-start.1 = ((bf16[32,2,24,8,256]{4,3,2,1,0:T(8,128)(2,1)}), bf16[32,2,24,8,256]{4,3,2,1,0:T(8,128)(2,1)}, u32[]{:S(2)}, u32[]{:S(2)}) async-start(bf16[32,2,24,8,256]{4,3,2,1,0:T(8,128)(2,1)} %shard_map.146), calls=%async_computation.1 | async-start | bytes 12582912 | tf_op jit(solution)/shard_map/all_to_all | solution.py:407
  24.8 23.9 %shard_map.148 = bf16[12,720,256]{2,1,0:T(8,128)(2,1)} custom-call(s32[2]{0:T(128)} %pad_add_fusion.base_ref, f32[24,3]{1,0:T(8,128)} %sine_divide_fusion.ratio_ref, f32[3,7,256]{2,1,0:T(8,128)} %select_reduce_fusion.weight_ref, bf16[24,720,256]{2,1,0:T(8,128)(2,1)} %after_ref.3, bf16[24,720,256]{2,1,0:T(8,128)(2,1)} %after_ref.3, ...), custom_call_target="tpu_custom_call" | custom-call | flops 884736000 | bytes 13271040 | tf_op jit(solution)/shard_map/pallas_call | solution.py:251
  57.5 7.4 %shard_map.145 = bf16[32,1,24,8,256]{4,3,2,1,0:T(8,128)(2,1)} custom-call(bf16[256,720]{1,0:T(8,128)(2,1)} %constant.67.clone.table_ref, bf16[24,720,256]{2,1,0:T(8,128)(2,1)} %after_ref.3), custom_call_target="tpu_custom_call" | custom-call | flops 2264924160 | bytes 8847360 | tf_op jit(solution)/shard_map/pallas_call | solution.py:54
  64.9 23.9 %shard_map.147.own_ref = bf16[12,720,256]{2,1,0:T(8,128)(2,1)} custom-call(s32[2]{0:T(128)} %pad_add_fusion.1.base_ref, f32[24,3]{1,0:T(8,128)} %sine_divide_fusion.ratio_ref, f32[3,7,256]{2,1,0:T(8,128)} %select_reduce_fusion.weight_ref, bf16[24,720,256]{2,1,0:T(8,128)(2,1)} %after_ref.3, bf16[24,720,256]{2,1,0:T(8,128)(2,1)} %after_ref.3, ...), custom_call_target="tpu_custom_call" | custom-call | flops 884736000 | bytes 13271040 | tf_op jit(solution)/shard_map/pallas_call | solution.py:251
  88.8 70.0 %collective-permute-done.2.other_ref = bf16[2,512,256]{2,1,0:T(8,128)(2,1)S(1)} collective-permute-done((bf16[2,512,256]{2,1,0:T(8,128)(2,1)S(1)}, bf16[2,512,256]{2,1,0:T(8,128)(2,1)S(1)}, u32[]{:S(2)}, u32[]{:S(2)}) %collective-permute-start.2) | collective-permute-done | bytes 524320 | tf_op jit(solution)/shard_map/ppermute | solution.py:392
  159.6 6.5 %all-to-all-start = ((bf16[32,1,24,8,256]{4,3,2,1,0:T(8,128)(2,1)}), bf16[32,1,24,8,256]{4,3,2,1,0:T(8,128)(2,1)S(1)}, u32[]{:S(2)}, u32[]{:S(2)}) async-start(bf16[32,1,24,8,256]{4,3,2,1,0:T(8,128)(2,1)} %shard_map.145), calls=%async_computation | async-start | bytes 6291456 | tf_op jit(solution)/shard_map/all_to_all | solution.py:407
  169.7 15.4 %shard_map.149 = (bf16[32,2,4,8,512]{4,3,2,1,0:T(8,128)(2,1)}, bf16[32,3,3,8,512]{4,3,2,1,0:T(8,128)(2,1)}, bf16[32,3,3,8,512]{4,3,2,1,0:T(8,128)(2,1)}, bf16[32,3,2,8,512]{4,3,2,1,0:T(8,128)(2,1)}) custom-call(s32[2]{0:T(128)} %get-tuple-element.92.at_ref.place_ref, bf16[16,2,2,24,8,256]{5,4,3,2,1,0:T(8,128)(2,1)} %bitcast.6.spec_ref, ...), custom_call_target="tpu_custom_call" | custom-call | flops 5637144576 | bytes 9175040 | tf_op jit(solution)/shard_map/pallas_call | solution.py:152
  185.1 15.4 %shard_map.150 = (bf16[32,2,4,8,512]{4,3,2,1,0:T(8,128)(2,1)}, bf16[32,3,3,8,512]{4,3,2,1,0:T(8,128)(2,1)}, bf16[32,3,3,8,512]{4,3,2,1,0:T(8,128)(2,1)}, bf16[32,3,2,8,512]{4,3,2,1,0:T(8,128)(2,1)}) custom-call(s32[2]{0:T(128)} %get-tuple-element.91.at_ref, ...), custom_call_target="tpu_custom_call", output_to_operand_aliasing={{0}: (7, {}), {1}: (8, {}), {2}: (9, {}), {3}: (10, {})} | custom-call | flops 5637144576 | bytes 9175040 | tf_op jit(solution)/shard_map/pallas_call | solution.py:152
  200.5 23.6 %collective-permute-done.5.got_ref = bf16[3,720,256]{2,1,0:T(8,128)(2,1)} collective-permute-done((bf16[3,720,256]{2,1,0:T(8,128)(2,1)}, bf16[3,720,256]{2,1,0:T(8,128)(2,1)}, u32[]{:S(2)}, u32[]{:S(2)}) %collective-permute-start.5) | collective-permute-done | bytes 1105952 | tf_op jit(solution)/shard_map/ppermute | solution.py:278
  224.1 11.3 %all-to-all-done = bf16[32,1,24,8,256]{4,3,2,1,0:T(8,128)(2,1)S(1)} async-done(((bf16[32,1,24,8,256]{4,3,2,1,0:T(8,128)(2,1)}), bf16[32,1,24,8,256]{4,3,2,1,0:T(8,128)(2,1)S(1)}, u32[]{:S(2)}, u32[]{:S(2)}) %all-to-all-start) | async-done | bytes 3145760 | tf_op jit(solution)/shard_map/all_to_all | solution.py:407
  245.4 15.3 %shard_map.151 = (bf16[32,1,4,8,512]{4,3,2,1,0:T(8,128)(2,1)}, bf16[32,3,3,8,512]{4,3,2,1,0:T(8,128)(2,1)}, bf16[32,3,3,8,512]{4,3,2,1,0:T(8,128)(2,1)}, bf16[32,3,2,8,512]{4,3,2,1,0:T(8,128)(2,1)}) custom-call(s32[2]{0:T(128)} %pad_add_fusion.2.at_ref, ...), custom_call_target="tpu_custom_call", output_to_operand_aliasing={{1}: (7, {}), {2}: (8, {}), {3}: (9, {})} | custom-call | flops 5637144576 | bytes 9175040 | tf_op jit(solution)/shard_map/pallas_call | solution.py:152
  260.7 19.9 %collective-permute-done.6.got_ref = bf16[2,720,256]{2,1,0:T(8,128)(2,1)} collective-permute-done((bf16[2,720,256]{2,1,0:T(8,128)(2,1)}, bf16[2,720,256]{2,1,0:T(8,128)(2,1)}, u32[]{:S(2)}, u32[]{:S(2)}) %collective-permute-start.6) | collective-permute-done | bytes 737312 | tf_op jit(solution)/shard_map/ppermute | solution.py:278
  280.6 7.3 %all-to-all-done.2.rest_0_ = bf16[32,2,4,8,512]{4,3,2,1,0:T(8,128)(2,1)} async-done(((bf16[32,2,4,8,512]{4,3,2,1,0:T(8,128)(2,1)}), bf16[32,2,4,8,512]{4,3,2,1,0:T(8,128)(2,1)}, u32[]{:S(2)}, u32[]{:S(2)}) %all-to-all-start.2) | async-done | bytes 2097184 | tf_op jit(solution)/shard_map/all_to_all | solution.py:430
  287.9 29.9 %all_to_all.35.rest_1_ = bf16[32,1,4,8,512]{4,3,2,1,0:T(8,128)(2,1)} all-to-all(bf16[32,1,4,8,512]{4,3,2,1,0:T(8,128)(2,1)} %get-tuple-element.66), channel_id=1, replica_groups=mesh['lat'=16,'chan'=2] {'lat','chan'}, dimensions={0} | all-to-all | bytes 2097152 | tf_op jit(solution)/shard_map/all_to_all | solution.py:430
  323.6 12.1 %shard_map.152 = (bf16[24,720,256]{2,1,0:T(8,128)(2,1)}, bf16[4,720,256]{2,1,0:T(8,128)(2,1)}) custom-call(s32[2]{0:T(128)} %get-tuple-element.92.at_ref.place_ref, bf16[12,720,256]{2,1,0:T(8,128)(2,1)} %shard_map.147.own_ref, bf16[4,720,256]{2,1,0:T(8,128)(2,1)} %collective-permute-done.3.got_ref, f32[1,512]{1,0:T(1,128)} %bitcast.9, ...), custom_call_target="tpu_custom_call" | custom-call | flops 5284823040 | bytes 11796480 | tf_op jit(solution)/shard_map/pallas_call | solution.py:332
  337.3 38.7 %all-to-all-done.4.rest_0_ = bf16[32,3,3,8,512]{4,3,2,1,0:T(8,128)(2,1)S(1)} async-done(((bf16[32,3,3,8,512]{4,3,2,1,0:T(8,128)(2,1)}), bf16[32,3,3,8,512]{4,3,2,1,0:T(8,128)(2,1)S(1)}, u32[]{:S(2)}, u32[]{:S(2)}) %all-to-all-start.4) | async-done | bytes 2359328 | tf_op jit(solution)/shard_map/all_to_all | solution.py:430
  375.9 7.2 %collective-permute-done.7 = bf16[4,720,256]{2,1,0:T(8,128)(2,1)} collective-permute-done((bf16[4,720,256]{2,1,0:T(8,128)(2,1)}, bf16[4,720,256]{2,1,0:T(8,128)(2,1)}, u32[]{:S(2)}, u32[]{:S(2)}) %collective-permute-start.7) | collective-permute-done | bytes 1474592 | tf_op jit(solution)/shard_map/ppermute | solution.py:445
  389.1 10.0 %shard_map.153 = (bf16[24,720,256]{2,1,0:T(8,128)(2,1)}, bf16[3,720,256]{2,1,0:T(8,128)(2,1)}) custom-call(s32[2]{0:T(128)} %get-tuple-element.92.at_ref.place_ref, bf16[12,720,256]{2,1,0:T(8,128)(2,1)} %shard_map.147.own_ref, bf16[3,720,256]{2,1,0:T(8,128)(2,1)} %collective-permute-done.4.got_ref, ...), custom_call_target="tpu_custom_call", output_to_operand_aliasing={{0}: (8, {})} | custom-call | flops 3963617280 | bytes 8847360 | tf_op jit(solution)/shard_map/pallas_call | solution.py:332
  400.6 40.8 %all-to-all-done.5.rest_0_ = bf16[32,3,3,8,512]{4,3,2,1,0:T(8,128)(2,1)} async-done(((bf16[32,3,3,8,512]{4,3,2,1,0:T(8,128)(2,1)}), bf16[32,3,3,8,512]{4,3,2,1,0:T(8,128)(2,1)}, u32[]{:S(2)}, u32[]{:S(2)}) %all-to-all-start.5) | async-done | bytes 2359328 | tf_op jit(solution)/shard_map/all_to_all | solution.py:430
  447.2 10.0 %shard_map.154 = (bf16[24,720,256]{2,1,0:T(8,128)(2,1)}, bf16[3,720,256]{2,1,0:T(8,128)(2,1)}) custom-call(s32[2]{0:T(128)} %get-tuple-element.92.at_ref.place_ref, bf16[12,720,256]{2,1,0:T(8,128)(2,1)} %shard_map.147.own_ref, bf16[3,720,256]{2,1,0:T(8,128)(2,1)} %collective-permute-done.5.got_ref, ...), custom_call_target="tpu_custom_call", output_to_operand_aliasing={{0}: (8, {})} | custom-call | flops 3963617280 | bytes 8847360 | tf_op jit(solution)/shard_map/pallas_call | solution.py:332
  458.7 23.8 %all-to-all-done.6.rest_0_ = bf16[32,3,2,8,512]{4,3,2,1,0:T(8,128)(2,1)S(1)} async-done(((bf16[32,3,2,8,512]{4,3,2,1,0:T(8,128)(2,1)}), bf16[32,3,2,8,512]{4,3,2,1,0:T(8,128)(2,1)S(1)}, u32[]{:S(2)}, u32[]{:S(2)}) %all-to-all-start.6) | async-done | bytes 1572896 | tf_op jit(solution)/shard_map/all_to_all | solution.py:430
  483.7 7.9 %shard_map.155 = (bf16[24,720,256]{2,1,0:T(8,128)(2,1)}, bf16[2,720,256]{2,1,0:T(8,128)(2,1)}) custom-call(s32[2]{0:T(128)} %get-tuple-element.92.at_ref.place_ref, bf16[12,720,256]{2,1,0:T(8,128)(2,1)} %shard_map.147.own_ref, bf16[2,720,256]{2,1,0:T(8,128)(2,1)} %collective-permute-done.6.got_ref, ...), custom_call_target="tpu_custom_call", output_to_operand_aliasing={{0}: (8, {})} | custom-call | flops 2642411520 | bytes 5898240 | tf_op jit(solution)/shard_map/pallas_call | solution.py:332
  499.0 11.4 %collective-permute-done.10 = bf16[2,720,256]{2,1,0:T(8,128)(2,1)S(1)} collective-permute-done((bf16[2,720,256]{2,1,0:T(8,128)(2,1)}, bf16[2,720,256]{2,1,0:T(8,128)(2,1)S(1)}, u32[]{:S(2)}, u32[]{:S(2)}) %collective-permute-start.10) | collective-permute-done | bytes 737312 | tf_op jit(solution)/shard_map/ppermute | solution.py:445
  (67 shorter events, 63.2 us)
Async XLA Ops:
  1.1 13.9 %collective-permute-start.1 = (bf16[1,720,256]{2,1,0:T(8,128)(2,1)S(1)}, bf16[1,720,256]{2,1,0:T(8,128)(2,1)S(1)}, u32[]{:S(2)}, u32[]{:S(2)}) collective-permute-start(bf16[1,720,256]{2,1,0:T(8,128)(2,1)S(1)} %get-tuple-element.87), channel_id=1, source_target_pairs={{2,0},{4,2},{6,4},{8,6},{10,8},{12,10},{14,12},{16,14},{18,16},{20... | collective-permute-start | bytes 1105928 | tf_op jit(solution)/shard_map/ppermute | solution.py:383
  3.1 12.0 %collective-permute-start = (bf16[1,720,256]{2,1,0:T(8,128)(2,1)S(1)}, bf16[1,720,256]{2,1,0:T(8,128)(2,1)S(1)}, u32[]{:S(2)}, u32[]{:S(2)}) collective-permute-start(bf16[1,720,256]{2,1,0:T(8,128)(2,1)S(1)} %get-tuple-element.88), channel_id=1, source_target_pairs={{0,2},{2,4},{4,6},{6,8},{8,10},{10,12},{12,14},{14,16},{16,18},{18... | collective-permute-start | bytes 1105928 | tf_op jit(solution)/shard_map/ppermute | solution.py:382
  15.1 8.1 %copy-start.10 = (s32[9]{0:T(128)S(1)}, s32[9]{0:T(128)}, u32[]{:S(2)}) copy-start(s32[9]{0:T(128)} %param.20) | copy-start | bytes 112
  15.1 8.1 %copy-start.9 = (s32[9]{0:T(128)S(1)}, s32[9]{0:T(128)}, u32[]{:S(2)}) copy-start(s32[9]{0:T(128)} %param.21) | copy-start | bytes 112
  15.1 8.3 %copy-start.7 = (f32[9,256]{1,0:T(8,128)S(1)}, f32[9,256]{1,0:T(8,128)}, u32[]{:S(2)}) copy-start(f32[9,256]{1,0:T(8,128)} %param.19) | copy-start | bytes 27652
  16.0 143.0 %all-to-all-start.1 = ((bf16[32,2,24,8,256]{4,3,2,1,0:T(8,128)(2,1)}), bf16[32,2,24,8,256]{4,3,2,1,0:T(8,128)(2,1)}, u32[]{:S(2)}, u32[]{:S(2)}) async-start(bf16[32,2,24,8,256]{4,3,2,1,0:T(8,128)(2,1)} %shard_map.146), calls=%async_computation.1 | async-start | bytes 12582912 | tf_op jit(solution)/shard_map/all_to_all | solution.py:407
  50.2 5.2 %copy-start.3 = (bf16[2,512,256]{2,1,0:T(8,128)(2,1)S(1)}, bf16[2,512,256]{2,1,0:T(8,128)(2,1)}, u32[]{:S(2)}) copy-start(bf16[2,512,256]{2,1,0:T(8,128)(2,1)} %own_ref.5) | copy-start | bytes 1572868
  50.2 108.6 %collective-permute-start.3 = (bf16[4,720,256]{2,1,0:T(8,128)(2,1)S(1)}, bf16[4,720,256]{2,1,0:T(8,128)(2,1)}, u32[]{:S(2)}, u32[]{:S(2)}) collective-permute-start(bf16[4,720,256]{2,1,0:T(8,128)(2,1)S(1)} %slice.24), channel_id=1, source_target_pairs={{0,1},{1,0},{2,3},{3,2},{4,5},{5,4},{6,7},{7,6},{8,9},{9,8},{10,11... | collective-permute-start | bytes 4423688 | tf_op jit(solution)/shard_map/ppermute | solution.py:278
  54.9 104.0 %collective-permute-start.4 = (bf16[3,720,256]{2,1,0:T(8,128)(2,1)}, bf16[3,720,256]{2,1,0:T(8,128)(2,1)}, u32[]{:S(2)}, u32[]{:S(2)}) collective-permute-start(bf16[3,720,256]{2,1,0:T(8,128)(2,1)} %get-tuple-element.90), channel_id=1, source_target_pairs={{0,1},{1,0},{2,3},{3,2},{4,5},{5,4},{6,7},{7,6},{8,9},{9,8},{10,11... | collective-permute-start | bytes 3317768 | tf_op jit(solution)/shard_map/ppermute | solution.py:278
  55.4 103.5 %collective-permute-start.2 = (bf16[2,512,256]{2,1,0:T(8,128)(2,1)S(1)}, bf16[2,512,256]{2,1,0:T(8,128)(2,1)S(1)}, u32[]{:S(2)}, u32[]{:S(2)}) collective-permute-start(bf16[2,512,256]{2,1,0:T(8,128)(2,1)S(1)} %copy-done.3), channel_id=1, source_target_pairs={{0,1},{1,0},{2,3},{3,2},{4,5},{5,4},{6,7},{7,6},{8,9},{9,8},{10,11... | collective-permute-start | bytes 1572872 | tf_op jit(solution)/shard_map/ppermute | solution.py:392
  88.8 80.1 %copy-start.8 = (f32[384]{0:T(512)S(1)}, f32[384]{0:T(512)}, u32[]{:S(2)}) copy-start(f32[384]{0:T(512)} %param.18) | copy-start | bytes 4612
  159.6 75.8 %all-to-all-start = ((bf16[32,1,24,8,256]{4,3,2,1,0:T(8,128)(2,1)}), bf16[32,1,24,8,256]{4,3,2,1,0:T(8,128)(2,1)S(1)}, u32[]{:S(2)}, u32[]{:S(2)}) async-start(bf16[32,1,24,8,256]{4,3,2,1,0:T(8,128)(2,1)} %shard_map.145), calls=%async_computation | async-start | bytes 6291456 | tf_op jit(solution)/shard_map/all_to_all | solution.py:407
  166.8 57.3 %collective-permute-start.5 = (bf16[3,720,256]{2,1,0:T(8,128)(2,1)}, bf16[3,720,256]{2,1,0:T(8,128)(2,1)}, u32[]{:S(2)}, u32[]{:S(2)}) collective-permute-start(bf16[3,720,256]{2,1,0:T(8,128)(2,1)} %get-tuple-element.89), channel_id=1, source_target_pairs={{0,1},{1,0},{2,3},{3,2},{4,5},{5,4},{6,7},{7,6},{8,9},{9,8},{10,11... | collective-permute-start | bytes 3317768 | tf_op jit(solution)/shard_map/ppermute | solution.py:278
  235.4 7.8 %copy-start = (bf16[32,1,24,8,256]{4,3,2,1,0:T(8,128)(2,1)}, bf16[32,1,24,8,256]{4,3,2,1,0:T(8,128)(2,1)S(1)}, u32[]{:S(2)}) copy-start(bf16[32,1,24,8,256]{4,3,2,1,0:T(8,128)(2,1)S(1)} %all-to-all-done) | copy-start | bytes 9437188
  235.4 52.5 %all-to-all-start.2 = ((bf16[32,2,4,8,512]{4,3,2,1,0:T(8,128)(2,1)}), bf16[32,2,4,8,512]{4,3,2,1,0:T(8,128)(2,1)}, u32[]{:S(2)}, u32[]{:S(2)}) async-start(bf16[32,2,4,8,512]{4,3,2,1,0:T(8,128)(2,1)} %get-tuple-element.61), calls=%async_computation.2 | async-start | bytes 4194304 | tf_op jit(solution)/shard_map/all_to_all | solution.py:430
  243.3 37.4 %collective-permute-start.6 = (bf16[2,720,256]{2,1,0:T(8,128)(2,1)}, bf16[2,720,256]{2,1,0:T(8,128)(2,1)}, u32[]{:S(2)}, u32[]{:S(2)}) collective-permute-start(bf16[2,720,256]{2,1,0:T(8,128)(2,1)} %slice.27), channel_id=1, source_target_pairs={{0,1},{1,0},{2,3},{3,2},{4,5},{5,4},{6,7},{7,6},{8,9},{9,8},{10,11... | collective-permute-start | bytes 2211848 | tf_op jit(solution)/shard_map/ppermute | solution.py:278
  317.8 58.1 %all-to-all-start.4 = ((bf16[32,3,3,8,512]{4,3,2,1,0:T(8,128)(2,1)}), bf16[32,3,3,8,512]{4,3,2,1,0:T(8,128)(2,1)S(1)}, u32[]{:S(2)}, u32[]{:S(2)}) async-start(bf16[32,3,3,8,512]{4,3,2,1,0:T(8,128)(2,1)} %get-tuple-element.67), calls=%async_computation.4 | async-start | bytes 4718592 | tf_op jit(solution)/shard_map/all_to_all | solution.py:430
  335.8 47.3 %collective-permute-start.7 = (bf16[4,720,256]{2,1,0:T(8,128)(2,1)}, bf16[4,720,256]{2,1,0:T(8,128)(2,1)}, u32[]{:S(2)}, u32[]{:S(2)}) collective-permute-start(bf16[4,720,256]{2,1,0:T(8,128)(2,1)} %get-tuple-element.72), channel_id=1, source_target_pairs={{0,1},{1,0},{2,3},{3,2},{4,5},{5,4},{6,7},{7,6},{8,9},{9,8},{10,11... | collective-permute-start | bytes 4423688 | tf_op jit(solution)/shard_map/ppermute | solution.py:445
  375.9 7.2 %copy-start.1 = (bf16[32,3,3,8,512]{4,3,2,1,0:T(8,128)(2,1)}, bf16[32,3,3,8,512]{4,3,2,1,0:T(8,128)(2,1)S(1)}, u32[]{:S(2)}) copy-start(bf16[32,3,3,8,512]{4,3,2,1,0:T(8,128)(2,1)S(1)} %all-to-all-done.4.rest_0_) | copy-start | bytes 7077892
  383.1 58.4 %all-to-all-start.5 = ((bf16[32,3,3,8,512]{4,3,2,1,0:T(8,128)(2,1)}), bf16[32,3,3,8,512]{4,3,2,1,0:T(8,128)(2,1)}, u32[]{:S(2)}, u32[]{:S(2)}) async-start(bf16[32,3,3,8,512]{4,3,2,1,0:T(8,128)(2,1)} %get-tuple-element.73), calls=%async_computation.5 | async-start | bytes 4718592 | tf_op jit(solution)/shard_map/all_to_all | solution.py:430
  399.1 42.4 %collective-permute-start.8 = (bf16[3,720,256]{2,1,0:T(8,128)(2,1)}, bf16[3,720,256]{2,1,0:T(8,128)(2,1)S(1)}, u32[]{:S(2)}, u32[]{:S(2)}) collective-permute-start(bf16[3,720,256]{2,1,0:T(8,128)(2,1)} %get-tuple-element.78), channel_id=1, source_target_pairs={{0,1},{1,0},{2,3},{3,2},{4,5},{5,4},{6,7},{7,6},{8,9},{9,8},{10,11... | collective-permute-start | bytes 3317768 | tf_op jit(solution)/shard_map/ppermute | solution.py:445
  441.5 41.0 %all-to-all-start.6 = ((bf16[32,3,2,8,512]{4,3,2,1,0:T(8,128)(2,1)}), bf16[32,3,2,8,512]{4,3,2,1,0:T(8,128)(2,1)S(1)}, u32[]{:S(2)}, u32[]{:S(2)}) async-start(bf16[32,3,2,8,512]{4,3,2,1,0:T(8,128)(2,1)} %get-tuple-element.79), calls=%async_computation.6 | async-start | bytes 3145728 | tf_op jit(solution)/shard_map/all_to_all | solution.py:430
  457.2 39.4 %collective-permute-start.9 = (bf16[3,720,256]{2,1,0:T(8,128)(2,1)}, bf16[3,720,256]{2,1,0:T(8,128)(2,1)}, u32[]{:S(2)}, u32[]{:S(2)}) collective-permute-start(bf16[3,720,256]{2,1,0:T(8,128)(2,1)} %get-tuple-element.85), channel_id=1, source_target_pairs={{0,1},{1,0},{2,3},{3,2},{4,5},{5,4},{6,7},{7,6},{8,9},{9,8},{10,11... | collective-permute-start | bytes 3317768 | tf_op jit(solution)/shard_map/ppermute | solution.py:445
  491.6 18.8 %collective-permute-start.10 = (bf16[2,720,256]{2,1,0:T(8,128)(2,1)}, bf16[2,720,256]{2,1,0:T(8,128)(2,1)S(1)}, u32[]{:S(2)}, u32[]{:S(2)}) collective-permute-start(bf16[2,720,256]{2,1,0:T(8,128)(2,1)} %get-tuple-element.86), channel_id=1, source_target_pairs={{0,1},{1,0},{2,3},{3,2},{4,5},{5,4},{6,7},{7,6},{8,9},{9,8},{10,11... | collective-permute-start | bytes 2211848 | tf_op jit(solution)/shard_map/ppermute | solution.py:445
  (4 other events, 3.6 us)

commit v11 on v10

--- a/solution.py
+++ b/solution.py
@@ -434,9 +434,9 @@
     sent = []
 
     def finished(at, backs, tables, result):
-        pieces = [counts[at]]
+        pieces = [counts[at] - 1, 1] if at == 0 and counts[at] > 1 else [counts[at]]
         low = 0
-        needed = []
+        needed = sent[1:2] if at == 1 else []
         for count in pieces:
             result, theirs = tail_part(
                 backs, tables, own, got[at], sum(counts[:at]), low, count, ln_gain[None, :],

time: 515 us -> 515 us (level)
    pallas_call x4 -> x5, Pallas kernels: 40.1 us -> 43.6 us  [tail_part(): pl.pallas_call(functools.partial(tail_kernel, len(backs)), out_shape=[jax...]
    ppermute x4 -> x5, waiting for transfers between devices: 18.5 us -> 18.3 us  [finished(): sent.append(lax.ppermute(theirs, 'chan', SWAP))]
  transfers between devices with their start and end apart: 17 -> 18, of which waited for: 11 -> 11; matrix products, arithmetic and copies ran while one was open for 4% -> 4% of each run, Pallas kernels for 30% -> 30%
where the time goes in v11:
time: 515 us; the launch traced here: 510 us
  waiting for transfers between devices  249 us (48%)
  Pallas kernels  155 us (30%)
  starting transfers between devices  52 us (10%)
  blocking collectives  29.9 us (6%)
  local copies, waits for them, and re-layouts  20.2 us (4%)
    all_to_all x4, waiting for transfers between devices, shuffled(): return lax.all_to_all(value, ('lat', 'chan'), 0, 0, tiled=True)  107 us
    ppermute x1, waiting for transfers between devices, fast(): other = lax.ppermute(mix_weight, 'chan', SWAP)  68.7 us
    pallas_call x2, Pallas kernels, local_part(): pl.pallas_call(local_rows, out_shape=jax.ShapeDtypeStruct((span, nlon, wi...  47.9 us
    pallas_call x3, Pallas kernels, middle_part(): pl.pallas_call(functools.partial(middle_kernel, plan), out_shape=[jax.Sha...  46.1 us
    pallas_call x5, Pallas kernels, tail_part(): pl.pallas_call(functools.partial(tail_kernel, len(backs)), out_shape=[jax...  43.6 us
    ppermute x4, waiting for transfers between devices, exchanged(): got.append(lax.ppermute(piece, 'chan', SWAP))  43.4 us
    all_to_all x1, blocking collectives, shuffled(): return lax.all_to_all(value, ('lat', 'chan'), 0, 0, tiled=True)  29.9 us
    all_to_all x4, starting transfers between devices, shuffled(): return lax.all_to_all(value, ('lat', 'chan'), 0, 0, tiled=True)  22.2 us
  transfers between devices with their start and end apart: 18, of which 11 were waited for; matrix products, arithmetic and copies ran while one was open for 4% of the time, Pallas kernels for 30%

profile of v11, /device:TPU:26, one launch (start us, length us, event | category | flops | bytes accessed | tf_op | source)
XLA Modules:
  0.0 510.4 jit_solution(9348354007071234654)
XLA Ops:
  5.5 9.6 %shard_map.146 = bf16[32,2,24,8,256]{4,3,2,1,0:T(8,128)(2,1)} custom-call(bf16[512,720]{1,0:T(8,128)(2,1)} %constant.70.clone.table_ref, bf16[24,720,256]{2,1,0:T(8,128)(2,1)} %after_ref.3), custom_call_target="tpu_custom_call" | custom-call | flops 4529848320 | bytes 8847360 | tf_op jit(solution)/shard_map/pallas_call | solution.py:54
  16.0 6.4 %all-to-all-start.1 = ((bf16[32,2,24,8,256]{4,3,2,1,0:T(8,128)(2,1)}), bf16[32,2,24,8,256]{4,3,2,1,0:T(8,128)(2,1)}, u32[]{:S(2)}, u32[]{:S(2)}) async-start(bf16[32,2,24,8,256]{4,3,2,1,0:T(8,128)(2,1)} %shard_map.146), calls=%async_computation.1 | async-start | bytes 12582912 | tf_op jit(solution)/shard_map/all_to_all | solution.py:407
  24.8 23.9 %shard_map.148 = bf16[12,720,256]{2,1,0:T(8,128)(2,1)} custom-call(s32[2]{0:T(128)} %pad_add_fusion.base_ref, f32[24,3]{1,0:T(8,128)} %sine_divide_fusion.ratio_ref, f32[3,7,256]{2,1,0:T(8,128)} %select_reduce_fusion.weight_ref, bf16[24,720,256]{2,1,0:T(8,128)(2,1)} %after_ref.3, bf16[24,720,256]{2,1,0:T(8,128)(2,1)} %after_ref.3, ...), custom_call_target="tpu_custom_call" | custom-call | flops 884736000 | bytes 13271040 | tf_op jit(solution)/shard_map/pallas_call | solution.py:251
  58.6 7.5 %shard_map.145 = bf16[32,1,24,8,256]{4,3,2,1,0:T(8,128)(2,1)} custom-call(bf16[256,720]{1,0:T(8,128)(2,1)} %constant.71.clone.table_ref, bf16[24,720,256]{2,1,0:T(8,128)(2,1)} %after_ref.3), custom_call_target="tpu_custom_call" | custom-call | flops 2264924160 | bytes 8847360 | tf_op jit(solution)/shard_map/pallas_call | solution.py:54
  66.1 24.0 %shard_map.147.own_ref = bf16[12,720,256]{2,1,0:T(8,128)(2,1)} custom-call(s32[2]{0:T(128)} %pad_add_fusion.1.base_ref, f32[24,3]{1,0:T(8,128)} %sine_divide_fusion.ratio_ref, f32[3,7,256]{2,1,0:T(8,128)} %select_reduce_fusion.weight_ref, bf16[24,720,256]{2,1,0:T(8,128)(2,1)} %after_ref.3, bf16[24,720,256]{2,1,0:T(8,128)(2,1)} %after_ref.3, ...), custom_call_target="tpu_custom_call" | custom-call | flops 884736000 | bytes 13271040 | tf_op jit(solution)/shard_map/pallas_call | solution.py:251
  90.1 68.7 %collective-permute-done.2.other_ref = bf16[2,512,256]{2,1,0:T(8,128)(2,1)S(1)} collective-permute-done((bf16[2,512,256]{2,1,0:T(8,128)(2,1)S(1)}, bf16[2,512,256]{2,1,0:T(8,128)(2,1)S(1)}, u32[]{:S(2)}, u32[]{:S(2)}) %collective-permute-start.2) | collective-permute-done | bytes 524320 | tf_op jit(solution)/shard_map/ppermute | solution.py:392
  160.1 6.1 %all-to-all-start = ((bf16[32,1,24,8,256]{4,3,2,1,0:T(8,128)(2,1)}), bf16[32,1,24,8,256]{4,3,2,1,0:T(8,128)(2,1)S(1)}, u32[]{:S(2)}, u32[]{:S(2)}) async-start(bf16[32,1,24,8,256]{4,3,2,1,0:T(8,128)(2,1)} %shard_map.145), calls=%async_computation | async-start | bytes 6291456 | tf_op jit(solution)/shard_map/all_to_all | solution.py:407
  169.8 15.4 %shard_map.149 = (bf16[32,2,4,8,512]{4,3,2,1,0:T(8,128)(2,1)}, bf16[32,3,3,8,512]{4,3,2,1,0:T(8,128)(2,1)}, bf16[32,3,3,8,512]{4,3,2,1,0:T(8,128)(2,1)}, bf16[32,3,2,8,512]{4,3,2,1,0:T(8,128)(2,1)}) custom-call(s32[2]{0:T(128)} %get-tuple-element.96.at_ref.place_ref, bf16[16,2,2,24,8,256]{5,4,3,2,1,0:T(8,128)(2,1)} %bitcast.6.spec_ref, ...), custom_call_target="tpu_custom_call" | custom-call | flops 5637144576 | bytes 9175040 | tf_op jit(solution)/shard_map/pallas_call | solution.py:152
  185.2 15.4 %shard_map.150 = (bf16[32,2,4,8,512]{4,3,2,1,0:T(8,128)(2,1)}, bf16[32,3,3,8,512]{4,3,2,1,0:T(8,128)(2,1)}, bf16[32,3,3,8,512]{4,3,2,1,0:T(8,128)(2,1)}, bf16[32,3,2,8,512]{4,3,2,1,0:T(8,128)(2,1)}) custom-call(s32[2]{0:T(128)} %get-tuple-element.95.at_ref, ...), custom_call_target="tpu_custom_call", output_to_operand_aliasing={{0}: (7, {}), {1}: (8, {}), {2}: (9, {}), {3}: (10, {})} | custom-call | flops 5637144576 | bytes 9175040 | tf_op jit(solution)/shard_map/pallas_call | solution.py:152
  200.6 23.5 %collective-permute-done.5.got_ref = bf16[3,720,256]{2,1,0:T(8,128)(2,1)} collective-permute-done((bf16[3,720,256]{2,1,0:T(8,128)(2,1)}, bf16[3,720,256]{2,1,0:T(8,128)(2,1)}, u32[]{:S(2)}, u32[]{:S(2)}) %collective-permute-start.5) | collective-permute-done | bytes 1105952 | tf_op jit(solution)/shard_map/ppermute | solution.py:278
  224.1 11.3 %all-to-all-done = bf16[32,1,24,8,256]{4,3,2,1,0:T(8,128)(2,1)S(1)} async-done(((bf16[32,1,24,8,256]{4,3,2,1,0:T(8,128)(2,1)}), bf16[32,1,24,8,256]{4,3,2,1,0:T(8,128)(2,1)S(1)}, u32[]{:S(2)}, u32[]{:S(2)}) %all-to-all-start) | async-done | bytes 3145760 | tf_op jit(solution)/shard_map/all_to_all | solution.py:407
  245.4 15.3 %shard_map.151 = (bf16[32,1,4,8,512]{4,3,2,1,0:T(8,128)(2,1)}, bf16[32,3,3,8,512]{4,3,2,1,0:T(8,128)(2,1)}, bf16[32,3,3,8,512]{4,3,2,1,0:T(8,128)(2,1)}, bf16[32,3,2,8,512]{4,3,2,1,0:T(8,128)(2,1)}) custom-call(s32[2]{0:T(128)} %pad_add_fusion.2.at_ref, ...), custom_call_target="tpu_custom_call", output_to_operand_aliasing={{1}: (7, {}), {2}: (8, {}), {3}: (9, {})} | custom-call | flops 5637144576 | bytes 9175040 | tf_op jit(solution)/shard_map/pallas_call | solution.py:152
  260.7 19.9 %collective-permute-done.6.got_ref = bf16[2,720,256]{2,1,0:T(8,128)(2,1)} collective-permute-done((bf16[2,720,256]{2,1,0:T(8,128)(2,1)}, bf16[2,720,256]{2,1,0:T(8,128)(2,1)}, u32[]{:S(2)}, u32[]{:S(2)}) %collective-permute-start.6) | collective-permute-done | bytes 737312 | tf_op jit(solution)/shard_map/ppermute | solution.py:278
  280.6 7.3 %all-to-all-done.2.rest_0_ = bf16[32,2,4,8,512]{4,3,2,1,0:T(8,128)(2,1)} async-done(((bf16[32,2,4,8,512]{4,3,2,1,0:T(8,128)(2,1)}), bf16[32,2,4,8,512]{4,3,2,1,0:T(8,128)(2,1)}, u32[]{:S(2)}, u32[]{:S(2)}) %all-to-all-start.2) | async-done | bytes 2097184 | tf_op jit(solution)/shard_map/all_to_all | solution.py:430
  287.9 29.9 %all_to_all.35.rest_1_ = bf16[32,1,4,8,512]{4,3,2,1,0:T(8,128)(2,1)} all-to-all(bf16[32,1,4,8,512]{4,3,2,1,0:T(8,128)(2,1)} %get-tuple-element.68), channel_id=1, replica_groups=mesh['lat'=16,'chan'=2] {'lat','chan'}, dimensions={0} | all-to-all | bytes 2097152 | tf_op jit(solution)/shard_map/all_to_all | solution.py:430
  323.6 10.0 %shard_map.152 = (bf16[24,720,256]{2,1,0:T(8,128)(2,1)}, bf16[3,720,256]{2,1,0:T(8,128)(2,1)}) custom-call(s32[2]{0:T(128)} %get-tuple-element.96.at_ref.place_ref, bf16[12,720,256]{2,1,0:T(8,128)(2,1)} %shard_map.147.own_ref, bf16[4,720,256]{2,1,0:T(8,128)(2,1)} %copy-done.7, f32[1,512]{1,0:T(1,128)} %bitcast.9, bf16[512,512]{1,0:T(8,128)(2,1)} %up_ref.9, ...), custom_call_target="tpu_custom_call" | custom-call | flops 3963617280 | bytes 8847360 | tf_op jit(solution)/shard_map/pallas_call | solution.py:332
  340.7 35.2 %all-to-all-done.4.rest_0_ = bf16[32,3,3,8,512]{4,3,2,1,0:T(8,128)(2,1)S(1)} async-done(((bf16[32,3,3,8,512]{4,3,2,1,0:T(8,128)(2,1)}), bf16[32,3,3,8,512]{4,3,2,1,0:T(8,128)(2,1)S(1)}, u32[]{:S(2)}, u32[]{:S(2)}) %all-to-all-start.4) | async-done | bytes 2359328 | tf_op jit(solution)/shard_map/all_to_all | solution.py:430
  383.0 10.0 %shard_map.154 = (bf16[24,720,256]{2,1,0:T(8,128)(2,1)}, bf16[3,720,256]{2,1,0:T(8,128)(2,1)}) custom-call(s32[2]{0:T(128)} %get-tuple-element.96.at_ref.place_ref, bf16[12,720,256]{2,1,0:T(8,128)(2,1)} %shard_map.147.own_ref, bf16[3,720,256]{2,1,0:T(8,128)(2,1)} %collective-permute-done.4.got_ref, ...), custom_call_target="tpu_custom_call", output_to_operand_aliasing={{0}: (8, {})} | custom-call | flops 3963617280 | bytes 8847360 | tf_op jit(solution)/shard_map/pallas_call | solution.py:332
  395.0 40.3 %all-to-all-done.5.rest_0_ = bf16[32,3,3,8,512]{4,3,2,1,0:T(8,128)(2,1)S(1)} async-done(((bf16[32,3,3,8,512]{4,3,2,1,0:T(8,128)(2,1)}), bf16[32,3,3,8,512]{4,3,2,1,0:T(8,128)(2,1)S(1)}, u32[]{:S(2)}, u32[]{:S(2)}) %all-to-all-start.5) | async-done | bytes 2359328 | tf_op jit(solution)/shard_map/all_to_all | solution.py:430
  435.3 7.2 %collective-permute-done.8 = bf16[1,720,256]{2,1,0:T(8,128)(2,1)} collective-permute-done((bf16[1,720,256]{2,1,0:T(8,128)(2,1)}, bf16[1,720,256]{2,1,0:T(8,128)(2,1)}, u32[]{:S(2)}, u32[]{:S(2)}) %collective-permute-start.8) | collective-permute-done | bytes 368672 | tf_op jit(solution)/shard_map/ppermute | solution.py:445
  447.5 10.0 %shard_map.155 = (bf16[24,720,256]{2,1,0:T(8,128)(2,1)}, bf16[3,720,256]{2,1,0:T(8,128)(2,1)}) custom-call(s32[2]{0:T(128)} %get-tuple-element.96.at_ref.place_ref, bf16[12,720,256]{2,1,0:T(8,128)(2,1)} %shard_map.147.own_ref, bf16[3,720,256]{2,1,0:T(8,128)(2,1)} %collective-permute-done.5.got_ref, ...), custom_call_target="tpu_custom_call", output_to_operand_aliasing={{0}: (8, {})} | custom-call | flops 3963617280 | bytes 8847360 | tf_op jit(solution)/shard_map/pallas_call | solution.py:332
  459.0 23.8 %all-to-all-done.6.rest_0_ = bf16[32,3,2,8,512]{4,3,2,1,0:T(8,128)(2,1)} async-done(((bf16[32,3,2,8,512]{4,3,2,1,0:T(8,128)(2,1)}), bf16[32,3,2,8,512]{4,3,2,1,0:T(8,128)(2,1)}, u32[]{:S(2)}, u32[]{:S(2)}) %all-to-all-start.6) | async-done | bytes 1572896 | tf_op jit(solution)/shard_map/all_to_all | solution.py:430
  482.8 7.9 %shard_map.156 = (bf16[24,720,256]{2,1,0:T(8,128)(2,1)}, bf16[2,720,256]{2,1,0:T(8,128)(2,1)}) custom-call(s32[2]{0:T(128)} %get-tuple-element.96.at_ref.place_ref, bf16[12,720,256]{2,1,0:T(8,128)(2,1)} %shard_map.147.own_ref, bf16[2,720,256]{2,1,0:T(8,128)(2,1)} %collective-permute-done.6.got_ref, ...), custom_call_target="tpu_custom_call", output_to_operand_aliasing={{0}: (8, {})} | custom-call | flops 2642411520 | bytes 5898240 | tf_op jit(solution)/shard_map/pallas_call | solution.py:332
  498.3 11.2 %collective-permute-done.11 = bf16[2,720,256]{2,1,0:T(8,128)(2,1)S(1)} collective-permute-done((bf16[2,720,256]{2,1,0:T(8,128)(2,1)}, bf16[2,720,256]{2,1,0:T(8,128)(2,1)S(1)}, u32[]{:S(2)}, u32[]{:S(2)}) %collective-permute-start.11) | collective-permute-done | bytes 737312 | tf_op jit(solution)/shard_map/ppermute | solution.py:445
  (73 shorter events, 70.5 us)
Async XLA Ops:
  1.1 13.9 %collective-permute-start.1 = (bf16[1,720,256]{2,1,0:T(8,128)(2,1)S(1)}, bf16[1,720,256]{2,1,0:T(8,128)(2,1)S(1)}, u32[]{:S(2)}, u32[]{:S(2)}) collective-permute-start(bf16[1,720,256]{2,1,0:T(8,128)(2,1)S(1)} %get-tuple-element.91), channel_id=1, source_target_pairs={{2,0},{4,2},{6,4},{8,6},{10,8},{12,10},{14,12},{16,14},{18,16},{20... | collective-permute-start | bytes 1105928 | tf_op jit(solution)/shard_map/ppermute | solution.py:383
  3.1 12.0 %collective-permute-start = (bf16[1,720,256]{2,1,0:T(8,128)(2,1)S(1)}, bf16[1,720,256]{2,1,0:T(8,128)(2,1)S(1)}, u32[]{:S(2)}, u32[]{:S(2)}) collective-permute-start(bf16[1,720,256]{2,1,0:T(8,128)(2,1)S(1)} %get-tuple-element.92), channel_id=1, source_target_pairs={{0,2},{2,4},{4,6},{6,8},{8,10},{10,12},{12,14},{14,16},{16,18},{18... | collective-permute-start | bytes 1105928 | tf_op jit(solution)/shard_map/ppermute | solution.py:382
  15.1 8.1 %copy-start.11 = (s32[9]{0:T(128)S(1)}, s32[9]{0:T(128)}, u32[]{:S(2)}) copy-start(s32[9]{0:T(128)} %param.20) | copy-start | bytes 112
  15.1 8.2 %copy-start.10 = (s32[9]{0:T(128)S(1)}, s32[9]{0:T(128)}, u32[]{:S(2)}) copy-start(s32[9]{0:T(128)} %param.21) | copy-start | bytes 112
  15.1 8.3 %copy-start.8 = (f32[9,256]{1,0:T(8,128)S(1)}, f32[9,256]{1,0:T(8,128)}, u32[]{:S(2)}) copy-start(f32[9,256]{1,0:T(8,128)} %param.19) | copy-start | bytes 27652
  16.0 143.0 %all-to-all-start.1 = ((bf16[32,2,24,8,256]{4,3,2,1,0:T(8,128)(2,1)}), bf16[32,2,24,8,256]{4,3,2,1,0:T(8,128)(2,1)}, u32[]{:S(2)}, u32[]{:S(2)}) async-start(bf16[32,2,24,8,256]{4,3,2,1,0:T(8,128)(2,1)} %shard_map.146), calls=%async_computation.1 | async-start | bytes 12582912 | tf_op jit(solution)/shard_map/all_to_all | solution.py:407
  51.3 107.5 %collective-permute-start.3 = (bf16[4,720,256]{2,1,0:T(8,128)(2,1)}, bf16[4,720,256]{2,1,0:T(8,128)(2,1)S(1)}, u32[]{:S(2)}, u32[]{:S(2)}) collective-permute-start(bf16[4,720,256]{2,1,0:T(8,128)(2,1)} %slice.24), channel_id=1, source_target_pairs={{0,1},{1,0},{2,3},{3,2},{4,5},{5,4},{6,7},{7,6},{8,9},{9,8},{10,11... | collective-permute-start | bytes 4423688 | tf_op jit(solution)/shard_map/ppermute | solution.py:278
  55.9 102.9 %collective-permute-start.4 = (bf16[3,720,256]{2,1,0:T(8,128)(2,1)}, bf16[3,720,256]{2,1,0:T(8,128)(2,1)}, u32[]{:S(2)}, u32[]{:S(2)}) collective-permute-start(bf16[3,720,256]{2,1,0:T(8,128)(2,1)} %get-tuple-element.94), channel_id=1, source_target_pairs={{0,1},{1,0},{2,3},{3,2},{4,5},{5,4},{6,7},{7,6},{8,9},{9,8},{10,11... | collective-permute-start | bytes 3317768 | tf_op jit(solution)/shard_map/ppermute | solution.py:278
  56.5 102.4 %collective-permute-start.2 = (bf16[2,512,256]{2,1,0:T(8,128)(2,1)S(1)}, bf16[2,512,256]{2,1,0:T(8,128)(2,1)S(1)}, u32[]{:S(2)}, u32[]{:S(2)}) collective-permute-start(bf16[2,512,256]{2,1,0:T(8,128)(2,1)S(1)} %copy-done.3), channel_id=1, source_target_pairs={{0,1},{1,0},{2,3},{3,2},{4,5},{5,4},{6,7},{7,6},{8,9},{9,8},{10,11... | collective-permute-start | bytes 1572872 | tf_op jit(solution)/shard_map/ppermute | solution.py:392
  90.1 78.9 %copy-start.9 = (f32[384]{0:T(512)S(1)}, f32[384]{0:T(512)}, u32[]{:S(2)}) copy-start(f32[384]{0:T(512)} %param.18) | copy-start | bytes 4612
  160.1 75.3 %all-to-all-start = ((bf16[32,1,24,8,256]{4,3,2,1,0:T(8,128)(2,1)}), bf16[32,1,24,8,256]{4,3,2,1,0:T(8,128)(2,1)S(1)}, u32[]{:S(2)}, u32[]{:S(2)}) async-start(bf16[32,1,24,8,256]{4,3,2,1,0:T(8,128)(2,1)} %shard_map.145), calls=%async_computation | async-start | bytes 6291456 | tf_op jit(solution)/shard_map/all_to_all | solution.py:407
  166.8 57.3 %collective-permute-start.5 = (bf16[3,720,256]{2,1,0:T(8,128)(2,1)}, bf16[3,720,256]{2,1,0:T(8,128)(2,1)}, u32[]{:S(2)}, u32[]{:S(2)}) collective-permute-start(bf16[3,720,256]{2,1,0:T(8,128)(2,1)} %get-tuple-element.93), channel_id=1, source_target_pairs={{0,1},{1,0},{2,3},{3,2},{4,5},{5,4},{6,7},{7,6},{8,9},{9,8},{10,11... | collective-permute-start | bytes 3317768 | tf_op jit(solution)/shard_map/ppermute | solution.py:278
  235.4 7.8 %copy-start = (bf16[32,1,24,8,256]{4,3,2,1,0:T(8,128)(2,1)}, bf16[32,1,24,8,256]{4,3,2,1,0:T(8,128)(2,1)S(1)}, u32[]{:S(2)}) copy-start(bf16[32,1,24,8,256]{4,3,2,1,0:T(8,128)(2,1)S(1)} %all-to-all-done) | copy-start | bytes 9437188
  235.4 52.5 %all-to-all-start.2 = ((bf16[32,2,4,8,512]{4,3,2,1,0:T(8,128)(2,1)}), bf16[32,2,4,8,512]{4,3,2,1,0:T(8,128)(2,1)}, u32[]{:S(2)}, u32[]{:S(2)}) async-start(bf16[32,2,4,8,512]{4,3,2,1,0:T(8,128)(2,1)} %get-tuple-element.63), calls=%async_computation.2 | async-start | bytes 4194304 | tf_op jit(solution)/shard_map/all_to_all | solution.py:430
  243.2 37.4 %collective-permute-start.6 = (bf16[2,720,256]{2,1,0:T(8,128)(2,1)}, bf16[2,720,256]{2,1,0:T(8,128)(2,1)}, u32[]{:S(2)}, u32[]{:S(2)}) collective-permute-start(bf16[2,720,256]{2,1,0:T(8,128)(2,1)} %slice.27), channel_id=1, source_target_pairs={{0,1},{1,0},{2,3},{3,2},{4,5},{5,4},{6,7},{7,6},{8,9},{9,8},{10,11... | collective-permute-start | bytes 2211848 | tf_op jit(solution)/shard_map/ppermute | solution.py:278
  317.8 58.1 %all-to-all-start.4 = ((bf16[32,3,3,8,512]{4,3,2,1,0:T(8,128)(2,1)}), bf16[32,3,3,8,512]{4,3,2,1,0:T(8,128)(2,1)S(1)}, u32[]{:S(2)}, u32[]{:S(2)}) async-start(bf16[32,3,3,8,512]{4,3,2,1,0:T(8,128)(2,1)} %get-tuple-element.69), calls=%async_computation.4 | async-start | bytes 4718592 | tf_op jit(solution)/shard_map/all_to_all | solution.py:430
  333.6 42.3 %collective-permute-start.7 = (bf16[3,720,256]{2,1,0:T(8,128)(2,1)}, bf16[3,720,256]{2,1,0:T(8,128)(2,1)S(1)}, u32[]{:S(2)}, u32[]{:S(2)}) collective-permute-start(bf16[3,720,256]{2,1,0:T(8,128)(2,1)} %get-tuple-element.74), channel_id=1, source_target_pairs={{0,1},{1,0},{2,3},{3,2},{4,5},{5,4},{6,7},{7,6},{8,9},{9,8},{10,11... | collective-permute-start | bytes 3317768 | tf_op jit(solution)/shard_map/ppermute | solution.py:445
  377.3 58.0 %all-to-all-start.5 = ((bf16[32,3,3,8,512]{4,3,2,1,0:T(8,128)(2,1)}), bf16[32,3,3,8,512]{4,3,2,1,0:T(8,128)(2,1)S(1)}, u32[]{:S(2)}, u32[]{:S(2)}) async-start(bf16[32,3,3,8,512]{4,3,2,1,0:T(8,128)(2,1)} %get-tuple-element.77), calls=%async_computation.5 | async-start | bytes 4718592 | tf_op jit(solution)/shard_map/all_to_all | solution.py:430
  393.0 49.5 %collective-permute-start.9 = (bf16[3,720,256]{2,1,0:T(8,128)(2,1)}, bf16[3,720,256]{2,1,0:T(8,128)(2,1)}, u32[]{:S(2)}, u32[]{:S(2)}) collective-permute-start(bf16[3,720,256]{2,1,0:T(8,128)(2,1)} %get-tuple-element.82), channel_id=1, source_target_pairs={{0,1},{1,0},{2,3},{3,2},{4,5},{5,4},{6,7},{7,6},{8,9},{9,8},{10,11... | collective-permute-start | bytes 3317768 | tf_op jit(solution)/shard_map/ppermute | solution.py:445
  394.5 48.0 %collective-permute-start.8 = (bf16[1,720,256]{2,1,0:T(8,128)(2,1)}, bf16[1,720,256]{2,1,0:T(8,128)(2,1)}, u32[]{:S(2)}, u32[]{:S(2)}) collective-permute-start(bf16[1,720,256]{2,1,0:T(8,128)(2,1)} %get-tuple-element.76), channel_id=1, source_target_pairs={{0,1},{1,0},{2,3},{3,2},{4,5},{5,4},{6,7},{7,6},{8,9},{9,8},{10,11... | collective-permute-start | bytes 1105928 | tf_op jit(solution)/shard_map/ppermute | solution.py:445
  435.3 12.1 %copy-start.1 = (bf16[32,3,3,8,512]{4,3,2,1,0:T(8,128)(2,1)}, bf16[32,3,3,8,512]{4,3,2,1,0:T(8,128)(2,1)S(1)}, u32[]{:S(2)}) copy-start(bf16[32,3,3,8,512]{4,3,2,1,0:T(8,128)(2,1)S(1)} %all-to-all-done.5.rest_0_) | copy-start | bytes 7077892
  442.5 40.3 %all-to-all-start.6 = ((bf16[32,3,2,8,512]{4,3,2,1,0:T(8,128)(2,1)}), bf16[32,3,2,8,512]{4,3,2,1,0:T(8,128)(2,1)}, u32[]{:S(2)}, u32[]{:S(2)}) async-start(bf16[32,3,2,8,512]{4,3,2,1,0:T(8,128)(2,1)} %get-tuple-element.83), calls=%async_computation.6 | async-start | bytes 3145728 | tf_op jit(solution)/shard_map/all_to_all | solution.py:430
  457.5 39.8 %collective-permute-start.10 = (bf16[3,720,256]{2,1,0:T(8,128)(2,1)}, bf16[3,720,256]{2,1,0:T(8,128)(2,1)S(1)}, u32[]{:S(2)}, u32[]{:S(2)}) collective-permute-start(bf16[3,720,256]{2,1,0:T(8,128)(2,1)} %get-tuple-element.89), channel_id=1, source_target_pairs={{0,1},{1,0},{2,3},{3,2},{4,5},{5,4},{6,7},{7,6},{8,9},{9,8},{10,11... | collective-permute-start | bytes 3317768 | tf_op jit(solution)/shard_map/ppermute | solution.py:445
  490.7 18.8 %collective-permute-start.11 = (bf16[2,720,256]{2,1,0:T(8,128)(2,1)}, bf16[2,720,256]{2,1,0:T(8,128)(2,1)S(1)}, u32[]{:S(2)}, u32[]{:S(2)}) collective-permute-start(bf16[2,720,256]{2,1,0:T(8,128)(2,1)} %get-tuple-element.90), channel_id=1, source_target_pairs={{0,1},{1,0},{2,3},{3,2},{4,5},{5,4},{6,7},{7,6},{8,9},{9,8},{10,11... | collective-permute-start | bytes 2211848 | tf_op jit(solution)/shard_map/ppermute | solution.py:445
  (6 other events, 10.2 us)
